TPU v7x, 32 devices: a whole 2x2x4 slice. The times are simulated.
32 devices in a mesh: groups: 2 (over y), row: 4 (over z), col: 2 (over x), sub: 2 (over core).
Axes of the slice: x: 2, y: 2, z: 4, core: 2. Of those that a mesh axis runs over, the one named last changes fastest.
Arguments:
- student: bfloat16 [1024, 1024], P(('groups', 'row', 'col'), 'sub'), parts along dimension 0, may hold values from -0.1875 to 0.1875
- teacher: bfloat16 [1024, 4096], P(('groups', 'row', 'col'), 'sub'), parts along dimension 0, may hold values from -6 to 6
- scale: bfloat16 [1024], P(('groups', 'row', 'col')), parts along dimension 0, may hold values from 0.2 to 36, as said below
Outputs:
- student_grad: float32 [1024, 1024], P(('groups', 'row', 'col'), 'sub'), parts along dimension 0
There are 2 independent parts, one for each index of `groups`. A program takes and returns all parts, laid end to end along the dimension named above; each array names one. Nothing has to cross between parts.
Inputs may be any that keep to these rules, and one draw needn't show every extreme that they name: `scale`: positive scales.
All inputs are finite; a program needn't handle non-finite values.
Results may differ from a plain program's by a relative error of at most 0.0075.
Values may be sent and summed in bfloat16 or wider, within the bound.
No kernel may reach another device: no remote copies, remote signals or barrier semaphores. Data moves between devices by JAX's collectives and lax.ppermute only.
A program may use at most 64 MiB of HBM per device.

v0:
```python
import jax
import jax.numpy as jnp
from jax import lax
from jax.sharding import PartitionSpec as P


def shards(student, teacher, scale):
    xs = student.astype(jnp.float32)
    row_norm = jnp.sqrt(lax.psum(jnp.sum(xs * xs, axis=1), "sub"))
    unit = xs / row_norm[:, None]
    unit_b = unit.astype(jnp.bfloat16)
    scales = scale.astype(jnp.float32)
    local_mass = jnp.sum(scales * scales * jnp.sum(jnp.square(teacher.astype(jnp.float32)), axis=1))
    own_rows = student.shape[0]
    n_rowgroups = lax.axis_size("row")
    n_colgroups = lax.axis_size("col")
    batch_rows = own_rows * n_rowgroups * n_colgroups
    mass = lax.psum(local_mass, ("row", "col", "sub")) / batch_rows
    row_unit, row_teach, row_scale = (
        lax.all_gather(unit_b, "col", axis=0, tiled=True),
        lax.all_gather(teacher, "col", axis=0, tiled=True),
        lax.all_gather(scale, "col", axis=0, tiled=True),
    )
    col_unit, col_teach, col_scale = (
        lax.all_gather(unit_b, "row", axis=0, tiled=True),
        lax.all_gather(teacher, "row", axis=0, tiled=True),
        lax.all_gather(scale, "row", axis=0, tiled=True),
    )
    inner = (((1,), (1,)), ((), ()))
    student_gram = lax.dot_general(row_unit, col_unit, inner, preferred_element_type=jnp.float32)
    teacher_gram = lax.dot_general(row_teach, col_teach, inner, preferred_element_type=jnp.float32)
    outer_scale = row_scale.astype(jnp.float32)[:, None] * col_scale.astype(jnp.float32)[None, :]
    partial_err = student_gram - outer_scale * teacher_gram / mass
    error_b = lax.psum(partial_err, "sub").astype(jnp.bfloat16)
    by_rows = lax.psum_scatter(
        jnp.dot(error_b, col_unit, preferred_element_type=jnp.float32),
        "col",
        scatter_dimension=0,
        tiled=True,
    )
    grads = 4.0 * by_rows
    along = lax.psum(jnp.sum(grads * unit, axis=1), "sub")
    return (grads - along[:, None] * unit) / row_norm[:, None]


def solution(mesh):
    return jax.shard_map(
        shards,
        mesh=mesh,
        in_specs=(
            P(("groups", "row", "col"), "sub"),
            P(("groups", "row", "col"), "sub"),
            P(("groups", "row", "col")),
        ),
        out_specs=P(("groups", "row", "col"), "sub"),
        check_vma=False,
    )
```

profile of v0, /device:TPU:0, one launch (start us, length us, event | category | flops | bytes accessed | tf_op | source)
XLA Modules:
  0.0 120.3 jit_solution(7340502996293162222)
XLA Ops:
  6.5 0.0 copy-start
  6.5 0.0 all-gather.2.cloned.1.call-start
  6.5 0.7 all-gather.2.cloned.1.call-update
  7.3 0.0 copy-start.3
  7.3 0.0 reduce-scatter.2.cloned.1.call-start
  7.3 0.2 copy-done
  7.5 0.0 copy-start.1
  7.5 0.2 multiply_reduce_fusion
  7.6 0.3 copy-done.3
  7.9 0.6 multiply_reduce_fusion.2
  8.5 36.0 %psum.29 = f32[]{:T(128)} all-reduce(f32[]{:T(128)} %multiply_reduce_fusion.2), channel_id=1, replica_groups=mesh['groups'=2,'row'=4,'col'=2,'sub'=2] {'row','col','sub'}, use_global_device_ids=true, to_apply=%region_4.0 | all-reduce | flops 1 | bytes 8 | tf_op jit(solution)/shard_map/psum | solution.py:18
  44.5 0.0 copy-start.5
  44.5 0.7 copy-done.5
  45.1 0.7 dynamic-slice.1
  46.5 0.2 dynamic-update-slice.1
  46.8 8.3 %all-reduce.1 = bf16[256]{0:T(256)(128)(2,1)S(1)} all-reduce(bf16[256]{0:T(256)(128)(2,1)S(1)} %dynamic-update-slice.1), channel_id=1, replica_groups=mesh['groups'=2,'row'=4,'col'=2,'sub'=2] {'row'}, use_global_device_ids=true, to_apply=%add.1 | all-reduce | flops 256 | bytes 1024
  55.1 0.0 copy-start.4
  55.1 0.6 copy-done.4
  55.8 0.7 dynamic-slice
  57.1 0.2 dynamic-update-slice
  57.4 4.9 %all-reduce = bf16[128]{0:T(256)(128)(2,1)S(1)} all-reduce(bf16[128]{0:T(256)(128)(2,1)S(1)} %dynamic-update-slice), channel_id=1, replica_groups=mesh['groups'=2,'row'=4,'col'=2,'sub'=2] {'col'}, use_global_device_ids=true, to_apply=%add | all-reduce | flops 128 | bytes 512
  62.3 0.0 copy-done.1
  62.3 0.1 fusion.1
  62.4 2.5 %psum.28 = f32[64]{0:T(128)S(1)} all-reduce(f32[64]{0:T(128)S(1)} %fusion.1), channel_id=1, replica_groups=mesh['groups'=2,'row'=4,'col'=2,'sub'=2] {'sub'}, use_global_device_ids=true, to_apply=%region_1.0 | all-reduce | flops 64 | bytes 512 | tf_op jit(solution)/shard_map/psum | solution.py:9
  65.5 0.1 fusion.4
  65.6 4.9 %all_gather.18 = bf16[128,512]{1,0:T(8,128)(2,1)S(1)} all-gather(bf16[64,512]{1,0:T(8,128)(2,1)S(1)} %fusion.4), channel_id=1, replica_groups=mesh['groups'=2,'row'=4,'col'=2,'sub'=2] {'col'}, dimensions={0}, use_global_device_ids=true | all-gather | bytes 196608 | tf_op jit(solution)/shard_map/all_gather | solution.py:20
  70.6 14.5 %all_gather.19 = bf16[256,512]{1,0:T(8,128)(2,1)S(1)} all-gather(bf16[64,512]{1,0:T(8,128)(2,1)S(1)} %fusion.4), channel_id=1, replica_groups=mesh['groups'=2,'row'=4,'col'=2,'sub'=2] {'row'}, dimensions={0}, use_global_device_ids=true | all-gather | bytes 327680 | tf_op jit(solution)/shard_map/all_gather | solution.py:25
  85.1 7.0 %all_gather.22 = bf16[128,2048]{1,0:T(8,128)(2,1)S(1)} all-gather(bf16[64,2048]{1,0:T(8,128)(2,1)S(1)} %copy-done), channel_id=1, replica_groups=mesh['groups'=2,'row'=4,'col'=2,'sub'=2] {'col'}, dimensions={0}, use_global_device_ids=true | all-gather | bytes 786432 | tf_op jit(solution)/shard_map/all_gather | solution.py:21
  92.1 0.0 all-gather.2.cloned.1.call-done
  92.1 1.7 %fusion = f32[128,256]{1,0:T(8,128)S(1)} fusion(bf16[128,2048]{1,0:T(8,128)(2,1)S(1)} %all_gather.22, bf16[256,2048]{1,0:T(8,128)(2,1)} %all-gather.2.cloned.1.call-done, f32[]{:T(128)S(6)} %div.25, f32[256]{0:T(256)S(1)} %convert_element_type.24, f32[128]{0:T(128)S(1)} %convert_element_type.23), kind=kOutput, calls=%fused_computation.2 | convolution fusion | flops 134316032 | bytes 1705476 | tf_op jit(solution)/shard_map/dot_general | solution.py:31
  93.9 0.2 convolution_subtract_fusion
  94.1 3.8 %all-reduce.3 = bf16[128,256]{1,0:T(8,128)(2,1)S(1)} all-reduce(f32[128,256]{1,0:T(8,128)S(1)} %convolution_subtract_fusion), channel_id=1, replica_groups=mesh['groups'=2,'row'=4,'col'=2,'sub'=2] {'sub'}, use_global_device_ids=true, to_apply=%region_5.0 | all-reduce | flops 32768 | bytes 196608 | tf_op jit(solution)/shard_map/psum | solution.py:34
  97.9 0.9 fusion.5
  98.8 0.0 reduce-scatter.2.cloned.1.call-update
  98.8 10.2 %reduce-scatter.2.cloned.1.call-done = f32[64,512]{1,0:T(8,128)} async-done(((f32[128,512]{1,0:T(8,128)}), f32[64,512]{1,0:T(8,128)}) %reduce-scatter.2.cloned.1.call-update) | async-done | bytes 131088 | tf_op jit(solution)/shard_map/reduce_scatter | solution.py:35
  109.1 0.0 copy-start.2
  109.1 1.2 multiply_reduce_fusion.1
  110.3 2.5 %psum.31 = f32[64]{0:T(128)S(1)} all-reduce(f32[64]{0:T(128)S(1)} %multiply_reduce_fusion.1), channel_id=1, replica_groups=mesh['groups'=2,'row'=4,'col'=2,'sub'=2] {'sub'}, use_global_device_ids=true, to_apply=%region_8.0 | all-reduce | flops 64 | bytes 512 | tf_op jit(solution)/shard_map/psum | solution.py:42
  112.7 0.0 copy-done.2
  112.7 0.8 subtract_divide_fusion
  (5 shorter events, 0.0 us)
Async XLA Ops:
  6.5 0.9 copy-start
  6.5 85.6 %all-gather.2.cloned.1.call-start = ((), (), s32[]{:S(2)}) async-start(), calls=%async_computation.1 | async-start | bytes 1310720 | tf_op jit(solution)/shard_map/all_gather | solution.py:26
  7.3 0.7 copy-start.3
  7.3 101.8 %reduce-scatter.2.cloned.1.call-start = ((), (), s32[]{:S(2)}) async-start(), calls=%async_computation.2 | async-start | bytes 393216 | tf_op jit(solution)/shard_map/reduce_scatter | solution.py:35
  7.5 54.8 %copy-start.1 = (bf16[64,512]{1,0:T(8,128)(2,1)S(1)}, bf16[64,512]{1,0:T(8,128)(2,1)}, u32[]{:S(2)}) copy-start(bf16[64,512]{1,0:T(8,128)(2,1)} %param.3) | copy-start | bytes 196612
  44.5 0.7 copy-start.5
  55.1 0.7 copy-start.4
  109.1 3.6 %copy-start.2 = (f32[64,512]{1,0:T(8,128)S(1)}, f32[64,512]{1,0:T(8,128)}, u32[]{:S(2)}) copy-start(f32[64,512]{1,0:T(8,128)} %reduce-scatter.2.cloned.1.call-done) | copy-start | bytes 393220
Sparse Core Ops, SparseCore 0:
  8.9 30.7 all-gather.1
  99.0 10.0 reduce-scatter.1
where the time goes:
time: 121 us; the launch traced here: 120 us
  blocking collectives  84.5 us (70%)
  between operations  15.5 us (13%)
  waiting for transfers between devices  11 us (9%)
  local copies, waits for them, and re-layouts  3.6 us (3%)
  other arithmetic  2.88 us (2%)
  matrix products  2.82 us (2%)
    psum x1, blocking collectives, shards(): mass = lax.psum(local_mass, ('row', 'col', 'sub')) / batch_rows  36 us
    all_gather x1, blocking collectives, shards(): lax.all_gather(unit_b, 'row', axis=0, tiled=True)  14.5 us
    unnamed x2, blocking collectives  13.3 us
    reduce_scatter x1, waiting for transfers between devices, shards(): lax.psum_scatter(jnp.dot(error_b, col_unit, preferred_element_type=jnp.fl...  10.2 us
    all_gather x1, blocking collectives, shards(): lax.all_gather(teacher, 'col', axis=0, tiled=True)  7.04 us
    all_gather x1, blocking collectives, shards(): lax.all_gather(unit_b, 'col', axis=0, tiled=True)  4.94 us
    psum x1, blocking collectives, shards(): error_b = lax.psum(partial_err, 'sub').astype(jnp.bfloat16)  3.85 us
    unnamed x18, local copies, waits for them, and re-layouts  3.59 us
  transfers between devices with their start and end apart: 2, of which 1 were waited for; matrix products, arithmetic and copies ran while one was open for 2% of the time, Pallas kernels for 0%

commit v1 on v0

v1 whole, which is shorter than its diff:
```python
import jax
import jax.numpy as jnp
from jax import lax
from jax.sharding import PartitionSpec as P

F32, BF16 = jnp.float32, jnp.bfloat16
INNER = (((1,), (1,)), ((), ()))


def shards(student, teacher, scale):
    rows, half = student.shape
    nrow, ncol = lax.axis_size("row"), lax.axis_size("col")
    batch = rows * nrow * ncol
    part = teacher.shape[1] // nrow

    scaled = (teacher.astype(F32) * scale.astype(F32)[:, None]).astype(BF16)
    by_feature = scaled.reshape(rows, nrow, part).transpose(1, 0, 2)
    spread = jnp.broadcast_to(student[None], (nrow, rows, half))
    packed = jnp.concatenate([by_feature, spread], axis=2)
    mine = lax.all_to_all(packed, "row", 0, 0, tiled=True).reshape(nrow * rows, part + half)
    pieces = [mine]
    for k in range(1, ncol):
        pieces.append(lax.ppermute(mine, "col", [(i, (i - k) % ncol) for i in range(ncol)]))
    every = jnp.concatenate(pieces, axis=0)
    teach, stud = every[:, :part], every[:, part:]

    partial = lax.dot_general(mine[:, :part], teach, INNER, preferred_element_type=F32)
    local_mass = jnp.sum(jnp.square(teach.astype(F32)))
    high = local_mass.astype(BF16)
    low = (local_mass - high.astype(F32)).astype(BF16)
    tail = jnp.concatenate([jnp.full((nrow, 8, batch), high), jnp.full((nrow, 8, batch), low)], axis=1)
    sent = jnp.concatenate([partial.reshape(nrow, rows, batch).astype(BF16), tail], axis=1)
    back = jnp.sum(lax.all_to_all(sent, "row", 0, 0, tiled=True).astype(F32), axis=0)
    teach_gram = back[:rows]
    mass_part = back[rows] + back[rows + 8]

    raw_gram = lax.dot_general(student, stud, INNER, preferred_element_type=F32)
    xs = stud.astype(F32)
    square_part = jnp.sum(xs * xs, axis=1)
    extra = jnp.concatenate([jnp.broadcast_to(square_part[None], (4, batch)), jnp.broadcast_to(mass_part[None], (4, batch))], axis=0)
    half_sums = jnp.concatenate([teach_gram, raw_gram, extra], axis=0)
    sums = half_sums + lax.ppermute(half_sums, "sub", [(0, 1), (1, 0)])
    norm = jnp.sqrt(sums[2 * rows])
    mass = sums[2 * rows + 4] / batch
    me = lax.axis_index("row") * rows
    own_norm = lax.dynamic_slice_in_dim(norm, me, rows)
    unit_b = (xs / norm[:, None]).astype(BF16)
    unit_gram = sums[rows : 2 * rows] / (own_norm[:, None] * norm[None, :])
    error_b = (unit_gram - sums[:rows] / mass[None, :]).astype(BF16)
    grads = 4.0 * jnp.dot(error_b, unit_b, preferred_element_type=F32)
    along = 4.0 * jnp.sum(error_b.astype(F32) * unit_gram, axis=1)
    unit = student.astype(F32) / own_norm[:, None]
    return (grads - along[:, None] * unit) / own_norm[:, None]


def solution(mesh):
    spec = P(("groups", "row", "col"), "sub")
    return jax.shard_map(
        shards,
        mesh=mesh,
        in_specs=(spec, spec, P(("groups", "row", "col"))),
        out_specs=spec,
        check_vma=False,
    )
```

time: 121 us -> 55.5 us (0.46)
  blocking collectives: 84.5 us -> 20.6 us
  between operations: 15.5 us -> 1.44 us
  waiting for transfers between devices: 11 us -> 21.1 us
  starting transfers between devices: 0.04 us -> 5.01 us
  local copies, waits for them, and re-layouts: 3.6 us -> 1.31 us
  other arithmetic: 2.88 us -> 4.12 us
  matrix products: 2.82 us -> 1.58 us
    psum x4 -> x0, blocking collectives: 44.7 us -> none  [the longest x1 36 us: shards(): mass = lax.psum(local_mass, ('row', 'col', 'sub')) / batch_rows]
    all_gather x3 -> x0, blocking collectives: 26.5 us -> none  [the longest x1 14.5 us: shards(): lax.all_gather(unit_b, 'row', axis=0, tiled=True)]
    all_to_all x0 -> x1, blocking collectives: none -> 20.6 us  [shards(): lax.all_to_all(packed, 'row', 0, 0, tiled=True)]
    unnamed x2 -> x0, blocking collectives: 13.3 us -> none
    ppermute x0 -> x2, waiting for transfers between devices: none -> 12.6 us  [the longest x1 11 us: shards(): lax.ppermute(mine, 'col', [(i, (i - k) % ncol) for i in range(ncol)])]
    reduce_scatter x1 -> x0, waiting for transfers between devices: 10.2 us -> none  [shards(): lax.psum_scatter(jnp.dot(error_b, col_unit, preferred_element_type=jnp.fl...]
    all_to_all x0 -> x1, waiting for transfers between devices: none -> 8.55 us  [shards(): lax.all_to_all(sent, 'row', 0, 0, tiled=True).astype(F32)]
    all_to_all x0 -> x1, starting transfers between devices: none -> 3.45 us  [shards(): lax.all_to_all(sent, 'row', 0, 0, tiled=True).astype(F32)]
  transfers between devices with their start and end apart: 2 -> 3, of which waited for: 1 -> 3; matrix products, arithmetic and copies ran while one was open for 2% -> 1% of each run, Pallas kernels for 0% -> 0%
where the time goes in v1:
time: 55.5 us; the launch traced here: 55.2 us
  waiting for transfers between devices  21.1 us (38%)
  blocking collectives  20.6 us (37%)
  starting transfers between devices  5.01 us (9%)
  other arithmetic  4.12 us (7%)
  matrix products  1.58 us (3%)
  between operations  1.44 us (3%)
  local copies, waits for them, and re-layouts  1.31 us (2%)
    all_to_all x1, blocking collectives, shards(): lax.all_to_all(packed, 'row', 0, 0, tiled=True)  20.6 us
    ppermute x1, waiting for transfers between devices, shards(): lax.ppermute(mine, 'col', [(i, (i - k) % ncol) for i in range(ncol)])  11 us
    all_to_all x1, waiting for transfers between devices, shards(): lax.all_to_all(sent, 'row', 0, 0, tiled=True).astype(F32)  8.55 us
    all_to_all x1, starting transfers between devices, shards(): lax.all_to_all(sent, 'row', 0, 0, tiled=True).astype(F32)  3.45 us
    convert_element_type x2, other arithmetic, shards(): scaled = (teacher.astype(F32) * scale.astype(F32)[:, None]).astype(BF16)  1.72 us
    ppermute x1, waiting for transfers between devices, shards(): sums = half_sums + lax.ppermute(half_sums, 'sub', [(0, 1), (1, 0)])  1.54 us
    ppermute x1, starting transfers between devices, shards(): lax.ppermute(mine, 'col', [(i, (i - k) % ncol) for i in range(ncol)])  1.49 us
  transfers between devices with their start and end apart: 3, of which 3 were waited for; matrix products, arithmetic and copies ran while one was open for 1% of the time, Pallas kernels for 0%

profile of v1, /device:TPU:0, one launch (start us, length us, event | category | flops | bytes accessed | tf_op | source)
XLA Modules:
  0.0 55.2 jit_solution(2635647388224323167)
XLA Ops:
  0.0 0.7 %convert_element_type.46 = f32[64]{0:T(128)S(1)} convert(bf16[64]{0:T(256)(128)(2,1)} %param.5) | non-fusion elementwise | flops 64 | bytes 384 | tf_op jit(solution)/shard_map/convert_element_type | solution.py:16
  0.7 1.1 %multiply_convert_fusion = bf16[64,2048]{1,0:T(8,128)(2,1)S(1)} fusion(bf16[64,2048]{1,0:T(8,128)(2,1)} %param.4, f32[64]{0:T(128)S(1)} %convert_element_type.46), kind=kLoop, calls=%fused_computation.16 | loop fusion | flops 393216 | bytes 524544 | tf_op jit(solution)/shard_map/convert_element_type | solution.py:16
  1.7 0.0 copy-start
  1.7 0.2 reshape.22
  1.9 0.6 %copy-done = bf16[64,512]{1,0:T(8,128)(2,1)S(1)} copy-done((bf16[64,512]{1,0:T(8,128)(2,1)S(1)}, bf16[64,512]{1,0:T(8,128)(2,1)}, u32[]{:S(2)}) %copy-start) | copy-done | bytes 65560
  2.6 0.1 broadcast_in_dim.12
  2.6 0.2 pad_maximum_fusion.1
  2.9 0.2 copy.5
  3.0 20.6 %all_to_all.10 = bf16[4,64,1024]{2,1,0:T(8,128)(2,1)S(1)} all-to-all(bf16[4,64,1024]{2,1,0:T(8,128)(2,1)S(1)} %copy.5), channel_id=1, replica_groups=mesh['groups'=2,'row'=4,'col'=2,'sub'=2] {'row'}, dimensions={0} | all-to-all | bytes 1048576 | tf_op jit(solution)/shard_map/all_to_all | solution.py:20
  23.6 1.5 %collective-permute-start = (bf16[256,1024]{1,0:T(8,128)(2,1)S(1)}, bf16[256,1024]{1,0:T(8,128)(2,1)S(1)}, u32[]{:S(2)}, u32[]{:S(2)}) collective-permute-start(bf16[256,1024]{1,0:T(8,128)(2,1)S(1)} %bitcast.12), channel_id=1, source_target_pairs={{0,2},{2,0},{1,3},{3,1},{4,6},{6,4},{5,7},{7,5},{8,10},{10,8},{9,1... | collective-permute-start | bytes 1572872 | tf_op jit(solution)/shard_map/ppermute | solution.py:23
  25.1 11.0 %collective-permute-done = bf16[256,1024]{1,0:T(8,128)(2,1)S(1)} collective-permute-done((bf16[256,1024]{1,0:T(8,128)(2,1)S(1)}, bf16[256,1024]{1,0:T(8,128)(2,1)S(1)}, u32[]{:S(2)}, u32[]{:S(2)}) %collective-permute-start) | collective-permute-done | bytes 524320 | tf_op jit(solution)/shard_map/ppermute | solution.py:23
  36.2 1.0 %fusion.2 = (f32[512]{0:T(512)S(1)}, f32[]{:T(128)}) fusion(bf16[256,1024]{1,0:T(8,128)(2,1)S(1)} %collective-permute-done, bf16[256,1024]{1,0:T(8,128)(2,1)S(1)} %bitcast.13), kind=kLoop, calls=%fused_computation.7 | loop fusion | flops 3145215 | bytes 1050628 | tf_op jit(solution)/shard_map/reduce_sum | solution.py:39
  38.5 0.1 pad.6.clone
  38.5 0.1 pad.5.clone
  38.6 0.3 convolution_convert_fusion
  39.0 0.9 %maximum_maximum_fusion = bf16[4,80,512]{2,1,0:T(8,128)(2,1)} fusion(bf16[4,64,512]{2,1,0:T(8,128)(2,1)S(1)} %bitcast.18, bf16[80]{0:T(256)(128)(2,1)S(1)} %pad.6.clone, bf16[80]{0:T(256)(128)(2,1)S(1)} %pad.5.clone), kind=kLoop, calls=%fused_computation.17 | loop fusion | flops 983040 | bytes 590144 | tf_op jit(solution)/shard_map/concatenate | solution.py:32
  39.8 3.5 %all-to-all-start.1 = ((bf16[4,80,512]{2,1,0:T(8,128)(2,1)}), bf16[4,80,512]{2,1,0:T(8,128)(2,1)S(1)}, u32[]{:S(2)}, u32[]{:S(2)}) async-start(bf16[4,80,512]{2,1,0:T(8,128)(2,1)} %maximum_maximum_fusion), calls=%async_computation.1 | async-start | bytes 655360 | tf_op jit(solution)/shard_map/all_to_all | solution.py:33
  43.3 0.3 convolution_bitcast_fusion
  43.6 8.6 %all-to-all-done.1 = bf16[4,80,512]{2,1,0:T(8,128)(2,1)S(1)} async-done(((bf16[4,80,512]{2,1,0:T(8,128)(2,1)}), bf16[4,80,512]{2,1,0:T(8,128)(2,1)S(1)}, u32[]{:S(2)}, u32[]{:S(2)}) %all-to-all-start.1) | async-done | bytes 327712 | tf_op jit(solution)/shard_map/all_to_all | solution.py:33
  52.3 0.1 collective-permute-start.1
  52.4 1.5 %collective-permute-done.1 = f32[136,512]{1,0:T(8,128)S(1)} collective-permute-done((f32[136,512]{1,0:T(8,128)S(1)}, f32[136,512]{1,0:T(8,128)S(1)}, u32[]{:S(2)}, u32[]{:S(2)}) %collective-permute-start.1) | collective-permute-done | bytes 278560 | tf_op jit(solution)/shard_map/ppermute | solution.py:42
  54.0 0.1 dynamic-slice_bitcast_fusion
  54.0 0.2 multiply_reduce_fusion.1
  54.2 1.0 %fusion.1 = f32[64,512]{1,0:T(8,128)} fusion(bf16[64,512]{1,0:T(8,128)(2,1)S(1)} %get-tuple-element.8, f32[512]{0:T(512)S(1)} %bitcast.21, bf16[64,512]{1,0:T(8,128)(2,1)S(1)} %copy-done, f32[64]{0:T(128)S(1)} %broadcast_multiply_fusion, f32[64]{0:T(128)S(1)} %dynamic-slice_bitcast_fusion, bf16[256,1024]{1,0:T(8,128)(2,1)S(1)} %collective-permute-done, ...), kind=kOutput, calls=%fused_computation.5 | convolution fusion | flops 35323904 | bytes 1313280 | tf_op jit(solution)/shard_map/dot_general | solution.py:50
  (11 shorter events, 0.2 us)
Async XLA Ops:
  1.7 0.8 %copy-start = (bf16[64,512]{1,0:T(8,128)(2,1)S(1)}, bf16[64,512]{1,0:T(8,128)(2,1)}, u32[]{:S(2)}) copy-start(bf16[64,512]{1,0:T(8,128)(2,1)} %param.3) | copy-start | bytes 196612
  23.6 12.5 %collective-permute-start = (bf16[256,1024]{1,0:T(8,128)(2,1)S(1)}, bf16[256,1024]{1,0:T(8,128)(2,1)S(1)}, u32[]{:S(2)}, u32[]{:S(2)}) collective-permute-start(bf16[256,1024]{1,0:T(8,128)(2,1)S(1)} %bitcast.12), channel_id=1, source_target_pairs={{0,2},{2,0},{1,3},{3,1},{4,6},{6,4},{5,7},{7,5},{8,10},{10,8},{9,1... | collective-permute-start | bytes 1572872 | tf_op jit(solution)/shard_map/ppermute | solution.py:23
  39.8 12.3 %all-to-all-start.1 = ((bf16[4,80,512]{2,1,0:T(8,128)(2,1)}), bf16[4,80,512]{2,1,0:T(8,128)(2,1)S(1)}, u32[]{:S(2)}, u32[]{:S(2)}) async-start(bf16[4,80,512]{2,1,0:T(8,128)(2,1)} %maximum_maximum_fusion), calls=%async_computation.1 | async-start | bytes 655360 | tf_op jit(solution)/shard_map/all_to_all | solution.py:33
  52.3 1.6 %collective-permute-start.1 = (f32[136,512]{1,0:T(8,128)S(1)}, f32[136,512]{1,0:T(8,128)S(1)}, u32[]{:S(2)}, u32[]{:S(2)}) collective-permute-start(f32[136,512]{1,0:T(8,128)S(1)} %pad_maximum_fusion.2), channel_id=1, source_target_pairs={{0,1},{1,0},{2,3},{3,2},{4,5},{5,4},{6,7},{7,6},{8,9},{9,8},{10,11... | collective-permute-start | bytes 835592 | tf_op jit(solution)/shard_map/ppermute | solution.py:42

commit v2 on v1

v2 whole, which is shorter than its diff:
```python
import functools

import jax
import jax.numpy as jnp
from jax import lax
from jax.experimental import pallas as pl
from jax.experimental.pallas import tpu as pltpu
from jax.sharding import PartitionSpec as P

F32, BF16 = jnp.float32, jnp.bfloat16
INNER = (((1,), (1,)), ((), ()))
TAIL = 16


def call(body, out_shape, operands, flops=0, space=pltpu.VMEM, scratch=()):
    outs = out_shape if isinstance(out_shape, (list, tuple)) else [out_shape]
    moved = sum(x.size * x.dtype.itemsize for x in list(operands) + list(outs))
    return pl.pallas_call(
        body,
        out_shape=out_shape,
        in_specs=[pl.BlockSpec(memory_space=space)] * len(operands),
        out_specs=jax.tree.map(lambda _: pl.BlockSpec(memory_space=space), out_shape),
        scratch_shapes=list(scratch),
        cost_estimate=pl.CostEstimate(flops=flops, bytes_accessed=moved, transcendentals=0),
        compiler_params=pltpu.CompilerParams(vmem_limit_bytes=min(56 << 20, (8 << 20) + 3 * moved)),
    )(*operands)


def column(row):
    n = row.shape[1]
    eye = lax.broadcasted_iota(jnp.int32, (n, n), 0) == lax.broadcasted_iota(jnp.int32, (n, n), 1)
    return jnp.sum(jnp.where(eye, row, 0.0), axis=1, keepdims=True)


def cut_kernel(nrow, teach, *refs):
    outs, sems = refs[:nrow], refs[nrow]
    part = teach.shape[1] // nrow
    z = lax.axis_index("row")
    copies = []
    for k in range(nrow):
        at = pl.multiple_of(lax.rem(z + k, nrow) * part, part)
        copies.append(pltpu.make_async_copy(teach.at[:, pl.ds(at, part)], outs[k], sems.at[k]))
    for c in copies:
        c.start()
    for c in copies:
        c.wait()


def square_kernel(stud, teach, scale, out):
    xs = stud[...].astype(F32)
    squares = jnp.sum(xs * xs, axis=1, keepdims=True)
    ts = teach[...].astype(F32)
    s = column(scale[...].astype(F32))
    mass = jnp.sum(s * s * jnp.sum(ts * ts, axis=1, keepdims=True), keepdims=True)
    lane = lax.broadcasted_iota(jnp.int32, out.shape, 1)
    out[...] = jnp.where(lane < 64, squares, mass)


def unit_kernel(stud, mine, other, scale, out):
    rows, half = stud.shape
    total = mine[...] + other[...]
    norm = jnp.sqrt(total[:, :1])
    out[:rows, :] = (stud[...].astype(F32) / norm).astype(BF16)
    mass = total[:1, 64:65]
    high = mass.astype(BF16).astype(F32)
    low = mass - high
    s = scale[...].astype(F32)
    twice = jnp.concatenate([s, s] + [jnp.zeros((1, half - 2 * rows), F32)], axis=1)
    at = lax.broadcasted_iota(jnp.int32, (TAIL, half), 0)
    tail = jnp.where(at == 0, twice, jnp.where(at == 1, high, low))
    out[rows:, :] = tail.astype(BF16)


def assemble(nrow, ncol, rows, pieces, held):
    z = lax.axis_index("row")
    for c in range(ncol):
        for j in range(nrow):
            owner = lax.rem(z - j + nrow, nrow)
            at = pl.multiple_of((owner * ncol + c) * rows, rows)
            held[pl.ds(at, rows), :] = pieces[c * nrow + j][:rows, :]


def gram_kernel(nrow, ncol, *refs):
    count = nrow * ncol
    pieces, outs, held = refs[:count], refs[count : count + nrow], refs[count + nrow]
    rows = pieces[0].shape[0]
    assemble(nrow, ncol, rows, pieces, held)
    for k in range(nrow):
        left = pieces[(nrow - k) % nrow][...]
        outs[k][...] = lax.dot_general(left, held[...], INNER, preferred_element_type=F32).astype(outs[k].dtype)


def unit_gram_kernel(nrow, ncol, rows, *refs):
    count = nrow * ncol
    pieces, (gram, vectors, units) = refs[:count], refs[count:]
    assemble(nrow, ncol, rows, pieces, units)
    gram[...] = lax.dot_general(pieces[0][:rows, :], units[...], INNER, preferred_element_type=F32)
    z = lax.axis_index("row")
    lane = lax.broadcasted_iota(jnp.int32, (TAIL, 2 * rows), 1)
    mass = jnp.zeros((TAIL, 2 * rows), F32)
    for j in range(nrow):
        owner = lax.rem(z - j + nrow, nrow)
        for c in range(0, ncol, 2):
            first = pieces[c * nrow + j][rows:, : 2 * rows].astype(F32)
            second = pieces[(c + 1) * nrow + j][rows:, : 2 * rows].astype(F32)
            at = pl.multiple_of((owner * ncol + c) * rows, 2 * rows)
            vectors[0:8, pl.ds(at, 2 * rows)] = jnp.where(lane < rows, first, second)[0:8]
            mass = mass + first + second
    total = mass[1:2, 0:1] + mass[2:3, 0:1]
    vectors[8:16, :] = jnp.broadcast_to(total, (8, vectors.shape[1]))


def sum_kernel(*refs):
    ins, out = refs[:-1], refs[-1]
    total = ins[0][...].astype(F32)
    for r in ins[1:]:
        total = total + r[...].astype(F32)
    out[...] = total


def final_kernel(nrow, ncol, batch, mine, other, gram_mine, gram_other, vectors, stud, sq_mine, sq_other, scale, *refs):
    if len(refs) > 2:
        pieces, out, units = refs[:-2], refs[-2], refs[-1]
        assemble(nrow, ncol, stud.shape[0], pieces, units)
    else:
        units, out = refs
    norm = jnp.sqrt(sq_mine[:, :1] + sq_other[:, :1])
    mass = vectors[8:9, 0:1] / batch
    unit_gram = gram_mine[...] + gram_other[...]
    outer = column(scale[...].astype(F32)) * vectors[0:1, :]
    error = unit_gram - outer * (mine[...] + other[...]) / mass
    error_b = error.astype(BF16)
    grads = 4.0 * jnp.dot(error_b, units[...], preferred_element_type=F32)
    along = 4.0 * jnp.sum(error_b.astype(F32) * unit_gram, axis=1, keepdims=True)
    unit = stud[...].astype(F32) / norm
    out[...] = (grads - along * unit) / norm


def shards(student, teacher, scale):
    rows, half = student.shape
    nrow, ncol = lax.axis_size("row"), lax.axis_size("col")
    batch = rows * nrow * ncol
    part = teacher.shape[1] // nrow
    sds = jax.ShapeDtypeStruct
    scale = scale.reshape(1, rows)

    def along_row(x, k):
        return lax.ppermute(x, "row", [(i, (i + k) % nrow) for i in range(nrow)])

    def along_col(x, c):
        return lax.ppermute(x, "col", [(i, (i - c) % ncol) for i in range(ncol)])

    def other_core(x):
        return lax.ppermute(x, "sub", [(0, 1), (1, 0)])

    cuts = call(
        functools.partial(cut_kernel, nrow),
        [sds((rows, part), BF16)] * nrow,
        [teacher],
        space=pl.ANY,
        scratch=[pltpu.SemaphoreType.DMA((nrow,))],
    )
    teach = [cuts[0]] + [along_row(cuts[k], k) for k in range(1, nrow)]
    teach += [along_col(t, c) for c in range(1, ncol) for t in teach[:nrow]]

    squares = call(square_kernel, sds((rows, 128), F32), [student, teacher, scale])
    squares_other = other_core(squares)
    unit = call(unit_kernel, sds((rows + TAIL, half), BF16), [student, squares, squares_other, scale])
    units = [unit] + [along_row(unit, k) for k in range(1, nrow)]
    units += [along_col(u, c) for c in range(1, ncol) for u in units[:nrow]]

    partial = call(
        functools.partial(gram_kernel, nrow, ncol),
        [sds((rows, batch), F32)] + [sds((rows, batch), BF16)] * (nrow - 1),
        teach,
        flops=2 * rows * nrow * batch * part,
        scratch=[pltpu.VMEM((batch, part), BF16)],
    )
    returned = [partial[0]] + [along_row(partial[k], k) for k in range(1, nrow)]
    teach_gram = call(sum_kernel, sds((rows, batch), F32), returned)
    teach_gram_other = other_core(teach_gram)

    keep = batch <= 2048
    held = [] if keep else [pltpu.VMEM((batch, half), BF16)]
    unit_gram, vectors, *all_units = call(
        functools.partial(unit_gram_kernel, nrow, ncol, rows),
        [sds((rows, batch), F32), sds((16, batch), F32)] + ([sds((batch, half), BF16)] if keep else []),
        units,
        flops=2 * rows * batch * half,
        scratch=held,
    )
    unit_gram_other = other_core(unit_gram)
    return call(
        functools.partial(final_kernel, nrow, ncol, batch),
        sds((rows, half), F32),
        [teach_gram, teach_gram_other, unit_gram, unit_gram_other, vectors, student, squares, squares_other, scale]
        + (all_units if keep else units),
        flops=2 * rows * batch * half,
        scratch=held,
    )


def solution(mesh):
    spec = P(("groups", "row", "col"), "sub")
    return jax.shard_map(
        shards,
        mesh=mesh,
        in_specs=(spec, spec, P(("groups", "row", "col"))),
        out_specs=spec,
        check_vma=False,
    )
```

time: 55.5 us -> 38.8 us (0.70)
  starting transfers between devices: 5.01 us -> 25.9 us
  blocking collectives: 20.6 us -> 0 us
  waiting for transfers between devices: 21.1 us -> 9.14 us
  other arithmetic: 4.12 us -> 0 us
  Pallas kernels: 0 us -> 2.53 us
  matrix products: 1.58 us -> 0 us
  between operations: 1.44 us -> 0.1 us
    ppermute x2 -> x20, starting transfers between devices: 1.56 us -> 25.9 us  [the longest x9 15.3 us: along_row(): return lax.ppermute(x, 'row', [(i, (i + k) % nrow) for i in range(nrow)])]
    all_to_all x1 -> x0, blocking collectives: 20.6 us -> none  [shards(): lax.all_to_all(packed, 'row', 0, 0, tiled=True)]
    all_to_all x1 -> x0, waiting for transfers between devices: 8.55 us -> none  [shards(): lax.all_to_all(sent, 'row', 0, 0, tiled=True).astype(F32)]
    all_to_all x1 -> x0, starting transfers between devices: 3.45 us -> none  [shards(): lax.all_to_all(sent, 'row', 0, 0, tiled=True).astype(F32)]
    ppermute x2 -> x20, waiting for transfers between devices: 12.6 us -> 9.14 us  [the longest x9 6.94 us: along_row(): return lax.ppermute(x, 'row', [(i, (i + k) % nrow) for i in range(nrow)])]
    pallas_call x0 -> x7, Pallas kernels: none -> 2.53 us  [call(): pl.pallas_call(body, out_shape=out_shape, in_specs=[pl.BlockSpec(memory_s...]
    convert_element_type x2 -> x0, other arithmetic: 1.72 us -> none  [shards(): scaled = (teacher.astype(F32) * scale.astype(F32)[:, None]).astype(BF16)]
    dot_general x3 -> x0, matrix products: 1.58 us -> none  [the longest x1 0.97 us: shards(): grads = 4.0 * jnp.dot(error_b, unit_b, preferred_element_type=F32)]
  transfers between devices with their start and end apart: 3 -> 20, of which waited for: 3 -> 7; matrix products, arithmetic and copies ran while one was open for 1% -> 0% of each run, Pallas kernels for 0% -> 4%
where the time goes in v2:
time: 38.8 us; the launch traced here: 38.7 us
  starting transfers between devices  25.9 us (67%)
  waiting for transfers between devices  9.14 us (24%)
  Pallas kernels  2.53 us (7%)
  local copies, waits for them, and re-layouts  0.96 us (2%)
    ppermute x9, starting transfers between devices, along_row(): return lax.ppermute(x, 'row', [(i, (i + k) % nrow) for i in range(nrow)])  15.3 us
    ppermute x8, starting transfers between devices, along_col(): return lax.ppermute(x, 'col', [(i, (i - c) % ncol) for i in range(ncol)])  9.97 us
    ppermute x9, waiting for transfers between devices, along_row(): return lax.ppermute(x, 'row', [(i, (i + k) % nrow) for i in range(nrow)])  6.94 us
    pallas_call x7, Pallas kernels, call(): pl.pallas_call(body, out_shape=out_shape, in_specs=[pl.BlockSpec(memory_s...  2.53 us
    ppermute x3, waiting for transfers between devices, other_core(): return lax.ppermute(x, 'sub', [(0, 1), (1, 0)])  2.18 us
    unnamed x6, local copies, waits for them, and re-layouts  0.96 us
  transfers between devices with their start and end apart: 20, of which 7 were waited for; matrix products, arithmetic and copies ran while one was open for 0% of the time, Pallas kernels for 4%

profile of v2, /device:TPU:0, one launch (start us, length us, event | category | flops | bytes accessed | tf_op | source)
XLA Modules:
  0.0 38.7 jit_solution(15738625548457255995)
XLA Ops:
  0.0 0.9 %copy-done = bf16[64,2048]{1,0:T(8,128)(2,1)S(1)} copy-done((bf16[64,2048]{1,0:T(8,128)(2,1)S(1)}, bf16[64,2048]{1,0:T(8,128)(2,1)}, u32[]{:S(2)}) %copy-start) | copy-done | bytes 262168
  1.0 0.1 shard_map.37
  1.0 3.1 %collective-permute-start = (bf16[64,512]{1,0:T(8,128)(2,1)S(1)}, bf16[64,512]{1,0:T(8,128)(2,1)S(1)}, u32[]{:S(2)}, u32[]{:S(2)}) collective-permute-start(bf16[64,512]{1,0:T(8,128)(2,1)S(1)} %get-tuple-element.17), channel_id=1, source_target_pairs={{0,4},{4,8},{8,12},{12,0},{1,5},{5,9},{9,13},{13,1},{2,6},{6,10},{... | collective-permute-start | bytes 196616 | tf_op jit(solution)/shard_map/ppermute | solution.py:148
  4.1 2.6 %collective-permute-start.1 = (bf16[64,512]{1,0:T(8,128)(2,1)S(1)}, bf16[64,512]{1,0:T(8,128)(2,1)S(1)}, u32[]{:S(2)}, u32[]{:S(2)}) collective-permute-start(bf16[64,512]{1,0:T(8,128)(2,1)S(1)} %get-tuple-element.18), channel_id=1, source_target_pairs={{0,8},{4,12},{8,0},{12,4},{1,9},{5,13},{9,1},{13,5},{2,10},{6,14},... | collective-permute-start | bytes 196616 | tf_op jit(solution)/shard_map/ppermute | solution.py:148
  6.7 1.3 %collective-permute-start.2 = (bf16[64,512]{1,0:T(8,128)(2,1)S(1)}, bf16[64,512]{1,0:T(8,128)(2,1)S(1)}, u32[]{:S(2)}, u32[]{:S(2)}) collective-permute-start(bf16[64,512]{1,0:T(8,128)(2,1)S(1)} %get-tuple-element.19), channel_id=1, source_target_pairs={{0,12},{4,0},{8,4},{12,8},{1,13},{5,1},{9,5},{13,9},{2,14},{6,2},{... | collective-permute-start | bytes 196616 | tf_op jit(solution)/shard_map/ppermute | solution.py:148
  8.1 1.5 %collective-permute-start.3 = (bf16[64,512]{1,0:T(8,128)(2,1)S(1)}, bf16[64,512]{1,0:T(8,128)(2,1)S(1)}, u32[]{:S(2)}, u32[]{:S(2)}) collective-permute-start(bf16[64,512]{1,0:T(8,128)(2,1)S(1)} %get-tuple-element.16.refs_0_), channel_id=1, source_target_pairs={{0,2},{2,0},{1,3},{3,1},{4,6},{6,4},{5,7},{7,5},{8,10},{10,8},{9,1... | collective-permute-start | bytes 196616 | tf_op jit(solution)/shard_map/ppermute | solution.py:151
  9.6 0.0 collective-permute-done.refs_1_
  9.6 1.0 %collective-permute-start.4 = (bf16[64,512]{1,0:T(8,128)(2,1)S(1)}, bf16[64,512]{1,0:T(8,128)(2,1)S(1)}, u32[]{:S(2)}, u32[]{:S(2)}) collective-permute-start(bf16[64,512]{1,0:T(8,128)(2,1)S(1)} %collective-permute-done.refs_1_), channel_id=1, source_target_pairs={{0,2},{2,0},{1,3},{3,1},{4,6},{6,4},{5,7},{7,5},{8,10},{10,8},{9,1... | collective-permute-start | bytes 196616 | tf_op jit(solution)/shard_map/ppermute | solution.py:151
  10.5 0.7 %collective-permute-done.1.refs_2_ = bf16[64,512]{1,0:T(8,128)(2,1)S(1)} collective-permute-done((bf16[64,512]{1,0:T(8,128)(2,1)S(1)}, bf16[64,512]{1,0:T(8,128)(2,1)S(1)}, u32[]{:S(2)}, u32[]{:S(2)}) %collective-permute-start.1) | collective-permute-done | bytes 65568 | tf_op jit(solution)/shard_map/ppermute | solution.py:148
  11.2 1.8 %collective-permute-start.5 = (bf16[64,512]{1,0:T(8,128)(2,1)S(1)}, bf16[64,512]{1,0:T(8,128)(2,1)S(1)}, u32[]{:S(2)}, u32[]{:S(2)}) collective-permute-start(bf16[64,512]{1,0:T(8,128)(2,1)S(1)} %collective-permute-done.1.refs_2_), channel_id=1, source_target_pairs={{0,2},{2,0},{1,3},{3,1},{4,6},{6,4},{5,7},{7,5},{8,10},{10,8},{9,1... | collective-permute-start | bytes 196616 | tf_op jit(solution)/shard_map/ppermute | solution.py:151
  13.0 0.0 collective-permute-done.2.refs_3_
  13.0 0.3 collective-permute-start.6
  13.2 0.0 copy-done.1
  13.2 0.3 shard_map.40.mine.sq_mine
  13.5 0.1 collective-permute-start.11
  13.6 1.2 %collective-permute-done.11.other.sq_other = f32[64,128]{1,0:T(8,128)S(1)} collective-permute-done((f32[64,128]{1,0:T(8,128)S(1)}, f32[64,128]{1,0:T(8,128)S(1)}, u32[]{:S(2)}, u32[]{:S(2)}) %collective-permute-start.11) | collective-permute-done | bytes 32800 | tf_op jit(solution)/shard_map/ppermute | solution.py:154
  14.8 0.1 shard_map.41.refs_0_
  14.9 1.3 %collective-permute-start.12 = (bf16[80,512]{1,0:T(8,128)(2,1)S(1)}, bf16[80,512]{1,0:T(8,128)(2,1)S(1)}, u32[]{:S(2)}, u32[]{:S(2)}) collective-permute-start(bf16[80,512]{1,0:T(8,128)(2,1)S(1)} %shard_map.41.refs_0_), channel_id=1, source_target_pairs={{0,4},{4,8},{8,12},{12,0},{1,5},{5,9},{9,13},{13,1},{2,6},{6,10},{... | collective-permute-start | bytes 245768 | tf_op jit(solution)/shard_map/ppermute | solution.py:148
  16.2 0.0 collective-permute-done.3.refs_4_
  16.2 2.6 %collective-permute-start.13 = (bf16[80,512]{1,0:T(8,128)(2,1)S(1)}, bf16[80,512]{1,0:T(8,128)(2,1)S(1)}, u32[]{:S(2)}, u32[]{:S(2)}) collective-permute-start(bf16[80,512]{1,0:T(8,128)(2,1)S(1)} %shard_map.41.refs_0_), channel_id=1, source_target_pairs={{0,8},{4,12},{8,0},{12,4},{1,9},{5,13},{9,1},{13,5},{2,10},{6,14},... | collective-permute-start | bytes 245768 | tf_op jit(solution)/shard_map/ppermute | solution.py:148
  18.8 0.0 collective-permute-done.4.refs_5_
  18.8 0.1 collective-permute-start.14
  18.9 0.0 collective-permute-done.5.refs_6_
  18.9 0.0 collective-permute-done.6.refs_7_
  18.9 0.8 %shard_map.38 = (f32[64,512]{1,0:T(8,128)S(1)}, bf16[64,512]{1,0:T(8,128)(2,1)S(1)}, bf16[64,512]{1,0:T(8,128)(2,1)S(1)}, bf16[64,512]{1,0:T(8,128)(2,1)S(1)}) custom-call(bf16[64,512]{1,0:T(8,128)(2,1)S(1)} %get-tuple-element.16.refs_0_, bf16[64,512]{1,0:T(8,128)(2,1)S(1)} %collective-permute-done.refs_1_, ...), custom_call_target="tpu_custom_call" | custom-call | flops 134217728 | bytes 851968 | tf_op jit(solution)/shard_map/pallas_call | solution.py:18
  19.7 1.9 %collective-permute-start.7 = (bf16[64,512]{1,0:T(8,128)(2,1)S(1)}, bf16[64,512]{1,0:T(8,128)(2,1)S(1)}, u32[]{:S(2)}, u32[]{:S(2)}) collective-permute-start(bf16[64,512]{1,0:T(8,128)(2,1)S(1)} %get-tuple-element.21), channel_id=1, source_target_pairs={{0,4},{4,8},{8,12},{12,0},{1,5},{5,9},{9,13},{13,1},{2,6},{6,10},{... | collective-permute-start | bytes 196616 | tf_op jit(solution)/shard_map/ppermute | solution.py:148
  21.7 0.4 collective-permute-start.8
  22.0 0.1 collective-permute-done.12.refs_1_
  22.1 1.8 %collective-permute-start.15 = (bf16[80,512]{1,0:T(8,128)(2,1)S(1)}, bf16[80,512]{1,0:T(8,128)(2,1)S(1)}, u32[]{:S(2)}, u32[]{:S(2)}) collective-permute-start(bf16[80,512]{1,0:T(8,128)(2,1)S(1)} %shard_map.41.refs_0_), channel_id=1, source_target_pairs={{0,2},{2,0},{1,3},{3,1},{4,6},{6,4},{5,7},{7,5},{8,10},{10,8},{9,1... | collective-permute-start | bytes 245768 | tf_op jit(solution)/shard_map/ppermute | solution.py:151
  23.9 3.8 %collective-permute-done.13.refs_2_ = bf16[80,512]{1,0:T(8,128)(2,1)S(1)} collective-permute-done((bf16[80,512]{1,0:T(8,128)(2,1)S(1)}, bf16[80,512]{1,0:T(8,128)(2,1)S(1)}, u32[]{:S(2)}, u32[]{:S(2)}) %collective-permute-start.13) | collective-permute-done | bytes 81952 | tf_op jit(solution)/shard_map/ppermute | solution.py:148
  27.7 1.7 %collective-permute-start.16 = (bf16[80,512]{1,0:T(8,128)(2,1)S(1)}, bf16[80,512]{1,0:T(8,128)(2,1)S(1)}, u32[]{:S(2)}, u32[]{:S(2)}) collective-permute-start(bf16[80,512]{1,0:T(8,128)(2,1)S(1)} %collective-permute-done.12.refs_1_), channel_id=1, source_target_pairs={{0,2},{2,0},{1,3},{3,1},{4,6},{6,4},{5,7},{7,5},{8,10},{10,8},{9,1... | collective-permute-start | bytes 245768 | tf_op jit(solution)/shard_map/ppermute | solution.py:151
  29.4 0.0 collective-permute-done.14.refs_3_
  29.4 0.3 collective-permute-start.17
  29.7 0.0 collective-permute-done.7.refs_1_
  29.8 1.7 %collective-permute-start.18 = (bf16[80,512]{1,0:T(8,128)(2,1)S(1)}, bf16[80,512]{1,0:T(8,128)(2,1)S(1)}, u32[]{:S(2)}, u32[]{:S(2)}) collective-permute-start(bf16[80,512]{1,0:T(8,128)(2,1)S(1)} %collective-permute-done.14.refs_3_), channel_id=1, source_target_pairs={{0,2},{2,0},{1,3},{3,1},{4,6},{6,4},{5,7},{7,5},{8,10},{10,8},{9,1... | collective-permute-start | bytes 245768 | tf_op jit(solution)/shard_map/ppermute | solution.py:151
  31.4 0.0 collective-permute-done.8.refs_2_
  31.4 1.9 %collective-permute-start.9 = (bf16[64,512]{1,0:T(8,128)(2,1)S(1)}, bf16[64,512]{1,0:T(8,128)(2,1)S(1)}, u32[]{:S(2)}, u32[]{:S(2)}) collective-permute-start(bf16[64,512]{1,0:T(8,128)(2,1)S(1)} %get-tuple-element.23), channel_id=1, source_target_pairs={{0,12},{4,0},{8,4},{12,8},{1,13},{5,1},{9,5},{13,9},{2,14},{6,2},{... | collective-permute-start | bytes 196616 | tf_op jit(solution)/shard_map/ppermute | solution.py:148
  33.4 2.3 %collective-permute-done.9.refs_3_ = bf16[64,512]{1,0:T(8,128)(2,1)S(1)} collective-permute-done((bf16[64,512]{1,0:T(8,128)(2,1)S(1)}, bf16[64,512]{1,0:T(8,128)(2,1)S(1)}, u32[]{:S(2)}, u32[]{:S(2)}) %collective-permute-start.9) | collective-permute-done | bytes 65568 | tf_op jit(solution)/shard_map/ppermute | solution.py:148
  35.7 0.1 collective-permute-start.10
  35.8 0.0 collective-permute-done.15.refs_4_
  35.8 0.0 collective-permute-done.16.refs_5_
  35.8 0.0 collective-permute-done.17.refs_6_
  35.9 0.0 collective-permute-done.18.refs_7_
  35.9 0.3 shard_map.42
  36.2 0.5 %collective-permute-start.19 = (f32[64,512]{1,0:T(8,128)S(1)}, f32[64,512]{1,0:T(8,128)S(1)}, u32[]{:S(2)}, u32[]{:S(2)}) collective-permute-start(f32[64,512]{1,0:T(8,128)S(1)} %get-tuple-element.24.gram_mine), channel_id=1, source_target_pairs={{0,1},{1,0},{2,3},{3,2},{4,5},{5,4},{6,7},{7,6},{8,9},{9,8},{10,11... | collective-permute-start | bytes 393224 | tf_op jit(solution)/shard_map/ppermute | solution.py:154
  36.7 0.4 %collective-permute-done.10.other = f32[64,512]{1,0:T(8,128)S(1)} collective-permute-done((f32[64,512]{1,0:T(8,128)S(1)}, f32[64,512]{1,0:T(8,128)S(1)}, u32[]{:S(2)}, u32[]{:S(2)}) %collective-permute-start.10) | collective-permute-done | bytes 131104 | tf_op jit(solution)/shard_map/ppermute | solution.py:154
  37.2 0.6 %collective-permute-done.19.gram_other = f32[64,512]{1,0:T(8,128)S(1)} collective-permute-done((f32[64,512]{1,0:T(8,128)S(1)}, f32[64,512]{1,0:T(8,128)S(1)}, u32[]{:S(2)}, u32[]{:S(2)}) %collective-permute-start.19) | collective-permute-done | bytes 131104 | tf_op jit(solution)/shard_map/ppermute | solution.py:154
  37.7 0.9 %shard_map.43 = f32[64,512]{1,0:T(8,128)} custom-call(f32[64,512]{1,0:T(8,128)S(1)} %shard_map.39.mine, f32[64,512]{1,0:T(8,128)S(1)} %collective-permute-done.10.other, f32[64,512]{1,0:T(8,128)S(1)} %get-tuple-element.24.gram_mine, f32[64,512]{1,0:T(8,128)S(1)} %collective-permute-done.19.gram_other, f32[16,512]{1,0:T(8,128)S(1)} %get-tuple-element.25.vectors, ...), custom_call_target="tpu_custom_call" | custom-call | flops 33554432 | bytes 1343616 | tf_op jit(solution)/shard_map/pallas_call | solution.py:18
  (5 shorter events, 0.0 us)
Async XLA Ops:
  0.0 0.9 %copy-start = (bf16[64,2048]{1,0:T(8,128)(2,1)S(1)}, bf16[64,2048]{1,0:T(8,128)(2,1)}, u32[]{:S(2)}) copy-start(bf16[64,2048]{1,0:T(8,128)(2,1)} %teach.3) | copy-start | bytes 786436
  1.0 12.3 %copy-start.1 = (bf16[64,512]{1,0:T(8,128)(2,1)S(1)}, bf16[64,512]{1,0:T(8,128)(2,1)}, u32[]{:S(2)}) copy-start(bf16[64,512]{1,0:T(8,128)(2,1)} %stud.5) | copy-start | bytes 196612
  1.0 8.5 %collective-permute-start = (bf16[64,512]{1,0:T(8,128)(2,1)S(1)}, bf16[64,512]{1,0:T(8,128)(2,1)S(1)}, u32[]{:S(2)}, u32[]{:S(2)}) collective-permute-start(bf16[64,512]{1,0:T(8,128)(2,1)S(1)} %get-tuple-element.17), channel_id=1, source_target_pairs={{0,4},{4,8},{8,12},{12,0},{1,5},{5,9},{9,13},{13,1},{2,6},{6,10},{... | collective-permute-start | bytes 196616 | tf_op jit(solution)/shard_map/ppermute | solution.py:148
  4.1 7.1 %collective-permute-start.1 = (bf16[64,512]{1,0:T(8,128)(2,1)S(1)}, bf16[64,512]{1,0:T(8,128)(2,1)S(1)}, u32[]{:S(2)}, u32[]{:S(2)}) collective-permute-start(bf16[64,512]{1,0:T(8,128)(2,1)S(1)} %get-tuple-element.18), channel_id=1, source_target_pairs={{0,8},{4,12},{8,0},{12,4},{1,9},{5,13},{9,1},{13,5},{2,10},{6,14},... | collective-permute-start | bytes 196616 | tf_op jit(solution)/shard_map/ppermute | solution.py:148
  6.7 6.3 %collective-permute-start.2 = (bf16[64,512]{1,0:T(8,128)(2,1)S(1)}, bf16[64,512]{1,0:T(8,128)(2,1)S(1)}, u32[]{:S(2)}, u32[]{:S(2)}) collective-permute-start(bf16[64,512]{1,0:T(8,128)(2,1)S(1)} %get-tuple-element.19), channel_id=1, source_target_pairs={{0,12},{4,0},{8,4},{12,8},{1,13},{5,1},{9,5},{13,9},{2,14},{6,2},{... | collective-permute-start | bytes 196616 | tf_op jit(solution)/shard_map/ppermute | solution.py:148
  8.1 5.2 %copy-start.2 = (bf16[64]{0:T(256)(128)(2,1)S(1)}, bf16[64]{0:T(256)(128)(2,1)}, u32[]{:S(2)}) copy-start(bf16[64]{0:T(256)(128)(2,1)} %param.5) | copy-start | bytes 388
  8.1 8.2 %collective-permute-start.3 = (bf16[64,512]{1,0:T(8,128)(2,1)S(1)}, bf16[64,512]{1,0:T(8,128)(2,1)S(1)}, u32[]{:S(2)}, u32[]{:S(2)}) collective-permute-start(bf16[64,512]{1,0:T(8,128)(2,1)S(1)} %get-tuple-element.16.refs_0_), channel_id=1, source_target_pairs={{0,2},{2,0},{1,3},{3,1},{4,6},{6,4},{5,7},{7,5},{8,10},{10,8},{9,1... | collective-permute-start | bytes 196616 | tf_op jit(solution)/shard_map/ppermute | solution.py:151
  9.6 9.2 %collective-permute-start.4 = (bf16[64,512]{1,0:T(8,128)(2,1)S(1)}, bf16[64,512]{1,0:T(8,128)(2,1)S(1)}, u32[]{:S(2)}, u32[]{:S(2)}) collective-permute-start(bf16[64,512]{1,0:T(8,128)(2,1)S(1)} %collective-permute-done.refs_1_), channel_id=1, source_target_pairs={{0,2},{2,0},{1,3},{3,1},{4,6},{6,4},{5,7},{7,5},{8,10},{10,8},{9,1... | collective-permute-start | bytes 196616 | tf_op jit(solution)/shard_map/ppermute | solution.py:151
  11.2 7.7 %collective-permute-start.5 = (bf16[64,512]{1,0:T(8,128)(2,1)S(1)}, bf16[64,512]{1,0:T(8,128)(2,1)S(1)}, u32[]{:S(2)}, u32[]{:S(2)}) collective-permute-start(bf16[64,512]{1,0:T(8,128)(2,1)S(1)} %collective-permute-done.1.refs_2_), channel_id=1, source_target_pairs={{0,2},{2,0},{1,3},{3,1},{4,6},{6,4},{5,7},{7,5},{8,10},{10,8},{9,1... | collective-permute-start | bytes 196616 | tf_op jit(solution)/shard_map/ppermute | solution.py:151
  13.0 6.0 %collective-permute-start.6 = (bf16[64,512]{1,0:T(8,128)(2,1)S(1)}, bf16[64,512]{1,0:T(8,128)(2,1)S(1)}, u32[]{:S(2)}, u32[]{:S(2)}) collective-permute-start(bf16[64,512]{1,0:T(8,128)(2,1)S(1)} %collective-permute-done.2.refs_3_), channel_id=1, source_target_pairs={{0,2},{2,0},{1,3},{3,1},{4,6},{6,4},{5,7},{7,5},{8,10},{10,8},{9,1... | collective-permute-start | bytes 196616 | tf_op jit(solution)/shard_map/ppermute | solution.py:151
  13.5 1.3 %collective-permute-start.11 = (f32[64,128]{1,0:T(8,128)S(1)}, f32[64,128]{1,0:T(8,128)S(1)}, u32[]{:S(2)}, u32[]{:S(2)}) collective-permute-start(f32[64,128]{1,0:T(8,128)S(1)} %shard_map.40.mine.sq_mine), channel_id=1, source_target_pairs={{0,1},{1,0},{2,3},{3,2},{4,5},{5,4},{6,7},{7,6},{8,9},{9,8},{10,11... | collective-permute-start | bytes 98312 | tf_op jit(solution)/shard_map/ppermute | solution.py:154
  14.9 7.2 %collective-permute-start.12 = (bf16[80,512]{1,0:T(8,128)(2,1)S(1)}, bf16[80,512]{1,0:T(8,128)(2,1)S(1)}, u32[]{:S(2)}, u32[]{:S(2)}) collective-permute-start(bf16[80,512]{1,0:T(8,128)(2,1)S(1)} %shard_map.41.refs_0_), channel_id=1, source_target_pairs={{0,4},{4,8},{8,12},{12,0},{1,5},{5,9},{9,13},{13,1},{2,6},{6,10},{... | collective-permute-start | bytes 245768 | tf_op jit(solution)/shard_map/ppermute | solution.py:148
  16.2 11.5 %collective-permute-start.13 = (bf16[80,512]{1,0:T(8,128)(2,1)S(1)}, bf16[80,512]{1,0:T(8,128)(2,1)S(1)}, u32[]{:S(2)}, u32[]{:S(2)}) collective-permute-start(bf16[80,512]{1,0:T(8,128)(2,1)S(1)} %shard_map.41.refs_0_), channel_id=1, source_target_pairs={{0,8},{4,12},{8,0},{12,4},{1,9},{5,13},{9,1},{13,5},{2,10},{6,14},... | collective-permute-start | bytes 245768 | tf_op jit(solution)/shard_map/ppermute | solution.py:148
  18.8 10.6 %collective-permute-start.14 = (bf16[80,512]{1,0:T(8,128)(2,1)S(1)}, bf16[80,512]{1,0:T(8,128)(2,1)S(1)}, u32[]{:S(2)}, u32[]{:S(2)}) collective-permute-start(bf16[80,512]{1,0:T(8,128)(2,1)S(1)} %shard_map.41.refs_0_), channel_id=1, source_target_pairs={{0,12},{4,0},{8,4},{12,8},{1,13},{5,1},{9,5},{13,9},{2,14},{6,2},{... | collective-permute-start | bytes 245768 | tf_op jit(solution)/shard_map/ppermute | solution.py:148
  19.7 10.0 %collective-permute-start.7 = (bf16[64,512]{1,0:T(8,128)(2,1)S(1)}, bf16[64,512]{1,0:T(8,128)(2,1)S(1)}, u32[]{:S(2)}, u32[]{:S(2)}) collective-permute-start(bf16[64,512]{1,0:T(8,128)(2,1)S(1)} %get-tuple-element.21), channel_id=1, source_target_pairs={{0,4},{4,8},{8,12},{12,0},{1,5},{5,9},{9,13},{13,1},{2,6},{6,10},{... | collective-permute-start | bytes 196616 | tf_op jit(solution)/shard_map/ppermute | solution.py:148
  21.7 9.8 %collective-permute-start.8 = (bf16[64,512]{1,0:T(8,128)(2,1)S(1)}, bf16[64,512]{1,0:T(8,128)(2,1)S(1)}, u32[]{:S(2)}, u32[]{:S(2)}) collective-permute-start(bf16[64,512]{1,0:T(8,128)(2,1)S(1)} %get-tuple-element.22), channel_id=1, source_target_pairs={{0,8},{4,12},{8,0},{12,4},{1,9},{5,13},{9,1},{13,5},{2,10},{6,14},... | collective-permute-start | bytes 196616 | tf_op jit(solution)/shard_map/ppermute | solution.py:148
  22.1 13.7 %collective-permute-start.15 = (bf16[80,512]{1,0:T(8,128)(2,1)S(1)}, bf16[80,512]{1,0:T(8,128)(2,1)S(1)}, u32[]{:S(2)}, u32[]{:S(2)}) collective-permute-start(bf16[80,512]{1,0:T(8,128)(2,1)S(1)} %shard_map.41.refs_0_), channel_id=1, source_target_pairs={{0,2},{2,0},{1,3},{3,1},{4,6},{6,4},{5,7},{7,5},{8,10},{10,8},{9,1... | collective-permute-start | bytes 245768 | tf_op jit(solution)/shard_map/ppermute | solution.py:151
  27.7 8.1 %collective-permute-start.16 = (bf16[80,512]{1,0:T(8,128)(2,1)S(1)}, bf16[80,512]{1,0:T(8,128)(2,1)S(1)}, u32[]{:S(2)}, u32[]{:S(2)}) collective-permute-start(bf16[80,512]{1,0:T(8,128)(2,1)S(1)} %collective-permute-done.12.refs_1_), channel_id=1, source_target_pairs={{0,2},{2,0},{1,3},{3,1},{4,6},{6,4},{5,7},{7,5},{8,10},{10,8},{9,1... | collective-permute-start | bytes 245768 | tf_op jit(solution)/shard_map/ppermute | solution.py:151
  29.4 6.4 %collective-permute-start.17 = (bf16[80,512]{1,0:T(8,128)(2,1)S(1)}, bf16[80,512]{1,0:T(8,128)(2,1)S(1)}, u32[]{:S(2)}, u32[]{:S(2)}) collective-permute-start(bf16[80,512]{1,0:T(8,128)(2,1)S(1)} %collective-permute-done.13.refs_2_), channel_id=1, source_target_pairs={{0,2},{2,0},{1,3},{3,1},{4,6},{6,4},{5,7},{7,5},{8,10},{10,8},{9,1... | collective-permute-start | bytes 245768 | tf_op jit(solution)/shard_map/ppermute | solution.py:151
  29.8 6.1 %collective-permute-start.18 = (bf16[80,512]{1,0:T(8,128)(2,1)S(1)}, bf16[80,512]{1,0:T(8,128)(2,1)S(1)}, u32[]{:S(2)}, u32[]{:S(2)}) collective-permute-start(bf16[80,512]{1,0:T(8,128)(2,1)S(1)} %collective-permute-done.14.refs_3_), channel_id=1, source_target_pairs={{0,2},{2,0},{1,3},{3,1},{4,6},{6,4},{5,7},{7,5},{8,10},{10,8},{9,1... | collective-permute-start | bytes 245768 | tf_op jit(solution)/shard_map/ppermute | solution.py:151
  31.4 4.3 %collective-permute-start.9 = (bf16[64,512]{1,0:T(8,128)(2,1)S(1)}, bf16[64,512]{1,0:T(8,128)(2,1)S(1)}, u32[]{:S(2)}, u32[]{:S(2)}) collective-permute-start(bf16[64,512]{1,0:T(8,128)(2,1)S(1)} %get-tuple-element.23), channel_id=1, source_target_pairs={{0,12},{4,0},{8,4},{12,8},{1,13},{5,1},{9,5},{13,9},{2,14},{6,2},{... | collective-permute-start | bytes 196616 | tf_op jit(solution)/shard_map/ppermute | solution.py:148
  35.7 1.4 %collective-permute-start.10 = (f32[64,512]{1,0:T(8,128)S(1)}, f32[64,512]{1,0:T(8,128)S(1)}, u32[]{:S(2)}, u32[]{:S(2)}) collective-permute-start(f32[64,512]{1,0:T(8,128)S(1)} %shard_map.39.mine), channel_id=1, source_target_pairs={{0,1},{1,0},{2,3},{3,2},{4,5},{5,4},{6,7},{7,6},{8,9},{9,8},{10,11... | collective-permute-start | bytes 393224 | tf_op jit(solution)/shard_map/ppermute | solution.py:154
  36.2 1.5 %collective-permute-start.19 = (f32[64,512]{1,0:T(8,128)S(1)}, f32[64,512]{1,0:T(8,128)S(1)}, u32[]{:S(2)}, u32[]{:S(2)}) collective-permute-start(f32[64,512]{1,0:T(8,128)S(1)} %get-tuple-element.24.gram_mine), channel_id=1, source_target_pairs={{0,1},{1,0},{2,3},{3,2},{4,5},{5,4},{6,7},{7,6},{8,9},{9,8},{10,11... | collective-permute-start | bytes 393224 | tf_op jit(solution)/shard_map/ppermute | solution.py:154

commit v3 on v2

v3 whole, which is shorter than its diff:
```python
import functools

import jax
import jax.numpy as jnp
from jax import lax
from jax.experimental import pallas as pl
from jax.experimental.pallas import tpu as pltpu
from jax.sharding import PartitionSpec as P

F32, BF16 = jnp.float32, jnp.bfloat16
INNER = (((1,), (1,)), ((), ()))
TAIL = 16


def call(body, out_shape, operands, flops=0, space=pltpu.VMEM, scratch=(), after=()):
    outs = out_shape if isinstance(out_shape, (list, tuple)) else [out_shape]
    moved = sum(x.size * x.dtype.itemsize for x in list(operands) + list(outs))

    def run(*refs):
        body(*refs[: len(operands)], *refs[len(operands) + len(after) :])

    return pl.pallas_call(
        run,
        out_shape=out_shape,
        in_specs=[pl.BlockSpec(memory_space=space)] * len(operands) + [pl.BlockSpec(memory_space=pl.ANY)] * len(after),
        out_specs=jax.tree.map(lambda _: pl.BlockSpec(memory_space=space), out_shape),
        scratch_shapes=list(scratch),
        cost_estimate=pl.CostEstimate(flops=flops, bytes_accessed=moved, transcendentals=0),
        compiler_params=pltpu.CompilerParams(vmem_limit_bytes=min(56 << 20, (8 << 20) + 3 * moved)),
    )(*operands, *after)


def column(row, first=0, count=None):
    shape = (count or row.shape[1], row.shape[1])
    eye = lax.broadcasted_iota(jnp.int32, shape, 0) + first == lax.broadcasted_iota(jnp.int32, shape, 1)
    return jnp.sum(jnp.where(eye, row, 0.0), axis=1, keepdims=True)


def tags_of(scales, mass):
    shape = (TAIL, scales.shape[1])
    at = lax.broadcasted_iota(jnp.int32, shape, 0)
    high = mass.astype(BF16).astype(F32)
    return jnp.where(at < 8, scales, jnp.where(at < 12, high, mass - high)).astype(BF16)


def read_tags(tags):
    tags = tags.astype(F32)
    return tags[0:1, :], tags[8:9, 0:1] + tags[12:13, 0:1]


def cut_kernel(nrow, teach, *refs):
    outs, sems = refs[:nrow], refs[nrow]
    part = teach.shape[1] // nrow
    z = lax.axis_index("row")
    copies = []
    for k in range(nrow):
        at = pl.multiple_of((z ^ k) * part, part)
        copies.append(pltpu.make_async_copy(teach.at[:, pl.ds(at, part)], outs[k], sems.at[k]))
    for c in copies:
        c.start()
    for c in copies:
        c.wait()


def square_kernel(stud, teach, scale, out):
    xs = stud[...].astype(F32)
    squares = jnp.sum(xs * xs, axis=1, keepdims=True)
    ts = teach[...].astype(F32)
    s = column(scale[...].astype(F32))
    mass = jnp.sum(s * s * jnp.sum(ts * ts, axis=1, keepdims=True), keepdims=True)
    lane = lax.broadcasted_iota(jnp.int32, out.shape, 1)
    out[...] = jnp.where(lane < 64, squares, mass)


def unit_kernel(stud, mine, other, scale, teach, unit, tagged):
    rows, part = teach.shape
    total = mine[...] + other[...]
    norm = jnp.sqrt(total[:, :1])
    unit[...] = (stud[...].astype(F32) / norm).astype(BF16)
    s = scale[...].astype(F32)
    tagged[:rows, :] = teach[...]
    tags = tags_of(jnp.concatenate([s, s], axis=1), total[:1, 64:65])
    tagged[rows:, :] = jnp.concatenate([tags] * (part // (2 * rows)), axis=1)


def pack_kernel(*refs):
    out, at = refs[-1], 0
    for r in refs[:-1]:
        out[at : at + r.shape[0], :] = r[...]
        at += r.shape[0]


def place(nrow, ncol, rows, k, c):
    return pl.multiple_of(((lax.axis_index("row") ^ k) * ncol + c) * rows, rows)


def assemble(nrow, ncol, rows, blocks, held):
    for c in range(ncol):
        for k, (ref, at) in blocks[c].items():
            held[pl.ds(place(nrow, ncol, rows, k, c), rows), :] = ref[at : at + rows, :]


def split(refs, groups, step):
    refs, blocks = list(refs), []
    for stack in groups:
        found = {}
        for keys in stack:
            ref = refs.pop(0)
            for n, k in enumerate(keys):
                found[k] = (ref, n * step)
        blocks.append(found)
    return blocks, refs


def gram_kernel(nrow, ncol, rows, groups, order, *refs):
    blocks, (kept, given, tags, held, left) = split(refs, groups, rows)
    assemble(nrow, ncol, rows, blocks, held)
    sub, half = rows // 2, nrow * rows // 2
    core = lax.axis_index("sub")
    for n, k in enumerate(order):
        ref, at = blocks[0][k]
        for target, which in ((0, core), (half, 1 - core)):
            rows_at = pl.multiple_of(at + which * sub, sub)
            left[target + n * sub : target + (n + 1) * sub, :] = ref[pl.ds(rows_at, sub), :]
    given[...] = lax.dot_general(left[half:, :], held[...], INNER, preferred_element_type=F32).astype(given.dtype)
    kept[...] = lax.dot_general(left[:half, :], held[...], INNER, preferred_element_type=F32).astype(kept.dtype)
    lane = lax.broadcasted_iota(jnp.int32, (TAIL, 2 * rows), 1)
    found = [[blocks[c + d][0][0][rows:, : 2 * rows].astype(F32) for d in (0, 1)] for c in range(0, ncol, 2)]
    mass = sum(read_tags(tag)[1] for pair in found for tag in pair)
    tags[...] = tags_of(jnp.zeros((1, tags.shape[1]), F32), mass)
    for c, pair in zip(range(0, ncol, 2), found):
        spot = pl.multiple_of(place(nrow, ncol, rows, 0, c), 2 * rows)
        tags[:, pl.ds(spot, 2 * rows)] = tags_of(jnp.where(lane < rows, *pair)[0:1, :], mass)


def fold_tags(tags, came, rows):
    if came.shape[0] == rows:
        return tags[...]
    (scales, mass), (more_scales, more_mass) = read_tags(tags[...]), read_tags(came[rows:, :])
    return tags_of(scales + more_scales, mass + more_mass)


def fold_kernel(kept, came, tags, keep, give, tags_out):
    rows = kept.shape[0]
    half = rows // 2
    folded = fold_tags(tags, came, rows)
    tags_out[...] = folded
    give[:half, :] = (kept[half:, :].astype(F32) + came[half:rows, :].astype(F32)).astype(BF16)
    give[half:, :] = folded
    keep[...] = (kept[:half, :].astype(F32) + came[:half, :].astype(F32)).astype(keep.dtype)


def error_kernel(batch, kept, came, tags, gram_mine, gram_other, scale, out):
    sub = kept.shape[0]
    first = lax.axis_index("sub") * sub
    at = pl.ds(pl.multiple_of(first, sub), sub)
    scales, mass = read_tags(fold_tags(tags, came, sub))
    total = kept[...].astype(F32) + came[:sub, :].astype(F32)
    outer = column(scale[...].astype(F32), first, sub) * scales
    error = gram_mine[at, :] + gram_other[at, :] - outer * total / (mass / batch)
    out[...] = error.astype(BF16)


def unit_gram_kernel(nrow, ncol, rows, groups, *refs):
    blocks, (gram, units) = split(refs, groups, rows)
    assemble(nrow, ncol, rows, blocks, units)
    own = blocks[0][0][0][:rows, :]
    gram[...] = lax.dot_general(own, units[...], INNER, preferred_element_type=F32)


def final_kernel(nrow, ncol, groups, mine, other, gram_mine, gram_other, stud, sq_mine, sq_other, *refs):
    rows = stud.shape[0]
    if groups:
        blocks, (out, error_b, units) = split(refs, groups, rows)
        assemble(nrow, ncol, rows, blocks, units)
    else:
        units, out, error_b = refs
    sub = rows // 2
    core = lax.axis_index("sub")
    error_b[pl.ds(pl.multiple_of(core * sub, sub), sub), :] = mine[...]
    error_b[pl.ds(pl.multiple_of((1 - core) * sub, sub), sub), :] = other[...]
    norm = jnp.sqrt(sq_mine[:, :1] + sq_other[:, :1])
    grads = 4.0 * jnp.dot(error_b[...], units[...], preferred_element_type=F32)
    unit_gram = gram_mine[...] + gram_other[...]
    along = 4.0 * jnp.sum(error_b[...].astype(F32) * unit_gram, axis=1, keepdims=True)
    unit = stud[...].astype(F32) / norm
    out[...] = (grads - along * unit) / norm


def shards(student, teacher, scale):
    rows, half = student.shape
    nrow, ncol = lax.axis_size("row"), lax.axis_size("col")
    batch = rows * nrow * ncol
    part = teacher.shape[1] // nrow
    small = batch <= 2048
    sds = jax.ShapeDtypeStruct
    scale = scale.reshape(1, rows)

    def along_row(x, k):
        return lax.ppermute(x, "row", [(i, i ^ k) for i in range(nrow)])

    def along_col(x, c):
        return lax.ppermute(x, "col", [(i, (i - c) % ncol) for i in range(ncol)])

    def other_core(x):
        return lax.ppermute(x, "sub", [(0, 1), (1, 0)])

    def pack(xs, after=()):
        if len(xs) == 1:
            return xs[0]
        return call(pack_kernel, sds((sum(x.shape[0] for x in xs), xs[0].shape[1]), BF16), xs, after=after)

    cuts = call(
        functools.partial(cut_kernel, nrow),
        [sds((rows, part), BF16)] * nrow,
        [teacher],
        space=pl.ANY,
        scratch=[pltpu.SemaphoreType.DMA((nrow,))],
    )
    teach = [None] + [along_row(cuts[k], k) for k in range(1, nrow)]
    squares = call(square_kernel, sds((rows, 128), F32), [student, teacher, scale], after=[cuts[0]])
    squares_other = other_core(squares)
    unit, teach[0] = call(
        unit_kernel,
        [sds((rows, half), BF16), sds((rows + TAIL, part), BF16)],
        [student, squares, squares_other, scale, cuts[0]],
        after=[teach[1]],
    )

    direct = [[k] for k in range(nrow)]
    early = nrow // 2
    teach_groups, teach_refs = [direct], list(teach)
    passed = [[along_col(t, c) for t in teach[:early]] for c in range(1, ncol)]
    late = pack(teach[early:], after=sum(passed, []))
    for c in range(1, ncol):
        teach_groups.append(direct[:early] + [list(range(early, nrow))])
        teach_refs += passed[c - 1] + [along_col(late, c)]

    stack, keys, k = unit, [0], nrow // 2
    while k > 1:
        stack = pack([stack, along_row(stack, k)])
        keys = keys + [n ^ k for n in keys]
        k //= 2
    stacks = [stack, along_row(stack, 1)]
    unit_groups = [[keys, [n ^ 1 for n in keys]]] * ncol
    units = stacks + [along_col(u, c) for c in range(1, ncol) for u in stacks]

    order = [0]
    while len(order) < nrow:
        order = [2 * n for n in order] + [2 * n + 1 for n in order]
    kept, given, tags = call(
        functools.partial(gram_kernel, nrow, ncol, rows, teach_groups, order),
        [sds((nrow * rows // 2, batch), F32 if small else BF16), sds((nrow * rows // 2, batch), BF16), sds((TAIL, batch), BF16)],
        teach_refs,
        flops=2 * rows * nrow * batch * part,
        scratch=[pltpu.VMEM((batch, part), BF16), pltpu.VMEM((nrow * rows, part), BF16)],
    )
    came, k = other_core(given), 1
    while k < nrow:
        count = kept.shape[0] // 2
        kept, give, tags = call(
            fold_kernel,
            [sds((count, batch), kept.dtype), sds((count + TAIL, batch), BF16), sds((TAIL, batch), BF16)],
            [kept, came, tags],
        )
        came = along_row(give, k)
        k *= 2

    held = [] if small else [pltpu.VMEM((batch, half), BF16)]
    unit_gram, *all_units = call(
        functools.partial(unit_gram_kernel, nrow, ncol, rows, unit_groups),
        [sds((rows, batch), F32)] + ([sds((batch, half), BF16)] if small else []),
        units,
        flops=2 * rows * batch * half,
        scratch=held,
    )
    unit_gram_other = other_core(unit_gram)
    error_b = call(
        functools.partial(error_kernel, batch),
        sds((rows // 2, batch), BF16),
        [kept, came, tags, unit_gram, unit_gram_other, scale],
    )
    return call(
        functools.partial(final_kernel, nrow, ncol, None if small else unit_groups),
        sds((rows, half), F32),
        [error_b, other_core(error_b), unit_gram, unit_gram_other, student, squares, squares_other] + (all_units if small else units),
        flops=2 * rows * batch * half,
        scratch=[pltpu.VMEM((rows, batch), BF16)] + held,
    )


def solution(mesh):
    spec = P(("groups", "row", "col"), "sub")
    return jax.shard_map(
        shards,
        mesh=mesh,
        in_specs=(spec, spec, P(("groups", "row", "col"))),
        out_specs=spec,
        check_vma=False,
    )
```

time: 38.8 us -> 40.5 us (1.044)
  waiting for transfers between devices: 9.14 us -> 18.5 us
  starting transfers between devices: 25.9 us -> 17.8 us
  local copies, waits for them, and re-layouts: 0.96 us -> 1.61 us
    ppermute x8 -> x5, waiting for transfers between devices: 0.02 us -> 7.28 us  [along_col(): return lax.ppermute(x, 'col', [(i, (i - c) % ncol) for i in range(ncol)])]
    ppermute x8 -> x5, starting transfers between devices: 9.97 us -> 3.43 us  [along_col(): return lax.ppermute(x, 'col', [(i, (i - c) % ncol) for i in range(ncol)])]
    ppermute x9 -> x7, waiting for transfers between devices: 6.94 us -> 8.79 us  [along_row(): return lax.ppermute(x, 'row', [(i, i ^ k) for i in range(nrow)])]
    ppermute x9 -> x7, starting transfers between devices: 15.3 us -> 14.1 us  [along_row(): return lax.ppermute(x, 'row', [(i, i ^ k) for i in range(nrow)])]
    unnamed x6, local copies, waits for them, and re-layouts: 0.96 us -> 1.61 us
    ppermute x3 -> x4, waiting for transfers between devices: 2.18 us -> 2.39 us  [other_core(): return lax.ppermute(x, 'sub', [(0, 1), (1, 0)])]
    pallas_call x7 -> x11, Pallas kernels: 2.53 us -> 2.36 us  [call(): pl.pallas_call(run, out_shape=out_shape, in_specs=[pl.BlockSpec(memory_sp...]
  transfers between devices with their start and end apart: 20 -> 16, of which waited for: 7 -> 10; matrix products, arithmetic and copies ran while one was open for 0% -> 0% of each run, Pallas kernels for 4% -> 3%
where the time goes in v3:
time: 40.5 us; the launch traced here: 40.4 us
  waiting for transfers between devices  18.5 us (46%)
  starting transfers between devices  17.8 us (44%)
  Pallas kernels  2.36 us (6%)
  local copies, waits for them, and re-layouts  1.61 us (4%)
    ppermute x7, starting transfers between devices, along_row(): return lax.ppermute(x, 'row', [(i, i ^ k) for i in range(nrow)])  14.1 us
    ppermute x7, waiting for transfers between devices, along_row(): return lax.ppermute(x, 'row', [(i, i ^ k) for i in range(nrow)])  8.79 us
    ppermute x5, waiting for transfers between devices, along_col(): return lax.ppermute(x, 'col', [(i, (i - c) % ncol) for i in range(ncol)])  7.28 us
    ppermute x5, starting transfers between devices, along_col(): return lax.ppermute(x, 'col', [(i, (i - c) % ncol) for i in range(ncol)])  3.43 us
    ppermute x4, waiting for transfers between devices, other_core(): return lax.ppermute(x, 'sub', [(0, 1), (1, 0)])  2.39 us
    pallas_call x11, Pallas kernels, call(): pl.pallas_call(run, out_shape=out_shape, in_specs=[pl.BlockSpec(memory_sp...  2.36 us
    unnamed x6, local copies, waits for them, and re-layouts  1.61 us
  transfers between devices with their start and end apart: 16, of which 10 were waited for; matrix products, arithmetic and copies ran while one was open for 0% of the time, Pallas kernels for 3%

profile of v3, /device:TPU:0, one launch (start us, length us, event | category | flops | bytes accessed | tf_op | source)
XLA Modules:
  0.0 40.4 jit_solution(12816944416008951194)
XLA Ops:
  0.0 0.0 copy-start
  0.0 0.9 %copy-done = bf16[64,2048]{1,0:T(8,128)(2,1)S(1)} copy-done((bf16[64,2048]{1,0:T(8,128)(2,1)S(1)}, bf16[64,2048]{1,0:T(8,128)(2,1)}, u32[]{:S(2)}) %copy-start) | copy-done | bytes 262168
  1.0 0.0 copy-start.1
  1.0 0.1 shard_map.37
  1.0 3.1 %collective-permute-start.1 = (bf16[64,512]{1,0:T(8,128)(2,1)S(1)}, bf16[64,512]{1,0:T(8,128)(2,1)S(1)}, u32[]{:S(2)}, u32[]{:S(2)}) collective-permute-start(bf16[64,512]{1,0:T(8,128)(2,1)S(1)} %get-tuple-element.23), channel_id=1, source_target_pairs={{0,4},{4,0},{8,12},{12,8},{1,5},{5,1},{9,13},{13,9},{2,6},{6,2},{1... | collective-permute-start | bytes 196616 | tf_op jit(solution)/shard_map/ppermute | solution.py:200
  4.1 0.0 copy-start.2
  4.1 0.0 copy-done.1
  4.1 0.7 %copy-done.2 = bf16[64]{0:T(256)(128)(2,1)S(1)} copy-done((bf16[64]{0:T(256)(128)(2,1)S(1)}, bf16[64]{0:T(256)(128)(2,1)}, u32[]{:S(2)}) %copy-start.2) | copy-done | bytes 152
  4.8 0.3 shard_map.38.refs_1_.refs_5_
  5.1 0.1 collective-permute-start
  5.1 1.2 %collective-permute-done.refs_2_.refs_6_ = f32[64,128]{1,0:T(8,128)S(1)} collective-permute-done((f32[64,128]{1,0:T(8,128)S(1)}, f32[64,128]{1,0:T(8,128)S(1)}, u32[]{:S(2)}, u32[]{:S(2)}) %collective-permute-start) | collective-permute-done | bytes 32800 | tf_op jit(solution)/shard_map/ppermute | solution.py:206
  6.3 0.1 collective-permute-done.1.refs_5_.refs_1_
  6.4 0.1 shard_map.39
  6.5 2.0 %collective-permute-start.4 = (bf16[80,512]{1,0:T(8,128)(2,1)S(1)}, bf16[80,512]{1,0:T(8,128)(2,1)S(1)}, u32[]{:S(2)}, u32[]{:S(2)}) collective-permute-start(bf16[80,512]{1,0:T(8,128)(2,1)S(1)} %get-tuple-element.24.refs_0_), channel_id=1, source_target_pairs={{0,2},{2,0},{1,3},{3,1},{4,6},{6,4},{5,7},{7,5},{8,10},{10,8},{9,1... | collective-permute-start | bytes 245768 | tf_op jit(solution)/shard_map/ppermute | solution.py:203
  8.5 2.6 %collective-permute-start.2 = (bf16[64,512]{1,0:T(8,128)(2,1)S(1)}, bf16[64,512]{1,0:T(8,128)(2,1)S(1)}, u32[]{:S(2)}, u32[]{:S(2)}) collective-permute-start(bf16[64,512]{1,0:T(8,128)(2,1)S(1)} %get-tuple-element.25), channel_id=1, source_target_pairs={{0,8},{4,12},{8,0},{12,4},{1,9},{5,13},{9,1},{13,5},{2,10},{6,14},... | collective-permute-start | bytes 196616 | tf_op jit(solution)/shard_map/ppermute | solution.py:200
  11.1 1.3 %collective-permute-start.3 = (bf16[64,512]{1,0:T(8,128)(2,1)S(1)}, bf16[64,512]{1,0:T(8,128)(2,1)S(1)}, u32[]{:S(2)}, u32[]{:S(2)}) collective-permute-start(bf16[64,512]{1,0:T(8,128)(2,1)S(1)} %get-tuple-element.26), channel_id=1, source_target_pairs={{0,12},{4,8},{8,4},{12,0},{1,13},{5,9},{9,5},{13,1},{2,14},{6,10},... | collective-permute-start | bytes 196616 | tf_op jit(solution)/shard_map/ppermute | solution.py:200
  12.4 0.5 %collective-permute-start.5 = (bf16[64,512]{1,0:T(8,128)(2,1)S(1)}, bf16[64,512]{1,0:T(8,128)(2,1)S(1)}, u32[]{:S(2)}, u32[]{:S(2)}) collective-permute-start(bf16[64,512]{1,0:T(8,128)(2,1)S(1)} %collective-permute-done.1.refs_5_.refs_1_), channel_id=1, source_target_pairs={{0,2},{2,0},{1,3},{3,1},{4,6},{6,4},{5,7},{7,5},{8,10},{10,8},{9,1... | collective-permute-start | bytes 196616 | tf_op jit(solution)/shard_map/ppermute | solution.py:203
  13.0 1.7 %collective-permute-start.10 = (bf16[64,512]{1,0:T(8,128)(2,1)S(1)}, bf16[64,512]{1,0:T(8,128)(2,1)S(1)}, u32[]{:S(2)}, u32[]{:S(2)}) collective-permute-start(bf16[64,512]{1,0:T(8,128)(2,1)S(1)} %get-tuple-element.36.refs_0_), channel_id=1, source_target_pairs={{0,8},{4,12},{8,0},{12,4},{1,9},{5,13},{9,1},{13,5},{2,10},{6,14},... | collective-permute-start | bytes 196616 | tf_op jit(solution)/shard_map/ppermute | solution.py:200
  14.7 3.2 %collective-permute-done.2.refs_0_.refs_2_ = bf16[64,512]{1,0:T(8,128)(2,1)S(1)} collective-permute-done((bf16[64,512]{1,0:T(8,128)(2,1)S(1)}, bf16[64,512]{1,0:T(8,128)(2,1)S(1)}, u32[]{:S(2)}, u32[]{:S(2)}) %collective-permute-start.2) | collective-permute-done | bytes 65568 | tf_op jit(solution)/shard_map/ppermute | solution.py:200
  17.9 0.0 collective-permute-done.3.refs_1_.refs_3_
  17.9 0.0 collective-permute-done.5.refs_3_.refs_5_
  17.9 0.0 collective-permute-done.4.refs_2_.refs_4_
  17.9 0.1 collective-permute-start.6
  18.0 1.9 %collective-permute-done.10.refs_1_ = bf16[64,512]{1,0:T(8,128)(2,1)S(1)} collective-permute-done((bf16[64,512]{1,0:T(8,128)(2,1)S(1)}, bf16[64,512]{1,0:T(8,128)(2,1)S(1)}, u32[]{:S(2)}, u32[]{:S(2)}) %collective-permute-start.10) | collective-permute-done | bytes 65568 | tf_op jit(solution)/shard_map/ppermute | solution.py:200
  19.9 0.5 %collective-permute-start.11 = (bf16[128,512]{1,0:T(8,128)(2,1)S(1)}, bf16[128,512]{1,0:T(8,128)(2,1)S(1)}, u32[]{:S(2)}, u32[]{:S(2)}) collective-permute-start(bf16[128,512]{1,0:T(8,128)(2,1)S(1)} %shard_map.44.refs_0_), channel_id=1, source_target_pairs={{0,4},{4,0},{8,12},{12,8},{1,5},{5,1},{9,13},{13,9},{2,6},{6,2},{1... | collective-permute-start | bytes 393224 | tf_op jit(solution)/shard_map/ppermute | solution.py:200
  20.4 2.6 %collective-permute-done.6.refs_6_ = bf16[128,512]{1,0:T(8,128)(2,1)S(1)} collective-permute-done((bf16[128,512]{1,0:T(8,128)(2,1)S(1)}, bf16[128,512]{1,0:T(8,128)(2,1)S(1)}, u32[]{:S(2)}, u32[]{:S(2)}) %collective-permute-start.6) | collective-permute-done | bytes 131104 | tf_op jit(solution)/shard_map/ppermute | solution.py:203
  22.9 0.5 %shard_map.41 = (f32[128,512]{1,0:T(8,128)S(1)}, bf16[128,512]{1,0:T(8,128)(2,1)S(1)}, bf16[16,512]{1,0:T(8,128)(2,1)S(1)}) custom-call(bf16[80,512]{1,0:T(8,128)(2,1)S(1)} %get-tuple-element.24.refs_0_, bf16[64,512]{1,0:T(8,128)(2,1)S(1)} %collective-permute-done.1.refs_5_.refs_1_, bf16[64,512]{1,0:T(8,128)(2,1)S(1)} %collective-permute-done.2.refs_0_.refs_2_, ...), custom_call_target="tpu_custom_call" | custom-call | flops 134217728 | bytes 966656 | tf_op jit(solution)/shard_map/pallas_call | solution.py:22
  23.5 0.1 collective-permute-start.7
  23.5 0.1 collective-permute-start.12
  23.6 1.3 %collective-permute-done.11.refs_1_ = bf16[128,512]{1,0:T(8,128)(2,1)S(1)} collective-permute-done((bf16[128,512]{1,0:T(8,128)(2,1)S(1)}, bf16[128,512]{1,0:T(8,128)(2,1)S(1)}, u32[]{:S(2)}, u32[]{:S(2)}) %collective-permute-start.11) | collective-permute-done | bytes 131104 | tf_op jit(solution)/shard_map/ppermute | solution.py:200
  24.9 0.8 %collective-permute-start.13 = (bf16[128,512]{1,0:T(8,128)(2,1)S(1)}, bf16[128,512]{1,0:T(8,128)(2,1)S(1)}, u32[]{:S(2)}, u32[]{:S(2)}) collective-permute-start(bf16[128,512]{1,0:T(8,128)(2,1)S(1)} %collective-permute-done.11.refs_1_), channel_id=1, source_target_pairs={{0,2},{2,0},{1,3},{3,1},{4,6},{6,4},{5,7},{7,5},{8,10},{10,8},{9,1... | collective-permute-start | bytes 393224 | tf_op jit(solution)/shard_map/ppermute | solution.py:203
  25.6 0.0 collective-permute-done.7.refs_1_
  25.7 1.9 %collective-permute-start.8 = (bf16[80,512]{1,0:T(8,128)(2,1)S(1)}, bf16[80,512]{1,0:T(8,128)(2,1)S(1)}, u32[]{:S(2)}, u32[]{:S(2)}) collective-permute-start(bf16[80,512]{1,0:T(8,128)(2,1)S(1)} %get-tuple-element.31), channel_id=1, source_target_pairs={{0,4},{4,0},{8,12},{12,8},{1,5},{5,1},{9,13},{13,9},{2,6},{6,2},{1... | collective-permute-start | bytes 245768 | tf_op jit(solution)/shard_map/ppermute | solution.py:200
  27.6 2.4 %collective-permute-done.12.refs_2_ = bf16[128,512]{1,0:T(8,128)(2,1)S(1)} collective-permute-done((bf16[128,512]{1,0:T(8,128)(2,1)S(1)}, bf16[128,512]{1,0:T(8,128)(2,1)S(1)}, u32[]{:S(2)}, u32[]{:S(2)}) %collective-permute-start.12) | collective-permute-done | bytes 131104 | tf_op jit(solution)/shard_map/ppermute | solution.py:203
  29.9 2.4 %collective-permute-done.13.refs_3_ = bf16[128,512]{1,0:T(8,128)(2,1)S(1)} collective-permute-done((bf16[128,512]{1,0:T(8,128)(2,1)S(1)}, bf16[128,512]{1,0:T(8,128)(2,1)S(1)}, u32[]{:S(2)}, u32[]{:S(2)}) %collective-permute-start.13) | collective-permute-done | bytes 131104 | tf_op jit(solution)/shard_map/ppermute | solution.py:203
  32.3 0.3 shard_map.45
  32.6 0.1 collective-permute-start.14
  32.7 0.0 collective-permute-done.8.refs_1_
  32.7 0.1 shard_map.43
  32.7 3.0 %collective-permute-start.9 = (bf16[48,512]{1,0:T(8,128)(2,1)S(1)}, bf16[48,512]{1,0:T(8,128)(2,1)S(1)}, u32[]{:S(2)}, u32[]{:S(2)}) collective-permute-start(bf16[48,512]{1,0:T(8,128)(2,1)S(1)} %get-tuple-element.34), channel_id=1, source_target_pairs={{0,8},{4,12},{8,0},{12,4},{1,9},{5,13},{9,1},{13,5},{2,10},{6,14},... | collective-permute-start | bytes 147464 | tf_op jit(solution)/shard_map/ppermute | solution.py:200
  35.7 0.0 collective-permute-done.14.refs_4_.refs_3_
  35.7 2.4 %collective-permute-done.9.refs_1_ = bf16[48,512]{1,0:T(8,128)(2,1)S(1)} collective-permute-done((bf16[48,512]{1,0:T(8,128)(2,1)S(1)}, bf16[48,512]{1,0:T(8,128)(2,1)S(1)}, u32[]{:S(2)}, u32[]{:S(2)}) %collective-permute-start.9) | collective-permute-done | bytes 49184 | tf_op jit(solution)/shard_map/ppermute | solution.py:200
  38.2 0.1 shard_map.46.refs_0_
  38.3 0.1 collective-permute-start.15
  38.3 1.2 %collective-permute-done.15.refs_1_ = bf16[32,512]{1,0:T(8,128)(2,1)S(1)} collective-permute-done((bf16[32,512]{1,0:T(8,128)(2,1)S(1)}, bf16[32,512]{1,0:T(8,128)(2,1)S(1)}, u32[]{:S(2)}, u32[]{:S(2)}) %collective-permute-start.15) | collective-permute-done | bytes 32800 | tf_op jit(solution)/shard_map/ppermute | solution.py:206
  39.5 0.9 %shard_map.47 = f32[64,512]{1,0:T(8,128)} custom-call(bf16[32,512]{1,0:T(8,128)(2,1)S(1)} %shard_map.46.refs_0_, bf16[32,512]{1,0:T(8,128)(2,1)S(1)} %collective-permute-done.15.refs_1_, f32[64,512]{1,0:T(8,128)S(1)} %get-tuple-element.37.refs_3_.refs_2_, f32[64,512]{1,0:T(8,128)S(1)} %collective-permute-done.14.refs_4_.refs_3_, ...), custom_call_target="tpu_custom_call" | custom-call | flops 33554432 | bytes 1114112 | tf_op jit(solution)/shard_map/pallas_call | solution.py:22
  (3 shorter events, 0.0 us)
Async XLA Ops:
  0.0 0.9 %copy-start = (bf16[64,2048]{1,0:T(8,128)(2,1)S(1)}, bf16[64,2048]{1,0:T(8,128)(2,1)}, u32[]{:S(2)}) copy-start(bf16[64,2048]{1,0:T(8,128)(2,1)} %refs_1_.1) | copy-start | bytes 786436
  1.0 3.2 %copy-start.1 = (bf16[64,512]{1,0:T(8,128)(2,1)S(1)}, bf16[64,512]{1,0:T(8,128)(2,1)}, u32[]{:S(2)}) copy-start(bf16[64,512]{1,0:T(8,128)(2,1)} %refs_4_.1) | copy-start | bytes 196612
  1.0 5.3 %collective-permute-start.1 = (bf16[64,512]{1,0:T(8,128)(2,1)S(1)}, bf16[64,512]{1,0:T(8,128)(2,1)S(1)}, u32[]{:S(2)}, u32[]{:S(2)}) collective-permute-start(bf16[64,512]{1,0:T(8,128)(2,1)S(1)} %get-tuple-element.23), channel_id=1, source_target_pairs={{0,4},{4,0},{8,12},{12,8},{1,5},{5,1},{9,13},{13,9},{2,6},{6,2},{1... | collective-permute-start | bytes 196616 | tf_op jit(solution)/shard_map/ppermute | solution.py:200
  4.1 0.7 %copy-start.2 = (bf16[64]{0:T(256)(128)(2,1)S(1)}, bf16[64]{0:T(256)(128)(2,1)}, u32[]{:S(2)}) copy-start(bf16[64]{0:T(256)(128)(2,1)} %param.5) | copy-start | bytes 388
  5.1 1.3 %collective-permute-start = (f32[64,128]{1,0:T(8,128)S(1)}, f32[64,128]{1,0:T(8,128)S(1)}, u32[]{:S(2)}, u32[]{:S(2)}) collective-permute-start(f32[64,128]{1,0:T(8,128)S(1)} %shard_map.38.refs_1_.refs_5_), channel_id=1, source_target_pairs={{0,1},{1,0},{2,3},{3,2},{4,5},{5,4},{6,7},{7,6},{8,9},{9,8},{10,11... | collective-permute-start | bytes 98312 | tf_op jit(solution)/shard_map/ppermute | solution.py:206
  6.5 11.4 %collective-permute-start.4 = (bf16[80,512]{1,0:T(8,128)(2,1)S(1)}, bf16[80,512]{1,0:T(8,128)(2,1)S(1)}, u32[]{:S(2)}, u32[]{:S(2)}) collective-permute-start(bf16[80,512]{1,0:T(8,128)(2,1)S(1)} %get-tuple-element.24.refs_0_), channel_id=1, source_target_pairs={{0,2},{2,0},{1,3},{3,1},{4,6},{6,4},{5,7},{7,5},{8,10},{10,8},{9,1... | collective-permute-start | bytes 245768 | tf_op jit(solution)/shard_map/ppermute | solution.py:203
  8.5 9.4 %collective-permute-start.2 = (bf16[64,512]{1,0:T(8,128)(2,1)S(1)}, bf16[64,512]{1,0:T(8,128)(2,1)S(1)}, u32[]{:S(2)}, u32[]{:S(2)}) collective-permute-start(bf16[64,512]{1,0:T(8,128)(2,1)S(1)} %get-tuple-element.25), channel_id=1, source_target_pairs={{0,8},{4,12},{8,0},{12,4},{1,9},{5,13},{9,1},{13,5},{2,10},{6,14},... | collective-permute-start | bytes 196616 | tf_op jit(solution)/shard_map/ppermute | solution.py:200
  11.1 6.8 %collective-permute-start.3 = (bf16[64,512]{1,0:T(8,128)(2,1)S(1)}, bf16[64,512]{1,0:T(8,128)(2,1)S(1)}, u32[]{:S(2)}, u32[]{:S(2)}) collective-permute-start(bf16[64,512]{1,0:T(8,128)(2,1)S(1)} %get-tuple-element.26), channel_id=1, source_target_pairs={{0,12},{4,8},{8,4},{12,0},{1,13},{5,9},{9,5},{13,1},{2,14},{6,10},... | collective-permute-start | bytes 196616 | tf_op jit(solution)/shard_map/ppermute | solution.py:200
  12.4 5.4 %collective-permute-start.5 = (bf16[64,512]{1,0:T(8,128)(2,1)S(1)}, bf16[64,512]{1,0:T(8,128)(2,1)S(1)}, u32[]{:S(2)}, u32[]{:S(2)}) collective-permute-start(bf16[64,512]{1,0:T(8,128)(2,1)S(1)} %collective-permute-done.1.refs_5_.refs_1_), channel_id=1, source_target_pairs={{0,2},{2,0},{1,3},{3,1},{4,6},{6,4},{5,7},{7,5},{8,10},{10,8},{9,1... | collective-permute-start | bytes 196616 | tf_op jit(solution)/shard_map/ppermute | solution.py:203
  13.0 6.9 %collective-permute-start.10 = (bf16[64,512]{1,0:T(8,128)(2,1)S(1)}, bf16[64,512]{1,0:T(8,128)(2,1)S(1)}, u32[]{:S(2)}, u32[]{:S(2)}) collective-permute-start(bf16[64,512]{1,0:T(8,128)(2,1)S(1)} %get-tuple-element.36.refs_0_), channel_id=1, source_target_pairs={{0,8},{4,12},{8,0},{12,4},{1,9},{5,13},{9,1},{13,5},{2,10},{6,14},... | collective-permute-start | bytes 196616 | tf_op jit(solution)/shard_map/ppermute | solution.py:200
  17.9 5.0 %collective-permute-start.6 = (bf16[128,512]{1,0:T(8,128)(2,1)S(1)}, bf16[128,512]{1,0:T(8,128)(2,1)S(1)}, u32[]{:S(2)}, u32[]{:S(2)}) collective-permute-start(bf16[128,512]{1,0:T(8,128)(2,1)S(1)} %shard_map.40), channel_id=1, source_target_pairs={{0,2},{2,0},{1,3},{3,1},{4,6},{6,4},{5,7},{7,5},{8,10},{10,8},{9,1... | collective-permute-start | bytes 393224 | tf_op jit(solution)/shard_map/ppermute | solution.py:203
  19.9 5.0 %collective-permute-start.11 = (bf16[128,512]{1,0:T(8,128)(2,1)S(1)}, bf16[128,512]{1,0:T(8,128)(2,1)S(1)}, u32[]{:S(2)}, u32[]{:S(2)}) collective-permute-start(bf16[128,512]{1,0:T(8,128)(2,1)S(1)} %shard_map.44.refs_0_), channel_id=1, source_target_pairs={{0,4},{4,0},{8,12},{12,8},{1,5},{5,1},{9,13},{13,9},{2,6},{6,2},{1... | collective-permute-start | bytes 393224 | tf_op jit(solution)/shard_map/ppermute | solution.py:200
  23.5 2.2 %collective-permute-start.7 = (bf16[128,512]{1,0:T(8,128)(2,1)S(1)}, bf16[128,512]{1,0:T(8,128)(2,1)S(1)}, u32[]{:S(2)}, u32[]{:S(2)}) collective-permute-start(bf16[128,512]{1,0:T(8,128)(2,1)S(1)} %get-tuple-element.28), channel_id=1, source_target_pairs={{0,1},{1,0},{2,3},{3,2},{4,5},{5,4},{6,7},{7,6},{8,9},{9,8},{10,11... | collective-permute-start | bytes 393224 | tf_op jit(solution)/shard_map/ppermute | solution.py:206
  23.5 6.4 %collective-permute-start.12 = (bf16[128,512]{1,0:T(8,128)(2,1)S(1)}, bf16[128,512]{1,0:T(8,128)(2,1)S(1)}, u32[]{:S(2)}, u32[]{:S(2)}) collective-permute-start(bf16[128,512]{1,0:T(8,128)(2,1)S(1)} %shard_map.44.refs_0_), channel_id=1, source_target_pairs={{0,2},{2,0},{1,3},{3,1},{4,6},{6,4},{5,7},{7,5},{8,10},{10,8},{9,1... | collective-permute-start | bytes 393224 | tf_op jit(solution)/shard_map/ppermute | solution.py:203
  24.9 7.4 %collective-permute-start.13 = (bf16[128,512]{1,0:T(8,128)(2,1)S(1)}, bf16[128,512]{1,0:T(8,128)(2,1)S(1)}, u32[]{:S(2)}, u32[]{:S(2)}) collective-permute-start(bf16[128,512]{1,0:T(8,128)(2,1)S(1)} %collective-permute-done.11.refs_1_), channel_id=1, source_target_pairs={{0,2},{2,0},{1,3},{3,1},{4,6},{6,4},{5,7},{7,5},{8,10},{10,8},{9,1... | collective-permute-start | bytes 393224 | tf_op jit(solution)/shard_map/ppermute | solution.py:203
  25.7 7.0 %collective-permute-start.8 = (bf16[80,512]{1,0:T(8,128)(2,1)S(1)}, bf16[80,512]{1,0:T(8,128)(2,1)S(1)}, u32[]{:S(2)}, u32[]{:S(2)}) collective-permute-start(bf16[80,512]{1,0:T(8,128)(2,1)S(1)} %get-tuple-element.31), channel_id=1, source_target_pairs={{0,4},{4,0},{8,12},{12,8},{1,5},{5,1},{9,13},{13,9},{2,6},{6,2},{1... | collective-permute-start | bytes 245768 | tf_op jit(solution)/shard_map/ppermute | solution.py:200
  32.6 3.2 %collective-permute-start.14 = (f32[64,512]{1,0:T(8,128)S(1)}, f32[64,512]{1,0:T(8,128)S(1)}, u32[]{:S(2)}, u32[]{:S(2)}) collective-permute-start(f32[64,512]{1,0:T(8,128)S(1)} %get-tuple-element.37.refs_3_.refs_2_), channel_id=1, source_target_pairs={{0,1},{1,0},{2,3},{3,2},{4,5},{5,4},{6,7},{7,6},{8,9},{9,8},{10,11... | collective-permute-start | bytes 393224 | tf_op jit(solution)/shard_map/ppermute | solution.py:206
  32.7 5.4 %collective-permute-start.9 = (bf16[48,512]{1,0:T(8,128)(2,1)S(1)}, bf16[48,512]{1,0:T(8,128)(2,1)S(1)}, u32[]{:S(2)}, u32[]{:S(2)}) collective-permute-start(bf16[48,512]{1,0:T(8,128)(2,1)S(1)} %get-tuple-element.34), channel_id=1, source_target_pairs={{0,8},{4,12},{8,0},{12,4},{1,9},{5,13},{9,1},{13,5},{2,10},{6,14},... | collective-permute-start | bytes 147464 | tf_op jit(solution)/shard_map/ppermute | solution.py:200
  38.3 1.3 %collective-permute-start.15 = (bf16[32,512]{1,0:T(8,128)(2,1)S(1)}, bf16[32,512]{1,0:T(8,128)(2,1)S(1)}, u32[]{:S(2)}, u32[]{:S(2)}) collective-permute-start(bf16[32,512]{1,0:T(8,128)(2,1)S(1)} %shard_map.46.refs_0_), channel_id=1, source_target_pairs={{0,1},{1,0},{2,3},{3,2},{4,5},{5,4},{6,7},{7,6},{8,9},{9,8},{10,11... | collective-permute-start | bytes 98312 | tf_op jit(solution)/shard_map/ppermute | solution.py:206

commit v4 on v3

v4 whole, which is shorter than its diff:
```python
import functools

import jax
import jax.numpy as jnp
from jax import lax
from jax.experimental import pallas as pl
from jax.experimental.pallas import tpu as pltpu
from jax.sharding import PartitionSpec as P

F32, BF16 = jnp.float32, jnp.bfloat16
INNER = (((1,), (1,)), ((), ()))
TAIL = 16


def call(body, out_shape, operands, space=pltpu.VMEM, scratch=(), after=()):
    outs = out_shape if isinstance(out_shape, (list, tuple)) else [out_shape]
    moved = sum(x.size * x.dtype.itemsize for x in list(operands) + list(outs))

    def run(*refs):
        body(*refs[: len(operands)], *refs[len(operands) + len(after) :])

    return pl.pallas_call(
        run,
        out_shape=out_shape,
        in_specs=[pl.BlockSpec(memory_space=space)] * len(operands) + [pl.BlockSpec(memory_space=pl.ANY)] * len(after),
        out_specs=jax.tree.map(lambda _: pl.BlockSpec(memory_space=pltpu.VMEM), out_shape),
        scratch_shapes=list(scratch),
        cost_estimate=pl.CostEstimate(flops=0, bytes_accessed=0, transcendentals=0),
        compiler_params=pltpu.CompilerParams(vmem_limit_bytes=min(56 << 20, (8 << 20) + 3 * moved)),
    )(*operands, *after)


def column(row, first=0, count=None):
    shape = (count or row.shape[1], row.shape[1])
    eye = lax.broadcasted_iota(jnp.int32, shape, 0) + first == lax.broadcasted_iota(jnp.int32, shape, 1)
    return jnp.sum(jnp.where(eye, row, 0.0), axis=1, keepdims=True)


def tags_of(scales, mass):
    shape = (TAIL, scales.shape[1])
    at = lax.broadcasted_iota(jnp.int32, shape, 0)
    high = mass.astype(BF16).astype(F32)
    return jnp.where(at < 8, scales, jnp.where(at < 12, high, mass - high)).astype(BF16)


def read_tags(tags):
    tags = tags.astype(F32)
    return tags[0:1, :], tags[8:9, 0:1] + tags[12:13, 0:1]


def cut_kernel(nrow, teach, *outs):
    part = teach.shape[1] // nrow
    z = lax.axis_index("row")
    for k in range(nrow):
        at = pl.multiple_of((z ^ k) * part, part)
        outs[k][...] = teach[:, pl.ds(at, part)]


def tag_kernel(piece, scale, *refs):
    cuts, out = refs[:-1], refs[-1]
    rows, part = piece.shape
    out[:rows, :] = piece[...]
    squares = sum(jnp.sum(jnp.square(c[...].astype(F32)), axis=1, keepdims=True) for c in cuts)
    s = scale[...].astype(F32)
    mass = jnp.sum(jnp.square(column(s)) * squares, keepdims=True)
    tags = tags_of(jnp.concatenate([s, s], axis=1), mass)
    out[rows:, :] = jnp.concatenate([tags] * (part // (2 * rows)), axis=1)


def pack_kernel(*refs):
    out, at = refs[-1], 0
    for r in refs[:-1]:
        out[at : at + r.shape[0], :] = r[...]
        at += r.shape[0]


def place(nrow, ncol, rows, k, c):
    return pl.multiple_of(((lax.axis_index("row") ^ k) * ncol + c) * rows, rows)


def assemble(nrow, ncol, rows, blocks, held):
    for c in range(ncol):
        for k, (ref, at) in blocks[c].items():
            held[pl.ds(place(nrow, ncol, rows, k, c), rows), :] = ref[at : at + rows, :]


def split(refs, groups, step):
    refs, blocks = list(refs), []
    for stack in groups:
        found = {}
        for keys in stack:
            ref = refs.pop(0)
            for n, k in enumerate(keys):
                found[k] = (ref, n * step)
        blocks.append(found)
    return blocks, refs


def gram_kernel(nrow, ncol, rows, groups, order, *refs):
    blocks, (kept, given, tags, held, left) = split(refs, groups, rows)
    assemble(nrow, ncol, rows, blocks, held)
    sub, half = rows // 2, nrow * rows // 2
    core = lax.axis_index("sub")
    for n, k in enumerate(order):
        ref, at = blocks[0][k]
        for target, which in ((0, core), (half, 1 - core)):
            rows_at = pl.multiple_of(at + which * sub, sub)
            left[target + n * sub : target + (n + 1) * sub, :] = ref[pl.ds(rows_at, sub), :]
    given[:half, :] = lax.dot_general(left[half:, :], held[...], INNER, preferred_element_type=F32).astype(BF16)
    kept[...] = lax.dot_general(left[:half, :], held[...], INNER, preferred_element_type=F32).astype(kept.dtype)
    lane = lax.broadcasted_iota(jnp.int32, (TAIL, 2 * rows), 1)
    found = [[blocks[c + d][0][0][rows:, : 2 * rows].astype(F32) for d in (0, 1)] for c in range(0, ncol, 2)]
    mass = sum(read_tags(tag)[1] for pair in found for tag in pair)
    tags[...] = tags_of(jnp.zeros((1, tags.shape[1]), F32), mass)
    for c, pair in zip(range(0, ncol, 2), found):
        spot = pl.multiple_of(place(nrow, ncol, rows, 0, c), 2 * rows)
        tags[:, pl.ds(spot, 2 * rows)] = tags_of(jnp.where(lane < rows, *pair)[0:1, :], mass)
    given[half:, :] = tags[...]


def fold_tags(same, tags, came):
    (scales, mass), (more_scales, more_mass) = read_tags(tags[...]), read_tags(came[came.shape[0] - TAIL :, :])
    return tags_of(scales if same else scales + more_scales, mass + more_mass)


def fold_kernel(same, kept, came, tags, keep, give, tags_out):
    rows = kept.shape[0]
    half = rows // 2
    folded = fold_tags(same, tags, came)
    tags_out[...] = folded
    give[:half, :] = (kept[half:, :].astype(F32) + came[half:rows, :].astype(F32)).astype(BF16)
    give[half:, :] = folded
    keep[...] = (kept[:half, :].astype(F32) + came[:half, :].astype(F32)).astype(keep.dtype)


def raw_gram_kernel(nrow, ncol, rows, groups, *refs):
    blocks, (out, raw) = split(refs, groups, rows)
    assemble(nrow, ncol, rows, blocks, raw)
    out[:rows, :] = lax.dot_general(blocks[0][0][0][:rows, :], raw[...], INNER, preferred_element_type=F32)
    batch, half = raw.shape
    step = min(batch, 512)
    for at in range(0, batch, step):
        squares = jnp.square(raw[at : at + step, :].astype(F32))
        out[rows:, at : at + step] = lax.dot_general(
            jnp.ones((8, half), F32), squares, INNER, precision=lax.Precision.HIGHEST, preferred_element_type=F32
        )


def normalize(raw, squares, units):
    for at in range(0, raw.shape[0], 128):
        norm = jnp.sqrt(column(squares[:1, at : at + 128]))
        units[at : at + 128, :] = (raw[at : at + 128, :].astype(F32) / norm).astype(BF16)


def unit_gram_kernel(ncol, mine, other, *refs):
    rows = mine.shape[0] - 8
    gram, norms, squares = refs[-4:-1] if len(refs) > 3 else refs
    squares[...] = mine[rows:, :] + other[rows:, :]
    spot = pl.multiple_of(lax.axis_index("row") * ncol * rows, 2 * rows)
    norm = jnp.sqrt(column(squares[:1, pl.ds(spot, 2 * rows)][:, :rows]))
    norms[...] = jnp.broadcast_to(norm, norms.shape)
    gram[...] = (mine[:rows, :] + other[:rows, :]) / (norm * jnp.sqrt(squares[:1, :]))
    if len(refs) > 3:
        normalize(refs[0], squares, refs[-1])


def error_kernel(batch, kept, came, tags, gram, scale, out):
    sub = kept.shape[0]
    first = lax.axis_index("sub") * sub
    scales, mass = read_tags(fold_tags(False, tags, came))
    total = kept[...].astype(F32) + came[:sub, :].astype(F32)
    outer = column(scale[...].astype(F32), first, sub) * scales
    error = gram[pl.ds(pl.multiple_of(first, sub), sub), :] - outer * total / (mass / batch)
    out[...] = error.astype(BF16)


def final_kernel(nrow, ncol, groups, mine, other, gram, norms, squares, stud, *refs):
    rows = stud.shape[0]
    if groups:
        blocks, (out, error_b, units) = split(refs, groups, rows)
        assemble(nrow, ncol, rows, blocks, units)
        normalize(units, squares, units)
    else:
        units, out, error_b = refs
    sub = rows // 2
    core = lax.axis_index("sub")
    error_b[pl.ds(pl.multiple_of(core * sub, sub), sub), :] = mine[...]
    error_b[pl.ds(pl.multiple_of((1 - core) * sub, sub), sub), :] = other[...]
    norm = norms[:, :1]
    grads = 4.0 * jnp.dot(error_b[...], units[...], preferred_element_type=F32)
    along = 4.0 * jnp.sum(error_b[...].astype(F32) * gram[...], axis=1, keepdims=True)
    unit = stud[...].astype(F32) / norm
    out[...] = (grads - along * unit) / norm


def shards(student, teacher, scale):
    rows, half = student.shape
    nrow, ncol = lax.axis_size("row"), lax.axis_size("col")
    batch = rows * nrow * ncol
    part = teacher.shape[1] // nrow
    small = batch <= 2048
    sds = jax.ShapeDtypeStruct
    scale = scale.reshape(1, rows)

    def along_row(x, k):
        return lax.ppermute(x, "row", [(i, i ^ k) for i in range(nrow)])

    def along_col(x, c):
        return lax.ppermute(x, "col", [(i, (i - c) % ncol) for i in range(ncol)])

    def other_core(x):
        return lax.ppermute(x, "sub", [(0, 1), (1, 0)])

    def pack(xs, after=()):
        if len(xs) == 1:
            return xs[0]
        return call(pack_kernel, sds((sum(x.shape[0] for x in xs), xs[0].shape[1]), BF16), xs, after=after)

    def columns(x):
        return [along_col(x, c) for c in range(1, ncol)]

    stack, keys, k = student, [0], nrow // 2
    while k > 1:
        stack = pack([stack, along_row(stack, k)])
        keys, k = keys + [n ^ k for n in keys], k // 2
    raw = [stack, along_row(stack, 1)]
    raw_groups = [[keys, [n ^ 1 for n in keys]]] * ncol
    raw_passed = [columns(r) for r in raw]
    raw_refs = raw + [p[c] for c in range(ncol - 1) for p in raw_passed]

    cuts = call(functools.partial(cut_kernel, nrow), [sds((rows, part), BF16)] * nrow, [teacher])
    tagged = call(tag_kernel, sds((rows + TAIL, part), BF16), [cuts[0], scale] + list(cuts))
    pieces = [along_row(cuts[k], k) for k in range(1, nrow)]
    tagged_passed = columns(tagged)
    late = pack(pieces, after=tagged_passed[:1] + [stack])
    late_passed = columns(late)
    teach_groups = [[[0], list(range(1, nrow))]] * ncol
    teach_refs = [tagged, late] + [p[c] for c in range(ncol - 1) for p in (tagged_passed, late_passed)]

    order = [0]
    while len(order) < nrow:
        order = [2 * n for n in order] + [2 * n + 1 for n in order]
    kept, given, tags = call(
        functools.partial(gram_kernel, nrow, ncol, rows, teach_groups, order),
        [sds((nrow * rows // 2, batch), F32 if small else BF16), sds((nrow * rows // 2 + TAIL, batch), BF16), sds((TAIL, batch), BF16)],
        teach_refs,
        scratch=[pltpu.VMEM((batch, part), BF16), pltpu.VMEM((nrow * rows, part), BF16)],
    )
    came, k = other_core(given), 1
    while k < nrow:
        count = kept.shape[0] // 2
        kept, give, tags = call(
            functools.partial(fold_kernel, k == 1),
            [sds((count, batch), kept.dtype), sds((count + TAIL, batch), BF16), sds((TAIL, batch), BF16)],
            [kept, came, tags],
        )
        came = along_row(give, k)
        folded = tags if k == 1 else folded
        k *= 2

    message, *all_raw = call(
        functools.partial(raw_gram_kernel, nrow, ncol, rows, raw_groups),
        [sds((rows + 8, batch), F32)] + ([sds((batch, half), BF16)] if small else []),
        raw_refs,
        after=[folded],
        scratch=[] if small else [pltpu.VMEM((batch, half), BF16)],
    )
    gram, norms, squares, *all_units = call(
        functools.partial(unit_gram_kernel, ncol),
        [sds((rows, batch), F32), sds((rows, 128), F32), sds((8, batch), F32)] + ([sds((batch, half), BF16)] if small else []),
        [message, other_core(message)] + all_raw,
    )
    error_b = call(
        functools.partial(error_kernel, batch),
        sds((rows // 2, batch), BF16),
        [kept, came, tags, gram, scale],
    )
    return call(
        functools.partial(final_kernel, nrow, ncol, None if small else raw_groups),
        sds((rows, half), F32),
        [error_b, other_core(error_b), gram, norms, squares, student] + (all_units if small else raw_refs),
        scratch=[pltpu.VMEM((rows, batch), BF16)] + ([] if small else [pltpu.VMEM((batch, half), BF16)]),
    )


def solution(mesh):
    spec = P(("groups", "row", "col"), "sub")
    return jax.shard_map(
        shards,
        mesh=mesh,
        in_specs=(spec, spec, P(("groups", "row", "col"))),
        out_specs=spec,
        check_vma=False,
    )
```

time: 40.5 us -> 45.6 us (1.13)
  waiting for transfers between devices: 18.5 us -> 21.4 us
  starting transfers between devices: 17.8 us -> 19.1 us
  Pallas kernels: 2.36 us -> 3.25 us
    ppermute x5 -> x4, waiting for transfers between devices: 7.28 us -> 10 us  [along_col(): return lax.ppermute(x, 'col', [(i, (i - c) % ncol) for i in range(ncol)])]
    ppermute x5 -> x4, starting transfers between devices: 3.43 us -> 5.68 us  [along_col(): return lax.ppermute(x, 'col', [(i, (i - c) % ncol) for i in range(ncol)])]
    ppermute x7, waiting for transfers between devices: 8.79 us -> 10.2 us  [along_row(): return lax.ppermute(x, 'row', [(i, i ^ k) for i in range(nrow)])]
    ppermute x4 -> x3, waiting for transfers between devices: 2.39 us -> 1.2 us  [other_core(): return lax.ppermute(x, 'sub', [(0, 1), (1, 0)])]
    pallas_call x11, Pallas kernels: 2.36 us -> 3.25 us  [call(): pl.pallas_call(run, out_shape=out_shape, in_specs=[pl.BlockSpec(memory_sp...]
    ppermute x7, starting transfers between devices: 14.1 us -> 13.3 us  [along_row(): return lax.ppermute(x, 'row', [(i, i ^ k) for i in range(nrow)])]
  transfers between devices with their start and end apart: 16 -> 14, of which waited for: 10 -> 8; matrix products, arithmetic and copies ran while one was open for 0% -> 0% of each run, Pallas kernels for 3% -> 2%
where the time goes in v4:
time: 45.6 us; the launch traced here: 45.5 us
  waiting for transfers between devices  21.4 us (47%)
  starting transfers between devices  19.1 us (42%)
  Pallas kernels  3.25 us (7%)
  local copies, waits for them, and re-layouts  1.6 us (4%)
    ppermute x7, starting transfers between devices, along_row(): return lax.ppermute(x, 'row', [(i, i ^ k) for i in range(nrow)])  13.3 us
    ppermute x7, waiting for transfers between devices, along_row(): return lax.ppermute(x, 'row', [(i, i ^ k) for i in range(nrow)])  10.2 us
    ppermute x4, waiting for transfers between devices, along_col(): return lax.ppermute(x, 'col', [(i, (i - c) % ncol) for i in range(ncol)])  10 us
    ppermute x4, starting transfers between devices, along_col(): return lax.ppermute(x, 'col', [(i, (i - c) % ncol) for i in range(ncol)])  5.68 us
    pallas_call x11, Pallas kernels, call(): pl.pallas_call(run, out_shape=out_shape, in_specs=[pl.BlockSpec(memory_sp...  3.25 us
    unnamed x6, local copies, waits for them, and re-layouts  1.6 us
    ppermute x3, waiting for transfers between devices, other_core(): return lax.ppermute(x, 'sub', [(0, 1), (1, 0)])  1.2 us
  transfers between devices with their start and end apart: 14, of which 8 were waited for; matrix products, arithmetic and copies ran while one was open for 0% of the time, Pallas kernels for 2%

profile of v4, /device:TPU:0, one launch (start us, length us, event | category | flops | bytes accessed | tf_op | source)
XLA Modules:
  0.0 45.5 jit_solution(14359121622616433621)
XLA Ops:
  0.0 0.0 copy-start
  0.0 0.9 %copy-done = bf16[64,2048]{1,0:T(8,128)(2,1)S(1)} copy-done((bf16[64,2048]{1,0:T(8,128)(2,1)S(1)}, bf16[64,2048]{1,0:T(8,128)(2,1)}, u32[]{:S(2)}) %copy-start) | copy-done | bytes 262168
  1.0 0.0 copy-start.2
  1.0 0.6 %copy-done.2 = bf16[64]{0:T(256)(128)(2,1)S(1)} copy-done((bf16[64]{0:T(256)(128)(2,1)S(1)}, bf16[64]{0:T(256)(128)(2,1)}, u32[]{:S(2)}) %copy-start.2) | copy-done | bytes 152
  1.6 0.0 copy-start.1
  1.6 0.3 shard_map.38.refs_0_
  1.9 3.0 %collective-permute-start.3 = (bf16[80,512]{1,0:T(8,128)(2,1)S(1)}, bf16[80,512]{1,0:T(8,128)(2,1)S(1)}, u32[]{:S(2)}, u32[]{:S(2)}) collective-permute-start(bf16[80,512]{1,0:T(8,128)(2,1)S(1)} %shard_map.38.refs_0_), channel_id=1, source_target_pairs={{0,2},{2,0},{1,3},{3,1},{4,6},{6,4},{5,7},{7,5},{8,10},{10,8},{9,1... | collective-permute-start | bytes 245768 | tf_op jit(solution)/shard_map/ppermute | solution.py:209
  4.9 0.0 copy-done.1
  4.9 2.6 %collective-permute-start.4 = (bf16[64,512]{1,0:T(8,128)(2,1)S(1)}, bf16[64,512]{1,0:T(8,128)(2,1)S(1)}, u32[]{:S(2)}, u32[]{:S(2)}) collective-permute-start(bf16[64,512]{1,0:T(8,128)(2,1)S(1)} %copy-done.1), channel_id=1, source_target_pairs={{0,8},{4,12},{8,0},{12,4},{1,9},{5,13},{9,1},{13,5},{2,10},{6,14},... | collective-permute-start | bytes 196616 | tf_op jit(solution)/shard_map/ppermute | solution.py:206
  7.5 1.6 %collective-permute-start = (bf16[64,512]{1,0:T(8,128)(2,1)S(1)}, bf16[64,512]{1,0:T(8,128)(2,1)S(1)}, u32[]{:S(2)}, u32[]{:S(2)}) collective-permute-start(bf16[64,512]{1,0:T(8,128)(2,1)S(1)} %get-tuple-element.25.refs_3_), channel_id=1, source_target_pairs={{0,4},{4,0},{8,12},{12,8},{1,5},{5,1},{9,13},{13,9},{2,6},{6,2},{1... | collective-permute-start | bytes 196616 | tf_op jit(solution)/shard_map/ppermute | solution.py:206
  9.1 0.3 collective-permute-start.1
  9.4 2.5 %collective-permute-start.2 = (bf16[64,512]{1,0:T(8,128)(2,1)S(1)}, bf16[64,512]{1,0:T(8,128)(2,1)S(1)}, u32[]{:S(2)}, u32[]{:S(2)}) collective-permute-start(bf16[64,512]{1,0:T(8,128)(2,1)S(1)} %get-tuple-element.27.refs_5_), channel_id=1, source_target_pairs={{0,12},{4,8},{8,4},{12,0},{1,13},{5,9},{9,5},{13,1},{2,14},{6,10},... | collective-permute-start | bytes 196616 | tf_op jit(solution)/shard_map/ppermute | solution.py:206
  11.9 0.0 collective-permute-done.4.refs_1_
  11.9 0.1 collective-permute-done.refs_0_
  12.0 4.3 %collective-permute-done.1.refs_1_ = bf16[64,512]{1,0:T(8,128)(2,1)S(1)} collective-permute-done((bf16[64,512]{1,0:T(8,128)(2,1)S(1)}, bf16[64,512]{1,0:T(8,128)(2,1)S(1)}, u32[]{:S(2)}, u32[]{:S(2)}) %collective-permute-start.1) | collective-permute-done | bytes 65568 | tf_op jit(solution)/shard_map/ppermute | solution.py:206
  16.3 0.0 collective-permute-done.2.refs_2_
  16.3 0.0 collective-permute-done.3.refs_3_.refs_2_
  16.3 0.6 %collective-permute-start.5 = (bf16[192,512]{1,0:T(8,128)(2,1)S(1)}, bf16[192,512]{1,0:T(8,128)(2,1)S(1)}, u32[]{:S(2)}, u32[]{:S(2)}) collective-permute-start(bf16[192,512]{1,0:T(8,128)(2,1)S(1)} %shard_map.40.refs_1_), channel_id=1, source_target_pairs={{0,2},{2,0},{1,3},{3,1},{4,6},{6,4},{5,7},{7,5},{8,10},{10,8},{9,1... | collective-permute-start | bytes 589832 | tf_op jit(solution)/shard_map/ppermute | solution.py:209
  16.9 1.7 %collective-permute-start.9 = (bf16[128,512]{1,0:T(8,128)(2,1)S(1)}, bf16[128,512]{1,0:T(8,128)(2,1)S(1)}, u32[]{:S(2)}, u32[]{:S(2)}) collective-permute-start(bf16[128,512]{1,0:T(8,128)(2,1)S(1)} %shard_map.39.refs_4_.refs_0_), channel_id=1, source_target_pairs={{0,4},{4,0},{8,12},{12,8},{1,5},{5,1},{9,13},{13,9},{2,6},{6,2},{1... | collective-permute-start | bytes 393224 | tf_op jit(solution)/shard_map/ppermute | solution.py:206
  18.6 3.5 %collective-permute-done.5.refs_3_ = bf16[192,512]{1,0:T(8,128)(2,1)S(1)} collective-permute-done((bf16[192,512]{1,0:T(8,128)(2,1)S(1)}, bf16[192,512]{1,0:T(8,128)(2,1)S(1)}, u32[]{:S(2)}, u32[]{:S(2)}) %collective-permute-start.5) | collective-permute-done | bytes 196640 | tf_op jit(solution)/shard_map/ppermute | solution.py:209
  22.0 0.5 %shard_map.41 = (f32[128,512]{1,0:T(8,128)S(1)}, bf16[144,512]{1,0:T(8,128)(2,1)S(1)}, bf16[16,512]{1,0:T(8,128)(2,1)S(1)}) custom-call(bf16[80,512]{1,0:T(8,128)(2,1)S(1)} %shard_map.38.refs_0_, bf16[192,512]{1,0:T(8,128)(2,1)S(1)} %shard_map.40.refs_1_, bf16[80,512]{1,0:T(8,128)(2,1)S(1)} %collective-permute-done.3.refs_3_.refs_2_, ...), custom_call_target="tpu_custom_call" | custom-call | tf_op jit(solution)/shard_map/pallas_call | solution.py:22
  22.6 0.1 collective-permute-start.6
  22.6 1.3 %collective-permute-start.10 = (bf16[128,512]{1,0:T(8,128)(2,1)S(1)}, bf16[128,512]{1,0:T(8,128)(2,1)S(1)}, u32[]{:S(2)}, u32[]{:S(2)}) collective-permute-start(bf16[128,512]{1,0:T(8,128)(2,1)S(1)} %shard_map.39.refs_4_.refs_0_), channel_id=1, source_target_pairs={{0,2},{2,0},{1,3},{3,1},{4,6},{6,4},{5,7},{7,5},{8,10},{10,8},{9,1... | collective-permute-start | bytes 393224 | tf_op jit(solution)/shard_map/ppermute | solution.py:209
  23.9 0.0 collective-permute-done.9.refs_1_
  23.9 0.8 %collective-permute-start.11 = (bf16[128,512]{1,0:T(8,128)(2,1)S(1)}, bf16[128,512]{1,0:T(8,128)(2,1)S(1)}, u32[]{:S(2)}, u32[]{:S(2)}) collective-permute-start(bf16[128,512]{1,0:T(8,128)(2,1)S(1)} %collective-permute-done.9.refs_1_), channel_id=1, source_target_pairs={{0,2},{2,0},{1,3},{3,1},{4,6},{6,4},{5,7},{7,5},{8,10},{10,8},{9,1... | collective-permute-start | bytes 393224 | tf_op jit(solution)/shard_map/ppermute | solution.py:209
  24.7 0.0 collective-permute-done.6.refs_1_
  24.8 4.2 %collective-permute-done.10.refs_2_ = bf16[128,512]{1,0:T(8,128)(2,1)S(1)} collective-permute-done((bf16[128,512]{1,0:T(8,128)(2,1)S(1)}, bf16[128,512]{1,0:T(8,128)(2,1)S(1)}, u32[]{:S(2)}, u32[]{:S(2)}) %collective-permute-start.10) | collective-permute-done | bytes 131104 | tf_op jit(solution)/shard_map/ppermute | solution.py:209
  29.0 2.4 %collective-permute-done.11.refs_3_ = bf16[128,512]{1,0:T(8,128)(2,1)S(1)} collective-permute-done((bf16[128,512]{1,0:T(8,128)(2,1)S(1)}, bf16[128,512]{1,0:T(8,128)(2,1)S(1)}, u32[]{:S(2)}, u32[]{:S(2)}) %collective-permute-start.11) | collective-permute-done | bytes 131104 | tf_op jit(solution)/shard_map/ppermute | solution.py:209
  31.4 1.1 %shard_map.44 = (f32[72,512]{1,0:T(8,128)S(1)}, bf16[512,512]{1,0:T(8,128)(2,1)S(1)}) custom-call(bf16[128,512]{1,0:T(8,128)(2,1)S(1)} %shard_map.39.refs_4_.refs_0_, bf16[128,512]{1,0:T(8,128)(2,1)S(1)} %collective-permute-done.9.refs_1_, bf16[128,512]{1,0:T(8,128)(2,1)S(1)} %collective-permute-done.10.refs_2_, ...), custom_call_target="tpu_custom_call" | custom-call | tf_op jit(solution)/shard_map/pallas_call | solution.py:22
  32.5 0.0 collective-permute-start.12
  32.5 2.1 %collective-permute-start.7 = (bf16[80,512]{1,0:T(8,128)(2,1)S(1)}, bf16[80,512]{1,0:T(8,128)(2,1)S(1)}, u32[]{:S(2)}, u32[]{:S(2)}) collective-permute-start(bf16[80,512]{1,0:T(8,128)(2,1)S(1)} %get-tuple-element.32), channel_id=1, source_target_pairs={{0,4},{4,0},{8,12},{12,8},{1,5},{5,1},{9,13},{13,9},{2,6},{6,2},{1... | collective-permute-start | bytes 245768 | tf_op jit(solution)/shard_map/ppermute | solution.py:206
  34.6 3.1 %collective-permute-done.7.refs_1_ = bf16[80,512]{1,0:T(8,128)(2,1)S(1)} collective-permute-done((bf16[80,512]{1,0:T(8,128)(2,1)S(1)}, bf16[80,512]{1,0:T(8,128)(2,1)S(1)}, u32[]{:S(2)}, u32[]{:S(2)}) %collective-permute-start.7) | collective-permute-done | bytes 81952 | tf_op jit(solution)/shard_map/ppermute | solution.py:206
  37.7 0.1 shard_map.43
  37.7 2.5 %collective-permute-start.8 = (bf16[48,512]{1,0:T(8,128)(2,1)S(1)}, bf16[48,512]{1,0:T(8,128)(2,1)S(1)}, u32[]{:S(2)}, u32[]{:S(2)}) collective-permute-start(bf16[48,512]{1,0:T(8,128)(2,1)S(1)} %get-tuple-element.35), channel_id=1, source_target_pairs={{0,8},{4,12},{8,0},{12,4},{1,9},{5,13},{9,1},{13,5},{2,10},{6,14},... | collective-permute-start | bytes 147464 | tf_op jit(solution)/shard_map/ppermute | solution.py:206
  40.3 0.0 collective-permute-done.12.refs_1_
  40.3 0.3 shard_map.45
  40.6 2.7 %collective-permute-done.8.refs_1_ = bf16[48,512]{1,0:T(8,128)(2,1)S(1)} collective-permute-done((bf16[48,512]{1,0:T(8,128)(2,1)S(1)}, bf16[48,512]{1,0:T(8,128)(2,1)S(1)}, u32[]{:S(2)}, u32[]{:S(2)}) %collective-permute-start.8) | collective-permute-done | bytes 49184 | tf_op jit(solution)/shard_map/ppermute | solution.py:206
  43.2 0.1 shard_map.46.refs_0_
  43.3 0.1 collective-permute-start.13
  43.4 1.2 %collective-permute-done.13.refs_1_ = bf16[32,512]{1,0:T(8,128)(2,1)S(1)} collective-permute-done((bf16[32,512]{1,0:T(8,128)(2,1)S(1)}, bf16[32,512]{1,0:T(8,128)(2,1)S(1)}, u32[]{:S(2)}, u32[]{:S(2)}) %collective-permute-start.13) | collective-permute-done | bytes 32800 | tf_op jit(solution)/shard_map/ppermute | solution.py:212
  44.6 0.9 %shard_map.47 = f32[64,512]{1,0:T(8,128)} custom-call(bf16[32,512]{1,0:T(8,128)(2,1)S(1)} %shard_map.46.refs_0_, bf16[32,512]{1,0:T(8,128)(2,1)S(1)} %collective-permute-done.13.refs_1_, f32[64,512]{1,0:T(8,128)S(1)} %get-tuple-element.39.refs_3_.refs_2_, f32[64,128]{1,0:T(8,128)S(1)} %get-tuple-element.40.refs_3_, f32[8,512]{1,0:T(8,128)S(1)} %get-tuple-element.41.refs_4_, ...), custom_call_target="tpu_custom_call" | custom-call | tf_op jit(solution)/shard_map/pallas_call | solution.py:22
  (4 shorter events, 0.1 us)
Async XLA Ops:
  0.0 0.9 %copy-start = (bf16[64,2048]{1,0:T(8,128)(2,1)S(1)}, bf16[64,2048]{1,0:T(8,128)(2,1)}, u32[]{:S(2)}) copy-start(bf16[64,2048]{1,0:T(8,128)(2,1)} %refs_0_.2) | copy-start | bytes 786436
  1.0 0.7 %copy-start.2 = (bf16[64]{0:T(256)(128)(2,1)S(1)}, bf16[64]{0:T(256)(128)(2,1)}, u32[]{:S(2)}) copy-start(bf16[64]{0:T(256)(128)(2,1)} %param.5) | copy-start | bytes 388
  1.6 3.3 %copy-start.1 = (bf16[64,512]{1,0:T(8,128)(2,1)S(1)}, bf16[64,512]{1,0:T(8,128)(2,1)}, u32[]{:S(2)}) copy-start(bf16[64,512]{1,0:T(8,128)(2,1)} %refs_5_.1) | copy-start | bytes 196612
  1.9 14.4 %collective-permute-start.3 = (bf16[80,512]{1,0:T(8,128)(2,1)S(1)}, bf16[80,512]{1,0:T(8,128)(2,1)S(1)}, u32[]{:S(2)}, u32[]{:S(2)}) collective-permute-start(bf16[80,512]{1,0:T(8,128)(2,1)S(1)} %shard_map.38.refs_0_), channel_id=1, source_target_pairs={{0,2},{2,0},{1,3},{3,1},{4,6},{6,4},{5,7},{7,5},{8,10},{10,8},{9,1... | collective-permute-start | bytes 245768 | tf_op jit(solution)/shard_map/ppermute | solution.py:209
  4.9 7.0 %collective-permute-start.4 = (bf16[64,512]{1,0:T(8,128)(2,1)S(1)}, bf16[64,512]{1,0:T(8,128)(2,1)S(1)}, u32[]{:S(2)}, u32[]{:S(2)}) collective-permute-start(bf16[64,512]{1,0:T(8,128)(2,1)S(1)} %copy-done.1), channel_id=1, source_target_pairs={{0,8},{4,12},{8,0},{12,4},{1,9},{5,13},{9,1},{13,5},{2,10},{6,14},... | collective-permute-start | bytes 196616 | tf_op jit(solution)/shard_map/ppermute | solution.py:206
  7.5 4.5 %collective-permute-start = (bf16[64,512]{1,0:T(8,128)(2,1)S(1)}, bf16[64,512]{1,0:T(8,128)(2,1)S(1)}, u32[]{:S(2)}, u32[]{:S(2)}) collective-permute-start(bf16[64,512]{1,0:T(8,128)(2,1)S(1)} %get-tuple-element.25.refs_3_), channel_id=1, source_target_pairs={{0,4},{4,0},{8,12},{12,8},{1,5},{5,1},{9,13},{13,9},{2,6},{6,2},{1... | collective-permute-start | bytes 196616 | tf_op jit(solution)/shard_map/ppermute | solution.py:206
  9.1 7.2 %collective-permute-start.1 = (bf16[64,512]{1,0:T(8,128)(2,1)S(1)}, bf16[64,512]{1,0:T(8,128)(2,1)S(1)}, u32[]{:S(2)}, u32[]{:S(2)}) collective-permute-start(bf16[64,512]{1,0:T(8,128)(2,1)S(1)} %get-tuple-element.26.refs_4_), channel_id=1, source_target_pairs={{0,8},{4,12},{8,0},{12,4},{1,9},{5,13},{9,1},{13,5},{2,10},{6,14},... | collective-permute-start | bytes 196616 | tf_op jit(solution)/shard_map/ppermute | solution.py:206
  9.4 6.9 %collective-permute-start.2 = (bf16[64,512]{1,0:T(8,128)(2,1)S(1)}, bf16[64,512]{1,0:T(8,128)(2,1)S(1)}, u32[]{:S(2)}, u32[]{:S(2)}) collective-permute-start(bf16[64,512]{1,0:T(8,128)(2,1)S(1)} %get-tuple-element.27.refs_5_), channel_id=1, source_target_pairs={{0,12},{4,8},{8,4},{12,0},{1,13},{5,9},{9,5},{13,1},{2,14},{6,10},... | collective-permute-start | bytes 196616 | tf_op jit(solution)/shard_map/ppermute | solution.py:206
  16.3 5.7 %collective-permute-start.5 = (bf16[192,512]{1,0:T(8,128)(2,1)S(1)}, bf16[192,512]{1,0:T(8,128)(2,1)S(1)}, u32[]{:S(2)}, u32[]{:S(2)}) collective-permute-start(bf16[192,512]{1,0:T(8,128)(2,1)S(1)} %shard_map.40.refs_1_), channel_id=1, source_target_pairs={{0,2},{2,0},{1,3},{3,1},{4,6},{6,4},{5,7},{7,5},{8,10},{10,8},{9,1... | collective-permute-start | bytes 589832 | tf_op jit(solution)/shard_map/ppermute | solution.py:209
  16.9 7.0 %collective-permute-start.9 = (bf16[128,512]{1,0:T(8,128)(2,1)S(1)}, bf16[128,512]{1,0:T(8,128)(2,1)S(1)}, u32[]{:S(2)}, u32[]{:S(2)}) collective-permute-start(bf16[128,512]{1,0:T(8,128)(2,1)S(1)} %shard_map.39.refs_4_.refs_0_), channel_id=1, source_target_pairs={{0,4},{4,0},{8,12},{12,8},{1,5},{5,1},{9,13},{13,9},{2,6},{6,2},{1... | collective-permute-start | bytes 393224 | tf_op jit(solution)/shard_map/ppermute | solution.py:206
  22.6 2.2 %collective-permute-start.6 = (bf16[144,512]{1,0:T(8,128)(2,1)S(1)}, bf16[144,512]{1,0:T(8,128)(2,1)S(1)}, u32[]{:S(2)}, u32[]{:S(2)}) collective-permute-start(bf16[144,512]{1,0:T(8,128)(2,1)S(1)} %get-tuple-element.29), channel_id=1, source_target_pairs={{0,1},{1,0},{2,3},{3,2},{4,5},{5,4},{6,7},{7,6},{8,9},{9,8},{10,11... | collective-permute-start | bytes 442376 | tf_op jit(solution)/shard_map/ppermute | solution.py:212
  22.6 6.4 %collective-permute-start.10 = (bf16[128,512]{1,0:T(8,128)(2,1)S(1)}, bf16[128,512]{1,0:T(8,128)(2,1)S(1)}, u32[]{:S(2)}, u32[]{:S(2)}) collective-permute-start(bf16[128,512]{1,0:T(8,128)(2,1)S(1)} %shard_map.39.refs_4_.refs_0_), channel_id=1, source_target_pairs={{0,2},{2,0},{1,3},{3,1},{4,6},{6,4},{5,7},{7,5},{8,10},{10,8},{9,1... | collective-permute-start | bytes 393224 | tf_op jit(solution)/shard_map/ppermute | solution.py:209
  23.9 7.5 %collective-permute-start.11 = (bf16[128,512]{1,0:T(8,128)(2,1)S(1)}, bf16[128,512]{1,0:T(8,128)(2,1)S(1)}, u32[]{:S(2)}, u32[]{:S(2)}) collective-permute-start(bf16[128,512]{1,0:T(8,128)(2,1)S(1)} %collective-permute-done.9.refs_1_), channel_id=1, source_target_pairs={{0,2},{2,0},{1,3},{3,1},{4,6},{6,4},{5,7},{7,5},{8,10},{10,8},{9,1... | collective-permute-start | bytes 393224 | tf_op jit(solution)/shard_map/ppermute | solution.py:209
  32.5 7.8 %collective-permute-start.12 = (f32[72,512]{1,0:T(8,128)S(1)}, f32[72,512]{1,0:T(8,128)S(1)}, u32[]{:S(2)}, u32[]{:S(2)}) collective-permute-start(f32[72,512]{1,0:T(8,128)S(1)} %get-tuple-element.37.refs_0_), channel_id=1, source_target_pairs={{0,1},{1,0},{2,3},{3,2},{4,5},{5,4},{6,7},{7,6},{8,9},{9,8},{10,11... | collective-permute-start | bytes 442376 | tf_op jit(solution)/shard_map/ppermute | solution.py:212
  32.5 5.2 %collective-permute-start.7 = (bf16[80,512]{1,0:T(8,128)(2,1)S(1)}, bf16[80,512]{1,0:T(8,128)(2,1)S(1)}, u32[]{:S(2)}, u32[]{:S(2)}) collective-permute-start(bf16[80,512]{1,0:T(8,128)(2,1)S(1)} %get-tuple-element.32), channel_id=1, source_target_pairs={{0,4},{4,0},{8,12},{12,8},{1,5},{5,1},{9,13},{13,9},{2,6},{6,2},{1... | collective-permute-start | bytes 245768 | tf_op jit(solution)/shard_map/ppermute | solution.py:206
  37.7 5.5 %collective-permute-start.8 = (bf16[48,512]{1,0:T(8,128)(2,1)S(1)}, bf16[48,512]{1,0:T(8,128)(2,1)S(1)}, u32[]{:S(2)}, u32[]{:S(2)}) collective-permute-start(bf16[48,512]{1,0:T(8,128)(2,1)S(1)} %get-tuple-element.35), channel_id=1, source_target_pairs={{0,8},{4,12},{8,0},{12,4},{1,9},{5,13},{9,1},{13,5},{2,10},{6,14},... | collective-permute-start | bytes 147464 | tf_op jit(solution)/shard_map/ppermute | solution.py:206
  43.3 1.3 %collective-permute-start.13 = (bf16[32,512]{1,0:T(8,128)(2,1)S(1)}, bf16[32,512]{1,0:T(8,128)(2,1)S(1)}, u32[]{:S(2)}, u32[]{:S(2)}) collective-permute-start(bf16[32,512]{1,0:T(8,128)(2,1)S(1)} %shard_map.46.refs_0_), channel_id=1, source_target_pairs={{0,1},{1,0},{2,3},{3,2},{4,5},{5,4},{6,7},{7,6},{8,9},{9,8},{10,11... | collective-permute-start | bytes 98312 | tf_op jit(solution)/shard_map/ppermute | solution.py:212

commit v5 on v1

v5 whole, which is shorter than its diff:
```python
import functools

import jax
import jax.numpy as jnp
from jax import lax
from jax.experimental import pallas as pl
from jax.experimental.pallas import tpu as pltpu
from jax.sharding import PartitionSpec as P

F32, BF16 = jnp.float32, jnp.bfloat16
INNER = (((1,), (1,)), ((), ()))
TAIL = 16


def call(body, out_shape, operands, space=pltpu.VMEM, scratch=(), after=()):
    outs = out_shape if isinstance(out_shape, (list, tuple)) else [out_shape]
    moved = sum(x.size * x.dtype.itemsize for x in list(operands) + list(outs))

    def run(*refs):
        body(*refs[: len(operands)], *refs[len(operands) + len(after) :])

    return pl.pallas_call(
        run,
        out_shape=out_shape,
        in_specs=[pl.BlockSpec(memory_space=space)] * len(operands) + [pl.BlockSpec(memory_space=pl.ANY)] * len(after),
        out_specs=jax.tree.map(lambda _: pl.BlockSpec(memory_space=pltpu.VMEM), out_shape),
        scratch_shapes=list(scratch),
        cost_estimate=pl.CostEstimate(flops=0, bytes_accessed=0, transcendentals=0),
        compiler_params=pltpu.CompilerParams(vmem_limit_bytes=min(56 << 20, (8 << 20) + 3 * moved)),
    )(*operands, *after)


def column(row, first=0, count=None):
    shape = (count or row.shape[1], row.shape[1])
    eye = lax.broadcasted_iota(jnp.int32, shape, 0) + first == lax.broadcasted_iota(jnp.int32, shape, 1)
    return jnp.sum(jnp.where(eye, row, 0.0), axis=1, keepdims=True)


def tags_of(scales, mass):
    shape = (TAIL, scales.shape[1])
    at = lax.broadcasted_iota(jnp.int32, shape, 0)
    high = mass.astype(BF16).astype(F32)
    return jnp.where(at < 8, scales, jnp.where(at < 12, high, mass - high)).astype(BF16)


def read_tags(tags):
    tags = tags.astype(F32)
    return tags[0:1, :], tags[8:9, 0:1] + tags[12:13, 0:1]


def cut_kernel(nrow, teach, *outs):
    part = teach.shape[1] // nrow
    z = lax.axis_index("row")
    for k in range(nrow):
        at = pl.multiple_of((z ^ k) * part, part)
        outs[k][...] = teach[:, pl.ds(at, part)]


def join_kernel(stud, scale, *refs):
    cuts, outs = refs[:-2], refs[-2:]
    rows, half = stud.shape
    squares = sum(jnp.sum(jnp.square(c[...].astype(F32)), axis=1, keepdims=True) for c in cuts)
    s = scale[...].astype(F32)
    mass = jnp.sum(jnp.square(column(s)) * squares, keepdims=True)
    tags = tags_of(jnp.concatenate([s, s], axis=1), mass)
    tags = jnp.concatenate([tags] * (half // (2 * rows)), axis=1)
    for out, cut in zip(outs, (cuts[0], cuts[len(cuts) // 2])):
        out[:rows, :] = stud[...]
        out[rows : rows + TAIL, :] = tags
        part = cut.shape[1]
        high = rows * part // half
        for n in range(half // part):
            out[rows + TAIL :, n * part : (n + 1) * part] = cut[n * high : (n + 1) * high, :]


def put(held, spot, rows, ref, at):
    width = held.shape[1]
    high = rows * width // ref.shape[1]
    for n in range(ref.shape[1] // width):
        held[pl.ds(spot + n * high, high), :] = ref[at : at + high, n * width : (n + 1) * width]


def late_kernel(rows, *refs):
    out = refs[-1]
    for k, ref in enumerate(refs[:-1]):
        put(out, k * rows, rows, ref, ref.shape[0] - rows * out.shape[1] // ref.shape[1])


def pack_kernel(spans, *refs):
    out, at = refs[-1], 0
    for r, (first, last) in zip(refs[:-1], spans):
        out[at : at + last - first, :] = r[first:last, :]
        at += last - first


def place(nrow, ncol, rows, k, c):
    return pl.multiple_of(((lax.axis_index("row") ^ k) * ncol + c) * rows, rows)


def gram_kernel(nrow, ncol, rows, *refs):
    outs, held = refs[2 * ncol : -1], refs[-1]
    for c in range(ncol):
        own, late = refs[2 * c : 2 * c + 2]
        put(held, place(nrow, ncol, rows, 0, c), rows, own, rows + TAIL)
        for k in range(1, nrow):
            put(held, place(nrow, ncol, rows, k, c), rows, late, (k - 1) * rows)
    for k in range(nrow):
        left = held[pl.ds(place(nrow, ncol, rows, k, 0), rows), :]
        outs[k][...] = lax.dot_general(left, held[...], INNER, preferred_element_type=F32).astype(outs[k].dtype)


def raw_blocks(ncol, step, keys, refs):
    blocks = []
    for c in range(ncol):
        own, rest = refs[2 * c : 2 * c + 2]
        blocks.append({0: (own, 0)} | {k: (rest, n * step) for n, k in enumerate(keys)})
    return blocks, refs[2 * ncol :]


def assemble(nrow, ncol, rows, blocks, held):
    for c in range(ncol):
        for k, (ref, at) in blocks[c].items():
            held[pl.ds(place(nrow, ncol, rows, k, c), rows), :] = ref[at : at + rows, :]


def raw_gram_kernel(nrow, ncol, rows, keys, *refs):
    step = rows + TAIL
    blocks, (out, vectors, raw) = raw_blocks(ncol, step, keys, refs)
    assemble(nrow, ncol, rows, blocks, raw)
    out[:rows, :] = lax.dot_general(blocks[0][0][0][:rows, :], raw[...], INNER, preferred_element_type=F32)
    batch, half = raw.shape
    chunk = min(batch, 512)
    for at in range(0, batch, chunk):
        squares = jnp.square(raw[at : at + chunk, :].astype(F32))
        out[rows:, at : at + chunk] = lax.dot_general(
            jnp.ones((8, half), F32), squares, INNER, precision=lax.Precision.HIGHEST, preferred_element_type=F32
        )
    lane = lax.broadcasted_iota(jnp.int32, (1, 2 * rows), 1)
    mass = jnp.zeros((1, 1), F32)
    for k in range(nrow):
        for c in range(0, ncol, 2):
            pair = []
            for d in (c, c + 1):
                ref, at = blocks[d][k]
                scales, part = read_tags(ref[at + rows : at + step, : 2 * rows])
                pair.append(scales)
                mass = mass + part
            spot = pl.multiple_of(place(nrow, ncol, rows, k, c), 2 * rows)
            vectors[0:8, pl.ds(spot, 2 * rows)] = jnp.broadcast_to(jnp.where(lane < rows, *pair), (8, 2 * rows))
    vectors[8:, :] = jnp.broadcast_to(mass, (8, batch))


def message_kernel(raw_gram, vectors, *refs):
    parts, out = refs[:-1], refs[-1]
    total = parts[0][...].astype(F32)
    for r in parts[1:]:
        total = total + r[...].astype(F32)
    rows = total.shape[0]
    out[:rows, :] = total
    out[rows : 2 * rows + 8, :] = raw_gram[...]
    out[2 * rows + 8 :, :] = vectors[8:, :]


def final_kernel(nrow, ncol, keys, mine, other, vectors, stud, scale, *refs):
    rows = stud.shape[0]
    if keys:
        blocks, (out, raw, units) = raw_blocks(ncol, rows + TAIL, keys, refs)
        assemble(nrow, ncol, rows, blocks, raw)
    else:
        raw, out, units = refs
    batch = mine.shape[1]
    squares = mine[2 * rows : 2 * rows + 8, :] + other[2 * rows : 2 * rows + 8, :]
    for at in range(0, batch, 128):
        norm = jnp.sqrt(column(squares[:1, at : at + 128]))
        units[at : at + 128, :] = (raw[at : at + 128, :].astype(F32) / norm).astype(BF16)
    own = squares_of_own(mine, other, ncol, rows)
    norm = jnp.sqrt(column(own))
    mass = (mine[2 * rows + 8 : 2 * rows + 9, :1] + other[2 * rows + 8 : 2 * rows + 9, :1]) / batch
    gram = (mine[rows : 2 * rows, :] + other[rows : 2 * rows, :]) / (norm * jnp.sqrt(squares[:1, :]))
    outer = column(scale[...].astype(F32)) * vectors[:1, :]
    error_b = (gram - outer * (mine[:rows, :] + other[:rows, :]) / mass).astype(BF16)
    grads = 4.0 * jnp.dot(error_b, units[...], preferred_element_type=F32)
    along = 4.0 * jnp.sum(error_b.astype(F32) * gram, axis=1, keepdims=True)
    unit = stud[...].astype(F32) / norm
    out[...] = (grads - along * unit) / norm


def squares_of_own(mine, other, ncol, rows):
    at = pl.ds(pl.multiple_of(lax.axis_index("row") * ncol * rows, 2 * rows), 2 * rows)
    return (mine[2 * rows : 2 * rows + 8, at] + other[2 * rows : 2 * rows + 8, at])[:1, :rows]


def shards(student, teacher, scale):
    rows, half = student.shape
    nrow, ncol = lax.axis_size("row"), lax.axis_size("col")
    batch = rows * nrow * ncol
    part = teacher.shape[1] // nrow
    small = batch <= 2048
    sds = jax.ShapeDtypeStruct
    scale = scale.reshape(1, rows)

    def along_row(x, k):
        return lax.ppermute(x, "row", [(i, i ^ k) for i in range(nrow)])

    def along_col(x, c):
        return lax.ppermute(x, "col", [(i, (i - c) % ncol) for i in range(ncol)])

    def other_core(x):
        return lax.ppermute(x, "sub", [(0, 1), (1, 0)])

    def pack(xs, spans, after=()):
        shape = (sum(last - first for first, last in spans), half)
        return call(functools.partial(pack_kernel, spans), sds(shape, BF16), xs, after=after)

    def with_columns(*xs):
        return [x if c == 0 else along_col(x, c) for c in range(ncol) for x in xs]

    step, middle = rows + TAIL, nrow // 2
    joined = sds((step + rows * part // half, half), BF16)
    cuts = call(functools.partial(cut_kernel, nrow), [sds((rows, part), BF16)] * nrow, [teacher])
    own, far = call(join_kernel, [joined, joined], [student, scale] + list(cuts))
    pieces = [along_row(far if k == middle else cuts[k], k) for k in range(1, nrow)]
    far = pieces[middle - 1]
    own = with_columns(own)
    late = call(functools.partial(late_kernel, rows), sds(((nrow - 1) * rows, part), BF16), pieces, after=own[1:2])
    late = with_columns(late)
    partial = call(
        functools.partial(gram_kernel, nrow, ncol, rows),
        [sds((rows, batch), F32)] + [sds((rows, batch), BF16)] * (nrow - 1),
        [r for pair in zip(own, late) for r in pair],
        scratch=[pltpu.VMEM((batch, part), BF16)],
    )
    returned = [partial[0]] + [along_row(partial[k], k) for k in range(1, nrow)]

    keys, received, spans = [0, middle], [far], [(0, step)]
    stack, k = pack([own[0], far], [(0, step)] * 2, after=late[:1]), middle // 2
    while k:
        received.append(along_row(stack, k))
        spans.append((0, stack.shape[0]))
        keys = keys + [n ^ k for n in keys]
        if k > 1:
            stack = pack([stack, received[-1]], [(0, stack.shape[0])] * 2)
        k //= 2
    keys = keys[1:]
    rest = with_columns(pack(received, spans))
    raw_refs = [r for pair in zip(own, rest) for r in pair]
    raw_gram, vectors, *all_raw = call(
        functools.partial(raw_gram_kernel, nrow, ncol, rows, keys),
        [sds((rows + 8, batch), F32), sds((16, batch), F32)] + ([sds((batch, half), BF16)] if small else []),
        raw_refs,
        scratch=[] if small else [pltpu.VMEM((batch, half), BF16)],
    )
    message = call(message_kernel, sds((2 * rows + 16, batch), F32), [raw_gram, vectors] + returned)
    return call(
        functools.partial(final_kernel, nrow, ncol, None if small else keys),
        sds((rows, half), F32),
        [message, other_core(message), vectors, student, scale] + (all_raw if small else raw_refs),
        scratch=([] if small else [pltpu.VMEM((batch, half), BF16)]) + [pltpu.VMEM((batch, half), BF16)],
    )


def solution(mesh):
    spec = P(("groups", "row", "col"), "sub")
    return jax.shard_map(
        shards,
        mesh=mesh,
        in_specs=(spec, spec, P(("groups", "row", "col"))),
        out_specs=spec,
        check_vma=False,
    )
```

time: 55.5 us -> 37.1 us (0.67)
  blocking collectives: 20.6 us -> 0 us
  starting transfers between devices: 5.01 us -> 16.3 us
  waiting for transfers between devices: 21.1 us -> 15.6 us
  other arithmetic: 4.12 us -> 0 us
  Pallas kernels: 0 us -> 3.39 us
  matrix products: 1.58 us -> 0 us
  between operations: 1.44 us -> 0.07 us
    all_to_all x1 -> x0, blocking collectives: 20.6 us -> none  [shards(): lax.all_to_all(packed, 'row', 0, 0, tiled=True)]
    ppermute x2 -> x11, starting transfers between devices: 1.56 us -> 16.3 us  [the longest x7 11.7 us: along_row(): return lax.ppermute(x, 'row', [(i, i ^ k) for i in range(nrow)])]
    all_to_all x1 -> x0, waiting for transfers between devices: 8.55 us -> none  [shards(): lax.all_to_all(sent, 'row', 0, 0, tiled=True).astype(F32)]
    all_to_all x1 -> x0, starting transfers between devices: 3.45 us -> none  [shards(): lax.all_to_all(sent, 'row', 0, 0, tiled=True).astype(F32)]
    pallas_call x0 -> x9, Pallas kernels: none -> 3.39 us  [call(): pl.pallas_call(run, out_shape=out_shape, in_specs=[pl.BlockSpec(memory_sp...]
    ppermute x2 -> x11, waiting for transfers between devices: 12.6 us -> 15.6 us  [the longest x7 12.7 us: along_row(): return lax.ppermute(x, 'row', [(i, i ^ k) for i in range(nrow)])]
    convert_element_type x2 -> x0, other arithmetic: 1.72 us -> none  [shards(): scaled = (teacher.astype(F32) * scale.astype(F32)[:, None]).astype(BF16)]
    dot_general x3 -> x0, matrix products: 1.58 us -> none  [the longest x1 0.97 us: shards(): grads = 4.0 * jnp.dot(error_b, unit_b, preferred_element_type=F32)]
  transfers between devices with their start and end apart: 3 -> 11, of which waited for: 3 -> 7; matrix products, arithmetic and copies ran while one was open for 1% -> 0% of each run, Pallas kernels for 0% -> 5%
where the time goes in v5:
time: 37.1 us; the launch traced here: 37 us
  starting transfers between devices  16.3 us (44%)
  waiting for transfers between devices  15.6 us (42%)
  Pallas kernels  3.39 us (9%)
  local copies, waits for them, and re-layouts  1.63 us (4%)
    ppermute x7, waiting for transfers between devices, along_row(): return lax.ppermute(x, 'row', [(i, i ^ k) for i in range(nrow)])  12.7 us
    ppermute x7, starting transfers between devices, along_row(): return lax.ppermute(x, 'row', [(i, i ^ k) for i in range(nrow)])  11.7 us
    ppermute x3, starting transfers between devices, along_col(): return lax.ppermute(x, 'col', [(i, (i - c) % ncol) for i in range(ncol)])  4.54 us
    pallas_call x9, Pallas kernels, call(): pl.pallas_call(run, out_shape=out_shape, in_specs=[pl.BlockSpec(memory_sp...  3.39 us
    unnamed x6, local copies, waits for them, and re-layouts  1.63 us
    ppermute x1, waiting for transfers between devices, other_core(): return lax.ppermute(x, 'sub', [(0, 1), (1, 0)])  1.57 us
    ppermute x3, waiting for transfers between devices, along_col(): return lax.ppermute(x, 'col', [(i, (i - c) % ncol) for i in range(ncol)])  1.34 us
  transfers between devices with their start and end apart: 11, of which 7 were waited for; matrix products, arithmetic and copies ran while one was open for 0% of the time, Pallas kernels for 5%

profile of v5, /device:TPU:0, one launch (start us, length us, event | category | flops | bytes accessed | tf_op | source)
XLA Modules:
  0.0 37.0 jit_solution(12854015662331092765)
XLA Ops:
  0.0 0.0 copy-start
  0.0 0.0 copy-start.1
  0.0 1.0 %copy-done.1 = bf16[64,2048]{1,0:T(8,128)(2,1)S(1)} copy-done((bf16[64,2048]{1,0:T(8,128)(2,1)S(1)}, bf16[64,2048]{1,0:T(8,128)(2,1)}, u32[]{:S(2)}) %copy-start.1) | copy-done | bytes 262168
  1.0 0.0 copy-start.2
  1.0 0.0 copy-done
  1.0 0.6 %copy-done.2 = bf16[64]{0:T(256)(128)(2,1)S(1)} copy-done((bf16[64]{0:T(256)(128)(2,1)S(1)}, bf16[64]{0:T(256)(128)(2,1)}, u32[]{:S(2)}) %copy-start.2) | copy-done | bytes 152
  1.7 0.3 shard_map.38
  1.9 4.1 %collective-permute-start = (bf16[144,512]{1,0:T(8,128)(2,1)S(1)}, bf16[144,512]{1,0:T(8,128)(2,1)S(1)}, u32[]{:S(2)}, u32[]{:S(2)}) collective-permute-start(bf16[144,512]{1,0:T(8,128)(2,1)S(1)} %get-tuple-element.23), channel_id=1, source_target_pairs={{0,8},{4,12},{8,0},{12,4},{1,9},{5,13},{9,1},{13,5},{2,10},{6,14},... | collective-permute-start | bytes 442376 | tf_op jit(solution)/shard_map/ppermute | solution.py:203
  6.0 1.5 %collective-permute-start.3 = (bf16[144,512]{1,0:T(8,128)(2,1)S(1)}, bf16[144,512]{1,0:T(8,128)(2,1)S(1)}, u32[]{:S(2)}, u32[]{:S(2)}) collective-permute-start(bf16[144,512]{1,0:T(8,128)(2,1)S(1)} %get-tuple-element.22.refs_0_), channel_id=1, source_target_pairs={{0,2},{2,0},{1,3},{3,1},{4,6},{6,4},{5,7},{7,5},{8,10},{10,8},{9,1... | collective-permute-start | bytes 442376 | tf_op jit(solution)/shard_map/ppermute | solution.py:206
  7.5 1.6 %collective-permute-start.1 = (bf16[64,512]{1,0:T(8,128)(2,1)S(1)}, bf16[64,512]{1,0:T(8,128)(2,1)S(1)}, u32[]{:S(2)}, u32[]{:S(2)}) collective-permute-start(bf16[64,512]{1,0:T(8,128)(2,1)S(1)} %get-tuple-element.19.refs_3_), channel_id=1, source_target_pairs={{0,4},{4,0},{8,12},{12,8},{1,5},{5,1},{9,13},{13,9},{2,6},{6,2},{1... | collective-permute-start | bytes 196616 | tf_op jit(solution)/shard_map/ppermute | solution.py:203
  9.1 0.2 collective-permute-start.2
  9.3 3.3 %collective-permute-done.1.refs_0_ = bf16[64,512]{1,0:T(8,128)(2,1)S(1)} collective-permute-done((bf16[64,512]{1,0:T(8,128)(2,1)S(1)}, bf16[64,512]{1,0:T(8,128)(2,1)S(1)}, u32[]{:S(2)}, u32[]{:S(2)}) %collective-permute-start.1) | collective-permute-done | bytes 65568 | tf_op jit(solution)/shard_map/ppermute | solution.py:203
  12.7 2.6 %collective-permute-done.2.refs_2_ = bf16[64,512]{1,0:T(8,128)(2,1)S(1)} collective-permute-done((bf16[64,512]{1,0:T(8,128)(2,1)S(1)}, bf16[64,512]{1,0:T(8,128)(2,1)S(1)}, u32[]{:S(2)}, u32[]{:S(2)}) %collective-permute-start.2) | collective-permute-done | bytes 65568 | tf_op jit(solution)/shard_map/ppermute | solution.py:203
  15.3 0.0 collective-permute-done.refs_1_.refs_0_
  15.3 0.0 collective-permute-done.3.refs_3_.refs_2_
  15.3 1.4 %collective-permute-start.4 = (bf16[160,512]{1,0:T(8,128)(2,1)S(1)}, bf16[160,512]{1,0:T(8,128)(2,1)S(1)}, u32[]{:S(2)}, u32[]{:S(2)}) collective-permute-start(bf16[160,512]{1,0:T(8,128)(2,1)S(1)} %shard_map.40), channel_id=1, source_target_pairs={{0,4},{4,0},{8,12},{12,8},{1,5},{5,1},{9,13},{13,9},{2,6},{6,2},{1... | collective-permute-start | bytes 491528 | tf_op jit(solution)/shard_map/ppermute | solution.py:203
  16.7 1.5 %collective-permute-start.6 = (bf16[192,512]{1,0:T(8,128)(2,1)S(1)}, bf16[192,512]{1,0:T(8,128)(2,1)S(1)}, u32[]{:S(2)}, u32[]{:S(2)}) collective-permute-start(bf16[192,512]{1,0:T(8,128)(2,1)S(1)} %shard_map.39.refs_2_.refs_1_), channel_id=1, source_target_pairs={{0,2},{2,0},{1,3},{3,1},{4,6},{6,4},{5,7},{7,5},{8,10},{10,8},{9,1... | collective-permute-start | bytes 589832 | tf_op jit(solution)/shard_map/ppermute | solution.py:206
  18.2 2.9 %collective-permute-done.4.refs_1_ = bf16[160,512]{1,0:T(8,128)(2,1)S(1)} collective-permute-done((bf16[160,512]{1,0:T(8,128)(2,1)S(1)}, bf16[160,512]{1,0:T(8,128)(2,1)S(1)}, u32[]{:S(2)}, u32[]{:S(2)}) %collective-permute-start.4) | collective-permute-done | bytes 163872 | tf_op jit(solution)/shard_map/ppermute | solution.py:203
  21.1 1.6 %collective-permute-start.5 = (bf16[240,512]{1,0:T(8,128)(2,1)S(1)}, bf16[240,512]{1,0:T(8,128)(2,1)S(1)}, u32[]{:S(2)}, u32[]{:S(2)}) collective-permute-start(bf16[240,512]{1,0:T(8,128)(2,1)S(1)} %shard_map.41.refs_1_), channel_id=1, source_target_pairs={{0,2},{2,0},{1,3},{3,1},{4,6},{6,4},{5,7},{7,5},{8,10},{10,8},{9,1... | collective-permute-start | bytes 737288 | tf_op jit(solution)/shard_map/ppermute | solution.py:206
  22.6 1.3 %collective-permute-done.6.refs_3_ = bf16[192,512]{1,0:T(8,128)(2,1)S(1)} collective-permute-done((bf16[192,512]{1,0:T(8,128)(2,1)S(1)}, bf16[192,512]{1,0:T(8,128)(2,1)S(1)}, u32[]{:S(2)}, u32[]{:S(2)}) %collective-permute-start.6) | collective-permute-done | bytes 196640 | tf_op jit(solution)/shard_map/ppermute | solution.py:206
  24.0 0.8 %shard_map.43 = (f32[64,512]{1,0:T(8,128)S(1)}, bf16[64,512]{1,0:T(8,128)(2,1)S(1)}, bf16[64,512]{1,0:T(8,128)(2,1)S(1)}, bf16[64,512]{1,0:T(8,128)(2,1)S(1)}) custom-call(bf16[144,512]{1,0:T(8,128)(2,1)S(1)} %get-tuple-element.22.refs_0_, bf16[192,512]{1,0:T(8,128)(2,1)S(1)} %shard_map.39.refs_2_.refs_1_, ...), custom_call_target="tpu_custom_call" | custom-call | tf_op jit(solution)/shard_map/pallas_call | solution.py:22
  24.8 0.5 %collective-permute-start.7 = (bf16[64,512]{1,0:T(8,128)(2,1)S(1)}, bf16[64,512]{1,0:T(8,128)(2,1)S(1)}, u32[]{:S(2)}, u32[]{:S(2)}) collective-permute-start(bf16[64,512]{1,0:T(8,128)(2,1)S(1)} %get-tuple-element.27), channel_id=1, source_target_pairs={{0,4},{4,0},{8,12},{12,8},{1,5},{5,1},{9,13},{13,9},{2,6},{6,2},{1... | collective-permute-start | bytes 196616 | tf_op jit(solution)/shard_map/ppermute | solution.py:203
  25.3 2.9 %collective-permute-start.8 = (bf16[64,512]{1,0:T(8,128)(2,1)S(1)}, bf16[64,512]{1,0:T(8,128)(2,1)S(1)}, u32[]{:S(2)}, u32[]{:S(2)}) collective-permute-start(bf16[64,512]{1,0:T(8,128)(2,1)S(1)} %get-tuple-element.28), channel_id=1, source_target_pairs={{0,8},{4,12},{8,0},{12,4},{1,9},{5,13},{9,1},{13,5},{2,10},{6,14},... | collective-permute-start | bytes 196616 | tf_op jit(solution)/shard_map/ppermute | solution.py:203
  28.1 1.1 %collective-permute-start.9 = (bf16[64,512]{1,0:T(8,128)(2,1)S(1)}, bf16[64,512]{1,0:T(8,128)(2,1)S(1)}, u32[]{:S(2)}, u32[]{:S(2)}) collective-permute-start(bf16[64,512]{1,0:T(8,128)(2,1)S(1)} %get-tuple-element.29), channel_id=1, source_target_pairs={{0,12},{4,8},{8,4},{12,0},{1,13},{5,9},{9,5},{13,1},{2,14},{6,10},... | collective-permute-start | bytes 196616 | tf_op jit(solution)/shard_map/ppermute | solution.py:203
  29.2 0.0 collective-permute-done.5.refs_3_
  29.2 1.1 %shard_map.42 = (f32[72,512]{1,0:T(8,128)S(1)}, f32[16,512]{1,0:T(8,128)S(1)}, bf16[512,512]{1,0:T(8,128)(2,1)S(1)}) custom-call(bf16[144,512]{1,0:T(8,128)(2,1)S(1)} %get-tuple-element.22.refs_0_, bf16[240,512]{1,0:T(8,128)(2,1)S(1)} %shard_map.41.refs_1_, bf16[144,512]{1,0:T(8,128)(2,1)S(1)} %collective-permute-done.3.refs_3_.refs_2_, ...), custom_call_target="tpu_custom_call" | custom-call | tf_op jit(solution)/shard_map/pallas_call | solution.py:22
  30.4 0.0 collective-permute-done.7.refs_3_
  30.4 2.0 %collective-permute-done.8.refs_4_ = bf16[64,512]{1,0:T(8,128)(2,1)S(1)} collective-permute-done((bf16[64,512]{1,0:T(8,128)(2,1)S(1)}, bf16[64,512]{1,0:T(8,128)(2,1)S(1)}, u32[]{:S(2)}, u32[]{:S(2)}) %collective-permute-start.8) | collective-permute-done | bytes 65568 | tf_op jit(solution)/shard_map/ppermute | solution.py:203
  32.4 1.8 %collective-permute-done.9.refs_5_ = bf16[64,512]{1,0:T(8,128)(2,1)S(1)} collective-permute-done((bf16[64,512]{1,0:T(8,128)(2,1)S(1)}, bf16[64,512]{1,0:T(8,128)(2,1)S(1)}, u32[]{:S(2)}, u32[]{:S(2)}) %collective-permute-start.9) | collective-permute-done | bytes 65568 | tf_op jit(solution)/shard_map/ppermute | solution.py:203
  34.2 0.1 collective-permute-start.10
  34.3 1.6 %collective-permute-done.10.refs_1_ = f32[144,512]{1,0:T(8,128)S(1)} collective-permute-done((f32[144,512]{1,0:T(8,128)S(1)}, f32[144,512]{1,0:T(8,128)S(1)}, u32[]{:S(2)}, u32[]{:S(2)}) %collective-permute-start.10) | collective-permute-done | bytes 294944 | tf_op jit(solution)/shard_map/ppermute | solution.py:209
  35.9 1.1 %shard_map.45 = f32[64,512]{1,0:T(8,128)} custom-call(f32[144,512]{1,0:T(8,128)S(1)} %shard_map.44.refs_0_, f32[144,512]{1,0:T(8,128)S(1)} %collective-permute-done.10.refs_1_, f32[16,512]{1,0:T(8,128)S(1)} %get-tuple-element.25.refs_1_.refs_2_, bf16[64,512]{1,0:T(8,128)(2,1)S(1)} %copy-done, bf16[1,64]{1,0:T(2,128)(2,1)S(1)} %bitcast.2, ...), custom_call_target="tpu_custom_call" | custom-call | tf_op jit(solution)/shard_map/pallas_call | solution.py:22
  (5 shorter events, 0.1 us)
Async XLA Ops:
  0.0 1.0 %copy-start = (bf16[64,512]{1,0:T(8,128)(2,1)S(1)}, bf16[64,512]{1,0:T(8,128)(2,1)}, u32[]{:S(2)}) copy-start(bf16[64,512]{1,0:T(8,128)(2,1)} %refs_3_.1) | copy-start | bytes 196612
  0.0 1.0 %copy-start.1 = (bf16[64,2048]{1,0:T(8,128)(2,1)S(1)}, bf16[64,2048]{1,0:T(8,128)(2,1)}, u32[]{:S(2)}) copy-start(bf16[64,2048]{1,0:T(8,128)(2,1)} %refs_0_.2) | copy-start | bytes 786436
  1.0 0.7 %copy-start.2 = (bf16[64]{0:T(256)(128)(2,1)S(1)}, bf16[64]{0:T(256)(128)(2,1)}, u32[]{:S(2)}) copy-start(bf16[64]{0:T(256)(128)(2,1)} %param.5) | copy-start | bytes 388
  1.9 13.3 %collective-permute-start = (bf16[144,512]{1,0:T(8,128)(2,1)S(1)}, bf16[144,512]{1,0:T(8,128)(2,1)S(1)}, u32[]{:S(2)}, u32[]{:S(2)}) collective-permute-start(bf16[144,512]{1,0:T(8,128)(2,1)S(1)} %get-tuple-element.23), channel_id=1, source_target_pairs={{0,8},{4,12},{8,0},{12,4},{1,9},{5,13},{9,1},{13,5},{2,10},{6,14},... | collective-permute-start | bytes 442376 | tf_op jit(solution)/shard_map/ppermute | solution.py:203
  6.0 9.2 %collective-permute-start.3 = (bf16[144,512]{1,0:T(8,128)(2,1)S(1)}, bf16[144,512]{1,0:T(8,128)(2,1)S(1)}, u32[]{:S(2)}, u32[]{:S(2)}) collective-permute-start(bf16[144,512]{1,0:T(8,128)(2,1)S(1)} %get-tuple-element.22.refs_0_), channel_id=1, source_target_pairs={{0,2},{2,0},{1,3},{3,1},{4,6},{6,4},{5,7},{7,5},{8,10},{10,8},{9,1... | collective-permute-start | bytes 442376 | tf_op jit(solution)/shard_map/ppermute | solution.py:206
  7.5 5.1 %collective-permute-start.1 = (bf16[64,512]{1,0:T(8,128)(2,1)S(1)}, bf16[64,512]{1,0:T(8,128)(2,1)S(1)}, u32[]{:S(2)}, u32[]{:S(2)}) collective-permute-start(bf16[64,512]{1,0:T(8,128)(2,1)S(1)} %get-tuple-element.19.refs_3_), channel_id=1, source_target_pairs={{0,4},{4,0},{8,12},{12,8},{1,5},{5,1},{9,13},{13,9},{2,6},{6,2},{1... | collective-permute-start | bytes 196616 | tf_op jit(solution)/shard_map/ppermute | solution.py:203
  9.1 6.2 %collective-permute-start.2 = (bf16[64,512]{1,0:T(8,128)(2,1)S(1)}, bf16[64,512]{1,0:T(8,128)(2,1)S(1)}, u32[]{:S(2)}, u32[]{:S(2)}) collective-permute-start(bf16[64,512]{1,0:T(8,128)(2,1)S(1)} %get-tuple-element.21.refs_5_), channel_id=1, source_target_pairs={{0,12},{4,8},{8,4},{12,0},{1,13},{5,9},{9,5},{13,1},{2,14},{6,10},... | collective-permute-start | bytes 196616 | tf_op jit(solution)/shard_map/ppermute | solution.py:203
  15.3 5.7 %collective-permute-start.4 = (bf16[160,512]{1,0:T(8,128)(2,1)S(1)}, bf16[160,512]{1,0:T(8,128)(2,1)S(1)}, u32[]{:S(2)}, u32[]{:S(2)}) collective-permute-start(bf16[160,512]{1,0:T(8,128)(2,1)S(1)} %shard_map.40), channel_id=1, source_target_pairs={{0,4},{4,0},{8,12},{12,8},{1,5},{5,1},{9,13},{13,9},{2,6},{6,2},{1... | collective-permute-start | bytes 491528 | tf_op jit(solution)/shard_map/ppermute | solution.py:203
  16.7 7.3 %collective-permute-start.6 = (bf16[192,512]{1,0:T(8,128)(2,1)S(1)}, bf16[192,512]{1,0:T(8,128)(2,1)S(1)}, u32[]{:S(2)}, u32[]{:S(2)}) collective-permute-start(bf16[192,512]{1,0:T(8,128)(2,1)S(1)} %shard_map.39.refs_2_.refs_1_), channel_id=1, source_target_pairs={{0,2},{2,0},{1,3},{3,1},{4,6},{6,4},{5,7},{7,5},{8,10},{10,8},{9,1... | collective-permute-start | bytes 589832 | tf_op jit(solution)/shard_map/ppermute | solution.py:206
  21.1 8.1 %collective-permute-start.5 = (bf16[240,512]{1,0:T(8,128)(2,1)S(1)}, bf16[240,512]{1,0:T(8,128)(2,1)S(1)}, u32[]{:S(2)}, u32[]{:S(2)}) collective-permute-start(bf16[240,512]{1,0:T(8,128)(2,1)S(1)} %shard_map.41.refs_1_), channel_id=1, source_target_pairs={{0,2},{2,0},{1,3},{3,1},{4,6},{6,4},{5,7},{7,5},{8,10},{10,8},{9,1... | collective-permute-start | bytes 737288 | tf_op jit(solution)/shard_map/ppermute | solution.py:206
  24.8 5.6 %collective-permute-start.7 = (bf16[64,512]{1,0:T(8,128)(2,1)S(1)}, bf16[64,512]{1,0:T(8,128)(2,1)S(1)}, u32[]{:S(2)}, u32[]{:S(2)}) collective-permute-start(bf16[64,512]{1,0:T(8,128)(2,1)S(1)} %get-tuple-element.27), channel_id=1, source_target_pairs={{0,4},{4,0},{8,12},{12,8},{1,5},{5,1},{9,13},{13,9},{2,6},{6,2},{1... | collective-permute-start | bytes 196616 | tf_op jit(solution)/shard_map/ppermute | solution.py:203
  25.3 7.1 %collective-permute-start.8 = (bf16[64,512]{1,0:T(8,128)(2,1)S(1)}, bf16[64,512]{1,0:T(8,128)(2,1)S(1)}, u32[]{:S(2)}, u32[]{:S(2)}) collective-permute-start(bf16[64,512]{1,0:T(8,128)(2,1)S(1)} %get-tuple-element.28), channel_id=1, source_target_pairs={{0,8},{4,12},{8,0},{12,4},{1,9},{5,13},{9,1},{13,5},{2,10},{6,14},... | collective-permute-start | bytes 196616 | tf_op jit(solution)/shard_map/ppermute | solution.py:203
  28.1 6.1 %collective-permute-start.9 = (bf16[64,512]{1,0:T(8,128)(2,1)S(1)}, bf16[64,512]{1,0:T(8,128)(2,1)S(1)}, u32[]{:S(2)}, u32[]{:S(2)}) collective-permute-start(bf16[64,512]{1,0:T(8,128)(2,1)S(1)} %get-tuple-element.29), channel_id=1, source_target_pairs={{0,12},{4,8},{8,4},{12,0},{1,13},{5,9},{9,5},{13,1},{2,14},{6,10},... | collective-permute-start | bytes 196616 | tf_op jit(solution)/shard_map/ppermute | solution.py:203
  34.2 1.6 %collective-permute-start.10 = (f32[144,512]{1,0:T(8,128)S(1)}, f32[144,512]{1,0:T(8,128)S(1)}, u32[]{:S(2)}, u32[]{:S(2)}) collective-permute-start(f32[144,512]{1,0:T(8,128)S(1)} %shard_map.44.refs_0_), channel_id=1, source_target_pairs={{0,1},{1,0},{2,3},{3,2},{4,5},{5,4},{6,7},{7,6},{8,9},{9,8},{10,11... | collective-permute-start | bytes 884744 | tf_op jit(solution)/shard_map/ppermute | solution.py:209

commit v6 on v5

v6 whole, which is shorter than its diff:
```python
import functools

import jax
import jax.numpy as jnp
from jax import lax
from jax.experimental import pallas as pl
from jax.experimental.pallas import tpu as pltpu
from jax.sharding import PartitionSpec as P

F32, BF16 = jnp.float32, jnp.bfloat16
INNER = (((1,), (1,)), ((), ()))
TAIL = 16


def call(body, out_shape, operands, space=pltpu.VMEM, scratch=(), after=()):
    outs = out_shape if isinstance(out_shape, (list, tuple)) else [out_shape]
    moved = sum(x.size * x.dtype.itemsize for x in list(operands) + list(outs))

    def run(*refs):
        body(*refs[: len(operands)], *refs[len(operands) + len(after) :])

    return pl.pallas_call(
        run,
        out_shape=out_shape,
        in_specs=[pl.BlockSpec(memory_space=space)] * len(operands) + [pl.BlockSpec(memory_space=pl.ANY)] * len(after),
        out_specs=jax.tree.map(lambda _: pl.BlockSpec(memory_space=pltpu.VMEM), out_shape),
        scratch_shapes=list(scratch),
        cost_estimate=pl.CostEstimate(flops=0, bytes_accessed=0, transcendentals=0),
        compiler_params=pltpu.CompilerParams(vmem_limit_bytes=min(56 << 20, (8 << 20) + 3 * moved)),
    )(*operands, *after)


def column(row):
    shape = (row.shape[1], row.shape[1])
    eye = lax.broadcasted_iota(jnp.int32, shape, 0) == lax.broadcasted_iota(jnp.int32, shape, 1)
    return jnp.sum(jnp.where(eye, row, 0.0), axis=1, keepdims=True)


def tags_of(scales, mass):
    shape = (TAIL, scales.shape[1])
    at = lax.broadcasted_iota(jnp.int32, shape, 0)
    high = mass.astype(BF16).astype(F32)
    return jnp.where(at < 8, scales, jnp.where(at < 12, high, mass - high)).astype(BF16)


def read_tags(tags):
    tags = tags.astype(F32)
    return tags[0:1, :], tags[8:9, 0:1] + tags[12:13, 0:1]


def lane_row(col):
    shape = (col.shape[0], col.shape[0])
    eye = lax.broadcasted_iota(jnp.int32, shape, 0) == lax.broadcasted_iota(jnp.int32, shape, 1)
    return jnp.sum(jnp.where(eye, col, 0.0), axis=0, keepdims=True)


def wide(out, at, piece):
    rows, part = piece.shape
    width = out.shape[1]
    high = rows * part // width
    for n in range(width // part):
        out[at : at + high, n * part : (n + 1) * part] = piece[n * high : (n + 1) * high, :]


def put(held, spot, rows, ref, at):
    width = held.shape[1]
    high = rows * width // ref.shape[1]
    for n in range(ref.shape[1] // width):
        held[pl.ds(spot + n * high, high), :] = ref[at : at + high, n * width : (n + 1) * width]


def cut_kernel(nrow, teach, *outs):
    part = teach.shape[1] // nrow
    z = lax.axis_index("row")
    for k in range(nrow):
        at = pl.multiple_of((z ^ k) * part, part)
        outs[k][...] = teach[:, pl.ds(at, part)]


def ride_kernel(stud, *refs):
    rows, count = stud.shape[0], len(refs) // 2
    for piece, out in zip(refs[:count], refs[count:]):
        out[:rows, :] = stud[...]
        wide(out, rows, piece)


def own_kernel(teach, stud, scale, cut, out):
    rows, half = stud.shape
    ts = teach[...].astype(F32)
    s = scale[...].astype(F32)
    mass = jnp.sum(jnp.square(column(s)) * jnp.sum(ts * ts, axis=1, keepdims=True), keepdims=True)
    tags = tags_of(jnp.concatenate([s, s], axis=1), mass)
    out[:rows, :] = stud[...]
    out[rows : rows + TAIL, :] = jnp.concatenate([tags] * (half // (2 * rows)), axis=1)
    wide(out, rows + TAIL, cut[...])


def take_kernel(rows, ref, out):
    put(out, 0, rows, ref, rows)


def pack_kernel(spans, *refs):
    out, at = refs[-1], 0
    for r, (first, last) in zip(refs[:-1], spans):
        out[at : at + last - first, :] = r[first:last, :]
        at += last - first


def place(nrow, ncol, rows, k, c):
    return pl.multiple_of(((lax.axis_index("row") ^ k) * ncol + c) * rows, rows)


def group_spot(nrow, ncol, rows, k):
    return pl.multiple_of((lax.axis_index("row") ^ k) * ncol * rows, 2 * rows)


def gram_kernel(nrow, ncol, rows, order, *refs):
    count = nrow * ncol
    outs, held, left = refs[count : count + nrow], refs[-2], refs[-1]
    for c in range(ncol):
        own = refs[c * nrow]
        put(held, place(nrow, ncol, rows, 0, c), rows, own, rows + TAIL)
        for k in range(1, nrow):
            put(held, place(nrow, ncol, rows, k, c), rows, refs[c * nrow + k], 0)
    for n, k in enumerate(order):
        left[n * rows : (n + 1) * rows, :] = held[pl.ds(place(nrow, ncol, rows, k, 0), rows), :]
    sub = rows // 2
    at = lax.broadcasted_iota(jnp.int32, (sub, 2 * rows), 0)
    lane = lax.broadcasted_iota(jnp.int32, (sub, 2 * rows), 1)
    note, mass = jnp.zeros((sub, 2 * rows), F32), jnp.zeros((1, 1), F32)
    for c in range(ncol):
        scales, part = read_tags(refs[c * nrow][rows : rows + TAIL, : 2 * rows])
        turned = jnp.concatenate([scales[:, sub:], scales[:, :sub]], axis=1)
        note = jnp.where(at == 2 * c, scales, jnp.where(at == 2 * c + 1, turned, note))
        mass = mass + part
    high = mass.astype(BF16).astype(F32)
    note = jnp.where(at < sub // 2, note, jnp.where(at < sub * 3 // 4, high, mass - high))
    per = max(1, 2048 * rows * nrow // held.shape[0] // rows // 8)
    for first in range(0, nrow, per):
        last = min(first + per, nrow)
        gram = lax.dot_general(left[first * rows : last * rows, :], held[...], INNER, preferred_element_type=F32)
        for n in range(first, last):
            out = outs[order[n]]
            out[...] = gram[(n - first) * rows : (n - first + 1) * rows, :].astype(out.dtype)
            spot = pl.ds(group_spot(nrow, ncol, rows, order[n]), 2 * rows)
            seen = out[sub:, spot].astype(F32)
            out[sub:, spot] = jnp.where(lane < sub, note, seen).astype(out.dtype)


def assemble(nrow, ncol, rows, keys, refs, held):
    each = len(keys)
    for c in range(ncol):
        for stack, ref in zip(keys, refs[c * each : (c + 1) * each]):
            for n, k in enumerate(stack):
                held[pl.ds(place(nrow, ncol, rows, k, c), rows), :] = ref[n * rows : (n + 1) * rows, :]


def raw_gram_kernel(nrow, ncol, rows, keys, *refs):
    count = len(keys) * ncol
    out, raw = refs[count:]
    assemble(nrow, ncol, rows, keys, refs, raw)
    out[:rows, :] = lax.dot_general(refs[0][:rows, :], raw[...], INNER, preferred_element_type=F32)
    for at in range(0, raw.shape[0], 128):
        squares = jnp.sum(jnp.square(raw[at : at + 128, :].astype(F32)), axis=1, keepdims=True)
        out[rows:, at : at + 128] = jnp.broadcast_to(lane_row(squares), (8, 128))


def message_kernel(nrow, ncol, raw_gram, *refs):
    parts, (out, vectors) = refs[:-2], refs[-2:]
    rows = parts[0].shape[0]
    sub = rows // 2
    total = parts[0][...].astype(F32)
    for r in parts[1:]:
        total = total + r[...].astype(F32)
    out[:rows, :] = total
    own = pl.ds(group_spot(nrow, ncol, rows, 0), 2 * rows)
    mirror = jnp.transpose(out[:sub, own])[sub : 2 * sub, :]
    out[sub:rows, own] = jnp.concatenate([mirror, out[sub:rows, own][:, sub:]], axis=1)
    mass = jnp.zeros((1, 1), F32)
    for k, part in enumerate(parts):
        note = part[sub:, own].astype(F32)[:, :sub]
        mass = mass + note[sub // 2 : sub // 2 + 1, :1] + note[sub * 3 // 4 : sub * 3 // 4 + 1, :1]
        line = jnp.concatenate([note[n : n + 1, :] for n in range(2 * ncol)], axis=1)
        vectors[:, pl.ds(group_spot(nrow, ncol, rows, k), ncol * rows)] = jnp.broadcast_to(line, (8, ncol * rows))
    out[rows : 2 * rows + 8, :] = raw_gram[...]
    out[2 * rows + 8 :, :] = jnp.broadcast_to(mass, (8, out.shape[1]))


def final_kernel(nrow, ncol, keys, mine, other, vectors, stud, scale, *refs):
    rows = stud.shape[0]
    if keys:
        out, raw, units = refs[-3:]
        assemble(nrow, ncol, rows, keys, refs, raw)
    else:
        raw, out, units = refs
    batch = mine.shape[1]
    squares = mine[2 * rows : 2 * rows + 8, :] + other[2 * rows : 2 * rows + 8, :]
    for at in range(0, batch, 128):
        norm = jnp.sqrt(column(squares[:1, at : at + 128]))
        units[at : at + 128, :] = (raw[at : at + 128, :].astype(F32) / norm).astype(BF16)
    at = pl.ds(group_spot(nrow, ncol, rows, 0), 2 * rows)
    own = (mine[2 * rows : 2 * rows + 8, at] + other[2 * rows : 2 * rows + 8, at])[:1, :rows]
    norm = jnp.sqrt(column(own))
    mass = (mine[2 * rows + 8 : 2 * rows + 9, :1] + other[2 * rows + 8 : 2 * rows + 9, :1]) / batch
    gram = (mine[rows : 2 * rows, :] + other[rows : 2 * rows, :]) / (norm * jnp.sqrt(squares[:1, :]))
    outer = column(scale[...].astype(F32)) * vectors[:1, :]
    error_b = (gram - outer * (mine[:rows, :] + other[:rows, :]) / mass).astype(BF16)
    grads = 4.0 * jnp.dot(error_b, units[...], preferred_element_type=F32)
    along = 4.0 * jnp.sum(error_b.astype(F32) * gram, axis=1, keepdims=True)
    unit = stud[...].astype(F32) / norm
    out[...] = (grads - along * unit) / norm


def shards(student, teacher, scale):
    rows, half = student.shape
    nrow, ncol = lax.axis_size("row"), lax.axis_size("col")
    batch = rows * nrow * ncol
    part = teacher.shape[1] // nrow
    small = batch <= 2048
    sds = jax.ShapeDtypeStruct
    scale = scale.reshape(1, rows)

    def along_row(x, k):
        return lax.ppermute(x, "row", [(i, i ^ k) for i in range(nrow)])

    def along_col(x, c):
        return lax.ppermute(x, "col", [(i, (i - c) % ncol) for i in range(ncol)])

    def other_core(x):
        return lax.ppermute(x, "sub", [(0, 1), (1, 0)])

    def pack(xs, spans, after=()):
        shape = (sum(last - first for first, last in spans), half)
        return call(functools.partial(pack_kernel, spans), sds(shape, BF16), xs, after=after)

    def with_columns(x):
        return [x if c == 0 else along_col(x, c) for c in range(ncol)]

    middle, high = nrow // 2, rows * part // half
    order = list(range(middle, nrow)) + list(range(middle))
    riders = (1, middle)
    cuts = call(functools.partial(cut_kernel, nrow), [sds((rows, part), BF16)] * nrow, [teacher])
    ridden = call(ride_kernel, [sds((rows + high, half), BF16)] * 2, [student] + [cuts[k] for k in riders])
    leaving = dict(enumerate(cuts)) | dict(zip(riders, ridden))
    came = {k: along_row(leaving[k], k) for k in order if k}
    own = call(own_kernel, sds((rows + TAIL + high, half), BF16), [teacher, student, scale, cuts[0]])
    columns = {0: with_columns(own)}
    for k in range(1, nrow):
        piece = came[k]
        if k in riders:
            piece = call(functools.partial(take_kernel, rows), sds((rows, part), BF16), [piece])
        columns[k] = with_columns(piece)
    partial = call(
        functools.partial(gram_kernel, nrow, ncol, rows, order),
        [sds((rows, batch), BF16 if k else F32) for k in range(nrow)],
        [columns[k][c] for c in range(ncol) for k in range(nrow)],
        scratch=[pltpu.VMEM((batch, part), BF16), pltpu.VMEM((nrow * rows, part), BF16)],
    )
    returned = {k: along_row(partial[k], k) if k else partial[0] for k in order}

    near, far = came[1], came[middle]
    stack, keys, k, spans, got, got_keys = [student, far], [0, middle], middle // 2, [(0, rows)] * 2, [], []
    while k:
        first = 1 if k == 1 else 0
        sent = pack(stack[first:], spans[first:])
        got.append(along_row(sent, k))
        got_keys += [n ^ k for n in keys[first:]]
        stack, spans, keys = stack + got[-1:], spans + [(0, len(keys) * rows)], keys + [n ^ k for n in keys]
        k //= 2
    rest = pack([near, far] + got, [(0, rows)] * 2 + [(0, g.shape[0]) for g in got], after=[partial[0]])
    raw_keys = [[0], [1, middle] + got_keys]
    sources = [columns[0], with_columns(rest)]
    raw_refs = [x[c] for c in range(ncol) for x in sources]
    raw_gram, *all_raw = call(
        functools.partial(raw_gram_kernel, nrow, ncol, rows, raw_keys),
        [sds((rows + 8, batch), F32)] + ([sds((batch, half), BF16)] if small else []),
        raw_refs,
        scratch=[] if small else [pltpu.VMEM((batch, half), BF16)],
    )
    message, vectors = call(
        functools.partial(message_kernel, nrow, ncol),
        [sds((2 * rows + 16, batch), F32), sds((8, batch), F32)],
        [raw_gram] + [returned[k] for k in range(nrow)],
    )
    return call(
        functools.partial(final_kernel, nrow, ncol, None if small else raw_keys),
        sds((rows, half), F32),
        [message, other_core(message), vectors, student, scale] + (all_raw if small else raw_refs),
        scratch=([] if small else [pltpu.VMEM((batch, half), BF16)]) + [pltpu.VMEM((batch, half), BF16)],
    )


def solution(mesh):
    spec = P(("groups", "row", "col"), "sub")
    return jax.shard_map(
        shards,
        mesh=mesh,
        in_specs=(spec, spec, P(("groups", "row", "col"))),
        out_specs=spec,
        check_vma=False,
    )
```

time: 37.1 us -> 35.8 us (0.965)
  waiting for transfers between devices: 15.6 us -> 12.8 us
  starting transfers between devices: 16.3 us -> 18 us
  Pallas kernels: 3.39 us -> 2.4 us
  local copies, waits for them, and re-layouts: 1.63 us -> 2.48 us
    ppermute x7, waiting for transfers between devices: 12.7 us -> 9.27 us  [along_row(): return lax.ppermute(x, 'row', [(i, i ^ k) for i in range(nrow)])]
    ppermute x3 -> x5, starting transfers between devices: 4.54 us -> 5.69 us  [along_col(): return lax.ppermute(x, 'col', [(i, (i - c) % ncol) for i in range(ncol)])]
    pallas_call x9 -> x11, Pallas kernels: 3.39 us -> 2.4 us  [call(): pl.pallas_call(run, out_shape=out_shape, in_specs=[pl.BlockSpec(memory_sp...]
    unnamed x6 -> x10, local copies, waits for them, and re-layouts: 1.63 us -> 2.48 us
    ppermute x3 -> x5, waiting for transfers between devices: 1.34 us -> 1.92 us  [along_col(): return lax.ppermute(x, 'col', [(i, (i - c) % ncol) for i in range(ncol)])]
    ppermute x7, starting transfers between devices: 11.7 us -> 12.2 us  [along_row(): return lax.ppermute(x, 'row', [(i, i ^ k) for i in range(nrow)])]
  transfers between devices with their start and end apart: 11 -> 13, of which waited for: 7 -> 6; matrix products, arithmetic and copies ran while one was open for 0% -> 0% of each run, Pallas kernels for 5% -> 3%
where the time goes in v6:
time: 35.8 us; the launch traced here: 35.7 us
  starting transfers between devices  18 us (50%)
  waiting for transfers between devices  12.8 us (36%)
  local copies, waits for them, and re-layouts  2.48 us (7%)
  Pallas kernels  2.4 us (7%)
    ppermute x7, starting transfers between devices, along_row(): return lax.ppermute(x, 'row', [(i, i ^ k) for i in range(nrow)])  12.2 us
    ppermute x7, waiting for transfers between devices, along_row(): return lax.ppermute(x, 'row', [(i, i ^ k) for i in range(nrow)])  9.27 us
    ppermute x5, starting transfers between devices, along_col(): return lax.ppermute(x, 'col', [(i, (i - c) % ncol) for i in range(ncol)])  5.69 us
    unnamed x10, local copies, waits for them, and re-layouts  2.48 us
    pallas_call x11, Pallas kernels, call(): pl.pallas_call(run, out_shape=out_shape, in_specs=[pl.BlockSpec(memory_sp...  2.4 us
    ppermute x5, waiting for transfers between devices, along_col(): return lax.ppermute(x, 'col', [(i, (i - c) % ncol) for i in range(ncol)])  1.92 us
    ppermute x1, waiting for transfers between devices, other_core(): return lax.ppermute(x, 'sub', [(0, 1), (1, 0)])  1.57 us
  transfers between devices with their start and end apart: 13, of which 6 were waited for; matrix products, arithmetic and copies ran while one was open for 0% of the time, Pallas kernels for 3%

profile of v6, /device:TPU:0, one launch (start us, length us, event | category | flops | bytes accessed | tf_op | source)
XLA Modules:
  0.0 35.7 jit_solution(2996896532650800057)
XLA Ops:
  0.0 0.0 copy-start
  0.0 0.9 %copy-done = bf16[64,2048]{1,0:T(8,128)(2,1)S(1)} copy-done((bf16[64,2048]{1,0:T(8,128)(2,1)S(1)}, bf16[64,2048]{1,0:T(8,128)(2,1)}, u32[]{:S(2)}) %copy-start) | copy-done | bytes 262168
  1.0 0.0 copy-start.1
  1.0 0.0 copy-start.2
  1.0 0.9 %copy-done.2 = bf16[64,512]{1,0:T(8,128)(2,1)S(1)} copy-done((bf16[64,512]{1,0:T(8,128)(2,1)S(1)}, bf16[64,512]{1,0:T(8,128)(2,1)}, u32[]{:S(2)}) %copy-start.2) | copy-done | bytes 65560
  1.9 0.0 copy-start.3
  1.9 3.1 %collective-permute-start = (bf16[128,512]{1,0:T(8,128)(2,1)S(1)}, bf16[128,512]{1,0:T(8,128)(2,1)S(1)}, u32[]{:S(2)}, u32[]{:S(2)}) collective-permute-start(bf16[128,512]{1,0:T(8,128)(2,1)S(1)} %get-tuple-element.22), channel_id=1, source_target_pairs={{0,4},{4,0},{8,12},{12,8},{1,5},{5,1},{9,13},{13,9},{2,6},{6,2},{1... | collective-permute-start | bytes 393224 | tf_op jit(solution)/shard_map/ppermute | solution.py:224
  5.0 2.6 %collective-permute-start.1 = (bf16[128,512]{1,0:T(8,128)(2,1)S(1)}, bf16[128,512]{1,0:T(8,128)(2,1)S(1)}, u32[]{:S(2)}, u32[]{:S(2)}) collective-permute-start(bf16[128,512]{1,0:T(8,128)(2,1)S(1)} %get-tuple-element.23), channel_id=1, source_target_pairs={{0,8},{4,12},{8,0},{12,4},{1,9},{5,13},{9,1},{13,5},{2,10},{6,14},... | collective-permute-start | bytes 393224 | tf_op jit(solution)/shard_map/ppermute | solution.py:224
  7.6 0.0 copy-start.4
  7.6 0.0 copy-done.1
  7.6 0.0 copy-done.3
  7.6 0.6 %copy-done.4 = bf16[64]{0:T(256)(128)(2,1)S(1)} copy-done((bf16[64]{0:T(256)(128)(2,1)S(1)}, bf16[64]{0:T(256)(128)(2,1)}, u32[]{:S(2)}) %copy-start.4) | copy-done | bytes 152
  8.2 0.3 shard_map.38.refs_0_
  8.5 1.6 %collective-permute-start.4 = (bf16[144,512]{1,0:T(8,128)(2,1)S(1)}, bf16[144,512]{1,0:T(8,128)(2,1)S(1)}, u32[]{:S(2)}, u32[]{:S(2)}) collective-permute-start(bf16[144,512]{1,0:T(8,128)(2,1)S(1)} %shard_map.38.refs_0_), channel_id=1, source_target_pairs={{0,2},{2,0},{1,3},{3,1},{4,6},{6,4},{5,7},{7,5},{8,10},{10,8},{9,1... | collective-permute-start | bytes 442376 | tf_op jit(solution)/shard_map/ppermute | solution.py:227
  10.0 0.2 collective-permute-start.3
  10.3 5.9 %collective-permute-done.3.refs_3_ = bf16[64,512]{1,0:T(8,128)(2,1)S(1)} collective-permute-done((bf16[64,512]{1,0:T(8,128)(2,1)S(1)}, bf16[64,512]{1,0:T(8,128)(2,1)S(1)}, u32[]{:S(2)}, u32[]{:S(2)}) %collective-permute-start.3) | collective-permute-done | bytes 65568 | tf_op jit(solution)/shard_map/ppermute | solution.py:224
  16.2 0.4 %collective-permute-start.7 = (bf16[64,512]{1,0:T(8,128)(2,1)S(1)}, bf16[64,512]{1,0:T(8,128)(2,1)S(1)}, u32[]{:S(2)}, u32[]{:S(2)}) collective-permute-start(bf16[64,512]{1,0:T(8,128)(2,1)S(1)} %collective-permute-done.3.refs_3_), channel_id=1, source_target_pairs={{0,2},{2,0},{1,3},{3,1},{4,6},{6,4},{5,7},{7,5},{8,10},{10,8},{9,1... | collective-permute-start | bytes 196616 | tf_op jit(solution)/shard_map/ppermute | solution.py:227
  16.6 0.0 collective-permute-done.refs_0_
  16.6 1.7 %collective-permute-start.5 = (bf16[64,512]{1,0:T(8,128)(2,1)S(1)}, bf16[64,512]{1,0:T(8,128)(2,1)S(1)}, u32[]{:S(2)}, u32[]{:S(2)}) collective-permute-start(bf16[64,512]{1,0:T(8,128)(2,1)S(1)} %shard_map.41.refs_1_), channel_id=1, source_target_pairs={{0,2},{2,0},{1,3},{3,1},{4,6},{6,4},{5,7},{7,5},{8,10},{10,8},{9,1... | collective-permute-start | bytes 196616 | tf_op jit(solution)/shard_map/ppermute | solution.py:227
  18.3 0.0 collective-permute-done.1.refs_0_.refs_1_
  18.3 0.5 %collective-permute-start.6 = (bf16[64,512]{1,0:T(8,128)(2,1)S(1)}, bf16[64,512]{1,0:T(8,128)(2,1)S(1)}, u32[]{:S(2)}, u32[]{:S(2)}) collective-permute-start(bf16[64,512]{1,0:T(8,128)(2,1)S(1)} %shard_map.42.refs_2_), channel_id=1, source_target_pairs={{0,2},{2,0},{1,3},{3,1},{4,6},{6,4},{5,7},{7,5},{8,10},{10,8},{9,1... | collective-permute-start | bytes 196616 | tf_op jit(solution)/shard_map/ppermute | solution.py:227
  18.8 1.9 %collective-permute-start.2 = (bf16[64,512]{1,0:T(8,128)(2,1)S(1)}, bf16[64,512]{1,0:T(8,128)(2,1)S(1)}, u32[]{:S(2)}, u32[]{:S(2)}) collective-permute-start(bf16[64,512]{1,0:T(8,128)(2,1)S(1)} %shard_map.40), channel_id=1, source_target_pairs={{0,4},{4,0},{8,12},{12,8},{1,5},{5,1},{9,13},{13,9},{2,6},{6,2},{1... | collective-permute-start | bytes 196616 | tf_op jit(solution)/shard_map/ppermute | solution.py:224
  20.7 0.0 collective-permute-done.7.refs_7_
  20.7 0.0 collective-permute-done.4.refs_4_.refs_2_
  20.7 0.4 %collective-permute-done.5.refs_5_ = bf16[64,512]{1,0:T(8,128)(2,1)S(1)} collective-permute-done((bf16[64,512]{1,0:T(8,128)(2,1)S(1)}, bf16[64,512]{1,0:T(8,128)(2,1)S(1)}, u32[]{:S(2)}, u32[]{:S(2)}) %collective-permute-start.5) | collective-permute-done | bytes 65568 | tf_op jit(solution)/shard_map/ppermute | solution.py:227
  21.2 1.5 %collective-permute-done.6.refs_6_ = bf16[64,512]{1,0:T(8,128)(2,1)S(1)} collective-permute-done((bf16[64,512]{1,0:T(8,128)(2,1)S(1)}, bf16[64,512]{1,0:T(8,128)(2,1)S(1)}, u32[]{:S(2)}, u32[]{:S(2)}) %collective-permute-start.6) | collective-permute-done | bytes 65568 | tf_op jit(solution)/shard_map/ppermute | solution.py:227
  22.7 0.5 %shard_map.43 = (f32[64,512]{1,0:T(8,128)S(1)}, bf16[64,512]{1,0:T(8,128)(2,1)S(1)}, bf16[64,512]{1,0:T(8,128)(2,1)S(1)}, bf16[64,512]{1,0:T(8,128)(2,1)S(1)}) custom-call(bf16[144,512]{1,0:T(8,128)(2,1)S(1)} %shard_map.38.refs_0_, bf16[64,512]{1,0:T(8,128)(2,1)S(1)} %shard_map.41.refs_1_, bf16[64,512]{1,0:T(8,128)(2,1)S(1)} %shard_map.42.refs_2_, ...), custom_call_target="tpu_custom_call" | custom-call | tf_op jit(solution)/shard_map/pallas_call | solution.py:22
  23.2 0.0 collective-permute-done.2.refs_2_
  23.2 1.6 %collective-permute-start.8 = (bf16[192,512]{1,0:T(8,128)(2,1)S(1)}, bf16[192,512]{1,0:T(8,128)(2,1)S(1)}, u32[]{:S(2)}, u32[]{:S(2)}) collective-permute-start(bf16[192,512]{1,0:T(8,128)(2,1)S(1)} %shard_map.44.refs_1_), channel_id=1, source_target_pairs={{0,2},{2,0},{1,3},{3,1},{4,6},{6,4},{5,7},{7,5},{8,10},{10,8},{9,1... | collective-permute-start | bytes 589832 | tf_op jit(solution)/shard_map/ppermute | solution.py:227
  24.8 0.9 %collective-permute-start.9 = (bf16[64,512]{1,0:T(8,128)(2,1)S(1)}, bf16[64,512]{1,0:T(8,128)(2,1)S(1)}, u32[]{:S(2)}, u32[]{:S(2)}) collective-permute-start(bf16[64,512]{1,0:T(8,128)(2,1)S(1)} %get-tuple-element.27), channel_id=1, source_target_pairs={{0,4},{4,0},{8,12},{12,8},{1,5},{5,1},{9,13},{13,9},{2,6},{6,2},{1... | collective-permute-start | bytes 196616 | tf_op jit(solution)/shard_map/ppermute | solution.py:224
  25.6 1.0 %collective-permute-start.10 = (bf16[64,512]{1,0:T(8,128)(2,1)S(1)}, bf16[64,512]{1,0:T(8,128)(2,1)S(1)}, u32[]{:S(2)}, u32[]{:S(2)}) collective-permute-start(bf16[64,512]{1,0:T(8,128)(2,1)S(1)} %get-tuple-element.28), channel_id=1, source_target_pairs={{0,8},{4,12},{8,0},{12,4},{1,9},{5,13},{9,1},{13,5},{2,10},{6,14},... | collective-permute-start | bytes 196616 | tf_op jit(solution)/shard_map/ppermute | solution.py:224
  26.6 2.5 %collective-permute-start.11 = (bf16[64,512]{1,0:T(8,128)(2,1)S(1)}, bf16[64,512]{1,0:T(8,128)(2,1)S(1)}, u32[]{:S(2)}, u32[]{:S(2)}) collective-permute-start(bf16[64,512]{1,0:T(8,128)(2,1)S(1)} %get-tuple-element.29), channel_id=1, source_target_pairs={{0,12},{4,8},{8,4},{12,0},{1,13},{5,9},{9,5},{13,1},{2,14},{6,10},... | collective-permute-start | bytes 196616 | tf_op jit(solution)/shard_map/ppermute | solution.py:224
  29.2 0.0 collective-permute-done.8.refs_3_
  29.2 0.3 shard_map.45
  29.5 0.0 collective-permute-done.9.refs_2_
  29.5 1.3 %collective-permute-done.10.refs_3_ = bf16[64,512]{1,0:T(8,128)(2,1)S(1)} collective-permute-done((bf16[64,512]{1,0:T(8,128)(2,1)S(1)}, bf16[64,512]{1,0:T(8,128)(2,1)S(1)}, u32[]{:S(2)}, u32[]{:S(2)}) %collective-permute-start.10) | collective-permute-done | bytes 65568 | tf_op jit(solution)/shard_map/ppermute | solution.py:224
  30.8 2.0 %collective-permute-done.11.refs_4_ = bf16[64,512]{1,0:T(8,128)(2,1)S(1)} collective-permute-done((bf16[64,512]{1,0:T(8,128)(2,1)S(1)}, bf16[64,512]{1,0:T(8,128)(2,1)S(1)}, u32[]{:S(2)}, u32[]{:S(2)}) %collective-permute-start.11) | collective-permute-done | bytes 65568 | tf_op jit(solution)/shard_map/ppermute | solution.py:224
  32.8 0.1 shard_map.46
  32.9 0.1 collective-permute-start.12
  33.0 1.6 %collective-permute-done.12.refs_1_ = f32[144,512]{1,0:T(8,128)S(1)} collective-permute-done((f32[144,512]{1,0:T(8,128)S(1)}, f32[144,512]{1,0:T(8,128)S(1)}, u32[]{:S(2)}, u32[]{:S(2)}) %collective-permute-start.12) | collective-permute-done | bytes 294944 | tf_op jit(solution)/shard_map/ppermute | solution.py:230
  34.6 1.1 %shard_map.47 = f32[64,512]{1,0:T(8,128)} custom-call(f32[144,512]{1,0:T(8,128)S(1)} %get-tuple-element.30.refs_0_, f32[144,512]{1,0:T(8,128)S(1)} %collective-permute-done.12.refs_1_, f32[8,512]{1,0:T(8,128)S(1)} %get-tuple-element.31.refs_2_, bf16[64,512]{1,0:T(8,128)(2,1)S(1)} %copy-done.3, bf16[1,64]{1,0:T(2,128)(2,1)S(1)} %bitcast.2, ...), custom_call_target="tpu_custom_call" | custom-call | tf_op jit(solution)/shard_map/pallas_call | solution.py:22
  (6 shorter events, 0.1 us)
Async XLA Ops:
  0.0 0.9 %copy-start = (bf16[64,2048]{1,0:T(8,128)(2,1)S(1)}, bf16[64,2048]{1,0:T(8,128)(2,1)}, u32[]{:S(2)}) copy-start(bf16[64,2048]{1,0:T(8,128)(2,1)} %refs_0_.4) | copy-start | bytes 786436
  1.0 6.6 %copy-start.1 = (bf16[64,2048]{1,0:T(8,128)(2,1)S(1)}, bf16[64,2048]{1,0:T(8,128)(2,1)}, u32[]{:S(2)}) copy-start(bf16[64,2048]{1,0:T(8,128)(2,1)} %refs_0_.4) | copy-start | bytes 786436
  1.0 0.9 %copy-start.2 = (bf16[64,512]{1,0:T(8,128)(2,1)S(1)}, bf16[64,512]{1,0:T(8,128)(2,1)}, u32[]{:S(2)}) copy-start(bf16[64,512]{1,0:T(8,128)(2,1)} %refs_3_.1) | copy-start | bytes 196612
  1.9 5.7 %copy-start.3 = (bf16[64,512]{1,0:T(8,128)(2,1)S(1)}, bf16[64,512]{1,0:T(8,128)(2,1)}, u32[]{:S(2)}) copy-start(bf16[64,512]{1,0:T(8,128)(2,1)} %refs_3_.1) | copy-start | bytes 196612
  1.9 14.8 %collective-permute-start = (bf16[128,512]{1,0:T(8,128)(2,1)S(1)}, bf16[128,512]{1,0:T(8,128)(2,1)S(1)}, u32[]{:S(2)}, u32[]{:S(2)}) collective-permute-start(bf16[128,512]{1,0:T(8,128)(2,1)S(1)} %get-tuple-element.22), channel_id=1, source_target_pairs={{0,4},{4,0},{8,12},{12,8},{1,5},{5,1},{9,13},{13,9},{2,6},{6,2},{1... | collective-permute-start | bytes 393224 | tf_op jit(solution)/shard_map/ppermute | solution.py:224
  5.0 13.3 %collective-permute-start.1 = (bf16[128,512]{1,0:T(8,128)(2,1)S(1)}, bf16[128,512]{1,0:T(8,128)(2,1)S(1)}, u32[]{:S(2)}, u32[]{:S(2)}) collective-permute-start(bf16[128,512]{1,0:T(8,128)(2,1)S(1)} %get-tuple-element.23), channel_id=1, source_target_pairs={{0,8},{4,12},{8,0},{12,4},{1,9},{5,13},{9,1},{13,5},{2,10},{6,14},... | collective-permute-start | bytes 393224 | tf_op jit(solution)/shard_map/ppermute | solution.py:224
  7.6 0.7 %copy-start.4 = (bf16[64]{0:T(256)(128)(2,1)S(1)}, bf16[64]{0:T(256)(128)(2,1)}, u32[]{:S(2)}) copy-start(bf16[64]{0:T(256)(128)(2,1)} %param.5) | copy-start | bytes 388
  8.5 12.3 %collective-permute-start.4 = (bf16[144,512]{1,0:T(8,128)(2,1)S(1)}, bf16[144,512]{1,0:T(8,128)(2,1)S(1)}, u32[]{:S(2)}, u32[]{:S(2)}) collective-permute-start(bf16[144,512]{1,0:T(8,128)(2,1)S(1)} %shard_map.38.refs_0_), channel_id=1, source_target_pairs={{0,2},{2,0},{1,3},{3,1},{4,6},{6,4},{5,7},{7,5},{8,10},{10,8},{9,1... | collective-permute-start | bytes 442376 | tf_op jit(solution)/shard_map/ppermute | solution.py:227
  10.0 6.2 %collective-permute-start.3 = (bf16[64,512]{1,0:T(8,128)(2,1)S(1)}, bf16[64,512]{1,0:T(8,128)(2,1)S(1)}, u32[]{:S(2)}, u32[]{:S(2)}) collective-permute-start(bf16[64,512]{1,0:T(8,128)(2,1)S(1)} %get-tuple-element.24), channel_id=1, source_target_pairs={{0,12},{4,8},{8,4},{12,0},{1,13},{5,9},{9,5},{13,1},{2,14},{6,10},... | collective-permute-start | bytes 196616 | tf_op jit(solution)/shard_map/ppermute | solution.py:224
  16.2 4.5 %collective-permute-start.7 = (bf16[64,512]{1,0:T(8,128)(2,1)S(1)}, bf16[64,512]{1,0:T(8,128)(2,1)S(1)}, u32[]{:S(2)}, u32[]{:S(2)}) collective-permute-start(bf16[64,512]{1,0:T(8,128)(2,1)S(1)} %collective-permute-done.3.refs_3_), channel_id=1, source_target_pairs={{0,2},{2,0},{1,3},{3,1},{4,6},{6,4},{5,7},{7,5},{8,10},{10,8},{9,1... | collective-permute-start | bytes 196616 | tf_op jit(solution)/shard_map/ppermute | solution.py:227
  16.6 4.5 %collective-permute-start.5 = (bf16[64,512]{1,0:T(8,128)(2,1)S(1)}, bf16[64,512]{1,0:T(8,128)(2,1)S(1)}, u32[]{:S(2)}, u32[]{:S(2)}) collective-permute-start(bf16[64,512]{1,0:T(8,128)(2,1)S(1)} %shard_map.41.refs_1_), channel_id=1, source_target_pairs={{0,2},{2,0},{1,3},{3,1},{4,6},{6,4},{5,7},{7,5},{8,10},{10,8},{9,1... | collective-permute-start | bytes 196616 | tf_op jit(solution)/shard_map/ppermute | solution.py:227
  18.3 4.3 %collective-permute-start.6 = (bf16[64,512]{1,0:T(8,128)(2,1)S(1)}, bf16[64,512]{1,0:T(8,128)(2,1)S(1)}, u32[]{:S(2)}, u32[]{:S(2)}) collective-permute-start(bf16[64,512]{1,0:T(8,128)(2,1)S(1)} %shard_map.42.refs_2_), channel_id=1, source_target_pairs={{0,2},{2,0},{1,3},{3,1},{4,6},{6,4},{5,7},{7,5},{8,10},{10,8},{9,1... | collective-permute-start | bytes 196616 | tf_op jit(solution)/shard_map/ppermute | solution.py:227
  18.8 4.4 %collective-permute-start.2 = (bf16[64,512]{1,0:T(8,128)(2,1)S(1)}, bf16[64,512]{1,0:T(8,128)(2,1)S(1)}, u32[]{:S(2)}, u32[]{:S(2)}) collective-permute-start(bf16[64,512]{1,0:T(8,128)(2,1)S(1)} %shard_map.40), channel_id=1, source_target_pairs={{0,4},{4,0},{8,12},{12,8},{1,5},{5,1},{9,13},{13,9},{2,6},{6,2},{1... | collective-permute-start | bytes 196616 | tf_op jit(solution)/shard_map/ppermute | solution.py:224
  23.2 5.9 %collective-permute-start.8 = (bf16[192,512]{1,0:T(8,128)(2,1)S(1)}, bf16[192,512]{1,0:T(8,128)(2,1)S(1)}, u32[]{:S(2)}, u32[]{:S(2)}) collective-permute-start(bf16[192,512]{1,0:T(8,128)(2,1)S(1)} %shard_map.44.refs_1_), channel_id=1, source_target_pairs={{0,2},{2,0},{1,3},{3,1},{4,6},{6,4},{5,7},{7,5},{8,10},{10,8},{9,1... | collective-permute-start | bytes 589832 | tf_op jit(solution)/shard_map/ppermute | solution.py:227
  24.8 4.7 %collective-permute-start.9 = (bf16[64,512]{1,0:T(8,128)(2,1)S(1)}, bf16[64,512]{1,0:T(8,128)(2,1)S(1)}, u32[]{:S(2)}, u32[]{:S(2)}) collective-permute-start(bf16[64,512]{1,0:T(8,128)(2,1)S(1)} %get-tuple-element.27), channel_id=1, source_target_pairs={{0,4},{4,0},{8,12},{12,8},{1,5},{5,1},{9,13},{13,9},{2,6},{6,2},{1... | collective-permute-start | bytes 196616 | tf_op jit(solution)/shard_map/ppermute | solution.py:224
  25.6 5.2 %collective-permute-start.10 = (bf16[64,512]{1,0:T(8,128)(2,1)S(1)}, bf16[64,512]{1,0:T(8,128)(2,1)S(1)}, u32[]{:S(2)}, u32[]{:S(2)}) collective-permute-start(bf16[64,512]{1,0:T(8,128)(2,1)S(1)} %get-tuple-element.28), channel_id=1, source_target_pairs={{0,8},{4,12},{8,0},{12,4},{1,9},{5,13},{9,1},{13,5},{2,10},{6,14},... | collective-permute-start | bytes 196616 | tf_op jit(solution)/shard_map/ppermute | solution.py:224
  26.6 6.2 %collective-permute-start.11 = (bf16[64,512]{1,0:T(8,128)(2,1)S(1)}, bf16[64,512]{1,0:T(8,128)(2,1)S(1)}, u32[]{:S(2)}, u32[]{:S(2)}) collective-permute-start(bf16[64,512]{1,0:T(8,128)(2,1)S(1)} %get-tuple-element.29), channel_id=1, source_target_pairs={{0,12},{4,8},{8,4},{12,0},{1,13},{5,9},{9,5},{13,1},{2,14},{6,10},... | collective-permute-start | bytes 196616 | tf_op jit(solution)/shard_map/ppermute | solution.py:224
  32.9 1.7 %collective-permute-start.12 = (f32[144,512]{1,0:T(8,128)S(1)}, f32[144,512]{1,0:T(8,128)S(1)}, u32[]{:S(2)}, u32[]{:S(2)}) collective-permute-start(f32[144,512]{1,0:T(8,128)S(1)} %get-tuple-element.30.refs_0_), channel_id=1, source_target_pairs={{0,1},{1,0},{2,3},{3,2},{4,5},{5,4},{6,7},{7,6},{8,9},{9,8},{10,11... | collective-permute-start | bytes 884744 | tf_op jit(solution)/shard_map/ppermute | solution.py:230

commit v7 on v6

--- a/solution.py
+++ b/solution.py
@@ -12,7 +12,7 @@
 TAIL = 16
 
 
-def call(body, out_shape, operands, space=pltpu.VMEM, scratch=(), after=()):
+def call(body, out_shape, operands, space=pltpu.VMEM, scratch=(), after=(), limit=None):
     outs = out_shape if isinstance(out_shape, (list, tuple)) else [out_shape]
     moved = sum(x.size * x.dtype.itemsize for x in list(operands) + list(outs))
 
@@ -23,10 +23,10 @@
         run,
         out_shape=out_shape,
         in_specs=[pl.BlockSpec(memory_space=space)] * len(operands) + [pl.BlockSpec(memory_space=pl.ANY)] * len(after),
-        out_specs=jax.tree.map(lambda _: pl.BlockSpec(memory_space=pltpu.VMEM), out_shape),
+        out_specs=jax.tree.map(lambda _: pl.BlockSpec(memory_space=space), out_shape),
         scratch_shapes=list(scratch),
         cost_estimate=pl.CostEstimate(flops=0, bytes_accessed=0, transcendentals=0),
-        compiler_params=pltpu.CompilerParams(vmem_limit_bytes=min(56 << 20, (8 << 20) + 3 * moved)),
+        compiler_params=pltpu.CompilerParams(vmem_limit_bytes=limit or min(56 << 20, (8 << 20) + 3 * moved)),
     )(*operands, *after)
 
 
@@ -69,30 +69,39 @@
         held[pl.ds(spot + n * high, high), :] = ref[at : at + high, n * width : (n + 1) * width]
 
 
-def cut_kernel(nrow, teach, *outs):
+def cut_kernel(nrow, riders, teach, stud, *refs):
+    outs, sems = (None, *refs[: nrow - 1]), refs[nrow - 1]
+    rows, half = stud.shape
     part = teach.shape[1] // nrow
+    high = rows * part // half
     z = lax.axis_index("row")
-    for k in range(nrow):
+    copies = []
+    for k in range(1, nrow):
         at = pl.multiple_of((z ^ k) * part, part)
-        outs[k][...] = teach[:, pl.ds(at, part)]
-
-
-def ride_kernel(stud, *refs):
-    rows, count = stud.shape[0], len(refs) // 2
-    for piece, out in zip(refs[:count], refs[count:]):
-        out[:rows, :] = stud[...]
-        wide(out, rows, piece)
-
-
-def own_kernel(teach, stud, scale, cut, out):
+        if k in riders:
+            copies.append((stud, outs[k].at[pl.ds(0, rows), :]))
+            for n in range(half // part):
+                target = outs[k].at[pl.ds(rows, high), pl.ds(n * part, part)]
+                copies.append((teach.at[pl.ds(n * high, high), pl.ds(at, part)], target))
+        else:
+            copies.append((teach.at[:, pl.ds(at, part)], outs[k]))
+    copies = [pltpu.make_async_copy(a, b, sems.at[n]) for n, (a, b) in enumerate(copies)]
+    for c in copies:
+        c.start()
+    for c in copies:
+        c.wait()
+
+
+def own_kernel(nrow, teach, stud, scale, out):
     rows, half = stud.shape
+    part = teach.shape[1] // nrow
     ts = teach[...].astype(F32)
     s = scale[...].astype(F32)
     mass = jnp.sum(jnp.square(column(s)) * jnp.sum(ts * ts, axis=1, keepdims=True), keepdims=True)
     tags = tags_of(jnp.concatenate([s, s], axis=1), mass)
     out[:rows, :] = stud[...]
     out[rows : rows + TAIL, :] = jnp.concatenate([tags] * (half // (2 * rows)), axis=1)
-    wide(out, rows + TAIL, cut[...])
+    wide(out, rows + TAIL, teach[:, pl.ds(pl.multiple_of(lax.axis_index("row") * part, part), part)])
 
 
 def take_kernel(rows, ref, out):
@@ -165,8 +174,8 @@
         out[rows:, at : at + 128] = jnp.broadcast_to(lane_row(squares), (8, 128))
 
 
-def message_kernel(nrow, ncol, raw_gram, *refs):
-    parts, (out, vectors) = refs[:-2], refs[-2:]
+def message_kernel(nrow, ncol, order, raw_gram, *refs):
+    parts, (out, vectors) = [refs[order.index(k)] for k in range(nrow)], refs[-2:]
     rows = parts[0].shape[0]
     sub = rows // 2
     total = parts[0][...].astype(F32)
@@ -239,11 +248,21 @@
     middle, high = nrow // 2, rows * part // half
     order = list(range(middle, nrow)) + list(range(middle))
     riders = (1, middle)
-    cuts = call(functools.partial(cut_kernel, nrow), [sds((rows, part), BF16)] * nrow, [teacher])
-    ridden = call(ride_kernel, [sds((rows + high, half), BF16)] * 2, [student] + [cuts[k] for k in riders])
-    leaving = dict(enumerate(cuts)) | dict(zip(riders, ridden))
-    came = {k: along_row(leaving[k], k) for k in order if k}
-    own = call(own_kernel, sds((rows + TAIL + high, half), BF16), [teacher, student, scale, cuts[0]])
+    cuts = call(
+        functools.partial(cut_kernel, nrow, riders),
+        [sds((rows + high, half) if k in riders else (rows, part), BF16) for k in range(1, nrow)],
+        [teacher, student],
+        space=pl.ANY,
+        scratch=[pltpu.SemaphoreType.DMA((nrow + 2 * (half // part),))],
+        limit=60 << 20,
+    )
+    came = {k: along_row(cuts[k - 1], k) for k in order if k}
+    own = call(
+        functools.partial(own_kernel, nrow),
+        sds((rows + TAIL + high, half), BF16),
+        [teacher, student, scale],
+        after=[came[nrow - 1]],
+    )
     columns = {0: with_columns(own)}
     for k in range(1, nrow):
         piece = came[k]
@@ -278,9 +297,9 @@
         scratch=[] if small else [pltpu.VMEM((batch, half), BF16)],
     )
     message, vectors = call(
-        functools.partial(message_kernel, nrow, ncol),
+        functools.partial(message_kernel, nrow, ncol, order),
         [sds((2 * rows + 16, batch), F32), sds((8, batch), F32)],
-        [raw_gram] + [returned[k] for k in range(nrow)],
+        [raw_gram] + [returned[k] for k in order],
     )
     return call(
         functools.partial(final_kernel, nrow, ncol, None if small else raw_keys),

time: 35.8 us -> 42.5 us (1.19)
  Pallas kernels: 2.4 us -> 13.4 us
  starting transfers between devices: 18 us -> 15.1 us
  local copies, waits for them, and re-layouts: 2.48 us -> 0.01 us
  waiting for transfers between devices: 12.8 us -> 13.7 us
    pallas_call x11 -> x10, Pallas kernels: 2.4 us -> 13.4 us  [call(): pl.pallas_call(run, out_shape=out_shape, in_specs=[pl.BlockSpec(memory_sp...]
    ppermute x7, starting transfers between devices: 12.2 us -> 9.25 us  [along_row(): return lax.ppermute(x, 'row', [(i, i ^ k) for i in range(nrow)])]
    ppermute x5, waiting for transfers between devices: 1.92 us -> 4.4 us  [along_col(): return lax.ppermute(x, 'col', [(i, (i - c) % ncol) for i in range(ncol)])]
    unnamed x10 -> x6, local copies, waits for them, and re-layouts: 2.48 us -> 0.01 us
    ppermute x7, waiting for transfers between devices: 9.27 us -> 7.75 us  [along_row(): return lax.ppermute(x, 'row', [(i, i ^ k) for i in range(nrow)])]
  transfers between devices with their start and end apart: 13 -> 13, of which waited for: 6 -> 10; matrix products, arithmetic and copies ran while one was open for 0% -> 0% of each run, Pallas kernels for 3% -> 3%
where the time goes in v7:
time: 42.5 us; the launch traced here: 42.4 us
  starting transfers between devices  15.1 us (36%)
  waiting for transfers between devices  13.7 us (32%)
  Pallas kernels  13.4 us (32%)
    pallas_call x10, Pallas kernels, call(): pl.pallas_call(run, out_shape=out_shape, in_specs=[pl.BlockSpec(memory_sp...  13.4 us
    ppermute x7, starting transfers between devices, along_row(): return lax.ppermute(x, 'row', [(i, i ^ k) for i in range(nrow)])  9.25 us
    ppermute x7, waiting for transfers between devices, along_row(): return lax.ppermute(x, 'row', [(i, i ^ k) for i in range(nrow)])  7.75 us
    ppermute x5, starting transfers between devices, along_col(): return lax.ppermute(x, 'col', [(i, (i - c) % ncol) for i in range(ncol)])  5.8 us
    ppermute x5, waiting for transfers between devices, along_col(): return lax.ppermute(x, 'col', [(i, (i - c) % ncol) for i in range(ncol)])  4.4 us
    ppermute x1, waiting for transfers between devices, other_core(): return lax.ppermute(x, 'sub', [(0, 1), (1, 0)])  1.57 us
  transfers between devices with their start and end apart: 13, of which 10 were waited for; matrix products, arithmetic and copies ran while one was open for 0% of the time, Pallas kernels for 3%

profile of v7, /device:TPU:0, one launch (start us, length us, event | category | flops | bytes accessed | tf_op | source)
XLA Modules:
  0.0 42.4 jit_solution(14236726709245560021)
XLA Ops:
  0.0 0.0 copy-start.1
  0.0 0.0 copy-start
  0.0 11.1 %shard_map.37 = (bf16[128,512]{1,0:T(8,128)(2,1)}, bf16[128,512]{1,0:T(8,128)(2,1)}, bf16[64,512]{1,0:T(8,128)(2,1)}) custom-call(bf16[64,2048]{1,0:T(8,128)(2,1)} %refs_0_.3, bf16[64,512]{1,0:T(8,128)(2,1)} %refs_3_.1), custom_call_target="tpu_custom_call" | custom-call | tf_op jit(solution)/shard_map/pallas_call | solution.py:22
  11.1 5.1 %collective-permute-start = (bf16[64,512]{1,0:T(8,128)(2,1)}, bf16[64,512]{1,0:T(8,128)(2,1)S(1)}, u32[]{:S(2)}, u32[]{:S(2)}) collective-permute-start(bf16[64,512]{1,0:T(8,128)(2,1)} %get-tuple-element.16), channel_id=1, source_target_pairs={{0,12},{4,8},{8,4},{12,0},{1,13},{5,9},{9,5},{13,1},{2,14},{6,10},... | collective-permute-start | bytes 196616 | tf_op jit(solution)/shard_map/ppermute | solution.py:233
  16.2 0.0 collective-permute-start.1
  16.2 0.0 copy-start.2
  16.2 0.6 %collective-permute-start.2 = (bf16[128,512]{1,0:T(8,128)(2,1)}, bf16[128,512]{1,0:T(8,128)(2,1)S(1)}, u32[]{:S(2)}, u32[]{:S(2)}) collective-permute-start(bf16[128,512]{1,0:T(8,128)(2,1)} %get-tuple-element.18), channel_id=1, source_target_pairs={{0,8},{4,12},{8,0},{12,4},{1,9},{5,13},{9,1},{13,5},{2,10},{6,14},... | collective-permute-start | bytes 393224 | tf_op jit(solution)/shard_map/ppermute | solution.py:233
  16.9 2.5 %collective-permute-done.refs_3_ = bf16[64,512]{1,0:T(8,128)(2,1)S(1)} collective-permute-done((bf16[64,512]{1,0:T(8,128)(2,1)}, bf16[64,512]{1,0:T(8,128)(2,1)S(1)}, u32[]{:S(2)}, u32[]{:S(2)}) %collective-permute-start) | collective-permute-done | bytes 65568 | tf_op jit(solution)/shard_map/ppermute | solution.py:233
  19.3 0.0 copy-done.1
  19.3 0.0 copy-done
  19.3 0.0 copy-done.2
  19.3 0.3 shard_map.38.refs_0_
  19.6 1.9 %collective-permute-start.4 = (bf16[144,512]{1,0:T(8,128)(2,1)S(1)}, bf16[144,512]{1,0:T(8,128)(2,1)S(1)}, u32[]{:S(2)}, u32[]{:S(2)}) collective-permute-start(bf16[144,512]{1,0:T(8,128)(2,1)S(1)} %shard_map.38.refs_0_), channel_id=1, source_target_pairs={{0,2},{2,0},{1,3},{3,1},{4,6},{6,4},{5,7},{7,5},{8,10},{10,8},{9,1... | collective-permute-start | bytes 442376 | tf_op jit(solution)/shard_map/ppermute | solution.py:236
  21.5 0.2 collective-permute-start.7
  21.7 2.0 %collective-permute-done.1.refs_0_ = bf16[128,512]{1,0:T(8,128)(2,1)S(1)} collective-permute-done((bf16[128,512]{1,0:T(8,128)(2,1)}, bf16[128,512]{1,0:T(8,128)(2,1)S(1)}, u32[]{:S(2)}, u32[]{:S(2)}) %collective-permute-start.1) | collective-permute-done | bytes 131104 | tf_op jit(solution)/shard_map/ppermute | solution.py:233
  23.7 1.6 %collective-permute-start.5 = (bf16[64,512]{1,0:T(8,128)(2,1)S(1)}, bf16[64,512]{1,0:T(8,128)(2,1)S(1)}, u32[]{:S(2)}, u32[]{:S(2)}) collective-permute-start(bf16[64,512]{1,0:T(8,128)(2,1)S(1)} %shard_map.40.refs_1_), channel_id=1, source_target_pairs={{0,2},{2,0},{1,3},{3,1},{4,6},{6,4},{5,7},{7,5},{8,10},{10,8},{9,1... | collective-permute-start | bytes 196616 | tf_op jit(solution)/shard_map/ppermute | solution.py:236
  25.2 0.0 collective-permute-done.2.refs_0_.refs_1_
  25.2 1.5 %collective-permute-start.6 = (bf16[64,512]{1,0:T(8,128)(2,1)S(1)}, bf16[64,512]{1,0:T(8,128)(2,1)S(1)}, u32[]{:S(2)}, u32[]{:S(2)}) collective-permute-start(bf16[64,512]{1,0:T(8,128)(2,1)S(1)} %shard_map.41.refs_2_), channel_id=1, source_target_pairs={{0,2},{2,0},{1,3},{3,1},{4,6},{6,4},{5,7},{7,5},{8,10},{10,8},{9,1... | collective-permute-start | bytes 196616 | tf_op jit(solution)/shard_map/ppermute | solution.py:236
  26.7 0.0 collective-permute-start.3
  26.7 0.0 collective-permute-done.7.refs_7_
  26.7 1.8 %collective-permute-done.5.refs_5_ = bf16[64,512]{1,0:T(8,128)(2,1)S(1)} collective-permute-done((bf16[64,512]{1,0:T(8,128)(2,1)S(1)}, bf16[64,512]{1,0:T(8,128)(2,1)S(1)}, u32[]{:S(2)}, u32[]{:S(2)}) %collective-permute-start.5) | collective-permute-done | bytes 65568 | tf_op jit(solution)/shard_map/ppermute | solution.py:236
  28.5 1.0 %collective-permute-done.6.refs_6_ = bf16[64,512]{1,0:T(8,128)(2,1)S(1)} collective-permute-done((bf16[64,512]{1,0:T(8,128)(2,1)S(1)}, bf16[64,512]{1,0:T(8,128)(2,1)S(1)}, u32[]{:S(2)}, u32[]{:S(2)}) %collective-permute-start.6) | collective-permute-done | bytes 65568 | tf_op jit(solution)/shard_map/ppermute | solution.py:236
  29.6 0.0 collective-permute-done.4.refs_4_.refs_2_
  29.6 0.5 %shard_map.42 = (f32[64,512]{1,0:T(8,128)S(1)}, bf16[64,512]{1,0:T(8,128)(2,1)S(1)}, bf16[64,512]{1,0:T(8,128)(2,1)S(1)}, bf16[64,512]{1,0:T(8,128)(2,1)S(1)}) custom-call(bf16[144,512]{1,0:T(8,128)(2,1)S(1)} %shard_map.38.refs_0_, bf16[64,512]{1,0:T(8,128)(2,1)S(1)} %shard_map.40.refs_1_, bf16[64,512]{1,0:T(8,128)(2,1)S(1)} %shard_map.41.refs_2_, ...), custom_call_target="tpu_custom_call" | custom-call | tf_op jit(solution)/shard_map/pallas_call | solution.py:22
  30.1 0.9 %collective-permute-done.3.refs_2_ = bf16[64,512]{1,0:T(8,128)(2,1)S(1)} collective-permute-done((bf16[64,512]{1,0:T(8,128)(2,1)S(1)}, bf16[64,512]{1,0:T(8,128)(2,1)S(1)}, u32[]{:S(2)}, u32[]{:S(2)}) %collective-permute-start.3) | collective-permute-done | bytes 65568 | tf_op jit(solution)/shard_map/ppermute | solution.py:233
  31.0 0.7 %collective-permute-start.8 = (bf16[192,512]{1,0:T(8,128)(2,1)S(1)}, bf16[192,512]{1,0:T(8,128)(2,1)S(1)}, u32[]{:S(2)}, u32[]{:S(2)}) collective-permute-start(bf16[192,512]{1,0:T(8,128)(2,1)S(1)} %shard_map.43.refs_1_), channel_id=1, source_target_pairs={{0,2},{2,0},{1,3},{3,1},{4,6},{6,4},{5,7},{7,5},{8,10},{10,8},{9,1... | collective-permute-start | bytes 589832 | tf_op jit(solution)/shard_map/ppermute | solution.py:236
  31.7 1.5 %collective-permute-start.9 = (bf16[64,512]{1,0:T(8,128)(2,1)S(1)}, bf16[64,512]{1,0:T(8,128)(2,1)S(1)}, u32[]{:S(2)}, u32[]{:S(2)}) collective-permute-start(bf16[64,512]{1,0:T(8,128)(2,1)S(1)} %get-tuple-element.21), channel_id=1, source_target_pairs={{0,8},{4,12},{8,0},{12,4},{1,9},{5,13},{9,1},{13,5},{2,10},{6,14},... | collective-permute-start | bytes 196616 | tf_op jit(solution)/shard_map/ppermute | solution.py:233
  33.2 1.3 %collective-permute-start.10 = (bf16[64,512]{1,0:T(8,128)(2,1)S(1)}, bf16[64,512]{1,0:T(8,128)(2,1)S(1)}, u32[]{:S(2)}, u32[]{:S(2)}) collective-permute-start(bf16[64,512]{1,0:T(8,128)(2,1)S(1)} %get-tuple-element.22), channel_id=1, source_target_pairs={{0,12},{4,8},{8,4},{12,0},{1,13},{5,9},{9,5},{13,1},{2,14},{6,10},... | collective-permute-start | bytes 196616 | tf_op jit(solution)/shard_map/ppermute | solution.py:233
  34.5 0.7 %collective-permute-start.11 = (bf16[64,512]{1,0:T(8,128)(2,1)S(1)}, bf16[64,512]{1,0:T(8,128)(2,1)S(1)}, u32[]{:S(2)}, u32[]{:S(2)}) collective-permute-start(bf16[64,512]{1,0:T(8,128)(2,1)S(1)} %get-tuple-element.23), channel_id=1, source_target_pairs={{0,4},{4,0},{8,12},{12,8},{1,5},{5,1},{9,13},{13,9},{2,6},{6,2},{1... | collective-permute-start | bytes 196616 | tf_op jit(solution)/shard_map/ppermute | solution.py:233
  35.2 1.5 %collective-permute-done.8.refs_3_ = bf16[192,512]{1,0:T(8,128)(2,1)S(1)} collective-permute-done((bf16[192,512]{1,0:T(8,128)(2,1)S(1)}, bf16[192,512]{1,0:T(8,128)(2,1)S(1)}, u32[]{:S(2)}, u32[]{:S(2)}) %collective-permute-start.8) | collective-permute-done | bytes 196640 | tf_op jit(solution)/shard_map/ppermute | solution.py:236
  36.7 0.3 shard_map.44
  37.0 0.5 %collective-permute-done.9.refs_1_ = bf16[64,512]{1,0:T(8,128)(2,1)S(1)} collective-permute-done((bf16[64,512]{1,0:T(8,128)(2,1)S(1)}, bf16[64,512]{1,0:T(8,128)(2,1)S(1)}, u32[]{:S(2)}, u32[]{:S(2)}) %collective-permute-start.9) | collective-permute-done | bytes 65568 | tf_op jit(solution)/shard_map/ppermute | solution.py:233
  37.5 1.9 %collective-permute-done.10.refs_2_ = bf16[64,512]{1,0:T(8,128)(2,1)S(1)} collective-permute-done((bf16[64,512]{1,0:T(8,128)(2,1)S(1)}, bf16[64,512]{1,0:T(8,128)(2,1)S(1)}, u32[]{:S(2)}, u32[]{:S(2)}) %collective-permute-start.10) | collective-permute-done | bytes 65568 | tf_op jit(solution)/shard_map/ppermute | solution.py:233
  39.4 0.1 collective-permute-done.11.refs_4_
  39.5 0.1 shard_map.45
  39.6 0.1 collective-permute-start.12
  39.7 1.6 %collective-permute-done.12.refs_1_ = f32[144,512]{1,0:T(8,128)S(1)} collective-permute-done((f32[144,512]{1,0:T(8,128)S(1)}, f32[144,512]{1,0:T(8,128)S(1)}, u32[]{:S(2)}, u32[]{:S(2)}) %collective-permute-start.12) | collective-permute-done | bytes 294944 | tf_op jit(solution)/shard_map/ppermute | solution.py:239
  41.2 1.1 %shard_map.46 = f32[64,512]{1,0:T(8,128)} custom-call(f32[144,512]{1,0:T(8,128)S(1)} %get-tuple-element.24.refs_0_, f32[144,512]{1,0:T(8,128)S(1)} %collective-permute-done.12.refs_1_, f32[8,512]{1,0:T(8,128)S(1)} %get-tuple-element.25.refs_2_, bf16[64,512]{1,0:T(8,128)(2,1)S(1)} %copy-done.1, bf16[1,64]{1,0:T(2,128)(2,1)S(1)} %bitcast.2, ...), custom_call_target="tpu_custom_call" | custom-call | tf_op jit(solution)/shard_map/pallas_call | solution.py:22
  (4 shorter events, 0.0 us)
Async XLA Ops:
  0.0 19.3 %copy-start.1 = (bf16[64,512]{1,0:T(8,128)(2,1)S(1)}, bf16[64,512]{1,0:T(8,128)(2,1)}, u32[]{:S(2)}) copy-start(bf16[64,512]{1,0:T(8,128)(2,1)} %refs_3_.1) | copy-start | bytes 196612
  0.0 19.3 %copy-start = (bf16[64,2048]{1,0:T(8,128)(2,1)S(1)}, bf16[64,2048]{1,0:T(8,128)(2,1)}, u32[]{:S(2)}) copy-start(bf16[64,2048]{1,0:T(8,128)(2,1)} %refs_0_.3) | copy-start | bytes 786436
  11.1 8.2 %collective-permute-start = (bf16[64,512]{1,0:T(8,128)(2,1)}, bf16[64,512]{1,0:T(8,128)(2,1)S(1)}, u32[]{:S(2)}, u32[]{:S(2)}) collective-permute-start(bf16[64,512]{1,0:T(8,128)(2,1)} %get-tuple-element.16), channel_id=1, source_target_pairs={{0,12},{4,8},{8,4},{12,0},{1,13},{5,9},{9,5},{13,1},{2,14},{6,10},... | collective-permute-start | bytes 196616 | tf_op jit(solution)/shard_map/ppermute | solution.py:233
  16.2 7.5 %collective-permute-start.1 = (bf16[128,512]{1,0:T(8,128)(2,1)}, bf16[128,512]{1,0:T(8,128)(2,1)S(1)}, u32[]{:S(2)}, u32[]{:S(2)}) collective-permute-start(bf16[128,512]{1,0:T(8,128)(2,1)} %get-tuple-element.17), channel_id=1, source_target_pairs={{0,4},{4,0},{8,12},{12,8},{1,5},{5,1},{9,13},{13,9},{2,6},{6,2},{1... | collective-permute-start | bytes 393224 | tf_op jit(solution)/shard_map/ppermute | solution.py:233
  16.2 3.1 %copy-start.2 = (bf16[64]{0:T(256)(128)(2,1)S(1)}, bf16[64]{0:T(256)(128)(2,1)}, u32[]{:S(2)}) copy-start(bf16[64]{0:T(256)(128)(2,1)} %param.5) | copy-start | bytes 388
  16.2 9.0 %collective-permute-start.2 = (bf16[128,512]{1,0:T(8,128)(2,1)}, bf16[128,512]{1,0:T(8,128)(2,1)S(1)}, u32[]{:S(2)}, u32[]{:S(2)}) collective-permute-start(bf16[128,512]{1,0:T(8,128)(2,1)} %get-tuple-element.18), channel_id=1, source_target_pairs={{0,8},{4,12},{8,0},{12,4},{1,9},{5,13},{9,1},{13,5},{2,10},{6,14},... | collective-permute-start | bytes 393224 | tf_op jit(solution)/shard_map/ppermute | solution.py:233
  19.6 10.0 %collective-permute-start.4 = (bf16[144,512]{1,0:T(8,128)(2,1)S(1)}, bf16[144,512]{1,0:T(8,128)(2,1)S(1)}, u32[]{:S(2)}, u32[]{:S(2)}) collective-permute-start(bf16[144,512]{1,0:T(8,128)(2,1)S(1)} %shard_map.38.refs_0_), channel_id=1, source_target_pairs={{0,2},{2,0},{1,3},{3,1},{4,6},{6,4},{5,7},{7,5},{8,10},{10,8},{9,1... | collective-permute-start | bytes 442376 | tf_op jit(solution)/shard_map/ppermute | solution.py:236
  21.5 5.2 %collective-permute-start.7 = (bf16[64,512]{1,0:T(8,128)(2,1)S(1)}, bf16[64,512]{1,0:T(8,128)(2,1)S(1)}, u32[]{:S(2)}, u32[]{:S(2)}) collective-permute-start(bf16[64,512]{1,0:T(8,128)(2,1)S(1)} %collective-permute-done.refs_3_), channel_id=1, source_target_pairs={{0,2},{2,0},{1,3},{3,1},{4,6},{6,4},{5,7},{7,5},{8,10},{10,8},{9,1... | collective-permute-start | bytes 196616 | tf_op jit(solution)/shard_map/ppermute | solution.py:236
  23.7 4.9 %collective-permute-start.5 = (bf16[64,512]{1,0:T(8,128)(2,1)S(1)}, bf16[64,512]{1,0:T(8,128)(2,1)S(1)}, u32[]{:S(2)}, u32[]{:S(2)}) collective-permute-start(bf16[64,512]{1,0:T(8,128)(2,1)S(1)} %shard_map.40.refs_1_), channel_id=1, source_target_pairs={{0,2},{2,0},{1,3},{3,1},{4,6},{6,4},{5,7},{7,5},{8,10},{10,8},{9,1... | collective-permute-start | bytes 196616 | tf_op jit(solution)/shard_map/ppermute | solution.py:236
  25.2 4.3 %collective-permute-start.6 = (bf16[64,512]{1,0:T(8,128)(2,1)S(1)}, bf16[64,512]{1,0:T(8,128)(2,1)S(1)}, u32[]{:S(2)}, u32[]{:S(2)}) collective-permute-start(bf16[64,512]{1,0:T(8,128)(2,1)S(1)} %shard_map.41.refs_2_), channel_id=1, source_target_pairs={{0,2},{2,0},{1,3},{3,1},{4,6},{6,4},{5,7},{7,5},{8,10},{10,8},{9,1... | collective-permute-start | bytes 196616 | tf_op jit(solution)/shard_map/ppermute | solution.py:236
  26.7 4.3 %collective-permute-start.3 = (bf16[64,512]{1,0:T(8,128)(2,1)S(1)}, bf16[64,512]{1,0:T(8,128)(2,1)S(1)}, u32[]{:S(2)}, u32[]{:S(2)}) collective-permute-start(bf16[64,512]{1,0:T(8,128)(2,1)S(1)} %shard_map.39), channel_id=1, source_target_pairs={{0,4},{4,0},{8,12},{12,8},{1,5},{5,1},{9,13},{13,9},{2,6},{6,2},{1... | collective-permute-start | bytes 196616 | tf_op jit(solution)/shard_map/ppermute | solution.py:233
  31.0 5.7 %collective-permute-start.8 = (bf16[192,512]{1,0:T(8,128)(2,1)S(1)}, bf16[192,512]{1,0:T(8,128)(2,1)S(1)}, u32[]{:S(2)}, u32[]{:S(2)}) collective-permute-start(bf16[192,512]{1,0:T(8,128)(2,1)S(1)} %shard_map.43.refs_1_), channel_id=1, source_target_pairs={{0,2},{2,0},{1,3},{3,1},{4,6},{6,4},{5,7},{7,5},{8,10},{10,8},{9,1... | collective-permute-start | bytes 589832 | tf_op jit(solution)/shard_map/ppermute | solution.py:236
  31.7 5.8 %collective-permute-start.9 = (bf16[64,512]{1,0:T(8,128)(2,1)S(1)}, bf16[64,512]{1,0:T(8,128)(2,1)S(1)}, u32[]{:S(2)}, u32[]{:S(2)}) collective-permute-start(bf16[64,512]{1,0:T(8,128)(2,1)S(1)} %get-tuple-element.21), channel_id=1, source_target_pairs={{0,8},{4,12},{8,0},{12,4},{1,9},{5,13},{9,1},{13,5},{2,10},{6,14},... | collective-permute-start | bytes 196616 | tf_op jit(solution)/shard_map/ppermute | solution.py:233
  33.2 6.2 %collective-permute-start.10 = (bf16[64,512]{1,0:T(8,128)(2,1)S(1)}, bf16[64,512]{1,0:T(8,128)(2,1)S(1)}, u32[]{:S(2)}, u32[]{:S(2)}) collective-permute-start(bf16[64,512]{1,0:T(8,128)(2,1)S(1)} %get-tuple-element.22), channel_id=1, source_target_pairs={{0,12},{4,8},{8,4},{12,0},{1,13},{5,9},{9,5},{13,1},{2,14},{6,10},... | collective-permute-start | bytes 196616 | tf_op jit(solution)/shard_map/ppermute | solution.py:233
  34.5 5.0 %collective-permute-start.11 = (bf16[64,512]{1,0:T(8,128)(2,1)S(1)}, bf16[64,512]{1,0:T(8,128)(2,1)S(1)}, u32[]{:S(2)}, u32[]{:S(2)}) collective-permute-start(bf16[64,512]{1,0:T(8,128)(2,1)S(1)} %get-tuple-element.23), channel_id=1, source_target_pairs={{0,4},{4,0},{8,12},{12,8},{1,5},{5,1},{9,13},{13,9},{2,6},{6,2},{1... | collective-permute-start | bytes 196616 | tf_op jit(solution)/shard_map/ppermute | solution.py:233
  39.6 1.7 %collective-permute-start.12 = (f32[144,512]{1,0:T(8,128)S(1)}, f32[144,512]{1,0:T(8,128)S(1)}, u32[]{:S(2)}, u32[]{:S(2)}) collective-permute-start(f32[144,512]{1,0:T(8,128)S(1)} %get-tuple-element.24.refs_0_), channel_id=1, source_target_pairs={{0,1},{1,0},{2,3},{3,2},{4,5},{5,4},{6,7},{7,6},{8,9},{9,8},{10,11... | collective-permute-start | bytes 884744 | tf_op jit(solution)/shard_map/ppermute | solution.py:239

commit v8 on v6

--- a/solution.py
+++ b/solution.py
@@ -12,7 +12,7 @@
 TAIL = 16
 
 
-def call(body, out_shape, operands, space=pltpu.VMEM, scratch=(), after=()):
+def call(body, out_shape, operands, scratch=(), after=()):
     outs = out_shape if isinstance(out_shape, (list, tuple)) else [out_shape]
     moved = sum(x.size * x.dtype.itemsize for x in list(operands) + list(outs))
 
@@ -22,7 +22,7 @@
     return pl.pallas_call(
         run,
         out_shape=out_shape,
-        in_specs=[pl.BlockSpec(memory_space=space)] * len(operands) + [pl.BlockSpec(memory_space=pl.ANY)] * len(after),
+        in_specs=[pl.BlockSpec(memory_space=pltpu.VMEM)] * len(operands) + [pl.BlockSpec(memory_space=pl.ANY)] * len(after),
         out_specs=jax.tree.map(lambda _: pl.BlockSpec(memory_space=pltpu.VMEM), out_shape),
         scratch_shapes=list(scratch),
         cost_estimate=pl.CostEstimate(flops=0, bytes_accessed=0, transcendentals=0),
@@ -72,9 +72,9 @@
 def cut_kernel(nrow, teach, *outs):
     part = teach.shape[1] // nrow
     z = lax.axis_index("row")
-    for k in range(nrow):
+    for k in range(1, nrow):
         at = pl.multiple_of((z ^ k) * part, part)
-        outs[k][...] = teach[:, pl.ds(at, part)]
+        outs[k - 1][...] = teach[:, pl.ds(at, part)]
 
 
 def ride_kernel(stud, *refs):
@@ -84,15 +84,16 @@
         wide(out, rows, piece)
 
 
-def own_kernel(teach, stud, scale, cut, out):
+def own_kernel(nrow, teach, stud, scale, out):
     rows, half = stud.shape
+    part = teach.shape[1] // nrow
     ts = teach[...].astype(F32)
     s = scale[...].astype(F32)
     mass = jnp.sum(jnp.square(column(s)) * jnp.sum(ts * ts, axis=1, keepdims=True), keepdims=True)
     tags = tags_of(jnp.concatenate([s, s], axis=1), mass)
     out[:rows, :] = stud[...]
     out[rows : rows + TAIL, :] = jnp.concatenate([tags] * (half // (2 * rows)), axis=1)
-    wide(out, rows + TAIL, cut[...])
+    wide(out, rows + TAIL, teach[:, pl.ds(pl.multiple_of(lax.axis_index("row") * part, part), part)])
 
 
 def take_kernel(rows, ref, out):
@@ -117,11 +118,10 @@
 def gram_kernel(nrow, ncol, rows, order, *refs):
     count = nrow * ncol
     outs, held, left = refs[count : count + nrow], refs[-2], refs[-1]
-    for c in range(ncol):
-        own = refs[c * nrow]
-        put(held, place(nrow, ncol, rows, 0, c), rows, own, rows + TAIL)
-        for k in range(1, nrow):
-            put(held, place(nrow, ncol, rows, k, c), rows, refs[c * nrow + k], 0)
+    own = order.index(0) * ncol
+    for n, k in enumerate(order):
+        for c in range(ncol):
+            put(held, place(nrow, ncol, rows, k, c), rows, refs[n * ncol + c], 0 if k else rows + TAIL)
     for n, k in enumerate(order):
         left[n * rows : (n + 1) * rows, :] = held[pl.ds(place(nrow, ncol, rows, k, 0), rows), :]
     sub = rows // 2
@@ -129,7 +129,7 @@
     lane = lax.broadcasted_iota(jnp.int32, (sub, 2 * rows), 1)
     note, mass = jnp.zeros((sub, 2 * rows), F32), jnp.zeros((1, 1), F32)
     for c in range(ncol):
-        scales, part = read_tags(refs[c * nrow][rows : rows + TAIL, : 2 * rows])
+        scales, part = read_tags(refs[own + c][rows : rows + TAIL, : 2 * rows])
         turned = jnp.concatenate([scales[:, sub:], scales[:, :sub]], axis=1)
         note = jnp.where(at == 2 * c, scales, jnp.where(at == 2 * c + 1, turned, note))
         mass = mass + part
@@ -165,8 +165,8 @@
         out[rows:, at : at + 128] = jnp.broadcast_to(lane_row(squares), (8, 128))
 
 
-def message_kernel(nrow, ncol, raw_gram, *refs):
-    parts, (out, vectors) = refs[:-2], refs[-2:]
+def message_kernel(nrow, ncol, order, raw_gram, *refs):
+    parts, (out, vectors) = [refs[order.index(k)] for k in range(nrow)], refs[-2:]
     rows = parts[0].shape[0]
     sub = rows // 2
     total = parts[0][...].astype(F32)
@@ -239,11 +239,16 @@
     middle, high = nrow // 2, rows * part // half
     order = list(range(middle, nrow)) + list(range(middle))
     riders = (1, middle)
-    cuts = call(functools.partial(cut_kernel, nrow), [sds((rows, part), BF16)] * nrow, [teacher])
-    ridden = call(ride_kernel, [sds((rows + high, half), BF16)] * 2, [student] + [cuts[k] for k in riders])
-    leaving = dict(enumerate(cuts)) | dict(zip(riders, ridden))
+    cuts = call(functools.partial(cut_kernel, nrow), [sds((rows, part), BF16)] * (nrow - 1), [teacher])
+    ridden = call(ride_kernel, [sds((rows + high, half), BF16)] * 2, [student] + [cuts[k - 1] for k in riders])
+    leaving = dict(enumerate(cuts, 1)) | dict(zip(riders, ridden))
     came = {k: along_row(leaving[k], k) for k in order if k}
-    own = call(own_kernel, sds((rows + TAIL + high, half), BF16), [teacher, student, scale, cuts[0]])
+    own = call(
+        functools.partial(own_kernel, nrow),
+        sds((rows + TAIL + high, half), BF16),
+        [teacher, student, scale],
+        after=[came[nrow - 1]],
+    )
     columns = {0: with_columns(own)}
     for k in range(1, nrow):
         piece = came[k]
@@ -253,7 +258,7 @@
     partial = call(
         functools.partial(gram_kernel, nrow, ncol, rows, order),
         [sds((rows, batch), BF16 if k else F32) for k in range(nrow)],
-        [columns[k][c] for c in range(ncol) for k in range(nrow)],
+        [columns[k][c] for k in order for c in range(ncol)],
         scratch=[pltpu.VMEM((batch, part), BF16), pltpu.VMEM((nrow * rows, part), BF16)],
     )
     returned = {k: along_row(partial[k], k) if k else partial[0] for k in order}
@@ -278,9 +283,9 @@
         scratch=[] if small else [pltpu.VMEM((batch, half), BF16)],
     )
     message, vectors = call(
-        functools.partial(message_kernel, nrow, ncol),
+        functools.partial(message_kernel, nrow, ncol, order),
         [sds((2 * rows + 16, batch), F32), sds((8, batch), F32)],
-        [raw_gram] + [returned[k] for k in range(nrow)],
+        [raw_gram] + [returned[k] for k in order],
     )
     return call(
         functools.partial(final_kernel, nrow, ncol, None if small else raw_keys),

time: 35.8 us -> 32.6 us (0.911)
  starting transfers between devices: 18 us -> 15 us
  local copies, waits for them, and re-layouts: 2.48 us -> 1.8 us
    ppermute x7, starting transfers between devices: 12.2 us -> 9.23 us  [along_row(): return lax.ppermute(x, 'row', [(i, i ^ k) for i in range(nrow)])]
    ppermute x5, waiting for transfers between devices: 1.92 us -> 4.39 us  [along_col(): return lax.ppermute(x, 'col', [(i, (i - c) % ncol) for i in range(ncol)])]
    ppermute x7, waiting for transfers between devices: 9.27 us -> 7.18 us  [along_row(): return lax.ppermute(x, 'row', [(i, i ^ k) for i in range(nrow)])]
    unnamed x10, local copies, waits for them, and re-layouts: 2.48 us -> 1.8 us
  transfers between devices with their start and end apart: 13 -> 13, of which waited for: 6 -> 11; matrix products, arithmetic and copies ran while one was open for 0% -> 0% of each run, Pallas kernels for 3% -> 4%
where the time goes in v8:
time: 32.6 us; the launch traced here: 32.4 us
  starting transfers between devices  15 us (46%)
  waiting for transfers between devices  13.1 us (40%)
  Pallas kernels  2.4 us (7%)
  local copies, waits for them, and re-layouts  1.8 us (6%)
    ppermute x7, starting transfers between devices, along_row(): return lax.ppermute(x, 'row', [(i, i ^ k) for i in range(nrow)])  9.23 us
    ppermute x7, waiting for transfers between devices, along_row(): return lax.ppermute(x, 'row', [(i, i ^ k) for i in range(nrow)])  7.18 us
    ppermute x5, starting transfers between devices, along_col(): return lax.ppermute(x, 'col', [(i, (i - c) % ncol) for i in range(ncol)])  5.68 us
    ppermute x5, waiting for transfers between devices, along_col(): return lax.ppermute(x, 'col', [(i, (i - c) % ncol) for i in range(ncol)])  4.39 us
    pallas_call x11, Pallas kernels, call(): pl.pallas_call(run, out_shape=out_shape, in_specs=[pl.BlockSpec(memory_sp...  2.4 us
    unnamed x10, local copies, waits for them, and re-layouts  1.8 us
    ppermute x1, waiting for transfers between devices, other_core(): return lax.ppermute(x, 'sub', [(0, 1), (1, 0)])  1.57 us
  transfers between devices with their start and end apart: 13, of which 11 were waited for; matrix products, arithmetic and copies ran while one was open for 0% of the time, Pallas kernels for 4%

profile of v8, /device:TPU:0, one launch (start us, length us, event | category | flops | bytes accessed | tf_op | source)
XLA Modules:
  0.0 32.4 jit_solution(4435009796147556695)
XLA Ops:
  0.0 0.0 copy-start
  0.0 0.9 %copy-done = bf16[64,2048]{1,0:T(8,128)(2,1)S(1)} copy-done((bf16[64,2048]{1,0:T(8,128)(2,1)S(1)}, bf16[64,2048]{1,0:T(8,128)(2,1)}, u32[]{:S(2)}) %copy-start) | copy-done | bytes 262168
  1.0 0.0 copy-start.1
  1.0 5.1 %collective-permute-start = (bf16[64,512]{1,0:T(8,128)(2,1)S(1)}, bf16[64,512]{1,0:T(8,128)(2,1)S(1)}, u32[]{:S(2)}, u32[]{:S(2)}) collective-permute-start(bf16[64,512]{1,0:T(8,128)(2,1)S(1)} %get-tuple-element.18), channel_id=1, source_target_pairs={{0,12},{4,8},{8,4},{12,0},{1,13},{5,9},{9,5},{13,1},{2,14},{6,10},... | collective-permute-start | bytes 196616 | tf_op jit(solution)/shard_map/ppermute | solution.py:224
  6.1 0.0 copy-start.2
  6.1 0.8 %copy-done.2 = bf16[64,512]{1,0:T(8,128)(2,1)S(1)} copy-done((bf16[64,512]{1,0:T(8,128)(2,1)S(1)}, bf16[64,512]{1,0:T(8,128)(2,1)}, u32[]{:S(2)}) %copy-start.2) | copy-done | bytes 65560
  6.9 0.1 collective-permute-start.1
  7.0 0.0 copy-start.4
  7.0 0.6 %collective-permute-start.2 = (bf16[128,512]{1,0:T(8,128)(2,1)S(1)}, bf16[128,512]{1,0:T(8,128)(2,1)S(1)}, u32[]{:S(2)}, u32[]{:S(2)}) collective-permute-start(bf16[128,512]{1,0:T(8,128)(2,1)S(1)} %get-tuple-element.22), channel_id=1, source_target_pairs={{0,8},{4,12},{8,0},{12,4},{1,9},{5,13},{9,1},{13,5},{2,10},{6,14},... | collective-permute-start | bytes 393224 | tf_op jit(solution)/shard_map/ppermute | solution.py:224
  7.6 1.1 %collective-permute-done.refs_3_.refs_2_ = bf16[64,512]{1,0:T(8,128)(2,1)S(1)} collective-permute-done((bf16[64,512]{1,0:T(8,128)(2,1)S(1)}, bf16[64,512]{1,0:T(8,128)(2,1)S(1)}, u32[]{:S(2)}, u32[]{:S(2)}) %collective-permute-start) | collective-permute-done | bytes 65568 | tf_op jit(solution)/shard_map/ppermute | solution.py:224
  8.7 0.0 copy-done.1
  8.7 0.0 copy-done.4
  8.7 0.3 shard_map.38.refs_4_.refs_0_
  9.0 1.9 %collective-permute-start.6 = (bf16[144,512]{1,0:T(8,128)(2,1)S(1)}, bf16[144,512]{1,0:T(8,128)(2,1)S(1)}, u32[]{:S(2)}, u32[]{:S(2)}) collective-permute-start(bf16[144,512]{1,0:T(8,128)(2,1)S(1)} %shard_map.38.refs_4_.refs_0_), channel_id=1, source_target_pairs={{0,2},{2,0},{1,3},{3,1},{4,6},{6,4},{5,7},{7,5},{8,10},{10,8},{9,1... | collective-permute-start | bytes 442376 | tf_op jit(solution)/shard_map/ppermute | solution.py:227
  10.9 0.2 collective-permute-start.5
  11.1 2.2 %collective-permute-done.1.refs_0_ = bf16[128,512]{1,0:T(8,128)(2,1)S(1)} collective-permute-done((bf16[128,512]{1,0:T(8,128)(2,1)S(1)}, bf16[128,512]{1,0:T(8,128)(2,1)S(1)}, u32[]{:S(2)}, u32[]{:S(2)}) %collective-permute-start.1) | collective-permute-done | bytes 131104 | tf_op jit(solution)/shard_map/ppermute | solution.py:224
  13.3 1.5 %collective-permute-start.7 = (bf16[64,512]{1,0:T(8,128)(2,1)S(1)}, bf16[64,512]{1,0:T(8,128)(2,1)S(1)}, u32[]{:S(2)}, u32[]{:S(2)}) collective-permute-start(bf16[64,512]{1,0:T(8,128)(2,1)S(1)} %shard_map.42.refs_6_), channel_id=1, source_target_pairs={{0,2},{2,0},{1,3},{3,1},{4,6},{6,4},{5,7},{7,5},{8,10},{10,8},{9,1... | collective-permute-start | bytes 196616 | tf_op jit(solution)/shard_map/ppermute | solution.py:227
  14.8 1.0 %collective-permute-done.2.refs_0_.refs_1_ = bf16[128,512]{1,0:T(8,128)(2,1)S(1)} collective-permute-done((bf16[128,512]{1,0:T(8,128)(2,1)S(1)}, bf16[128,512]{1,0:T(8,128)(2,1)S(1)}, u32[]{:S(2)}, u32[]{:S(2)}) %collective-permute-start.2) | collective-permute-done | bytes 131104 | tf_op jit(solution)/shard_map/ppermute | solution.py:224
  15.8 1.5 %collective-permute-start.4 = (bf16[64,512]{1,0:T(8,128)(2,1)S(1)}, bf16[64,512]{1,0:T(8,128)(2,1)S(1)}, u32[]{:S(2)}, u32[]{:S(2)}) collective-permute-start(bf16[64,512]{1,0:T(8,128)(2,1)S(1)} %shard_map.41.refs_0_), channel_id=1, source_target_pairs={{0,2},{2,0},{1,3},{3,1},{4,6},{6,4},{5,7},{7,5},{8,10},{10,8},{9,1... | collective-permute-start | bytes 196616 | tf_op jit(solution)/shard_map/ppermute | solution.py:227
  17.3 0.0 collective-permute-start.3
  17.3 0.0 collective-permute-done.5.refs_3_
  17.3 0.6 %collective-permute-done.7.refs_7_ = bf16[64,512]{1,0:T(8,128)(2,1)S(1)} collective-permute-done((bf16[64,512]{1,0:T(8,128)(2,1)S(1)}, bf16[64,512]{1,0:T(8,128)(2,1)S(1)}, u32[]{:S(2)}, u32[]{:S(2)}) %collective-permute-start.7) | collective-permute-done | bytes 65568 | tf_op jit(solution)/shard_map/ppermute | solution.py:227
  17.9 2.2 %collective-permute-done.4.refs_1_ = bf16[64,512]{1,0:T(8,128)(2,1)S(1)} collective-permute-done((bf16[64,512]{1,0:T(8,128)(2,1)S(1)}, bf16[64,512]{1,0:T(8,128)(2,1)S(1)}, u32[]{:S(2)}, u32[]{:S(2)}) %collective-permute-start.4) | collective-permute-done | bytes 65568 | tf_op jit(solution)/shard_map/ppermute | solution.py:227
  20.1 0.0 collective-permute-done.6.refs_5_.refs_2_
  20.1 0.5 %shard_map.43 = (f32[64,512]{1,0:T(8,128)S(1)}, bf16[64,512]{1,0:T(8,128)(2,1)S(1)}, bf16[64,512]{1,0:T(8,128)(2,1)S(1)}, bf16[64,512]{1,0:T(8,128)(2,1)S(1)}) custom-call(bf16[64,512]{1,0:T(8,128)(2,1)S(1)} %shard_map.41.refs_0_, bf16[64,512]{1,0:T(8,128)(2,1)S(1)} %collective-permute-done.4.refs_1_, ...), custom_call_target="tpu_custom_call" | custom-call | tf_op jit(solution)/shard_map/pallas_call | solution.py:22
  20.6 1.0 %collective-permute-done.3.refs_2_ = bf16[64,512]{1,0:T(8,128)(2,1)S(1)} collective-permute-done((bf16[64,512]{1,0:T(8,128)(2,1)S(1)}, bf16[64,512]{1,0:T(8,128)(2,1)S(1)}, u32[]{:S(2)}, u32[]{:S(2)}) %collective-permute-start.3) | collective-permute-done | bytes 65568 | tf_op jit(solution)/shard_map/ppermute | solution.py:224
  21.6 0.6 %collective-permute-start.8 = (bf16[192,512]{1,0:T(8,128)(2,1)S(1)}, bf16[192,512]{1,0:T(8,128)(2,1)S(1)}, u32[]{:S(2)}, u32[]{:S(2)}) collective-permute-start(bf16[192,512]{1,0:T(8,128)(2,1)S(1)} %shard_map.44.refs_1_), channel_id=1, source_target_pairs={{0,2},{2,0},{1,3},{3,1},{4,6},{6,4},{5,7},{7,5},{8,10},{10,8},{9,1... | collective-permute-start | bytes 589832 | tf_op jit(solution)/shard_map/ppermute | solution.py:227
  22.2 0.9 %collective-permute-start.9 = (bf16[64,512]{1,0:T(8,128)(2,1)S(1)}, bf16[64,512]{1,0:T(8,128)(2,1)S(1)}, u32[]{:S(2)}, u32[]{:S(2)}) collective-permute-start(bf16[64,512]{1,0:T(8,128)(2,1)S(1)} %get-tuple-element.25), channel_id=1, source_target_pairs={{0,8},{4,12},{8,0},{12,4},{1,9},{5,13},{9,1},{13,5},{2,10},{6,14},... | collective-permute-start | bytes 196616 | tf_op jit(solution)/shard_map/ppermute | solution.py:224
  23.2 1.4 %collective-permute-start.10 = (bf16[64,512]{1,0:T(8,128)(2,1)S(1)}, bf16[64,512]{1,0:T(8,128)(2,1)S(1)}, u32[]{:S(2)}, u32[]{:S(2)}) collective-permute-start(bf16[64,512]{1,0:T(8,128)(2,1)S(1)} %get-tuple-element.26), channel_id=1, source_target_pairs={{0,12},{4,8},{8,4},{12,0},{1,13},{5,9},{9,5},{13,1},{2,14},{6,10},... | collective-permute-start | bytes 196616 | tf_op jit(solution)/shard_map/ppermute | solution.py:224
  24.6 1.1 %collective-permute-start.11 = (bf16[64,512]{1,0:T(8,128)(2,1)S(1)}, bf16[64,512]{1,0:T(8,128)(2,1)S(1)}, u32[]{:S(2)}, u32[]{:S(2)}) collective-permute-start(bf16[64,512]{1,0:T(8,128)(2,1)S(1)} %get-tuple-element.27), channel_id=1, source_target_pairs={{0,4},{4,0},{8,12},{12,8},{1,5},{5,1},{9,13},{13,9},{2,6},{6,2},{1... | collective-permute-start | bytes 196616 | tf_op jit(solution)/shard_map/ppermute | solution.py:224
  25.7 1.6 %collective-permute-done.8.refs_3_ = bf16[192,512]{1,0:T(8,128)(2,1)S(1)} collective-permute-done((bf16[192,512]{1,0:T(8,128)(2,1)S(1)}, bf16[192,512]{1,0:T(8,128)(2,1)S(1)}, u32[]{:S(2)}, u32[]{:S(2)}) %collective-permute-start.8) | collective-permute-done | bytes 196640 | tf_op jit(solution)/shard_map/ppermute | solution.py:227
  27.3 0.3 %shard_map.45 = (f32[72,512]{1,0:T(8,128)S(1)}, bf16[512,512]{1,0:T(8,128)(2,1)S(1)}) custom-call(bf16[144,512]{1,0:T(8,128)(2,1)S(1)} %shard_map.38.refs_4_.refs_0_, bf16[192,512]{1,0:T(8,128)(2,1)S(1)} %shard_map.44.refs_1_, bf16[144,512]{1,0:T(8,128)(2,1)S(1)} %collective-permute-done.6.refs_5_.refs_2_, bf16[192,512]{1,0:T(8,128)(2,1)S(1)} %collective-permute-done.8.refs_3_), custom_call_target="tpu_custom_call" | custom-call | tf_op jit(solution)/shard_map/pallas_call | solution.py:22
  27.7 0.1 collective-permute-done.9.refs_1_
  27.8 1.6 %collective-permute-done.10.refs_2_ = bf16[64,512]{1,0:T(8,128)(2,1)S(1)} collective-permute-done((bf16[64,512]{1,0:T(8,128)(2,1)S(1)}, bf16[64,512]{1,0:T(8,128)(2,1)S(1)}, u32[]{:S(2)}, u32[]{:S(2)}) %collective-permute-start.10) | collective-permute-done | bytes 65568 | tf_op jit(solution)/shard_map/ppermute | solution.py:224
  29.3 0.2 collective-permute-done.11.refs_4_
  29.5 0.0 copy-start.3
  29.5 0.1 shard_map.46
  29.6 0.1 collective-permute-start.12
  29.7 1.6 %collective-permute-done.12.refs_1_ = f32[144,512]{1,0:T(8,128)S(1)} collective-permute-done((f32[144,512]{1,0:T(8,128)S(1)}, f32[144,512]{1,0:T(8,128)S(1)}, u32[]{:S(2)}, u32[]{:S(2)}) %collective-permute-start.12) | collective-permute-done | bytes 294944 | tf_op jit(solution)/shard_map/ppermute | solution.py:230
  31.3 0.0 copy-done.3
  31.3 1.1 %shard_map.47 = f32[64,512]{1,0:T(8,128)} custom-call(f32[144,512]{1,0:T(8,128)S(1)} %get-tuple-element.28.refs_0_, f32[144,512]{1,0:T(8,128)S(1)} %collective-permute-done.12.refs_1_, f32[8,512]{1,0:T(8,128)S(1)} %get-tuple-element.29.refs_2_, bf16[64,512]{1,0:T(8,128)(2,1)S(1)} %copy-done.3, bf16[1,64]{1,0:T(2,128)(2,1)S(1)} %bitcast.2, ...), custom_call_target="tpu_custom_call" | custom-call | tf_op jit(solution)/shard_map/pallas_call | solution.py:22
  (6 shorter events, 0.1 us)
Async XLA Ops:
  0.0 0.9 %copy-start = (bf16[64,2048]{1,0:T(8,128)(2,1)S(1)}, bf16[64,2048]{1,0:T(8,128)(2,1)}, u32[]{:S(2)}) copy-start(bf16[64,2048]{1,0:T(8,128)(2,1)} %refs_0_.4) | copy-start | bytes 786436
  1.0 7.8 %copy-start.1 = (bf16[64,2048]{1,0:T(8,128)(2,1)S(1)}, bf16[64,2048]{1,0:T(8,128)(2,1)}, u32[]{:S(2)}) copy-start(bf16[64,2048]{1,0:T(8,128)(2,1)} %refs_0_.4) | copy-start | bytes 786436
  1.0 7.7 %collective-permute-start = (bf16[64,512]{1,0:T(8,128)(2,1)S(1)}, bf16[64,512]{1,0:T(8,128)(2,1)S(1)}, u32[]{:S(2)}, u32[]{:S(2)}) collective-permute-start(bf16[64,512]{1,0:T(8,128)(2,1)S(1)} %get-tuple-element.18), channel_id=1, source_target_pairs={{0,12},{4,8},{8,4},{12,0},{1,13},{5,9},{9,5},{13,1},{2,14},{6,10},... | collective-permute-start | bytes 196616 | tf_op jit(solution)/shard_map/ppermute | solution.py:224
  6.1 0.8 %copy-start.2 = (bf16[64,512]{1,0:T(8,128)(2,1)S(1)}, bf16[64,512]{1,0:T(8,128)(2,1)}, u32[]{:S(2)}) copy-start(bf16[64,512]{1,0:T(8,128)(2,1)} %refs_3_.1) | copy-start | bytes 196612
  6.9 6.4 %collective-permute-start.1 = (bf16[128,512]{1,0:T(8,128)(2,1)S(1)}, bf16[128,512]{1,0:T(8,128)(2,1)S(1)}, u32[]{:S(2)}, u32[]{:S(2)}) collective-permute-start(bf16[128,512]{1,0:T(8,128)(2,1)S(1)} %get-tuple-element.21), channel_id=1, source_target_pairs={{0,4},{4,0},{8,12},{12,8},{1,5},{5,1},{9,13},{13,9},{2,6},{6,2},{1... | collective-permute-start | bytes 393224 | tf_op jit(solution)/shard_map/ppermute | solution.py:224
  7.0 1.7 %copy-start.4 = (bf16[64]{0:T(256)(128)(2,1)S(1)}, bf16[64]{0:T(256)(128)(2,1)}, u32[]{:S(2)}) copy-start(bf16[64]{0:T(256)(128)(2,1)} %param.5) | copy-start | bytes 388
  7.0 8.8 %collective-permute-start.2 = (bf16[128,512]{1,0:T(8,128)(2,1)S(1)}, bf16[128,512]{1,0:T(8,128)(2,1)S(1)}, u32[]{:S(2)}, u32[]{:S(2)}) collective-permute-start(bf16[128,512]{1,0:T(8,128)(2,1)S(1)} %get-tuple-element.22), channel_id=1, source_target_pairs={{0,8},{4,12},{8,0},{12,4},{1,9},{5,13},{9,1},{13,5},{2,10},{6,14},... | collective-permute-start | bytes 393224 | tf_op jit(solution)/shard_map/ppermute | solution.py:224
  9.0 11.1 %collective-permute-start.6 = (bf16[144,512]{1,0:T(8,128)(2,1)S(1)}, bf16[144,512]{1,0:T(8,128)(2,1)S(1)}, u32[]{:S(2)}, u32[]{:S(2)}) collective-permute-start(bf16[144,512]{1,0:T(8,128)(2,1)S(1)} %shard_map.38.refs_4_.refs_0_), channel_id=1, source_target_pairs={{0,2},{2,0},{1,3},{3,1},{4,6},{6,4},{5,7},{7,5},{8,10},{10,8},{9,1... | collective-permute-start | bytes 442376 | tf_op jit(solution)/shard_map/ppermute | solution.py:227
  10.9 6.4 %collective-permute-start.5 = (bf16[64,512]{1,0:T(8,128)(2,1)S(1)}, bf16[64,512]{1,0:T(8,128)(2,1)S(1)}, u32[]{:S(2)}, u32[]{:S(2)}) collective-permute-start(bf16[64,512]{1,0:T(8,128)(2,1)S(1)} %collective-permute-done.refs_3_.refs_2_), channel_id=1, source_target_pairs={{0,2},{2,0},{1,3},{3,1},{4,6},{6,4},{5,7},{7,5},{8,10},{10,8},{9,1... | collective-permute-start | bytes 196616 | tf_op jit(solution)/shard_map/ppermute | solution.py:227
  13.3 4.6 %collective-permute-start.7 = (bf16[64,512]{1,0:T(8,128)(2,1)S(1)}, bf16[64,512]{1,0:T(8,128)(2,1)S(1)}, u32[]{:S(2)}, u32[]{:S(2)}) collective-permute-start(bf16[64,512]{1,0:T(8,128)(2,1)S(1)} %shard_map.42.refs_6_), channel_id=1, source_target_pairs={{0,2},{2,0},{1,3},{3,1},{4,6},{6,4},{5,7},{7,5},{8,10},{10,8},{9,1... | collective-permute-start | bytes 196616 | tf_op jit(solution)/shard_map/ppermute | solution.py:227
  15.8 4.3 %collective-permute-start.4 = (bf16[64,512]{1,0:T(8,128)(2,1)S(1)}, bf16[64,512]{1,0:T(8,128)(2,1)S(1)}, u32[]{:S(2)}, u32[]{:S(2)}) collective-permute-start(bf16[64,512]{1,0:T(8,128)(2,1)S(1)} %shard_map.41.refs_0_), channel_id=1, source_target_pairs={{0,2},{2,0},{1,3},{3,1},{4,6},{6,4},{5,7},{7,5},{8,10},{10,8},{9,1... | collective-permute-start | bytes 196616 | tf_op jit(solution)/shard_map/ppermute | solution.py:227
  17.3 4.3 %collective-permute-start.3 = (bf16[64,512]{1,0:T(8,128)(2,1)S(1)}, bf16[64,512]{1,0:T(8,128)(2,1)S(1)}, u32[]{:S(2)}, u32[]{:S(2)}) collective-permute-start(bf16[64,512]{1,0:T(8,128)(2,1)S(1)} %shard_map.40), channel_id=1, source_target_pairs={{0,4},{4,0},{8,12},{12,8},{1,5},{5,1},{9,13},{13,9},{2,6},{6,2},{1... | collective-permute-start | bytes 196616 | tf_op jit(solution)/shard_map/ppermute | solution.py:224
  21.6 5.7 %collective-permute-start.8 = (bf16[192,512]{1,0:T(8,128)(2,1)S(1)}, bf16[192,512]{1,0:T(8,128)(2,1)S(1)}, u32[]{:S(2)}, u32[]{:S(2)}) collective-permute-start(bf16[192,512]{1,0:T(8,128)(2,1)S(1)} %shard_map.44.refs_1_), channel_id=1, source_target_pairs={{0,2},{2,0},{1,3},{3,1},{4,6},{6,4},{5,7},{7,5},{8,10},{10,8},{9,1... | collective-permute-start | bytes 589832 | tf_op jit(solution)/shard_map/ppermute | solution.py:227
  22.2 5.6 %collective-permute-start.9 = (bf16[64,512]{1,0:T(8,128)(2,1)S(1)}, bf16[64,512]{1,0:T(8,128)(2,1)S(1)}, u32[]{:S(2)}, u32[]{:S(2)}) collective-permute-start(bf16[64,512]{1,0:T(8,128)(2,1)S(1)} %get-tuple-element.25), channel_id=1, source_target_pairs={{0,8},{4,12},{8,0},{12,4},{1,9},{5,13},{9,1},{13,5},{2,10},{6,14},... | collective-permute-start | bytes 196616 | tf_op jit(solution)/shard_map/ppermute | solution.py:224
  23.2 6.2 %collective-permute-start.10 = (bf16[64,512]{1,0:T(8,128)(2,1)S(1)}, bf16[64,512]{1,0:T(8,128)(2,1)S(1)}, u32[]{:S(2)}, u32[]{:S(2)}) collective-permute-start(bf16[64,512]{1,0:T(8,128)(2,1)S(1)} %get-tuple-element.26), channel_id=1, source_target_pairs={{0,12},{4,8},{8,4},{12,0},{1,13},{5,9},{9,5},{13,1},{2,14},{6,10},... | collective-permute-start | bytes 196616 | tf_op jit(solution)/shard_map/ppermute | solution.py:224
  24.6 5.0 %collective-permute-start.11 = (bf16[64,512]{1,0:T(8,128)(2,1)S(1)}, bf16[64,512]{1,0:T(8,128)(2,1)S(1)}, u32[]{:S(2)}, u32[]{:S(2)}) collective-permute-start(bf16[64,512]{1,0:T(8,128)(2,1)S(1)} %get-tuple-element.27), channel_id=1, source_target_pairs={{0,4},{4,0},{8,12},{12,8},{1,5},{5,1},{9,13},{13,9},{2,6},{6,2},{1... | collective-permute-start | bytes 196616 | tf_op jit(solution)/shard_map/ppermute | solution.py:224
  29.5 1.8 %copy-start.3 = (bf16[64,512]{1,0:T(8,128)(2,1)S(1)}, bf16[64,512]{1,0:T(8,128)(2,1)}, u32[]{:S(2)}) copy-start(bf16[64,512]{1,0:T(8,128)(2,1)} %refs_3_.1) | copy-start | bytes 196612
  29.6 1.7 %collective-permute-start.12 = (f32[144,512]{1,0:T(8,128)S(1)}, f32[144,512]{1,0:T(8,128)S(1)}, u32[]{:S(2)}, u32[]{:S(2)}) collective-permute-start(f32[144,512]{1,0:T(8,128)S(1)} %get-tuple-element.28.refs_0_), channel_id=1, source_target_pairs={{0,1},{1,0},{2,3},{3,2},{4,5},{5,4},{6,7},{7,6},{8,9},{9,8},{10,11... | collective-permute-start | bytes 884744 | tf_op jit(solution)/shard_map/ppermute | solution.py:230

commit v9 on v8

--- a/solution.py
+++ b/solution.py
@@ -77,11 +77,10 @@
         outs[k - 1][...] = teach[:, pl.ds(at, part)]
 
 
-def ride_kernel(stud, *refs):
-    rows, count = stud.shape[0], len(refs) // 2
-    for piece, out in zip(refs[:count], refs[count:]):
-        out[:rows, :] = stud[...]
-        wide(out, rows, piece)
+def ride_kernel(stud, piece, out):
+    rows = stud.shape[0]
+    out[:rows, :] = stud[...]
+    wide(out, rows, piece[...])
 
 
 def own_kernel(nrow, teach, stud, scale, out):
@@ -196,19 +195,19 @@
     batch = mine.shape[1]
     squares = mine[2 * rows : 2 * rows + 8, :] + other[2 * rows : 2 * rows + 8, :]
     for at in range(0, batch, 128):
-        norm = jnp.sqrt(column(squares[:1, at : at + 128]))
-        units[at : at + 128, :] = (raw[at : at + 128, :].astype(F32) / norm).astype(BF16)
+        inverse = 1.0 / jnp.sqrt(column(squares[:1, at : at + 128]))
+        units[at : at + 128, :] = (raw[at : at + 128, :].astype(F32) * inverse).astype(BF16)
     at = pl.ds(group_spot(nrow, ncol, rows, 0), 2 * rows)
     own = (mine[2 * rows : 2 * rows + 8, at] + other[2 * rows : 2 * rows + 8, at])[:1, :rows]
-    norm = jnp.sqrt(column(own))
+    inverse = 1.0 / jnp.sqrt(column(own))
     mass = (mine[2 * rows + 8 : 2 * rows + 9, :1] + other[2 * rows + 8 : 2 * rows + 9, :1]) / batch
-    gram = (mine[rows : 2 * rows, :] + other[rows : 2 * rows, :]) / (norm * jnp.sqrt(squares[:1, :]))
-    outer = column(scale[...].astype(F32)) * vectors[:1, :]
-    error_b = (gram - outer * (mine[:rows, :] + other[:rows, :]) / mass).astype(BF16)
+    gram = (mine[rows : 2 * rows, :] + other[rows : 2 * rows, :]) * (inverse * (1.0 / jnp.sqrt(squares[:1, :])))
+    outer = (column(scale[...].astype(F32)) / mass) * vectors[:1, :]
+    error_b = (gram - outer * (mine[:rows, :] + other[:rows, :])).astype(BF16)
     grads = 4.0 * jnp.dot(error_b, units[...], preferred_element_type=F32)
     along = 4.0 * jnp.sum(error_b.astype(F32) * gram, axis=1, keepdims=True)
-    unit = stud[...].astype(F32) / norm
-    out[...] = (grads - along * unit) / norm
+    unit = stud[...].astype(F32) * inverse
+    out[...] = (grads - along * unit) * inverse
 
 
 def shards(student, teacher, scale):
@@ -240,9 +239,14 @@
     order = list(range(middle, nrow)) + list(range(middle))
     riders = (1, middle)
     cuts = call(functools.partial(cut_kernel, nrow), [sds((rows, part), BF16)] * (nrow - 1), [teacher])
-    ridden = call(ride_kernel, [sds((rows + high, half), BF16)] * 2, [student] + [cuts[k - 1] for k in riders])
-    leaving = dict(enumerate(cuts, 1)) | dict(zip(riders, ridden))
-    came = {k: along_row(leaving[k], k) for k in order if k}
+    last = nrow - 1
+    came, landed = {last: along_row(cuts[last - 1], last)}, ()
+    for k in [k for k in order if k not in (0, 1, last)] + [1]:
+        leaving = cuts[k - 1]
+        if k in riders:
+            leaving = call(ride_kernel, sds((rows + high, half), BF16), [student, leaving], after=landed)
+            landed = (came[last],)
+        came[k] = along_row(leaving, k)
     own = call(
         functools.partial(own_kernel, nrow),
         sds((rows + TAIL + high, half), BF16),

time: 32.6 us -> 34.6 us (1.061)
  starting transfers between devices: 15 us -> 20.1 us
  waiting for transfers between devices: 13.1 us -> 10.8 us
  local copies, waits for them, and re-layouts: 1.8 us -> 1 us
    ppermute x7, starting transfers between devices: 9.23 us -> 14.5 us  [along_row(): return lax.ppermute(x, 'row', [(i, i ^ k) for i in range(nrow)])]
    ppermute x7, waiting for transfers between devices: 7.18 us -> 5.47 us  [along_row(): return lax.ppermute(x, 'row', [(i, i ^ k) for i in range(nrow)])]
    unnamed x10 -> x8, local copies, waits for them, and re-layouts: 1.8 us -> 1 us
    ppermute x5, waiting for transfers between devices: 4.39 us -> 3.78 us  [along_col(): return lax.ppermute(x, 'col', [(i, (i - c) % ncol) for i in range(ncol)])]
    pallas_call x11 -> x12, Pallas kernels: 2.4 us -> 2.42 us  [call(): pl.pallas_call(run, out_shape=out_shape, in_specs=[pl.BlockSpec(memory_sp...]
  transfers between devices with their start and end apart: 13 -> 13, of which waited for: 11 -> 9; matrix products, arithmetic and copies ran while one was open for 0% -> 0% of each run, Pallas kernels for 4% -> 3%
where the time goes in v9:
time: 34.6 us; the launch traced here: 34.5 us
  starting transfers between devices  20.1 us (58%)
  waiting for transfers between devices  10.8 us (31%)
  Pallas kernels  2.42 us (7%)
  local copies, waits for them, and re-layouts  1 us (3%)
    ppermute x7, starting transfers between devices, along_row(): return lax.ppermute(x, 'row', [(i, i ^ k) for i in range(nrow)])  14.5 us
    ppermute x5, starting transfers between devices, along_col(): return lax.ppermute(x, 'col', [(i, (i - c) % ncol) for i in range(ncol)])  5.53 us
    ppermute x7, waiting for transfers between devices, along_row(): return lax.ppermute(x, 'row', [(i, i ^ k) for i in range(nrow)])  5.47 us
    ppermute x5, waiting for transfers between devices, along_col(): return lax.ppermute(x, 'col', [(i, (i - c) % ncol) for i in range(ncol)])  3.78 us
    pallas_call x12, Pallas kernels, call(): pl.pallas_call(run, out_shape=out_shape, in_specs=[pl.BlockSpec(memory_sp...  2.42 us
    ppermute x1, waiting for transfers between devices, other_core(): return lax.ppermute(x, 'sub', [(0, 1), (1, 0)])  1.57 us
    unnamed x8, local copies, waits for them, and re-layouts  1 us
  transfers between devices with their start and end apart: 13, of which 9 were waited for; matrix products, arithmetic and copies ran while one was open for 0% of the time, Pallas kernels for 3%

profile of v9, /device:TPU:0, one launch (start us, length us, event | category | flops | bytes accessed | tf_op | source)
XLA Modules:
  0.0 34.5 jit_solution(4399915965216156475)
XLA Ops:
  0.0 0.0 copy-start
  0.0 0.0 copy-start.1
  0.0 1.0 %copy-done.1 = bf16[64,2048]{1,0:T(8,128)(2,1)S(1)} copy-done((bf16[64,2048]{1,0:T(8,128)(2,1)S(1)}, bf16[64,2048]{1,0:T(8,128)(2,1)}, u32[]{:S(2)}) %copy-start.1) | copy-done | bytes 262168
  1.0 5.1 %collective-permute-start = (bf16[64,512]{1,0:T(8,128)(2,1)S(1)}, bf16[64,512]{1,0:T(8,128)(2,1)S(1)}, u32[]{:S(2)}, u32[]{:S(2)}) collective-permute-start(bf16[64,512]{1,0:T(8,128)(2,1)S(1)} %get-tuple-element.16), channel_id=1, source_target_pairs={{0,12},{4,8},{8,4},{12,0},{1,13},{5,9},{9,5},{13,1},{2,14},{6,10},... | collective-permute-start | bytes 196616 | tf_op jit(solution)/shard_map/ppermute | solution.py:223
  6.1 0.0 copy-done
  6.1 0.0 copy-start.2
  6.1 0.1 collective-permute-start.2
  6.2 2.4 %collective-permute-done.refs_3_.refs_2_ = bf16[64,512]{1,0:T(8,128)(2,1)S(1)} collective-permute-done((bf16[64,512]{1,0:T(8,128)(2,1)S(1)}, bf16[64,512]{1,0:T(8,128)(2,1)S(1)}, u32[]{:S(2)}, u32[]{:S(2)}) %collective-permute-start) | collective-permute-done | bytes 65568 | tf_op jit(solution)/shard_map/ppermute | solution.py:223
  8.6 0.0 copy-start.3
  8.6 4.2 %collective-permute-start.1 = (bf16[128,512]{1,0:T(8,128)(2,1)S(1)}, bf16[128,512]{1,0:T(8,128)(2,1)S(1)}, u32[]{:S(2)}, u32[]{:S(2)}) collective-permute-start(bf16[128,512]{1,0:T(8,128)(2,1)S(1)} %shard_map.39), channel_id=1, source_target_pairs={{0,4},{4,0},{8,12},{12,8},{1,5},{5,1},{9,13},{13,9},{2,6},{6,2},{1... | collective-permute-start | bytes 393224 | tf_op jit(solution)/shard_map/ppermute | solution.py:223
  12.9 0.0 copy-done.2
  12.9 0.0 copy-done.3
  12.9 0.3 shard_map.38.refs_4_.refs_0_
  13.1 1.3 %collective-permute-start.6 = (bf16[144,512]{1,0:T(8,128)(2,1)S(1)}, bf16[144,512]{1,0:T(8,128)(2,1)S(1)}, u32[]{:S(2)}, u32[]{:S(2)}) collective-permute-start(bf16[144,512]{1,0:T(8,128)(2,1)S(1)} %shard_map.38.refs_4_.refs_0_), channel_id=1, source_target_pairs={{0,2},{2,0},{1,3},{3,1},{4,6},{6,4},{5,7},{7,5},{8,10},{10,8},{9,1... | collective-permute-start | bytes 442376 | tf_op jit(solution)/shard_map/ppermute | solution.py:226
  14.4 0.8 %collective-permute-start.5 = (bf16[64,512]{1,0:T(8,128)(2,1)S(1)}, bf16[64,512]{1,0:T(8,128)(2,1)S(1)}, u32[]{:S(2)}, u32[]{:S(2)}) collective-permute-start(bf16[64,512]{1,0:T(8,128)(2,1)S(1)} %collective-permute-done.refs_3_.refs_2_), channel_id=1, source_target_pairs={{0,2},{2,0},{1,3},{3,1},{4,6},{6,4},{5,7},{7,5},{8,10},{10,8},{9,1... | collective-permute-start | bytes 196616 | tf_op jit(solution)/shard_map/ppermute | solution.py:226
  15.2 0.0 collective-permute-done.2.refs_0_.refs_1_
  15.2 1.3 %collective-permute-start.4 = (bf16[64,512]{1,0:T(8,128)(2,1)S(1)}, bf16[64,512]{1,0:T(8,128)(2,1)S(1)}, u32[]{:S(2)}, u32[]{:S(2)}) collective-permute-start(bf16[64,512]{1,0:T(8,128)(2,1)S(1)} %shard_map.42.refs_0_), channel_id=1, source_target_pairs={{0,2},{2,0},{1,3},{3,1},{4,6},{6,4},{5,7},{7,5},{8,10},{10,8},{9,1... | collective-permute-start | bytes 196616 | tf_op jit(solution)/shard_map/ppermute | solution.py:226
  16.5 0.0 collective-permute-done.1.refs_0_
  16.5 0.9 %collective-permute-start.7 = (bf16[64,512]{1,0:T(8,128)(2,1)S(1)}, bf16[64,512]{1,0:T(8,128)(2,1)S(1)}, u32[]{:S(2)}, u32[]{:S(2)}) collective-permute-start(bf16[64,512]{1,0:T(8,128)(2,1)S(1)} %shard_map.43.refs_6_), channel_id=1, source_target_pairs={{0,2},{2,0},{1,3},{3,1},{4,6},{6,4},{5,7},{7,5},{8,10},{10,8},{9,1... | collective-permute-start | bytes 196616 | tf_op jit(solution)/shard_map/ppermute | solution.py:226
  17.4 1.6 %collective-permute-start.3 = (bf16[64,512]{1,0:T(8,128)(2,1)S(1)}, bf16[64,512]{1,0:T(8,128)(2,1)S(1)}, u32[]{:S(2)}, u32[]{:S(2)}) collective-permute-start(bf16[64,512]{1,0:T(8,128)(2,1)S(1)} %shard_map.41), channel_id=1, source_target_pairs={{0,4},{4,0},{8,12},{12,8},{1,5},{5,1},{9,13},{13,9},{2,6},{6,2},{1... | collective-permute-start | bytes 196616 | tf_op jit(solution)/shard_map/ppermute | solution.py:223
  19.1 1.4 %collective-permute-done.5.refs_3_ = bf16[64,512]{1,0:T(8,128)(2,1)S(1)} collective-permute-done((bf16[64,512]{1,0:T(8,128)(2,1)S(1)}, bf16[64,512]{1,0:T(8,128)(2,1)S(1)}, u32[]{:S(2)}, u32[]{:S(2)}) %collective-permute-start.5) | collective-permute-done | bytes 65568 | tf_op jit(solution)/shard_map/ppermute | solution.py:226
  20.5 0.7 %collective-permute-done.4.refs_1_ = bf16[64,512]{1,0:T(8,128)(2,1)S(1)} collective-permute-done((bf16[64,512]{1,0:T(8,128)(2,1)S(1)}, bf16[64,512]{1,0:T(8,128)(2,1)S(1)}, u32[]{:S(2)}, u32[]{:S(2)}) %collective-permute-start.4) | collective-permute-done | bytes 65568 | tf_op jit(solution)/shard_map/ppermute | solution.py:226
  21.2 0.0 collective-permute-done.6.refs_5_.refs_2_
  21.2 0.7 %collective-permute-done.7.refs_7_ = bf16[64,512]{1,0:T(8,128)(2,1)S(1)} collective-permute-done((bf16[64,512]{1,0:T(8,128)(2,1)S(1)}, bf16[64,512]{1,0:T(8,128)(2,1)S(1)}, u32[]{:S(2)}, u32[]{:S(2)}) %collective-permute-start.7) | collective-permute-done | bytes 65568 | tf_op jit(solution)/shard_map/ppermute | solution.py:226
  21.9 0.5 %shard_map.44 = (f32[64,512]{1,0:T(8,128)S(1)}, bf16[64,512]{1,0:T(8,128)(2,1)S(1)}, bf16[64,512]{1,0:T(8,128)(2,1)S(1)}, bf16[64,512]{1,0:T(8,128)(2,1)S(1)}) custom-call(bf16[64,512]{1,0:T(8,128)(2,1)S(1)} %shard_map.42.refs_0_, bf16[64,512]{1,0:T(8,128)(2,1)S(1)} %collective-permute-done.4.refs_1_, ...), custom_call_target="tpu_custom_call" | custom-call | tf_op jit(solution)/shard_map/pallas_call | solution.py:22
  22.4 0.0 collective-permute-done.3.refs_2_
  22.4 1.3 %collective-permute-start.8 = (bf16[192,512]{1,0:T(8,128)(2,1)S(1)}, bf16[192,512]{1,0:T(8,128)(2,1)S(1)}, u32[]{:S(2)}, u32[]{:S(2)}) collective-permute-start(bf16[192,512]{1,0:T(8,128)(2,1)S(1)} %shard_map.45.refs_1_), channel_id=1, source_target_pairs={{0,2},{2,0},{1,3},{3,1},{4,6},{6,4},{5,7},{7,5},{8,10},{10,8},{9,1... | collective-permute-start | bytes 589832 | tf_op jit(solution)/shard_map/ppermute | solution.py:226
  23.7 1.5 %collective-permute-start.9 = (bf16[64,512]{1,0:T(8,128)(2,1)S(1)}, bf16[64,512]{1,0:T(8,128)(2,1)S(1)}, u32[]{:S(2)}, u32[]{:S(2)}) collective-permute-start(bf16[64,512]{1,0:T(8,128)(2,1)S(1)} %get-tuple-element.21), channel_id=1, source_target_pairs={{0,8},{4,12},{8,0},{12,4},{1,9},{5,13},{9,1},{13,5},{2,10},{6,14},... | collective-permute-start | bytes 196616 | tf_op jit(solution)/shard_map/ppermute | solution.py:223
  25.2 1.4 %collective-permute-start.10 = (bf16[64,512]{1,0:T(8,128)(2,1)S(1)}, bf16[64,512]{1,0:T(8,128)(2,1)S(1)}, u32[]{:S(2)}, u32[]{:S(2)}) collective-permute-start(bf16[64,512]{1,0:T(8,128)(2,1)S(1)} %get-tuple-element.22), channel_id=1, source_target_pairs={{0,12},{4,8},{8,4},{12,0},{1,13},{5,9},{9,5},{13,1},{2,14},{6,10},... | collective-permute-start | bytes 196616 | tf_op jit(solution)/shard_map/ppermute | solution.py:223
  26.6 0.6 %collective-permute-start.11 = (bf16[64,512]{1,0:T(8,128)(2,1)S(1)}, bf16[64,512]{1,0:T(8,128)(2,1)S(1)}, u32[]{:S(2)}, u32[]{:S(2)}) collective-permute-start(bf16[64,512]{1,0:T(8,128)(2,1)S(1)} %get-tuple-element.23), channel_id=1, source_target_pairs={{0,4},{4,0},{8,12},{12,8},{1,5},{5,1},{9,13},{13,9},{2,6},{6,2},{1... | collective-permute-start | bytes 196616 | tf_op jit(solution)/shard_map/ppermute | solution.py:223
  27.2 1.0 %collective-permute-done.8.refs_3_ = bf16[192,512]{1,0:T(8,128)(2,1)S(1)} collective-permute-done((bf16[192,512]{1,0:T(8,128)(2,1)S(1)}, bf16[192,512]{1,0:T(8,128)(2,1)S(1)}, u32[]{:S(2)}, u32[]{:S(2)}) %collective-permute-start.8) | collective-permute-done | bytes 196640 | tf_op jit(solution)/shard_map/ppermute | solution.py:226
  28.2 0.3 shard_map.46
  28.5 1.0 %collective-permute-done.9.refs_1_ = bf16[64,512]{1,0:T(8,128)(2,1)S(1)} collective-permute-done((bf16[64,512]{1,0:T(8,128)(2,1)S(1)}, bf16[64,512]{1,0:T(8,128)(2,1)S(1)}, u32[]{:S(2)}, u32[]{:S(2)}) %collective-permute-start.9) | collective-permute-done | bytes 65568 | tf_op jit(solution)/shard_map/ppermute | solution.py:223
  29.5 1.9 %collective-permute-done.10.refs_2_ = bf16[64,512]{1,0:T(8,128)(2,1)S(1)} collective-permute-done((bf16[64,512]{1,0:T(8,128)(2,1)S(1)}, bf16[64,512]{1,0:T(8,128)(2,1)S(1)}, u32[]{:S(2)}, u32[]{:S(2)}) %collective-permute-start.10) | collective-permute-done | bytes 65568 | tf_op jit(solution)/shard_map/ppermute | solution.py:223
  31.4 0.1 collective-permute-done.11.refs_4_
  31.6 0.1 shard_map.47
  31.7 0.1 collective-permute-start.12
  31.7 1.6 %collective-permute-done.12.refs_1_ = f32[144,512]{1,0:T(8,128)S(1)} collective-permute-done((f32[144,512]{1,0:T(8,128)S(1)}, f32[144,512]{1,0:T(8,128)S(1)}, u32[]{:S(2)}, u32[]{:S(2)}) %collective-permute-start.12) | collective-permute-done | bytes 294944 | tf_op jit(solution)/shard_map/ppermute | solution.py:229
  33.3 1.1 %shard_map.48 = f32[64,512]{1,0:T(8,128)} custom-call(f32[144,512]{1,0:T(8,128)S(1)} %get-tuple-element.24.refs_0_, f32[144,512]{1,0:T(8,128)S(1)} %collective-permute-done.12.refs_1_, f32[8,512]{1,0:T(8,128)S(1)} %get-tuple-element.25.refs_2_, bf16[64,512]{1,0:T(8,128)(2,1)S(1)} %copy-done, bf16[1,64]{1,0:T(2,128)(2,1)S(1)} %bitcast.2, ...), custom_call_target="tpu_custom_call" | custom-call | tf_op jit(solution)/shard_map/pallas_call | solution.py:22
  (7 shorter events, 0.1 us)
Async XLA Ops:
  0.0 6.1 %copy-start = (bf16[64,512]{1,0:T(8,128)(2,1)S(1)}, bf16[64,512]{1,0:T(8,128)(2,1)}, u32[]{:S(2)}) copy-start(bf16[64,512]{1,0:T(8,128)(2,1)} %refs_3_.1) | copy-start | bytes 196612
  0.0 1.0 %copy-start.1 = (bf16[64,2048]{1,0:T(8,128)(2,1)S(1)}, bf16[64,2048]{1,0:T(8,128)(2,1)}, u32[]{:S(2)}) copy-start(bf16[64,2048]{1,0:T(8,128)(2,1)} %refs_0_.5) | copy-start | bytes 786436
  1.0 7.6 %collective-permute-start = (bf16[64,512]{1,0:T(8,128)(2,1)S(1)}, bf16[64,512]{1,0:T(8,128)(2,1)S(1)}, u32[]{:S(2)}, u32[]{:S(2)}) collective-permute-start(bf16[64,512]{1,0:T(8,128)(2,1)S(1)} %get-tuple-element.16), channel_id=1, source_target_pairs={{0,12},{4,8},{8,4},{12,0},{1,13},{5,9},{9,5},{13,1},{2,14},{6,10},... | collective-permute-start | bytes 196616 | tf_op jit(solution)/shard_map/ppermute | solution.py:223
  6.1 6.8 %copy-start.2 = (bf16[64,2048]{1,0:T(8,128)(2,1)S(1)}, bf16[64,2048]{1,0:T(8,128)(2,1)}, u32[]{:S(2)}) copy-start(bf16[64,2048]{1,0:T(8,128)(2,1)} %refs_0_.5) | copy-start | bytes 786436
  6.1 9.1 %collective-permute-start.2 = (bf16[128,512]{1,0:T(8,128)(2,1)S(1)}, bf16[128,512]{1,0:T(8,128)(2,1)S(1)}, u32[]{:S(2)}, u32[]{:S(2)}) collective-permute-start(bf16[128,512]{1,0:T(8,128)(2,1)S(1)} %shard_map.40), channel_id=1, source_target_pairs={{0,8},{4,12},{8,0},{12,4},{1,9},{5,13},{9,1},{13,5},{2,10},{6,14},... | collective-permute-start | bytes 393224 | tf_op jit(solution)/shard_map/ppermute | solution.py:223
  8.6 4.2 %copy-start.3 = (bf16[64]{0:T(256)(128)(2,1)S(1)}, bf16[64]{0:T(256)(128)(2,1)}, u32[]{:S(2)}) copy-start(bf16[64]{0:T(256)(128)(2,1)} %param.5) | copy-start | bytes 388
  8.6 7.9 %collective-permute-start.1 = (bf16[128,512]{1,0:T(8,128)(2,1)S(1)}, bf16[128,512]{1,0:T(8,128)(2,1)S(1)}, u32[]{:S(2)}, u32[]{:S(2)}) collective-permute-start(bf16[128,512]{1,0:T(8,128)(2,1)S(1)} %shard_map.39), channel_id=1, source_target_pairs={{0,4},{4,0},{8,12},{12,8},{1,5},{5,1},{9,13},{13,9},{2,6},{6,2},{1... | collective-permute-start | bytes 393224 | tf_op jit(solution)/shard_map/ppermute | solution.py:223
  13.1 8.0 %collective-permute-start.6 = (bf16[144,512]{1,0:T(8,128)(2,1)S(1)}, bf16[144,512]{1,0:T(8,128)(2,1)S(1)}, u32[]{:S(2)}, u32[]{:S(2)}) collective-permute-start(bf16[144,512]{1,0:T(8,128)(2,1)S(1)} %shard_map.38.refs_4_.refs_0_), channel_id=1, source_target_pairs={{0,2},{2,0},{1,3},{3,1},{4,6},{6,4},{5,7},{7,5},{8,10},{10,8},{9,1... | collective-permute-start | bytes 442376 | tf_op jit(solution)/shard_map/ppermute | solution.py:226
  14.4 6.0 %collective-permute-start.5 = (bf16[64,512]{1,0:T(8,128)(2,1)S(1)}, bf16[64,512]{1,0:T(8,128)(2,1)S(1)}, u32[]{:S(2)}, u32[]{:S(2)}) collective-permute-start(bf16[64,512]{1,0:T(8,128)(2,1)S(1)} %collective-permute-done.refs_3_.refs_2_), channel_id=1, source_target_pairs={{0,2},{2,0},{1,3},{3,1},{4,6},{6,4},{5,7},{7,5},{8,10},{10,8},{9,1... | collective-permute-start | bytes 196616 | tf_op jit(solution)/shard_map/ppermute | solution.py:226
  15.2 5.9 %collective-permute-start.4 = (bf16[64,512]{1,0:T(8,128)(2,1)S(1)}, bf16[64,512]{1,0:T(8,128)(2,1)S(1)}, u32[]{:S(2)}, u32[]{:S(2)}) collective-permute-start(bf16[64,512]{1,0:T(8,128)(2,1)S(1)} %shard_map.42.refs_0_), channel_id=1, source_target_pairs={{0,2},{2,0},{1,3},{3,1},{4,6},{6,4},{5,7},{7,5},{8,10},{10,8},{9,1... | collective-permute-start | bytes 196616 | tf_op jit(solution)/shard_map/ppermute | solution.py:226
  16.5 5.3 %collective-permute-start.7 = (bf16[64,512]{1,0:T(8,128)(2,1)S(1)}, bf16[64,512]{1,0:T(8,128)(2,1)S(1)}, u32[]{:S(2)}, u32[]{:S(2)}) collective-permute-start(bf16[64,512]{1,0:T(8,128)(2,1)S(1)} %shard_map.43.refs_6_), channel_id=1, source_target_pairs={{0,2},{2,0},{1,3},{3,1},{4,6},{6,4},{5,7},{7,5},{8,10},{10,8},{9,1... | collective-permute-start | bytes 196616 | tf_op jit(solution)/shard_map/ppermute | solution.py:226
  17.4 5.0 %collective-permute-start.3 = (bf16[64,512]{1,0:T(8,128)(2,1)S(1)}, bf16[64,512]{1,0:T(8,128)(2,1)S(1)}, u32[]{:S(2)}, u32[]{:S(2)}) collective-permute-start(bf16[64,512]{1,0:T(8,128)(2,1)S(1)} %shard_map.41), channel_id=1, source_target_pairs={{0,4},{4,0},{8,12},{12,8},{1,5},{5,1},{9,13},{13,9},{2,6},{6,2},{1... | collective-permute-start | bytes 196616 | tf_op jit(solution)/shard_map/ppermute | solution.py:223
  22.4 5.7 %collective-permute-start.8 = (bf16[192,512]{1,0:T(8,128)(2,1)S(1)}, bf16[192,512]{1,0:T(8,128)(2,1)S(1)}, u32[]{:S(2)}, u32[]{:S(2)}) collective-permute-start(bf16[192,512]{1,0:T(8,128)(2,1)S(1)} %shard_map.45.refs_1_), channel_id=1, source_target_pairs={{0,2},{2,0},{1,3},{3,1},{4,6},{6,4},{5,7},{7,5},{8,10},{10,8},{9,1... | collective-permute-start | bytes 589832 | tf_op jit(solution)/shard_map/ppermute | solution.py:226
  23.7 5.8 %collective-permute-start.9 = (bf16[64,512]{1,0:T(8,128)(2,1)S(1)}, bf16[64,512]{1,0:T(8,128)(2,1)S(1)}, u32[]{:S(2)}, u32[]{:S(2)}) collective-permute-start(bf16[64,512]{1,0:T(8,128)(2,1)S(1)} %get-tuple-element.21), channel_id=1, source_target_pairs={{0,8},{4,12},{8,0},{12,4},{1,9},{5,13},{9,1},{13,5},{2,10},{6,14},... | collective-permute-start | bytes 196616 | tf_op jit(solution)/shard_map/ppermute | solution.py:223
  25.2 6.2 %collective-permute-start.10 = (bf16[64,512]{1,0:T(8,128)(2,1)S(1)}, bf16[64,512]{1,0:T(8,128)(2,1)S(1)}, u32[]{:S(2)}, u32[]{:S(2)}) collective-permute-start(bf16[64,512]{1,0:T(8,128)(2,1)S(1)} %get-tuple-element.22), channel_id=1, source_target_pairs={{0,12},{4,8},{8,4},{12,0},{1,13},{5,9},{9,5},{13,1},{2,14},{6,10},... | collective-permute-start | bytes 196616 | tf_op jit(solution)/shard_map/ppermute | solution.py:223
  26.6 5.0 %collective-permute-start.11 = (bf16[64,512]{1,0:T(8,128)(2,1)S(1)}, bf16[64,512]{1,0:T(8,128)(2,1)S(1)}, u32[]{:S(2)}, u32[]{:S(2)}) collective-permute-start(bf16[64,512]{1,0:T(8,128)(2,1)S(1)} %get-tuple-element.23), channel_id=1, source_target_pairs={{0,4},{4,0},{8,12},{12,8},{1,5},{5,1},{9,13},{13,9},{2,6},{6,2},{1... | collective-permute-start | bytes 196616 | tf_op jit(solution)/shard_map/ppermute | solution.py:223
  31.7 1.7 %collective-permute-start.12 = (f32[144,512]{1,0:T(8,128)S(1)}, f32[144,512]{1,0:T(8,128)S(1)}, u32[]{:S(2)}, u32[]{:S(2)}) collective-permute-start(f32[144,512]{1,0:T(8,128)S(1)} %get-tuple-element.24.refs_0_), channel_id=1, source_target_pairs={{0,1},{1,0},{2,3},{3,2},{4,5},{5,4},{6,7},{7,6},{8,9},{9,8},{10,11... | collective-permute-start | bytes 884744 | tf_op jit(solution)/shard_map/ppermute | solution.py:229

commit v10 on v9

--- a/solution.py
+++ b/solution.py
@@ -239,26 +239,27 @@
     order = list(range(middle, nrow)) + list(range(middle))
     riders = (1, middle)
     cuts = call(functools.partial(cut_kernel, nrow), [sds((rows, part), BF16)] * (nrow - 1), [teacher])
-    last = nrow - 1
-    came, landed = {last: along_row(cuts[last - 1], last)}, ()
-    for k in [k for k in order if k not in (0, 1, last)] + [1]:
-        leaving = cuts[k - 1]
-        if k in riders:
-            leaving = call(ride_kernel, sds((rows + high, half), BF16), [student, leaving], after=landed)
-            landed = (came[last],)
-        came[k] = along_row(leaving, k)
+    came = {}
+    for k in order:
+        if k:
+            leaving = cuts[k - 1]
+            if k in riders:
+                leaving = call(ride_kernel, sds((rows + high, half), BF16), [student, leaving])
+            came[k] = along_row(leaving, k)
     own = call(
         functools.partial(own_kernel, nrow),
         sds((rows + TAIL + high, half), BF16),
         [teacher, student, scale],
         after=[came[nrow - 1]],
     )
-    columns = {0: with_columns(own)}
-    for k in range(1, nrow):
-        piece = came[k]
+    columns, taken = {0: with_columns(own)}, ()
+    for k in order:
+        piece = came.get(k)
         if k in riders:
-            piece = call(functools.partial(take_kernel, rows), sds((rows, part), BF16), [piece])
-        columns[k] = with_columns(piece)
+            piece = call(functools.partial(take_kernel, rows), sds((rows, part), BF16), [piece], after=taken)
+            taken = (piece,)
+        if k:
+            columns[k] = with_columns(piece)
     partial = call(
         functools.partial(gram_kernel, nrow, ncol, rows, order),
         [sds((rows, batch), BF16 if k else F32) for k in range(nrow)],
@@ -276,8 +277,8 @@
         got_keys += [n ^ k for n in keys[first:]]
         stack, spans, keys = stack + got[-1:], spans + [(0, len(keys) * rows)], keys + [n ^ k for n in keys]
         k //= 2
-    rest = pack([near, far] + got, [(0, rows)] * 2 + [(0, g.shape[0]) for g in got], after=[partial[0]])
-    raw_keys = [[0], [1, middle] + got_keys]
+    rest = pack([far, near] + got, [(0, rows)] * 2 + [(0, g.shape[0]) for g in got], after=[partial[0]])
+    raw_keys = [[0], [middle, 1] + got_keys]
     sources = [columns[0], with_columns(rest)]
     raw_refs = [x[c] for c in range(ncol) for x in sources]
     raw_gram, *all_raw = call(

time: 34.6 us -> 33.7 us (0.974)
  starting transfers between devices: 20.1 us -> 16.8 us
  waiting for transfers between devices: 10.8 us -> 13.2 us
    ppermute x7, starting transfers between devices: 14.5 us -> 11 us  [along_row(): return lax.ppermute(x, 'row', [(i, i ^ k) for i in range(nrow)])]
    ppermute x7, waiting for transfers between devices: 5.47 us -> 7.91 us  [along_row(): return lax.ppermute(x, 'row', [(i, i ^ k) for i in range(nrow)])]
where the time goes in v10:
time: 33.7 us; the launch traced here: 33.5 us
  starting transfers between devices  16.8 us (50%)
  waiting for transfers between devices  13.2 us (39%)
  Pallas kernels  2.43 us (7%)
  local copies, waits for them, and re-layouts  0.96 us (3%)
    ppermute x7, starting transfers between devices, along_row(): return lax.ppermute(x, 'row', [(i, i ^ k) for i in range(nrow)])  11 us
    ppermute x7, waiting for transfers between devices, along_row(): return lax.ppermute(x, 'row', [(i, i ^ k) for i in range(nrow)])  7.91 us
    ppermute x5, starting transfers between devices, along_col(): return lax.ppermute(x, 'col', [(i, (i - c) % ncol) for i in range(ncol)])  5.73 us
    ppermute x5, waiting for transfers between devices, along_col(): return lax.ppermute(x, 'col', [(i, (i - c) % ncol) for i in range(ncol)])  3.75 us
    pallas_call x12, Pallas kernels, call(): pl.pallas_call(run, out_shape=out_shape, in_specs=[pl.BlockSpec(memory_sp...  2.43 us
    ppermute x1, waiting for transfers between devices, other_core(): return lax.ppermute(x, 'sub', [(0, 1), (1, 0)])  1.57 us
    unnamed x8, local copies, waits for them, and re-layouts  0.96 us
  transfers between devices with their start and end apart: 13, of which 9 were waited for; matrix products, arithmetic and copies ran while one was open for 0% of the time, Pallas kernels for 3%

profile of v10, /device:TPU:0, one launch (start us, length us, event | category | flops | bytes accessed | tf_op | source)
XLA Modules:
  0.0 33.5 jit_solution(8834154298590589570)
XLA Ops:
  0.0 0.0 copy-start
  0.0 0.9 %copy-done = bf16[64,2048]{1,0:T(8,128)(2,1)S(1)} copy-done((bf16[64,2048]{1,0:T(8,128)(2,1)S(1)}, bf16[64,2048]{1,0:T(8,128)(2,1)}, u32[]{:S(2)}) %copy-start) | copy-done | bytes 262168
  1.0 0.0 copy-start.2
  1.0 5.1 %collective-permute-start = (bf16[64,512]{1,0:T(8,128)(2,1)S(1)}, bf16[64,512]{1,0:T(8,128)(2,1)S(1)}, u32[]{:S(2)}, u32[]{:S(2)}) collective-permute-start(bf16[64,512]{1,0:T(8,128)(2,1)S(1)} %get-tuple-element.16), channel_id=1, source_target_pairs={{0,12},{4,8},{8,4},{12,0},{1,13},{5,9},{9,5},{13,1},{2,14},{6,10},... | collective-permute-start | bytes 196616 | tf_op jit(solution)/shard_map/ppermute | solution.py:223
  6.1 0.0 copy-done.2
  6.1 0.0 copy-start.1
  6.1 0.1 collective-permute-start.1
  6.2 0.0 copy-start.3
  6.2 1.4 %collective-permute-start.2 = (bf16[128,512]{1,0:T(8,128)(2,1)S(1)}, bf16[128,512]{1,0:T(8,128)(2,1)S(1)}, u32[]{:S(2)}, u32[]{:S(2)}) collective-permute-start(bf16[128,512]{1,0:T(8,128)(2,1)S(1)} %shard_map.40), channel_id=1, source_target_pairs={{0,4},{4,0},{8,12},{12,8},{1,5},{5,1},{9,13},{13,9},{2,6},{6,2},{1... | collective-permute-start | bytes 393224 | tf_op jit(solution)/shard_map/ppermute | solution.py:223
  7.6 1.0 %collective-permute-done.refs_3_.refs_2_ = bf16[64,512]{1,0:T(8,128)(2,1)S(1)} collective-permute-done((bf16[64,512]{1,0:T(8,128)(2,1)S(1)}, bf16[64,512]{1,0:T(8,128)(2,1)S(1)}, u32[]{:S(2)}, u32[]{:S(2)}) %collective-permute-start) | collective-permute-done | bytes 65568 | tf_op jit(solution)/shard_map/ppermute | solution.py:223
  8.6 0.0 copy-done.1
  8.6 0.0 copy-done.3
  8.6 0.3 shard_map.38.refs_4_.refs_0_
  8.9 2.0 %collective-permute-start.6 = (bf16[144,512]{1,0:T(8,128)(2,1)S(1)}, bf16[144,512]{1,0:T(8,128)(2,1)S(1)}, u32[]{:S(2)}, u32[]{:S(2)}) collective-permute-start(bf16[144,512]{1,0:T(8,128)(2,1)S(1)} %shard_map.38.refs_4_.refs_0_), channel_id=1, source_target_pairs={{0,2},{2,0},{1,3},{3,1},{4,6},{6,4},{5,7},{7,5},{8,10},{10,8},{9,1... | collective-permute-start | bytes 442376 | tf_op jit(solution)/shard_map/ppermute | solution.py:226
  10.9 0.1 collective-permute-start.5
  10.9 3.5 %collective-permute-done.1.refs_0_ = bf16[128,512]{1,0:T(8,128)(2,1)S(1)} collective-permute-done((bf16[128,512]{1,0:T(8,128)(2,1)S(1)}, bf16[128,512]{1,0:T(8,128)(2,1)S(1)}, u32[]{:S(2)}, u32[]{:S(2)}) %collective-permute-start.1) | collective-permute-done | bytes 131104 | tf_op jit(solution)/shard_map/ppermute | solution.py:223
  14.5 0.0 collective-permute-done.2.refs_0_.refs_1_
  14.5 1.6 %collective-permute-start.7 = (bf16[64,512]{1,0:T(8,128)(2,1)S(1)}, bf16[64,512]{1,0:T(8,128)(2,1)S(1)}, u32[]{:S(2)}, u32[]{:S(2)}) collective-permute-start(bf16[64,512]{1,0:T(8,128)(2,1)S(1)} %shard_map.43.refs_6_), channel_id=1, source_target_pairs={{0,2},{2,0},{1,3},{3,1},{4,6},{6,4},{5,7},{7,5},{8,10},{10,8},{9,1... | collective-permute-start | bytes 196616 | tf_op jit(solution)/shard_map/ppermute | solution.py:226
  16.1 0.5 %collective-permute-start.4 = (bf16[64,512]{1,0:T(8,128)(2,1)S(1)}, bf16[64,512]{1,0:T(8,128)(2,1)S(1)}, u32[]{:S(2)}, u32[]{:S(2)}) collective-permute-start(bf16[64,512]{1,0:T(8,128)(2,1)S(1)} %shard_map.42.refs_1_.refs_0_), channel_id=1, source_target_pairs={{0,2},{2,0},{1,3},{3,1},{4,6},{6,4},{5,7},{7,5},{8,10},{10,8},{9,1... | collective-permute-start | bytes 196616 | tf_op jit(solution)/shard_map/ppermute | solution.py:226
  16.6 1.0 %collective-permute-start.3 = (bf16[64,512]{1,0:T(8,128)(2,1)S(1)}, bf16[64,512]{1,0:T(8,128)(2,1)S(1)}, u32[]{:S(2)}, u32[]{:S(2)}) collective-permute-start(bf16[64,512]{1,0:T(8,128)(2,1)S(1)} %shard_map.41), channel_id=1, source_target_pairs={{0,4},{4,0},{8,12},{12,8},{1,5},{5,1},{9,13},{13,9},{2,6},{6,2},{1... | collective-permute-start | bytes 196616 | tf_op jit(solution)/shard_map/ppermute | solution.py:223
  17.6 0.0 collective-permute-done.5.refs_3_
  17.6 1.8 %collective-permute-done.7.refs_7_ = bf16[64,512]{1,0:T(8,128)(2,1)S(1)} collective-permute-done((bf16[64,512]{1,0:T(8,128)(2,1)S(1)}, bf16[64,512]{1,0:T(8,128)(2,1)S(1)}, u32[]{:S(2)}, u32[]{:S(2)}) %collective-permute-start.7) | collective-permute-done | bytes 65568 | tf_op jit(solution)/shard_map/ppermute | solution.py:226
  19.4 0.9 %collective-permute-done.4.refs_1_ = bf16[64,512]{1,0:T(8,128)(2,1)S(1)} collective-permute-done((bf16[64,512]{1,0:T(8,128)(2,1)S(1)}, bf16[64,512]{1,0:T(8,128)(2,1)S(1)}, u32[]{:S(2)}, u32[]{:S(2)}) %collective-permute-start.4) | collective-permute-done | bytes 65568 | tf_op jit(solution)/shard_map/ppermute | solution.py:226
  20.3 0.0 collective-permute-done.6.refs_5_.refs_2_
  20.4 0.5 %shard_map.44 = (f32[64,512]{1,0:T(8,128)S(1)}, bf16[64,512]{1,0:T(8,128)(2,1)S(1)}, bf16[64,512]{1,0:T(8,128)(2,1)S(1)}, bf16[64,512]{1,0:T(8,128)(2,1)S(1)}) custom-call(bf16[64,512]{1,0:T(8,128)(2,1)S(1)} %shard_map.42.refs_1_.refs_0_, bf16[64,512]{1,0:T(8,128)(2,1)S(1)} %collective-permute-done.4.refs_1_, ...), custom_call_target="tpu_custom_call" | custom-call | tf_op jit(solution)/shard_map/pallas_call | solution.py:22
  20.9 0.0 collective-permute-done.3.refs_2_
  20.9 1.5 %collective-permute-start.8 = (bf16[192,512]{1,0:T(8,128)(2,1)S(1)}, bf16[192,512]{1,0:T(8,128)(2,1)S(1)}, u32[]{:S(2)}, u32[]{:S(2)}) collective-permute-start(bf16[192,512]{1,0:T(8,128)(2,1)S(1)} %shard_map.45.refs_1_), channel_id=1, source_target_pairs={{0,2},{2,0},{1,3},{3,1},{4,6},{6,4},{5,7},{7,5},{8,10},{10,8},{9,1... | collective-permute-start | bytes 589832 | tf_op jit(solution)/shard_map/ppermute | solution.py:226
  22.5 1.3 %collective-permute-start.9 = (bf16[64,512]{1,0:T(8,128)(2,1)S(1)}, bf16[64,512]{1,0:T(8,128)(2,1)S(1)}, u32[]{:S(2)}, u32[]{:S(2)}) collective-permute-start(bf16[64,512]{1,0:T(8,128)(2,1)S(1)} %get-tuple-element.21), channel_id=1, source_target_pairs={{0,8},{4,12},{8,0},{12,4},{1,9},{5,13},{9,1},{13,5},{2,10},{6,14},... | collective-permute-start | bytes 196616 | tf_op jit(solution)/shard_map/ppermute | solution.py:223
  23.8 2.0 %collective-permute-start.10 = (bf16[64,512]{1,0:T(8,128)(2,1)S(1)}, bf16[64,512]{1,0:T(8,128)(2,1)S(1)}, u32[]{:S(2)}, u32[]{:S(2)}) collective-permute-start(bf16[64,512]{1,0:T(8,128)(2,1)S(1)} %get-tuple-element.22), channel_id=1, source_target_pairs={{0,12},{4,8},{8,4},{12,0},{1,13},{5,9},{9,5},{13,1},{2,14},{6,10},... | collective-permute-start | bytes 196616 | tf_op jit(solution)/shard_map/ppermute | solution.py:223
  25.8 0.1 collective-permute-start.11
  26.0 1.0 %collective-permute-done.8.refs_3_ = bf16[192,512]{1,0:T(8,128)(2,1)S(1)} collective-permute-done((bf16[192,512]{1,0:T(8,128)(2,1)S(1)}, bf16[192,512]{1,0:T(8,128)(2,1)S(1)}, u32[]{:S(2)}, u32[]{:S(2)}) %collective-permute-start.8) | collective-permute-done | bytes 196640 | tf_op jit(solution)/shard_map/ppermute | solution.py:226
  27.0 0.3 shard_map.46
  27.3 1.5 %collective-permute-done.9.refs_1_ = bf16[64,512]{1,0:T(8,128)(2,1)S(1)} collective-permute-done((bf16[64,512]{1,0:T(8,128)(2,1)S(1)}, bf16[64,512]{1,0:T(8,128)(2,1)S(1)}, u32[]{:S(2)}, u32[]{:S(2)}) %collective-permute-start.9) | collective-permute-done | bytes 65568 | tf_op jit(solution)/shard_map/ppermute | solution.py:223
  28.8 1.2 %collective-permute-done.10.refs_2_ = bf16[64,512]{1,0:T(8,128)(2,1)S(1)} collective-permute-done((bf16[64,512]{1,0:T(8,128)(2,1)S(1)}, bf16[64,512]{1,0:T(8,128)(2,1)S(1)}, u32[]{:S(2)}, u32[]{:S(2)}) %collective-permute-start.10) | collective-permute-done | bytes 65568 | tf_op jit(solution)/shard_map/ppermute | solution.py:223
  30.0 0.6 %collective-permute-done.11.refs_4_ = bf16[64,512]{1,0:T(8,128)(2,1)S(1)} collective-permute-done((bf16[64,512]{1,0:T(8,128)(2,1)S(1)}, bf16[64,512]{1,0:T(8,128)(2,1)S(1)}, u32[]{:S(2)}, u32[]{:S(2)}) %collective-permute-start.11) | collective-permute-done | bytes 65568 | tf_op jit(solution)/shard_map/ppermute | solution.py:223
  30.6 0.1 shard_map.47
  30.7 0.1 collective-permute-start.12
  30.8 1.6 %collective-permute-done.12.refs_1_ = f32[144,512]{1,0:T(8,128)S(1)} collective-permute-done((f32[144,512]{1,0:T(8,128)S(1)}, f32[144,512]{1,0:T(8,128)S(1)}, u32[]{:S(2)}, u32[]{:S(2)}) %collective-permute-start.12) | collective-permute-done | bytes 294944 | tf_op jit(solution)/shard_map/ppermute | solution.py:229
  32.4 1.1 %shard_map.48 = f32[64,512]{1,0:T(8,128)} custom-call(f32[144,512]{1,0:T(8,128)S(1)} %get-tuple-element.24.refs_0_, f32[144,512]{1,0:T(8,128)S(1)} %collective-permute-done.12.refs_1_, f32[8,512]{1,0:T(8,128)S(1)} %get-tuple-element.25.refs_2_, bf16[64,512]{1,0:T(8,128)(2,1)S(1)} %copy-done.2, bf16[1,64]{1,0:T(2,128)(2,1)S(1)} %bitcast.2, ...), custom_call_target="tpu_custom_call" | custom-call | tf_op jit(solution)/shard_map/pallas_call | solution.py:22
  (7 shorter events, 0.1 us)
Async XLA Ops:
  0.0 0.9 %copy-start = (bf16[64,2048]{1,0:T(8,128)(2,1)S(1)}, bf16[64,2048]{1,0:T(8,128)(2,1)}, u32[]{:S(2)}) copy-start(bf16[64,2048]{1,0:T(8,128)(2,1)} %refs_0_.5) | copy-start | bytes 786436
  1.0 5.1 %copy-start.2 = (bf16[64,512]{1,0:T(8,128)(2,1)S(1)}, bf16[64,512]{1,0:T(8,128)(2,1)}, u32[]{:S(2)}) copy-start(bf16[64,512]{1,0:T(8,128)(2,1)} %refs_3_.1) | copy-start | bytes 196612
  1.0 7.6 %collective-permute-start = (bf16[64,512]{1,0:T(8,128)(2,1)S(1)}, bf16[64,512]{1,0:T(8,128)(2,1)S(1)}, u32[]{:S(2)}, u32[]{:S(2)}) collective-permute-start(bf16[64,512]{1,0:T(8,128)(2,1)S(1)} %get-tuple-element.16), channel_id=1, source_target_pairs={{0,12},{4,8},{8,4},{12,0},{1,13},{5,9},{9,5},{13,1},{2,14},{6,10},... | collective-permute-start | bytes 196616 | tf_op jit(solution)/shard_map/ppermute | solution.py:223
  6.1 2.5 %copy-start.1 = (bf16[64,2048]{1,0:T(8,128)(2,1)S(1)}, bf16[64,2048]{1,0:T(8,128)(2,1)}, u32[]{:S(2)}) copy-start(bf16[64,2048]{1,0:T(8,128)(2,1)} %refs_0_.5) | copy-start | bytes 786436
  6.1 8.4 %collective-permute-start.1 = (bf16[128,512]{1,0:T(8,128)(2,1)S(1)}, bf16[128,512]{1,0:T(8,128)(2,1)S(1)}, u32[]{:S(2)}, u32[]{:S(2)}) collective-permute-start(bf16[128,512]{1,0:T(8,128)(2,1)S(1)} %shard_map.39), channel_id=1, source_target_pairs={{0,8},{4,12},{8,0},{12,4},{1,9},{5,13},{9,1},{13,5},{2,10},{6,14},... | collective-permute-start | bytes 393224 | tf_op jit(solution)/shard_map/ppermute | solution.py:223
  6.2 2.4 %copy-start.3 = (bf16[64]{0:T(256)(128)(2,1)S(1)}, bf16[64]{0:T(256)(128)(2,1)}, u32[]{:S(2)}) copy-start(bf16[64]{0:T(256)(128)(2,1)} %param.5) | copy-start | bytes 388
  6.2 8.3 %collective-permute-start.2 = (bf16[128,512]{1,0:T(8,128)(2,1)S(1)}, bf16[128,512]{1,0:T(8,128)(2,1)S(1)}, u32[]{:S(2)}, u32[]{:S(2)}) collective-permute-start(bf16[128,512]{1,0:T(8,128)(2,1)S(1)} %shard_map.40), channel_id=1, source_target_pairs={{0,4},{4,0},{8,12},{12,8},{1,5},{5,1},{9,13},{13,9},{2,6},{6,2},{1... | collective-permute-start | bytes 393224 | tf_op jit(solution)/shard_map/ppermute | solution.py:223
  8.9 11.5 %collective-permute-start.6 = (bf16[144,512]{1,0:T(8,128)(2,1)S(1)}, bf16[144,512]{1,0:T(8,128)(2,1)S(1)}, u32[]{:S(2)}, u32[]{:S(2)}) collective-permute-start(bf16[144,512]{1,0:T(8,128)(2,1)S(1)} %shard_map.38.refs_4_.refs_0_), channel_id=1, source_target_pairs={{0,2},{2,0},{1,3},{3,1},{4,6},{6,4},{5,7},{7,5},{8,10},{10,8},{9,1... | collective-permute-start | bytes 442376 | tf_op jit(solution)/shard_map/ppermute | solution.py:226
  10.9 6.8 %collective-permute-start.5 = (bf16[64,512]{1,0:T(8,128)(2,1)S(1)}, bf16[64,512]{1,0:T(8,128)(2,1)S(1)}, u32[]{:S(2)}, u32[]{:S(2)}) collective-permute-start(bf16[64,512]{1,0:T(8,128)(2,1)S(1)} %collective-permute-done.refs_3_.refs_2_), channel_id=1, source_target_pairs={{0,2},{2,0},{1,3},{3,1},{4,6},{6,4},{5,7},{7,5},{8,10},{10,8},{9,1... | collective-permute-start | bytes 196616 | tf_op jit(solution)/shard_map/ppermute | solution.py:226
  14.5 4.9 %collective-permute-start.7 = (bf16[64,512]{1,0:T(8,128)(2,1)S(1)}, bf16[64,512]{1,0:T(8,128)(2,1)S(1)}, u32[]{:S(2)}, u32[]{:S(2)}) collective-permute-start(bf16[64,512]{1,0:T(8,128)(2,1)S(1)} %shard_map.43.refs_6_), channel_id=1, source_target_pairs={{0,2},{2,0},{1,3},{3,1},{4,6},{6,4},{5,7},{7,5},{8,10},{10,8},{9,1... | collective-permute-start | bytes 196616 | tf_op jit(solution)/shard_map/ppermute | solution.py:226
  16.1 4.3 %collective-permute-start.4 = (bf16[64,512]{1,0:T(8,128)(2,1)S(1)}, bf16[64,512]{1,0:T(8,128)(2,1)S(1)}, u32[]{:S(2)}, u32[]{:S(2)}) collective-permute-start(bf16[64,512]{1,0:T(8,128)(2,1)S(1)} %shard_map.42.refs_1_.refs_0_), channel_id=1, source_target_pairs={{0,2},{2,0},{1,3},{3,1},{4,6},{6,4},{5,7},{7,5},{8,10},{10,8},{9,1... | collective-permute-start | bytes 196616 | tf_op jit(solution)/shard_map/ppermute | solution.py:226
  16.6 4.3 %collective-permute-start.3 = (bf16[64,512]{1,0:T(8,128)(2,1)S(1)}, bf16[64,512]{1,0:T(8,128)(2,1)S(1)}, u32[]{:S(2)}, u32[]{:S(2)}) collective-permute-start(bf16[64,512]{1,0:T(8,128)(2,1)S(1)} %shard_map.41), channel_id=1, source_target_pairs={{0,4},{4,0},{8,12},{12,8},{1,5},{5,1},{9,13},{13,9},{2,6},{6,2},{1... | collective-permute-start | bytes 196616 | tf_op jit(solution)/shard_map/ppermute | solution.py:223
  20.9 6.1 %collective-permute-start.8 = (bf16[192,512]{1,0:T(8,128)(2,1)S(1)}, bf16[192,512]{1,0:T(8,128)(2,1)S(1)}, u32[]{:S(2)}, u32[]{:S(2)}) collective-permute-start(bf16[192,512]{1,0:T(8,128)(2,1)S(1)} %shard_map.45.refs_1_), channel_id=1, source_target_pairs={{0,2},{2,0},{1,3},{3,1},{4,6},{6,4},{5,7},{7,5},{8,10},{10,8},{9,1... | collective-permute-start | bytes 589832 | tf_op jit(solution)/shard_map/ppermute | solution.py:226
  22.5 6.3 %collective-permute-start.9 = (bf16[64,512]{1,0:T(8,128)(2,1)S(1)}, bf16[64,512]{1,0:T(8,128)(2,1)S(1)}, u32[]{:S(2)}, u32[]{:S(2)}) collective-permute-start(bf16[64,512]{1,0:T(8,128)(2,1)S(1)} %get-tuple-element.21), channel_id=1, source_target_pairs={{0,8},{4,12},{8,0},{12,4},{1,9},{5,13},{9,1},{13,5},{2,10},{6,14},... | collective-permute-start | bytes 196616 | tf_op jit(solution)/shard_map/ppermute | solution.py:223
  23.8 6.2 %collective-permute-start.10 = (bf16[64,512]{1,0:T(8,128)(2,1)S(1)}, bf16[64,512]{1,0:T(8,128)(2,1)S(1)}, u32[]{:S(2)}, u32[]{:S(2)}) collective-permute-start(bf16[64,512]{1,0:T(8,128)(2,1)S(1)} %get-tuple-element.22), channel_id=1, source_target_pairs={{0,12},{4,8},{8,4},{12,0},{1,13},{5,9},{9,5},{13,1},{2,14},{6,10},... | collective-permute-start | bytes 196616 | tf_op jit(solution)/shard_map/ppermute | solution.py:223
  25.8 4.8 %collective-permute-start.11 = (bf16[64,512]{1,0:T(8,128)(2,1)S(1)}, bf16[64,512]{1,0:T(8,128)(2,1)S(1)}, u32[]{:S(2)}, u32[]{:S(2)}) collective-permute-start(bf16[64,512]{1,0:T(8,128)(2,1)S(1)} %get-tuple-element.23), channel_id=1, source_target_pairs={{0,4},{4,0},{8,12},{12,8},{1,5},{5,1},{9,13},{13,9},{2,6},{6,2},{1... | collective-permute-start | bytes 196616 | tf_op jit(solution)/shard_map/ppermute | solution.py:223
  30.7 1.7 %collective-permute-start.12 = (f32[144,512]{1,0:T(8,128)S(1)}, f32[144,512]{1,0:T(8,128)S(1)}, u32[]{:S(2)}, u32[]{:S(2)}) collective-permute-start(f32[144,512]{1,0:T(8,128)S(1)} %get-tuple-element.24.refs_0_), channel_id=1, source_target_pairs={{0,1},{1,0},{2,3},{3,2},{4,5},{5,4},{6,7},{7,6},{8,9},{9,8},{10,11... | collective-permute-start | bytes 884744 | tf_op jit(solution)/shard_map/ppermute | solution.py:229

commit v11 on v10

--- a/solution.py
+++ b/solution.py
@@ -237,7 +237,7 @@
 
     middle, high = nrow // 2, rows * part // half
     order = list(range(middle, nrow)) + list(range(middle))
-    riders = (1, middle)
+    riders = (1,)
     cuts = call(functools.partial(cut_kernel, nrow), [sds((rows, part), BF16)] * (nrow - 1), [teacher])
     came = {}
     for k in order:
@@ -250,7 +250,7 @@
         functools.partial(own_kernel, nrow),
         sds((rows + TAIL + high, half), BF16),
         [teacher, student, scale],
-        after=[came[nrow - 1]],
+        after=[came[n] for n in (nrow - 1,)],
     )
     columns, taken = {0: with_columns(own)}, ()
     for k in order:
@@ -268,17 +268,13 @@
     )
     returned = {k: along_row(partial[k], k) if k else partial[0] for k in order}
 
-    near, far = came[1], came[middle]
-    stack, keys, k, spans, got, got_keys = [student, far], [0, middle], middle // 2, [(0, rows)] * 2, [], []
-    while k:
-        first = 1 if k == 1 else 0
-        sent = pack(stack[first:], spans[first:])
-        got.append(along_row(sent, k))
-        got_keys += [n ^ k for n in keys[first:]]
-        stack, spans, keys = stack + got[-1:], spans + [(0, len(keys) * rows)], keys + [n ^ k for n in keys]
-        k //= 2
-    rest = pack([far, near] + got, [(0, rows)] * 2 + [(0, g.shape[0]) for g in got], after=[partial[0]])
-    raw_keys = [[0], [middle, 1] + got_keys]
+    stack, spans, keys, k = [student, came[1]], [(0, rows)] * 2, [0, 1], 2
+    while k < nrow:
+        sent = pack(stack, spans, after=[came[n] for n in (middle, nrow - 1)] if k == 2 else ())
+        stack, spans = stack + [along_row(sent, k)], spans + [(0, len(keys) * rows)]
+        keys, k = keys + [n ^ k for n in keys], 2 * k
+    rest = pack(stack[1:], spans[1:], after=[partial[0]])
+    raw_keys = [[0], keys[1:]]
     sources = [columns[0], with_columns(rest)]
     raw_refs = [x[c] for c in range(ncol) for x in sources]
     raw_gram, *all_raw = call(

time: 33.7 us -> 35 us (1.039)
  waiting for transfers between devices: 13.2 us -> 15 us
  starting transfers between devices: 16.8 us -> 16.3 us
    ppermute x5, waiting for transfers between devices: 3.75 us -> 5.45 us  [along_col(): return lax.ppermute(x, 'col', [(i, (i - c) % ncol) for i in range(ncol)])]
    ppermute x5, starting transfers between devices: 5.73 us -> 5.09 us  [along_col(): return lax.ppermute(x, 'col', [(i, (i - c) % ncol) for i in range(ncol)])]
    pallas_call x12 -> x10, Pallas kernels: 2.43 us -> 2.41 us  [call(): pl.pallas_call(run, out_shape=out_shape, in_specs=[pl.BlockSpec(memory_sp...]
where the time goes in v11:
time: 35 us; the launch traced here: 34.8 us
  starting transfers between devices  16.3 us (47%)
  waiting for transfers between devices  15 us (43%)
  Pallas kernels  2.41 us (7%)
  local copies, waits for them, and re-layouts  0.99 us (3%)
    ppermute x7, starting transfers between devices, along_row(): return lax.ppermute(x, 'row', [(i, i ^ k) for i in range(nrow)])  11.2 us
    ppermute x7, waiting for transfers between devices, along_row(): return lax.ppermute(x, 'row', [(i, i ^ k) for i in range(nrow)])  7.99 us
    ppermute x5, waiting for transfers between devices, along_col(): return lax.ppermute(x, 'col', [(i, (i - c) % ncol) for i in range(ncol)])  5.45 us
    ppermute x5, starting transfers between devices, along_col(): return lax.ppermute(x, 'col', [(i, (i - c) % ncol) for i in range(ncol)])  5.09 us
    pallas_call x10, Pallas kernels, call(): pl.pallas_call(run, out_shape=out_shape, in_specs=[pl.BlockSpec(memory_sp...  2.41 us
    ppermute x1, waiting for transfers between devices, other_core(): return lax.ppermute(x, 'sub', [(0, 1), (1, 0)])  1.57 us
    unnamed x8, local copies, waits for them, and re-layouts  0.99 us
  transfers between devices with their start and end apart: 13, of which 9 were waited for; matrix products, arithmetic and copies ran while one was open for 0% of the time, Pallas kernels for 3%

profile of v11, /device:TPU:0, one launch (start us, length us, event | category | flops | bytes accessed | tf_op | source)
XLA Modules:
  0.0 34.8 jit_solution(2416566755443902216)
XLA Ops:
  0.0 0.0 copy-start
  0.0 0.0 copy-start.1
  0.0 1.0 %copy-done.1 = bf16[64,2048]{1,0:T(8,128)(2,1)S(1)} copy-done((bf16[64,2048]{1,0:T(8,128)(2,1)S(1)}, bf16[64,2048]{1,0:T(8,128)(2,1)}, u32[]{:S(2)}) %copy-start.1) | copy-done | bytes 262168
  1.0 0.0 copy-start.2
  1.0 0.0 copy-done
  1.0 3.1 %collective-permute-start.1 = (bf16[128,512]{1,0:T(8,128)(2,1)S(1)}, bf16[128,512]{1,0:T(8,128)(2,1)S(1)}, u32[]{:S(2)}, u32[]{:S(2)}) collective-permute-start(bf16[128,512]{1,0:T(8,128)(2,1)S(1)} %shard_map.39), channel_id=1, source_target_pairs={{0,4},{4,0},{8,12},{12,8},{1,5},{5,1},{9,13},{13,9},{2,6},{6,2},{1... | collective-permute-start | bytes 393224 | tf_op jit(solution)/shard_map/ppermute | solution.py:223
  4.1 2.5 %collective-permute-start = (bf16[64,512]{1,0:T(8,128)(2,1)S(1)}, bf16[64,512]{1,0:T(8,128)(2,1)S(1)}, u32[]{:S(2)}, u32[]{:S(2)}) collective-permute-start(bf16[64,512]{1,0:T(8,128)(2,1)S(1)} %get-tuple-element.16), channel_id=1, source_target_pairs={{0,12},{4,8},{8,4},{12,0},{1,13},{5,9},{9,5},{13,1},{2,14},{6,10},... | collective-permute-start | bytes 196616 | tf_op jit(solution)/shard_map/ppermute | solution.py:223
  6.6 0.0 copy-start.3
  6.6 0.1 collective-permute-start.2
  6.7 5.3 %collective-permute-done.refs_3_.refs_2_ = bf16[64,512]{1,0:T(8,128)(2,1)S(1)} collective-permute-done((bf16[64,512]{1,0:T(8,128)(2,1)S(1)}, bf16[64,512]{1,0:T(8,128)(2,1)S(1)}, u32[]{:S(2)}, u32[]{:S(2)}) %collective-permute-start) | collective-permute-done | bytes 65568 | tf_op jit(solution)/shard_map/ppermute | solution.py:223
  12.0 0.0 copy-done.2
  12.0 0.0 copy-done.3
  12.0 0.3 shard_map.38.refs_4_.refs_0_
  12.3 1.6 %collective-permute-start.6 = (bf16[144,512]{1,0:T(8,128)(2,1)S(1)}, bf16[144,512]{1,0:T(8,128)(2,1)S(1)}, u32[]{:S(2)}, u32[]{:S(2)}) collective-permute-start(bf16[144,512]{1,0:T(8,128)(2,1)S(1)} %shard_map.38.refs_4_.refs_0_), channel_id=1, source_target_pairs={{0,2},{2,0},{1,3},{3,1},{4,6},{6,4},{5,7},{7,5},{8,10},{10,8},{9,1... | collective-permute-start | bytes 442376 | tf_op jit(solution)/shard_map/ppermute | solution.py:226
  13.8 0.0 collective-permute-done.2.refs_2_.refs_0_
  13.8 0.0 collective-permute-done.1.refs_1_.refs_0_
  13.9 2.0 %collective-permute-start.3 = (bf16[128,512]{1,0:T(8,128)(2,1)S(1)}, bf16[128,512]{1,0:T(8,128)(2,1)S(1)}, u32[]{:S(2)}, u32[]{:S(2)}) collective-permute-start(bf16[128,512]{1,0:T(8,128)(2,1)S(1)} %shard_map.40), channel_id=1, source_target_pairs={{0,8},{4,12},{8,0},{12,4},{1,9},{5,13},{9,1},{13,5},{2,10},{6,14},... | collective-permute-start | bytes 393224 | tf_op jit(solution)/shard_map/ppermute | solution.py:223
  15.9 0.5 %collective-permute-start.5 = (bf16[64,512]{1,0:T(8,128)(2,1)S(1)}, bf16[64,512]{1,0:T(8,128)(2,1)S(1)}, u32[]{:S(2)}, u32[]{:S(2)}) collective-permute-start(bf16[64,512]{1,0:T(8,128)(2,1)S(1)} %collective-permute-done.refs_3_.refs_2_), channel_id=1, source_target_pairs={{0,2},{2,0},{1,3},{3,1},{4,6},{6,4},{5,7},{7,5},{8,10},{10,8},{9,1... | collective-permute-start | bytes 196616 | tf_op jit(solution)/shard_map/ppermute | solution.py:226
  16.4 1.5 %collective-permute-start.4 = (bf16[64,512]{1,0:T(8,128)(2,1)S(1)}, bf16[64,512]{1,0:T(8,128)(2,1)S(1)}, u32[]{:S(2)}, u32[]{:S(2)}) collective-permute-start(bf16[64,512]{1,0:T(8,128)(2,1)S(1)} %collective-permute-done.2.refs_2_.refs_0_), channel_id=1, source_target_pairs={{0,2},{2,0},{1,3},{3,1},{4,6},{6,4},{5,7},{7,5},{8,10},{10,8},{9,1... | collective-permute-start | bytes 196616 | tf_op jit(solution)/shard_map/ppermute | solution.py:226
  17.9 0.5 %collective-permute-start.7 = (bf16[64,512]{1,0:T(8,128)(2,1)S(1)}, bf16[64,512]{1,0:T(8,128)(2,1)S(1)}, u32[]{:S(2)}, u32[]{:S(2)}) collective-permute-start(bf16[64,512]{1,0:T(8,128)(2,1)S(1)} %shard_map.41.refs_6_), channel_id=1, source_target_pairs={{0,2},{2,0},{1,3},{3,1},{4,6},{6,4},{5,7},{7,5},{8,10},{10,8},{9,1... | collective-permute-start | bytes 196616 | tf_op jit(solution)/shard_map/ppermute | solution.py:226
  18.4 1.7 %collective-permute-done.5.refs_3_ = bf16[64,512]{1,0:T(8,128)(2,1)S(1)} collective-permute-done((bf16[64,512]{1,0:T(8,128)(2,1)S(1)}, bf16[64,512]{1,0:T(8,128)(2,1)S(1)}, u32[]{:S(2)}, u32[]{:S(2)}) %collective-permute-start.5) | collective-permute-done | bytes 65568 | tf_op jit(solution)/shard_map/ppermute | solution.py:226
  20.1 0.7 %collective-permute-done.4.refs_1_ = bf16[64,512]{1,0:T(8,128)(2,1)S(1)} collective-permute-done((bf16[64,512]{1,0:T(8,128)(2,1)S(1)}, bf16[64,512]{1,0:T(8,128)(2,1)S(1)}, u32[]{:S(2)}, u32[]{:S(2)}) %collective-permute-start.4) | collective-permute-done | bytes 65568 | tf_op jit(solution)/shard_map/ppermute | solution.py:226
  20.8 1.8 %collective-permute-done.7.refs_7_ = bf16[64,512]{1,0:T(8,128)(2,1)S(1)} collective-permute-done((bf16[64,512]{1,0:T(8,128)(2,1)S(1)}, bf16[64,512]{1,0:T(8,128)(2,1)S(1)}, u32[]{:S(2)}, u32[]{:S(2)}) %collective-permute-start.7) | collective-permute-done | bytes 65568 | tf_op jit(solution)/shard_map/ppermute | solution.py:226
  22.6 0.0 collective-permute-done.6.refs_5_.refs_2_
  22.6 0.5 %shard_map.42 = (f32[64,512]{1,0:T(8,128)S(1)}, bf16[64,512]{1,0:T(8,128)(2,1)S(1)}, bf16[64,512]{1,0:T(8,128)(2,1)S(1)}, bf16[64,512]{1,0:T(8,128)(2,1)S(1)}) custom-call(bf16[64,512]{1,0:T(8,128)(2,1)S(1)} %collective-permute-done.2.refs_2_.refs_0_, bf16[64,512]{1,0:T(8,128)(2,1)S(1)} %collective-permute-done.4.refs_1_, ...), custom_call_target="tpu_custom_call" | custom-call | tf_op jit(solution)/shard_map/pallas_call | solution.py:22
  23.1 0.0 collective-permute-done.3.refs_1_
  23.2 1.0 %collective-permute-start.8 = (bf16[192,512]{1,0:T(8,128)(2,1)S(1)}, bf16[192,512]{1,0:T(8,128)(2,1)S(1)}, u32[]{:S(2)}, u32[]{:S(2)}) collective-permute-start(bf16[192,512]{1,0:T(8,128)(2,1)S(1)} %shard_map.43.refs_1_), channel_id=1, source_target_pairs={{0,2},{2,0},{1,3},{3,1},{4,6},{6,4},{5,7},{7,5},{8,10},{10,8},{9,1... | collective-permute-start | bytes 589832 | tf_op jit(solution)/shard_map/ppermute | solution.py:226
  24.2 0.9 %collective-permute-start.9 = (bf16[64,512]{1,0:T(8,128)(2,1)S(1)}, bf16[64,512]{1,0:T(8,128)(2,1)S(1)}, u32[]{:S(2)}, u32[]{:S(2)}) collective-permute-start(bf16[64,512]{1,0:T(8,128)(2,1)S(1)} %get-tuple-element.21), channel_id=1, source_target_pairs={{0,8},{4,12},{8,0},{12,4},{1,9},{5,13},{9,1},{13,5},{2,10},{6,14},... | collective-permute-start | bytes 196616 | tf_op jit(solution)/shard_map/ppermute | solution.py:223
  25.1 1.9 %collective-permute-start.10 = (bf16[64,512]{1,0:T(8,128)(2,1)S(1)}, bf16[64,512]{1,0:T(8,128)(2,1)S(1)}, u32[]{:S(2)}, u32[]{:S(2)}) collective-permute-start(bf16[64,512]{1,0:T(8,128)(2,1)S(1)} %get-tuple-element.22), channel_id=1, source_target_pairs={{0,12},{4,8},{8,4},{12,0},{1,13},{5,9},{9,5},{13,1},{2,14},{6,10},... | collective-permute-start | bytes 196616 | tf_op jit(solution)/shard_map/ppermute | solution.py:223
  27.0 0.7 %collective-permute-start.11 = (bf16[64,512]{1,0:T(8,128)(2,1)S(1)}, bf16[64,512]{1,0:T(8,128)(2,1)S(1)}, u32[]{:S(2)}, u32[]{:S(2)}) collective-permute-start(bf16[64,512]{1,0:T(8,128)(2,1)S(1)} %get-tuple-element.23), channel_id=1, source_target_pairs={{0,4},{4,0},{8,12},{12,8},{1,5},{5,1},{9,13},{13,9},{2,6},{6,2},{1... | collective-permute-start | bytes 196616 | tf_op jit(solution)/shard_map/ppermute | solution.py:223
  27.6 1.3 %collective-permute-done.8.refs_3_ = bf16[192,512]{1,0:T(8,128)(2,1)S(1)} collective-permute-done((bf16[192,512]{1,0:T(8,128)(2,1)S(1)}, bf16[192,512]{1,0:T(8,128)(2,1)S(1)}, u32[]{:S(2)}, u32[]{:S(2)}) %collective-permute-start.8) | collective-permute-done | bytes 196640 | tf_op jit(solution)/shard_map/ppermute | solution.py:226
  28.9 0.3 shard_map.44
  29.2 0.7 %collective-permute-done.9.refs_1_ = bf16[64,512]{1,0:T(8,128)(2,1)S(1)} collective-permute-done((bf16[64,512]{1,0:T(8,128)(2,1)S(1)}, bf16[64,512]{1,0:T(8,128)(2,1)S(1)}, u32[]{:S(2)}, u32[]{:S(2)}) %collective-permute-start.9) | collective-permute-done | bytes 65568 | tf_op jit(solution)/shard_map/ppermute | solution.py:223
  29.9 1.4 %collective-permute-done.10.refs_2_ = bf16[64,512]{1,0:T(8,128)(2,1)S(1)} collective-permute-done((bf16[64,512]{1,0:T(8,128)(2,1)S(1)}, bf16[64,512]{1,0:T(8,128)(2,1)S(1)}, u32[]{:S(2)}, u32[]{:S(2)}) %collective-permute-start.10) | collective-permute-done | bytes 65568 | tf_op jit(solution)/shard_map/ppermute | solution.py:223
  31.4 0.6 %collective-permute-done.11.refs_4_ = bf16[64,512]{1,0:T(8,128)(2,1)S(1)} collective-permute-done((bf16[64,512]{1,0:T(8,128)(2,1)S(1)}, bf16[64,512]{1,0:T(8,128)(2,1)S(1)}, u32[]{:S(2)}, u32[]{:S(2)}) %collective-permute-start.11) | collective-permute-done | bytes 65568 | tf_op jit(solution)/shard_map/ppermute | solution.py:223
  31.9 0.1 shard_map.45
  32.0 0.1 collective-permute-start.12
  32.1 1.6 %collective-permute-done.12.refs_1_ = f32[144,512]{1,0:T(8,128)S(1)} collective-permute-done((f32[144,512]{1,0:T(8,128)S(1)}, f32[144,512]{1,0:T(8,128)S(1)}, u32[]{:S(2)}, u32[]{:S(2)}) %collective-permute-start.12) | collective-permute-done | bytes 294944 | tf_op jit(solution)/shard_map/ppermute | solution.py:229
  33.7 1.1 %shard_map.46 = f32[64,512]{1,0:T(8,128)} custom-call(f32[144,512]{1,0:T(8,128)S(1)} %get-tuple-element.24.refs_0_, f32[144,512]{1,0:T(8,128)S(1)} %collective-permute-done.12.refs_1_, f32[8,512]{1,0:T(8,128)S(1)} %get-tuple-element.25.refs_2_, bf16[64,512]{1,0:T(8,128)(2,1)S(1)} %copy-done, bf16[1,64]{1,0:T(2,128)(2,1)S(1)} %bitcast.2, ...), custom_call_target="tpu_custom_call" | custom-call | tf_op jit(solution)/shard_map/pallas_call | solution.py:22
  (5 shorter events, 0.1 us)
Async XLA Ops:
  0.0 1.0 %copy-start = (bf16[64,512]{1,0:T(8,128)(2,1)S(1)}, bf16[64,512]{1,0:T(8,128)(2,1)}, u32[]{:S(2)}) copy-start(bf16[64,512]{1,0:T(8,128)(2,1)} %refs_3_.1) | copy-start | bytes 196612
  0.0 1.0 %copy-start.1 = (bf16[64,2048]{1,0:T(8,128)(2,1)S(1)}, bf16[64,2048]{1,0:T(8,128)(2,1)}, u32[]{:S(2)}) copy-start(bf16[64,2048]{1,0:T(8,128)(2,1)} %refs_0_.5) | copy-start | bytes 786436
  1.0 11.0 %copy-start.2 = (bf16[64,2048]{1,0:T(8,128)(2,1)S(1)}, bf16[64,2048]{1,0:T(8,128)(2,1)}, u32[]{:S(2)}) copy-start(bf16[64,2048]{1,0:T(8,128)(2,1)} %refs_0_.5) | copy-start | bytes 786436
  1.0 12.8 %collective-permute-start.1 = (bf16[128,512]{1,0:T(8,128)(2,1)S(1)}, bf16[128,512]{1,0:T(8,128)(2,1)S(1)}, u32[]{:S(2)}, u32[]{:S(2)}) collective-permute-start(bf16[128,512]{1,0:T(8,128)(2,1)S(1)} %shard_map.39), channel_id=1, source_target_pairs={{0,4},{4,0},{8,12},{12,8},{1,5},{5,1},{9,13},{13,9},{2,6},{6,2},{1... | collective-permute-start | bytes 393224 | tf_op jit(solution)/shard_map/ppermute | solution.py:223
  4.1 7.9 %collective-permute-start = (bf16[64,512]{1,0:T(8,128)(2,1)S(1)}, bf16[64,512]{1,0:T(8,128)(2,1)S(1)}, u32[]{:S(2)}, u32[]{:S(2)}) collective-permute-start(bf16[64,512]{1,0:T(8,128)(2,1)S(1)} %get-tuple-element.16), channel_id=1, source_target_pairs={{0,12},{4,8},{8,4},{12,0},{1,13},{5,9},{9,5},{13,1},{2,14},{6,10},... | collective-permute-start | bytes 196616 | tf_op jit(solution)/shard_map/ppermute | solution.py:223
  6.6 5.4 %copy-start.3 = (bf16[64]{0:T(256)(128)(2,1)S(1)}, bf16[64]{0:T(256)(128)(2,1)}, u32[]{:S(2)}) copy-start(bf16[64]{0:T(256)(128)(2,1)} %param.5) | copy-start | bytes 388
  6.6 7.2 %collective-permute-start.2 = (bf16[64,512]{1,0:T(8,128)(2,1)S(1)}, bf16[64,512]{1,0:T(8,128)(2,1)S(1)}, u32[]{:S(2)}, u32[]{:S(2)}) collective-permute-start(bf16[64,512]{1,0:T(8,128)(2,1)S(1)} %get-tuple-element.18), channel_id=1, source_target_pairs={{0,8},{4,12},{8,0},{12,4},{1,9},{5,13},{9,1},{13,5},{2,10},{6,14},... | collective-permute-start | bytes 196616 | tf_op jit(solution)/shard_map/ppermute | solution.py:223
  12.3 10.3 %collective-permute-start.6 = (bf16[144,512]{1,0:T(8,128)(2,1)S(1)}, bf16[144,512]{1,0:T(8,128)(2,1)S(1)}, u32[]{:S(2)}, u32[]{:S(2)}) collective-permute-start(bf16[144,512]{1,0:T(8,128)(2,1)S(1)} %shard_map.38.refs_4_.refs_0_), channel_id=1, source_target_pairs={{0,2},{2,0},{1,3},{3,1},{4,6},{6,4},{5,7},{7,5},{8,10},{10,8},{9,1... | collective-permute-start | bytes 442376 | tf_op jit(solution)/shard_map/ppermute | solution.py:226
  13.9 9.3 %collective-permute-start.3 = (bf16[128,512]{1,0:T(8,128)(2,1)S(1)}, bf16[128,512]{1,0:T(8,128)(2,1)S(1)}, u32[]{:S(2)}, u32[]{:S(2)}) collective-permute-start(bf16[128,512]{1,0:T(8,128)(2,1)S(1)} %shard_map.40), channel_id=1, source_target_pairs={{0,8},{4,12},{8,0},{12,4},{1,9},{5,13},{9,1},{13,5},{2,10},{6,14},... | collective-permute-start | bytes 393224 | tf_op jit(solution)/shard_map/ppermute | solution.py:223
  15.9 4.3 %collective-permute-start.5 = (bf16[64,512]{1,0:T(8,128)(2,1)S(1)}, bf16[64,512]{1,0:T(8,128)(2,1)S(1)}, u32[]{:S(2)}, u32[]{:S(2)}) collective-permute-start(bf16[64,512]{1,0:T(8,128)(2,1)S(1)} %collective-permute-done.refs_3_.refs_2_), channel_id=1, source_target_pairs={{0,2},{2,0},{1,3},{3,1},{4,6},{6,4},{5,7},{7,5},{8,10},{10,8},{9,1... | collective-permute-start | bytes 196616 | tf_op jit(solution)/shard_map/ppermute | solution.py:226
  16.4 4.4 %collective-permute-start.4 = (bf16[64,512]{1,0:T(8,128)(2,1)S(1)}, bf16[64,512]{1,0:T(8,128)(2,1)S(1)}, u32[]{:S(2)}, u32[]{:S(2)}) collective-permute-start(bf16[64,512]{1,0:T(8,128)(2,1)S(1)} %collective-permute-done.2.refs_2_.refs_0_), channel_id=1, source_target_pairs={{0,2},{2,0},{1,3},{3,1},{4,6},{6,4},{5,7},{7,5},{8,10},{10,8},{9,1... | collective-permute-start | bytes 196616 | tf_op jit(solution)/shard_map/ppermute | solution.py:226
  17.9 4.7 %collective-permute-start.7 = (bf16[64,512]{1,0:T(8,128)(2,1)S(1)}, bf16[64,512]{1,0:T(8,128)(2,1)S(1)}, u32[]{:S(2)}, u32[]{:S(2)}) collective-permute-start(bf16[64,512]{1,0:T(8,128)(2,1)S(1)} %shard_map.41.refs_6_), channel_id=1, source_target_pairs={{0,2},{2,0},{1,3},{3,1},{4,6},{6,4},{5,7},{7,5},{8,10},{10,8},{9,1... | collective-permute-start | bytes 196616 | tf_op jit(solution)/shard_map/ppermute | solution.py:226
  23.2 5.7 %collective-permute-start.8 = (bf16[192,512]{1,0:T(8,128)(2,1)S(1)}, bf16[192,512]{1,0:T(8,128)(2,1)S(1)}, u32[]{:S(2)}, u32[]{:S(2)}) collective-permute-start(bf16[192,512]{1,0:T(8,128)(2,1)S(1)} %shard_map.43.refs_1_), channel_id=1, source_target_pairs={{0,2},{2,0},{1,3},{3,1},{4,6},{6,4},{5,7},{7,5},{8,10},{10,8},{9,1... | collective-permute-start | bytes 589832 | tf_op jit(solution)/shard_map/ppermute | solution.py:226
  24.2 5.8 %collective-permute-start.9 = (bf16[64,512]{1,0:T(8,128)(2,1)S(1)}, bf16[64,512]{1,0:T(8,128)(2,1)S(1)}, u32[]{:S(2)}, u32[]{:S(2)}) collective-permute-start(bf16[64,512]{1,0:T(8,128)(2,1)S(1)} %get-tuple-element.21), channel_id=1, source_target_pairs={{0,8},{4,12},{8,0},{12,4},{1,9},{5,13},{9,1},{13,5},{2,10},{6,14},... | collective-permute-start | bytes 196616 | tf_op jit(solution)/shard_map/ppermute | solution.py:223
  25.1 6.3 %collective-permute-start.10 = (bf16[64,512]{1,0:T(8,128)(2,1)S(1)}, bf16[64,512]{1,0:T(8,128)(2,1)S(1)}, u32[]{:S(2)}, u32[]{:S(2)}) collective-permute-start(bf16[64,512]{1,0:T(8,128)(2,1)S(1)} %get-tuple-element.22), channel_id=1, source_target_pairs={{0,12},{4,8},{8,4},{12,0},{1,13},{5,9},{9,5},{13,1},{2,14},{6,10},... | collective-permute-start | bytes 196616 | tf_op jit(solution)/shard_map/ppermute | solution.py:223
  27.0 5.0 %collective-permute-start.11 = (bf16[64,512]{1,0:T(8,128)(2,1)S(1)}, bf16[64,512]{1,0:T(8,128)(2,1)S(1)}, u32[]{:S(2)}, u32[]{:S(2)}) collective-permute-start(bf16[64,512]{1,0:T(8,128)(2,1)S(1)} %get-tuple-element.23), channel_id=1, source_target_pairs={{0,4},{4,0},{8,12},{12,8},{1,5},{5,1},{9,13},{13,9},{2,6},{6,2},{1... | collective-permute-start | bytes 196616 | tf_op jit(solution)/shard_map/ppermute | solution.py:223
  32.0 1.7 %collective-permute-start.12 = (f32[144,512]{1,0:T(8,128)S(1)}, f32[144,512]{1,0:T(8,128)S(1)}, u32[]{:S(2)}, u32[]{:S(2)}) collective-permute-start(f32[144,512]{1,0:T(8,128)S(1)} %get-tuple-element.24.refs_0_), channel_id=1, source_target_pairs={{0,1},{1,0},{2,3},{3,2},{4,5},{5,4},{6,7},{7,6},{8,9},{9,8},{10,11... | collective-permute-start | bytes 884744 | tf_op jit(solution)/shard_map/ppermute | solution.py:229

commit v12 on v11

--- a/solution.py
+++ b/solution.py
@@ -72,9 +72,9 @@
 def cut_kernel(nrow, teach, *outs):
     part = teach.shape[1] // nrow
     z = lax.axis_index("row")
-    for k in range(1, nrow):
+    for k in range(nrow):
         at = pl.multiple_of((z ^ k) * part, part)
-        outs[k - 1][...] = teach[:, pl.ds(at, part)]
+        outs[k][...] = teach[:, pl.ds(at, part)]
 
 
 def ride_kernel(stud, piece, out):
@@ -83,20 +83,20 @@
     wide(out, rows, piece[...])
 
 
-def own_kernel(nrow, teach, stud, scale, out):
-    rows, half = stud.shape
-    part = teach.shape[1] // nrow
+def tag_kernel(teach, scale, out):
+    rows, width = teach.shape[0], out.shape[1]
     ts = teach[...].astype(F32)
     s = scale[...].astype(F32)
     mass = jnp.sum(jnp.square(column(s)) * jnp.sum(ts * ts, axis=1, keepdims=True), keepdims=True)
     tags = tags_of(jnp.concatenate([s, s], axis=1), mass)
-    out[:rows, :] = stud[...]
-    out[rows : rows + TAIL, :] = jnp.concatenate([tags] * (half // (2 * rows)), axis=1)
-    wide(out, rows + TAIL, teach[:, pl.ds(pl.multiple_of(lax.axis_index("row") * part, part), part)])
-
-
-def take_kernel(rows, ref, out):
-    put(out, 0, rows, ref, rows)
+    out[...] = jnp.concatenate([tags] * (width // (2 * rows)), axis=1)
+
+
+def late_kernel(order, rows, tags, *refs):
+    out = refs[-1]
+    for n, (k, ref) in enumerate(zip(order, refs[:-1])):
+        put(out, n * rows, rows, ref, rows if k == 1 else 0)
+    out[len(order) * rows :, :] = tags[...]
 
 
 def pack_kernel(spans, *refs):
@@ -115,12 +115,11 @@
 
 
 def gram_kernel(nrow, ncol, rows, order, *refs):
-    count = nrow * ncol
-    outs, held, left = refs[count : count + nrow], refs[-2], refs[-1]
-    own = order.index(0) * ncol
-    for n, k in enumerate(order):
-        for c in range(ncol):
-            put(held, place(nrow, ncol, rows, k, c), rows, refs[n * ncol + c], 0 if k else rows + TAIL)
+    outs, held, left = refs[2 * ncol : 2 * ncol + nrow], refs[-2], refs[-1]
+    for c in range(ncol):
+        put(held, place(nrow, ncol, rows, 0, c), rows, refs[2 * c], 0)
+        for n, k in enumerate([k for k in order if k]):
+            put(held, place(nrow, ncol, rows, k, c), rows, refs[2 * c + 1], n * rows)
     for n, k in enumerate(order):
         left[n * rows : (n + 1) * rows, :] = held[pl.ds(place(nrow, ncol, rows, k, 0), rows), :]
     sub = rows // 2
@@ -128,7 +127,7 @@
     lane = lax.broadcasted_iota(jnp.int32, (sub, 2 * rows), 1)
     note, mass = jnp.zeros((sub, 2 * rows), F32), jnp.zeros((1, 1), F32)
     for c in range(ncol):
-        scales, part = read_tags(refs[own + c][rows : rows + TAIL, : 2 * rows])
+        scales, part = read_tags(refs[2 * c + 1][(nrow - 1) * rows :, : 2 * rows])
         turned = jnp.concatenate([scales[:, sub:], scales[:, :sub]], axis=1)
         note = jnp.where(at == 2 * c, scales, jnp.where(at == 2 * c + 1, turned, note))
         mass = mass + part
@@ -154,24 +153,14 @@
                 held[pl.ds(place(nrow, ncol, rows, k, c), rows), :] = ref[n * rows : (n + 1) * rows, :]
 
 
-def raw_gram_kernel(nrow, ncol, rows, keys, *refs):
-    count = len(keys) * ncol
-    out, raw = refs[count:]
-    assemble(nrow, ncol, rows, keys, refs, raw)
-    out[:rows, :] = lax.dot_general(refs[0][:rows, :], raw[...], INNER, preferred_element_type=F32)
-    for at in range(0, raw.shape[0], 128):
-        squares = jnp.sum(jnp.square(raw[at : at + 128, :].astype(F32)), axis=1, keepdims=True)
-        out[rows:, at : at + 128] = jnp.broadcast_to(lane_row(squares), (8, 128))
-
-
-def message_kernel(nrow, ncol, order, raw_gram, *refs):
+def sum_kernel(nrow, ncol, order, *refs):
     parts, (out, vectors) = [refs[order.index(k)] for k in range(nrow)], refs[-2:]
     rows = parts[0].shape[0]
     sub = rows // 2
     total = parts[0][...].astype(F32)
     for r in parts[1:]:
         total = total + r[...].astype(F32)
-    out[:rows, :] = total
+    out[...] = total
     own = pl.ds(group_spot(nrow, ncol, rows, 0), 2 * rows)
     mirror = jnp.transpose(out[:sub, own])[sub : 2 * sub, :]
     out[sub:rows, own] = jnp.concatenate([mirror, out[sub:rows, own][:, sub:]], axis=1)
@@ -180,9 +169,20 @@
         note = part[sub:, own].astype(F32)[:, :sub]
         mass = mass + note[sub // 2 : sub // 2 + 1, :1] + note[sub * 3 // 4 : sub * 3 // 4 + 1, :1]
         line = jnp.concatenate([note[n : n + 1, :] for n in range(2 * ncol)], axis=1)
-        vectors[:, pl.ds(group_spot(nrow, ncol, rows, k), ncol * rows)] = jnp.broadcast_to(line, (8, ncol * rows))
-    out[rows : 2 * rows + 8, :] = raw_gram[...]
-    out[2 * rows + 8 :, :] = jnp.broadcast_to(mass, (8, out.shape[1]))
+        vectors[:8, pl.ds(group_spot(nrow, ncol, rows, k), ncol * rows)] = jnp.broadcast_to(line, (8, ncol * rows))
+    vectors[8:, :] = jnp.broadcast_to(mass, (8, out.shape[1]))
+
+
+def message_kernel(nrow, ncol, keys, total, vectors, *refs):
+    out, raw = refs[-2:]
+    rows = total.shape[0]
+    assemble(nrow, ncol, rows, keys, refs, raw)
+    out[:rows, :] = total[...]
+    out[rows : 2 * rows, :] = lax.dot_general(refs[0][:rows, :], raw[...], INNER, preferred_element_type=F32)
+    for at in range(0, raw.shape[0], 128):
+        squares = jnp.sum(jnp.square(raw[at : at + 128, :].astype(F32)), axis=1, keepdims=True)
+        out[2 * rows : 2 * rows + 8, at : at + 128] = jnp.broadcast_to(lane_row(squares), (8, 128))
+    out[2 * rows + 8 :, :] = vectors[8:, :]
 
 
 def final_kernel(nrow, ncol, keys, mine, other, vectors, stud, scale, *refs):
@@ -238,55 +238,54 @@
     middle, high = nrow // 2, rows * part // half
     order = list(range(middle, nrow)) + list(range(middle))
     riders = (1,)
-    cuts = call(functools.partial(cut_kernel, nrow), [sds((rows, part), BF16)] * (nrow - 1), [teacher])
+    cuts = call(functools.partial(cut_kernel, nrow), [sds((rows, part), BF16)] * nrow, [teacher])
     came = {}
     for k in order:
         if k:
-            leaving = cuts[k - 1]
+            leaving = cuts[k]
             if k in riders:
                 leaving = call(ride_kernel, sds((rows + high, half), BF16), [student, leaving])
             came[k] = along_row(leaving, k)
-    own = call(
-        functools.partial(own_kernel, nrow),
-        sds((rows + TAIL + high, half), BF16),
-        [teacher, student, scale],
-        after=[came[n] for n in (nrow - 1,)],
-    )
-    columns, taken = {0: with_columns(own)}, ()
-    for k in order:
-        piece = came.get(k)
-        if k in riders:
-            piece = call(functools.partial(take_kernel, rows), sds((rows, part), BF16), [piece], after=taken)
-            taken = (piece,)
-        if k:
-            columns[k] = with_columns(piece)
+    tags = call(tag_kernel, sds((TAIL, part), BF16), [teacher, scale], after=[came[n] for n in ()])
+    own = with_columns(cuts[0])
+    mine = with_columns(student)
+    others = [k for k in order if k]
+    late = call(
+        functools.partial(late_kernel, others, rows),
+        sds(((nrow - 1) * rows + TAIL, part), BF16),
+        [tags] + [came[k] for k in others],
+        after=own[1:2] + mine[1:2],
+    )
+    late = with_columns(late)
     partial = call(
         functools.partial(gram_kernel, nrow, ncol, rows, order),
         [sds((rows, batch), BF16 if k else F32) for k in range(nrow)],
-        [columns[k][c] for k in order for c in range(ncol)],
+        [r for pair in zip(own, late) for r in pair],
         scratch=[pltpu.VMEM((batch, part), BF16), pltpu.VMEM((nrow * rows, part), BF16)],
     )
     returned = {k: along_row(partial[k], k) if k else partial[0] for k in order}
 
     stack, spans, keys, k = [student, came[1]], [(0, rows)] * 2, [0, 1], 2
     while k < nrow:
-        sent = pack(stack, spans, after=[came[n] for n in (middle, nrow - 1)] if k == 2 else ())
-        stack, spans = stack + [along_row(sent, k)], spans + [(0, len(keys) * rows)]
+        stack.append(along_row(pack(stack, spans), k))
+        spans.append((0, len(keys) * rows))
         keys, k = keys + [n ^ k for n in keys], 2 * k
-    rest = pack(stack[1:], spans[1:], after=[partial[0]])
-    raw_keys = [[0], keys[1:]]
-    sources = [columns[0], with_columns(rest)]
-    raw_refs = [x[c] for c in range(ncol) for x in sources]
-    raw_gram, *all_raw = call(
-        functools.partial(raw_gram_kernel, nrow, ncol, rows, raw_keys),
-        [sds((rows + 8, batch), F32)] + ([sds((batch, half), BF16)] if small else []),
-        raw_refs,
+    cut = (len(keys) - 2) // 2 * rows
+    near = with_columns(pack(stack[1:2], spans[1:2], after=[partial[0]]))
+    rest = pack(stack[2:], spans[2:], after=[partial[0]]) if len(stack) > 3 else stack[2]
+    rest = [with_columns(pack([rest], [span], after=[partial[0]])) for span in ((0, cut), (cut, 2 * cut))]
+    raw_keys = [[0], [1], keys[2 : 2 + cut // rows], keys[2 + cut // rows :]]
+    raw_refs = [x[c] for c in range(ncol) for x in (mine, near, *rest)]
+    total, vectors = call(
+        functools.partial(sum_kernel, nrow, ncol, order),
+        [sds((rows, batch), F32), sds((16, batch), F32)],
+        [returned[k] for k in order],
+    )
+    message, *all_raw = call(
+        functools.partial(message_kernel, nrow, ncol, raw_keys),
+        [sds((2 * rows + 16, batch), F32)] + ([sds((batch, half), BF16)] if small else []),
+        [total, vectors] + raw_refs,
         scratch=[] if small else [pltpu.VMEM((batch, half), BF16)],
-    )
-    message, vectors = call(
-        functools.partial(message_kernel, nrow, ncol, order),
-        [sds((2 * rows + 16, batch), F32), sds((8, batch), F32)],
-        [raw_gram] + [returned[k] for k in order],
     )
     return call(
         functools.partial(final_kernel, nrow, ncol, None if small else raw_keys),

time: 35 us -> 36.7 us (1.049)
  local copies, waits for them, and re-layouts: 0.99 us -> 2.11 us
  starting transfers between devices: 16.3 us -> 16.9 us
    unnamed x8 -> x6, local copies, waits for them, and re-layouts: 0.99 us -> 2.11 us
    ppermute x5 -> x6, waiting for transfers between devices: 5.45 us -> 4.56 us  [along_col(): return lax.ppermute(x, 'col', [(i, (i - c) % ncol) for i in range(ncol)])]
    ppermute x7, waiting for transfers between devices: 7.99 us -> 8.85 us  [along_row(): return lax.ppermute(x, 'row', [(i, i ^ k) for i in range(nrow)])]
    ppermute x5 -> x6, starting transfers between devices: 5.09 us -> 5.61 us  [along_col(): return lax.ppermute(x, 'col', [(i, (i - c) % ncol) for i in range(ncol)])]
    pallas_call x10 -> x12, Pallas kernels: 2.41 us -> 2.43 us  [call(): pl.pallas_call(run, out_shape=out_shape, in_specs=[pl.BlockSpec(memory_sp...]
  transfers between devices with their start and end apart: 13 -> 14, of which waited for: 9 -> 8; matrix products, arithmetic and copies ran while one was open for 0% -> 0% of each run, Pallas kernels for 3% -> 3%
where the time goes in v12:
time: 36.7 us; the launch traced here: 36.5 us
  starting transfers between devices  16.9 us (46%)
  waiting for transfers between devices  15 us (41%)
  Pallas kernels  2.43 us (7%)
  local copies, waits for them, and re-layouts  2.11 us (6%)
    ppermute x7, starting transfers between devices, along_row(): return lax.ppermute(x, 'row', [(i, i ^ k) for i in range(nrow)])  11.3 us
    ppermute x7, waiting for transfers between devices, along_row(): return lax.ppermute(x, 'row', [(i, i ^ k) for i in range(nrow)])  8.85 us
    ppermute x6, starting transfers between devices, along_col(): return lax.ppermute(x, 'col', [(i, (i - c) % ncol) for i in range(ncol)])  5.61 us
    ppermute x6, waiting for transfers between devices, along_col(): return lax.ppermute(x, 'col', [(i, (i - c) % ncol) for i in range(ncol)])  4.56 us
    pallas_call x12, Pallas kernels, call(): pl.pallas_call(run, out_shape=out_shape, in_specs=[pl.BlockSpec(memory_sp...  2.43 us
    unnamed x6, local copies, waits for them, and re-layouts  2.11 us
    ppermute x1, waiting for transfers between devices, other_core(): return lax.ppermute(x, 'sub', [(0, 1), (1, 0)])  1.57 us
  transfers between devices with their start and end apart: 14, of which 8 were waited for; matrix products, arithmetic and copies ran while one was open for 0% of the time, Pallas kernels for 3%

profile of v12, /device:TPU:0, one launch (start us, length us, event | category | flops | bytes accessed | tf_op | source)
XLA Modules:
  0.0 36.5 jit_solution(6255295834832759396)
XLA Ops:
  0.0 0.0 copy-start
  0.0 0.9 %copy-done = bf16[64,2048]{1,0:T(8,128)(2,1)S(1)} copy-done((bf16[64,2048]{1,0:T(8,128)(2,1)S(1)}, bf16[64,2048]{1,0:T(8,128)(2,1)}, u32[]{:S(2)}) %copy-start) | copy-done | bytes 262168
  1.0 0.0 copy-start.1
  1.0 0.8 %copy-done.1 = bf16[64,512]{1,0:T(8,128)(2,1)S(1)} copy-done((bf16[64,512]{1,0:T(8,128)(2,1)S(1)}, bf16[64,512]{1,0:T(8,128)(2,1)}, u32[]{:S(2)}) %copy-start.1) | copy-done | bytes 65560
  1.8 3.1 %collective-permute-start.2 = (bf16[128,512]{1,0:T(8,128)(2,1)S(1)}, bf16[128,512]{1,0:T(8,128)(2,1)S(1)}, u32[]{:S(2)}, u32[]{:S(2)}) collective-permute-start(bf16[128,512]{1,0:T(8,128)(2,1)S(1)} %shard_map.39), channel_id=1, source_target_pairs={{0,4},{4,0},{8,12},{12,8},{1,5},{5,1},{9,13},{13,9},{2,6},{6,2},{1... | collective-permute-start | bytes 393224 | tf_op jit(solution)/shard_map/ppermute | solution.py:223
  4.9 1.5 %collective-permute-start.4 = (bf16[64,512]{1,0:T(8,128)(2,1)S(1)}, bf16[64,512]{1,0:T(8,128)(2,1)S(1)}, u32[]{:S(2)}, u32[]{:S(2)}) collective-permute-start(bf16[64,512]{1,0:T(8,128)(2,1)S(1)} %copy-done.1), channel_id=1, source_target_pairs={{0,2},{2,0},{1,3},{3,1},{4,6},{6,4},{5,7},{7,5},{8,10},{10,8},{9,1... | collective-permute-start | bytes 196616 | tf_op jit(solution)/shard_map/ppermute | solution.py:226
  6.4 2.6 %collective-permute-start = (bf16[64,512]{1,0:T(8,128)(2,1)S(1)}, bf16[64,512]{1,0:T(8,128)(2,1)S(1)}, u32[]{:S(2)}, u32[]{:S(2)}) collective-permute-start(bf16[64,512]{1,0:T(8,128)(2,1)S(1)} %get-tuple-element.18), channel_id=1, source_target_pairs={{0,8},{4,12},{8,0},{12,4},{1,9},{5,13},{9,1},{13,5},{2,10},{6,14},... | collective-permute-start | bytes 196616 | tf_op jit(solution)/shard_map/ppermute | solution.py:223
  9.0 0.2 collective-permute-start.1
  9.2 0.0 copy-start.2
  9.2 0.3 collective-permute-start.3
  9.5 0.3 copy-done.2
  9.9 0.3 shard_map.38.refs_0_
  10.1 0.0 collective-permute-done.4.refs_5_.refs_6_
  10.1 3.3 %collective-permute-done.refs_1_ = bf16[64,512]{1,0:T(8,128)(2,1)S(1)} collective-permute-done((bf16[64,512]{1,0:T(8,128)(2,1)S(1)}, bf16[64,512]{1,0:T(8,128)(2,1)S(1)}, u32[]{:S(2)}, u32[]{:S(2)}) %collective-permute-start) | collective-permute-done | bytes 65568 | tf_op jit(solution)/shard_map/ppermute | solution.py:223
  13.4 1.6 %collective-permute-done.1.refs_2_ = bf16[64,512]{1,0:T(8,128)(2,1)S(1)} collective-permute-done((bf16[64,512]{1,0:T(8,128)(2,1)S(1)}, bf16[64,512]{1,0:T(8,128)(2,1)S(1)}, u32[]{:S(2)}, u32[]{:S(2)}) %collective-permute-start.1) | collective-permute-done | bytes 65568 | tf_op jit(solution)/shard_map/ppermute | solution.py:223
  15.0 0.0 collective-permute-done.3.refs_4_.refs_2_
  15.0 0.0 collective-permute-done.2.refs_3_.refs_0_.refs_1_
  15.1 0.7 %collective-permute-start.5 = (bf16[208,512]{1,0:T(8,128)(2,1)S(1)}, bf16[208,512]{1,0:T(8,128)(2,1)S(1)}, u32[]{:S(2)}, u32[]{:S(2)}) collective-permute-start(bf16[208,512]{1,0:T(8,128)(2,1)S(1)} %shard_map.40.refs_1_), channel_id=1, source_target_pairs={{0,2},{2,0},{1,3},{3,1},{4,6},{6,4},{5,7},{7,5},{8,10},{10,8},{9,1... | collective-permute-start | bytes 638984 | tf_op jit(solution)/shard_map/ppermute | solution.py:226
  15.8 1.3 %collective-permute-start.9 = (bf16[128,512]{1,0:T(8,128)(2,1)S(1)}, bf16[128,512]{1,0:T(8,128)(2,1)S(1)}, u32[]{:S(2)}, u32[]{:S(2)}) collective-permute-start(bf16[128,512]{1,0:T(8,128)(2,1)S(1)} %shard_map.44), channel_id=1, source_target_pairs={{0,8},{4,12},{8,0},{12,4},{1,9},{5,13},{9,1},{13,5},{2,10},{6,14},... | collective-permute-start | bytes 393224 | tf_op jit(solution)/shard_map/ppermute | solution.py:223
  17.1 3.9 %collective-permute-done.5.refs_3_ = bf16[208,512]{1,0:T(8,128)(2,1)S(1)} collective-permute-done((bf16[208,512]{1,0:T(8,128)(2,1)S(1)}, bf16[208,512]{1,0:T(8,128)(2,1)S(1)}, u32[]{:S(2)}, u32[]{:S(2)}) %collective-permute-start.5) | collective-permute-done | bytes 213024 | tf_op jit(solution)/shard_map/ppermute | solution.py:226
  21.0 0.5 %shard_map.41 = (f32[64,512]{1,0:T(8,128)S(1)}, bf16[64,512]{1,0:T(8,128)(2,1)S(1)}, bf16[64,512]{1,0:T(8,128)(2,1)S(1)}, bf16[64,512]{1,0:T(8,128)(2,1)S(1)}) custom-call(bf16[64,512]{1,0:T(8,128)(2,1)S(1)} %get-tuple-element.17.refs_0_, bf16[208,512]{1,0:T(8,128)(2,1)S(1)} %shard_map.40.refs_1_, ...), custom_call_target="tpu_custom_call" | custom-call | tf_op jit(solution)/shard_map/pallas_call | solution.py:22
  21.5 1.6 %collective-permute-start.6 = (bf16[64,512]{1,0:T(8,128)(2,1)S(1)}, bf16[64,512]{1,0:T(8,128)(2,1)S(1)}, u32[]{:S(2)}, u32[]{:S(2)}) collective-permute-start(bf16[64,512]{1,0:T(8,128)(2,1)S(1)} %get-tuple-element.21), channel_id=1, source_target_pairs={{0,8},{4,12},{8,0},{12,4},{1,9},{5,13},{9,1},{13,5},{2,10},{6,14},... | collective-permute-start | bytes 196616 | tf_op jit(solution)/shard_map/ppermute | solution.py:223
  23.1 1.8 %collective-permute-done.9.refs_0_ = bf16[128,512]{1,0:T(8,128)(2,1)S(1)} collective-permute-done((bf16[128,512]{1,0:T(8,128)(2,1)S(1)}, bf16[128,512]{1,0:T(8,128)(2,1)S(1)}, u32[]{:S(2)}, u32[]{:S(2)}) %collective-permute-start.9) | collective-permute-done | bytes 131104 | tf_op jit(solution)/shard_map/ppermute | solution.py:223
  24.9 0.9 %collective-permute-start.11 = (bf16[64,512]{1,0:T(8,128)(2,1)S(1)}, bf16[64,512]{1,0:T(8,128)(2,1)S(1)}, u32[]{:S(2)}, u32[]{:S(2)}) collective-permute-start(bf16[64,512]{1,0:T(8,128)(2,1)S(1)} %shard_map.45.refs_4_), channel_id=1, source_target_pairs={{0,2},{2,0},{1,3},{3,1},{4,6},{6,4},{5,7},{7,5},{8,10},{10,8},{9,1... | collective-permute-start | bytes 196616 | tf_op jit(solution)/shard_map/ppermute | solution.py:226
  25.9 2.5 %collective-permute-start.7 = (bf16[64,512]{1,0:T(8,128)(2,1)S(1)}, bf16[64,512]{1,0:T(8,128)(2,1)S(1)}, u32[]{:S(2)}, u32[]{:S(2)}) collective-permute-start(bf16[64,512]{1,0:T(8,128)(2,1)S(1)} %get-tuple-element.22), channel_id=1, source_target_pairs={{0,12},{4,8},{8,4},{12,0},{1,13},{5,9},{9,5},{13,1},{2,14},{6,10},... | collective-permute-start | bytes 196616 | tf_op jit(solution)/shard_map/ppermute | solution.py:223
  28.4 0.0 collective-permute-start.8
  28.4 0.4 %collective-permute-start.12 = (bf16[64,512]{1,0:T(8,128)(2,1)S(1)}, bf16[64,512]{1,0:T(8,128)(2,1)S(1)}, u32[]{:S(2)}, u32[]{:S(2)}) collective-permute-start(bf16[64,512]{1,0:T(8,128)(2,1)S(1)} %shard_map.46.refs_5_), channel_id=1, source_target_pairs={{0,2},{2,0},{1,3},{3,1},{4,6},{6,4},{5,7},{7,5},{8,10},{10,8},{9,1... | collective-permute-start | bytes 196616 | tf_op jit(solution)/shard_map/ppermute | solution.py:226
  28.8 0.0 collective-permute-done.6.refs_0_
  28.8 1.7 %collective-permute-start.10 = (bf16[64,512]{1,0:T(8,128)(2,1)S(1)}, bf16[64,512]{1,0:T(8,128)(2,1)S(1)}, u32[]{:S(2)}, u32[]{:S(2)}) collective-permute-start(bf16[64,512]{1,0:T(8,128)(2,1)S(1)} %shard_map.43.refs_3_), channel_id=1, source_target_pairs={{0,2},{2,0},{1,3},{3,1},{4,6},{6,4},{5,7},{7,5},{8,10},{10,8},{9,1... | collective-permute-start | bytes 196616 | tf_op jit(solution)/shard_map/ppermute | solution.py:226
  30.6 1.4 %collective-permute-done.7.refs_1_ = bf16[64,512]{1,0:T(8,128)(2,1)S(1)} collective-permute-done((bf16[64,512]{1,0:T(8,128)(2,1)S(1)}, bf16[64,512]{1,0:T(8,128)(2,1)S(1)}, u32[]{:S(2)}, u32[]{:S(2)}) %collective-permute-start.7) | collective-permute-done | bytes 65568 | tf_op jit(solution)/shard_map/ppermute | solution.py:223
  32.0 0.7 %collective-permute-done.8.refs_3_ = bf16[64,512]{1,0:T(8,128)(2,1)S(1)} collective-permute-done((bf16[64,512]{1,0:T(8,128)(2,1)S(1)}, bf16[64,512]{1,0:T(8,128)(2,1)S(1)}, u32[]{:S(2)}, u32[]{:S(2)}) %collective-permute-start.8) | collective-permute-done | bytes 65568 | tf_op jit(solution)/shard_map/ppermute | solution.py:223
  32.7 0.1 shard_map.42
  32.8 0.0 collective-permute-done.11.refs_8_
  32.8 0.0 collective-permute-done.12.refs_9_
  32.8 0.6 %collective-permute-done.10.refs_7_ = bf16[64,512]{1,0:T(8,128)(2,1)S(1)} collective-permute-done((bf16[64,512]{1,0:T(8,128)(2,1)S(1)}, bf16[64,512]{1,0:T(8,128)(2,1)S(1)}, u32[]{:S(2)}, u32[]{:S(2)}) %collective-permute-start.10) | collective-permute-done | bytes 65568 | tf_op jit(solution)/shard_map/ppermute | solution.py:226
  33.4 0.3 shard_map.47
  33.7 0.1 collective-permute-start.13
  33.8 1.6 %collective-permute-done.13.refs_1_ = f32[144,512]{1,0:T(8,128)S(1)} collective-permute-done((f32[144,512]{1,0:T(8,128)S(1)}, f32[144,512]{1,0:T(8,128)S(1)}, u32[]{:S(2)}, u32[]{:S(2)}) %collective-permute-start.13) | collective-permute-done | bytes 294944 | tf_op jit(solution)/shard_map/ppermute | solution.py:229
  35.4 1.1 %shard_map.48 = f32[64,512]{1,0:T(8,128)} custom-call(f32[144,512]{1,0:T(8,128)S(1)} %get-tuple-element.27.refs_0_, f32[144,512]{1,0:T(8,128)S(1)} %collective-permute-done.13.refs_1_, f32[16,512]{1,0:T(8,128)S(1)} %get-tuple-element.26.refs_1_.refs_2_, bf16[64,512]{1,0:T(8,128)(2,1)S(1)} %copy-done.1, bf16[1,64]{1,0:T(2,128)(2,1)S(1)} %bitcast.2, ...), custom_call_target="tpu_custom_call" | custom-call | tf_op jit(solution)/shard_map/pallas_call | solution.py:22
  (7 shorter events, 0.1 us)
Async XLA Ops:
  0.0 0.9 %copy-start = (bf16[64,2048]{1,0:T(8,128)(2,1)S(1)}, bf16[64,2048]{1,0:T(8,128)(2,1)}, u32[]{:S(2)}) copy-start(bf16[64,2048]{1,0:T(8,128)(2,1)} %refs_0_.5) | copy-start | bytes 786436
  1.0 0.8 %copy-start.1 = (bf16[64,512]{1,0:T(8,128)(2,1)S(1)}, bf16[64,512]{1,0:T(8,128)(2,1)}, u32[]{:S(2)}) copy-start(bf16[64,512]{1,0:T(8,128)(2,1)} %refs_3_.1) | copy-start | bytes 196612
  1.8 13.2 %collective-permute-start.2 = (bf16[128,512]{1,0:T(8,128)(2,1)S(1)}, bf16[128,512]{1,0:T(8,128)(2,1)S(1)}, u32[]{:S(2)}, u32[]{:S(2)}) collective-permute-start(bf16[128,512]{1,0:T(8,128)(2,1)S(1)} %shard_map.39), channel_id=1, source_target_pairs={{0,4},{4,0},{8,12},{12,8},{1,5},{5,1},{9,13},{13,9},{2,6},{6,2},{1... | collective-permute-start | bytes 393224 | tf_op jit(solution)/shard_map/ppermute | solution.py:223
  4.9 5.2 %collective-permute-start.4 = (bf16[64,512]{1,0:T(8,128)(2,1)S(1)}, bf16[64,512]{1,0:T(8,128)(2,1)S(1)}, u32[]{:S(2)}, u32[]{:S(2)}) collective-permute-start(bf16[64,512]{1,0:T(8,128)(2,1)S(1)} %copy-done.1), channel_id=1, source_target_pairs={{0,2},{2,0},{1,3},{3,1},{4,6},{6,4},{5,7},{7,5},{8,10},{10,8},{9,1... | collective-permute-start | bytes 196616 | tf_op jit(solution)/shard_map/ppermute | solution.py:226
  6.4 7.1 %collective-permute-start = (bf16[64,512]{1,0:T(8,128)(2,1)S(1)}, bf16[64,512]{1,0:T(8,128)(2,1)S(1)}, u32[]{:S(2)}, u32[]{:S(2)}) collective-permute-start(bf16[64,512]{1,0:T(8,128)(2,1)S(1)} %get-tuple-element.18), channel_id=1, source_target_pairs={{0,8},{4,12},{8,0},{12,4},{1,9},{5,13},{9,1},{13,5},{2,10},{6,14},... | collective-permute-start | bytes 196616 | tf_op jit(solution)/shard_map/ppermute | solution.py:223
  9.0 6.1 %collective-permute-start.1 = (bf16[64,512]{1,0:T(8,128)(2,1)S(1)}, bf16[64,512]{1,0:T(8,128)(2,1)S(1)}, u32[]{:S(2)}, u32[]{:S(2)}) collective-permute-start(bf16[64,512]{1,0:T(8,128)(2,1)S(1)} %get-tuple-element.19), channel_id=1, source_target_pairs={{0,12},{4,8},{8,4},{12,0},{1,13},{5,9},{9,5},{13,1},{2,14},{6,10},... | collective-permute-start | bytes 196616 | tf_op jit(solution)/shard_map/ppermute | solution.py:223
  9.2 0.7 %copy-start.2 = (bf16[64]{0:T(256)(128)(2,1)S(1)}, bf16[64]{0:T(256)(128)(2,1)}, u32[]{:S(2)}) copy-start(bf16[64]{0:T(256)(128)(2,1)} %param.5) | copy-start | bytes 388
  9.2 5.8 %collective-permute-start.3 = (bf16[64,512]{1,0:T(8,128)(2,1)S(1)}, bf16[64,512]{1,0:T(8,128)(2,1)S(1)}, u32[]{:S(2)}, u32[]{:S(2)}) collective-permute-start(bf16[64,512]{1,0:T(8,128)(2,1)S(1)} %get-tuple-element.17.refs_0_), channel_id=1, source_target_pairs={{0,2},{2,0},{1,3},{3,1},{4,6},{6,4},{5,7},{7,5},{8,10},{10,8},{9,1... | collective-permute-start | bytes 196616 | tf_op jit(solution)/shard_map/ppermute | solution.py:226
  15.1 5.9 %collective-permute-start.5 = (bf16[208,512]{1,0:T(8,128)(2,1)S(1)}, bf16[208,512]{1,0:T(8,128)(2,1)S(1)}, u32[]{:S(2)}, u32[]{:S(2)}) collective-permute-start(bf16[208,512]{1,0:T(8,128)(2,1)S(1)} %shard_map.40.refs_1_), channel_id=1, source_target_pairs={{0,2},{2,0},{1,3},{3,1},{4,6},{6,4},{5,7},{7,5},{8,10},{10,8},{9,1... | collective-permute-start | bytes 638984 | tf_op jit(solution)/shard_map/ppermute | solution.py:226
  15.8 9.2 %collective-permute-start.9 = (bf16[128,512]{1,0:T(8,128)(2,1)S(1)}, bf16[128,512]{1,0:T(8,128)(2,1)S(1)}, u32[]{:S(2)}, u32[]{:S(2)}) collective-permute-start(bf16[128,512]{1,0:T(8,128)(2,1)S(1)} %shard_map.44), channel_id=1, source_target_pairs={{0,8},{4,12},{8,0},{12,4},{1,9},{5,13},{9,1},{13,5},{2,10},{6,14},... | collective-permute-start | bytes 393224 | tf_op jit(solution)/shard_map/ppermute | solution.py:223
  21.5 7.3 %collective-permute-start.6 = (bf16[64,512]{1,0:T(8,128)(2,1)S(1)}, bf16[64,512]{1,0:T(8,128)(2,1)S(1)}, u32[]{:S(2)}, u32[]{:S(2)}) collective-permute-start(bf16[64,512]{1,0:T(8,128)(2,1)S(1)} %get-tuple-element.21), channel_id=1, source_target_pairs={{0,8},{4,12},{8,0},{12,4},{1,9},{5,13},{9,1},{13,5},{2,10},{6,14},... | collective-permute-start | bytes 196616 | tf_op jit(solution)/shard_map/ppermute | solution.py:223
  24.9 7.8 %collective-permute-start.11 = (bf16[64,512]{1,0:T(8,128)(2,1)S(1)}, bf16[64,512]{1,0:T(8,128)(2,1)S(1)}, u32[]{:S(2)}, u32[]{:S(2)}) collective-permute-start(bf16[64,512]{1,0:T(8,128)(2,1)S(1)} %shard_map.45.refs_4_), channel_id=1, source_target_pairs={{0,2},{2,0},{1,3},{3,1},{4,6},{6,4},{5,7},{7,5},{8,10},{10,8},{9,1... | collective-permute-start | bytes 196616 | tf_op jit(solution)/shard_map/ppermute | solution.py:226
  25.9 6.1 %collective-permute-start.7 = (bf16[64,512]{1,0:T(8,128)(2,1)S(1)}, bf16[64,512]{1,0:T(8,128)(2,1)S(1)}, u32[]{:S(2)}, u32[]{:S(2)}) collective-permute-start(bf16[64,512]{1,0:T(8,128)(2,1)S(1)} %get-tuple-element.22), channel_id=1, source_target_pairs={{0,12},{4,8},{8,4},{12,0},{1,13},{5,9},{9,5},{13,1},{2,14},{6,10},... | collective-permute-start | bytes 196616 | tf_op jit(solution)/shard_map/ppermute | solution.py:223
  28.4 4.3 %collective-permute-start.8 = (bf16[64,512]{1,0:T(8,128)(2,1)S(1)}, bf16[64,512]{1,0:T(8,128)(2,1)S(1)}, u32[]{:S(2)}, u32[]{:S(2)}) collective-permute-start(bf16[64,512]{1,0:T(8,128)(2,1)S(1)} %get-tuple-element.24), channel_id=1, source_target_pairs={{0,4},{4,0},{8,12},{12,8},{1,5},{5,1},{9,13},{13,9},{2,6},{6,2},{1... | collective-permute-start | bytes 196616 | tf_op jit(solution)/shard_map/ppermute | solution.py:223
  28.4 4.4 %collective-permute-start.12 = (bf16[64,512]{1,0:T(8,128)(2,1)S(1)}, bf16[64,512]{1,0:T(8,128)(2,1)S(1)}, u32[]{:S(2)}, u32[]{:S(2)}) collective-permute-start(bf16[64,512]{1,0:T(8,128)(2,1)S(1)} %shard_map.46.refs_5_), channel_id=1, source_target_pairs={{0,2},{2,0},{1,3},{3,1},{4,6},{6,4},{5,7},{7,5},{8,10},{10,8},{9,1... | collective-permute-start | bytes 196616 | tf_op jit(solution)/shard_map/ppermute | solution.py:226
  28.8 4.6 %collective-permute-start.10 = (bf16[64,512]{1,0:T(8,128)(2,1)S(1)}, bf16[64,512]{1,0:T(8,128)(2,1)S(1)}, u32[]{:S(2)}, u32[]{:S(2)}) collective-permute-start(bf16[64,512]{1,0:T(8,128)(2,1)S(1)} %shard_map.43.refs_3_), channel_id=1, source_target_pairs={{0,2},{2,0},{1,3},{3,1},{4,6},{6,4},{5,7},{7,5},{8,10},{10,8},{9,1... | collective-permute-start | bytes 196616 | tf_op jit(solution)/shard_map/ppermute | solution.py:226
  33.7 1.6 %collective-permute-start.13 = (f32[144,512]{1,0:T(8,128)S(1)}, f32[144,512]{1,0:T(8,128)S(1)}, u32[]{:S(2)}, u32[]{:S(2)}) collective-permute-start(f32[144,512]{1,0:T(8,128)S(1)} %get-tuple-element.27.refs_0_), channel_id=1, source_target_pairs={{0,1},{1,0},{2,3},{3,2},{4,5},{5,4},{6,7},{7,6},{8,9},{9,8},{10,11... | collective-permute-start | bytes 884744 | tf_op jit(solution)/shard_map/ppermute | solution.py:229

commit v13 on v1

v13 whole, which is shorter than its diff:
```python
import functools

import jax
import jax.numpy as jnp
from jax import lax
from jax.experimental import pallas as pl
from jax.experimental.pallas import tpu as pltpu
from jax.sharding import PartitionSpec as P

F32, BF16 = jnp.float32, jnp.bfloat16
INNER = (((1,), (1,)), ((), ()))


def call(body, out_shape, operands, scratch=(), after=()):
    outs = out_shape if isinstance(out_shape, (list, tuple)) else [out_shape]
    moved = sum(x.size * x.dtype.itemsize for x in list(operands) + list(outs))

    def run(*refs):
        body(*refs[: len(operands)], *refs[len(operands) + len(after) :])

    return pl.pallas_call(
        run,
        out_shape=out_shape,
        in_specs=[pl.BlockSpec(memory_space=pltpu.VMEM)] * len(operands) + [pl.BlockSpec(memory_space=pl.ANY)] * len(after),
        out_specs=jax.tree.map(lambda _: pl.BlockSpec(memory_space=pltpu.VMEM), out_shape),
        scratch_shapes=list(scratch),
        cost_estimate=pl.CostEstimate(flops=0, bytes_accessed=0, transcendentals=0),
        compiler_params=pltpu.CompilerParams(vmem_limit_bytes=min(56 << 20, (8 << 20) + 3 * moved)),
    )(*operands, *after)


def column(row):
    shape = (row.shape[1], row.shape[1])
    eye = lax.broadcasted_iota(jnp.int32, shape, 0) == lax.broadcasted_iota(jnp.int32, shape, 1)
    return jnp.sum(jnp.where(eye, row, 0.0), axis=1, keepdims=True)


def lane_row(col):
    shape = (col.shape[0], col.shape[0])
    eye = lax.broadcasted_iota(jnp.int32, shape, 0) == lax.broadcasted_iota(jnp.int32, shape, 1)
    return jnp.sum(jnp.where(eye, col, 0.0), axis=0, keepdims=True)


def place(nrow, ncol, rows, k, c):
    return pl.multiple_of(((lax.axis_index("row") ^ k) * ncol + c) * rows, rows)


def group(ncol, rows, k):
    at = (lax.axis_index("row") ^ k) * ncol * rows
    return pl.ds(pl.multiple_of(at, 2 * rows), ncol * rows)


def side(k):
    top = k.bit_length() - 1
    return lax.rem(lax.shift_right_logical(lax.axis_index("row"), top), 2)


def cut_kernel(nrow, teach, *outs):
    part = teach.shape[1] // 2
    for k in range(1, nrow):
        at = pl.multiple_of((1 - side(k)) * part, part)
        outs[k - 1][...] = teach[:, pl.ds(at, part)]


def tag_kernel(teach, scale, out):
    ts = teach[...].astype(F32)
    s = scale[...].astype(F32)
    mass = jnp.sum(jnp.square(column(s)) * jnp.sum(ts * ts, axis=1, keepdims=True), keepdims=True)
    at = lax.broadcasted_iota(jnp.int32, out.shape, 0)
    out[...] = jnp.where(at < 4, jnp.concatenate([s, s], axis=1), mass)


def gram_kernel(nrow, ncol, rows, *refs):
    own, tags, pieces = refs[:ncol], refs[ncol : 2 * ncol], refs[2 * ncol : 2 * ncol + nrow - 1]
    local, note, *outs = refs[2 * ncol + nrow - 1 : -1]
    held = refs[-1]
    away, beside = outs[: nrow - 1], outs[nrow - 1 :]
    part = held.shape[1] // 2
    for c in range(ncol):
        held[c * rows : (c + 1) * rows, :] = own[c][...]
    lane = lax.broadcasted_iota(jnp.int32, (8, 2 * rows), 1)
    at = lax.broadcasted_iota(jnp.int32, (8, 2 * rows), 0)
    mass = sum(t[4:5, :1] for t in tags)
    for c in range(0, ncol, 2):
        pair = jnp.where(lane < rows, tags[c][0:1, :], tags[c + 1][0:1, :])
        note[:, c * rows : (c + 2) * rows] = jnp.where(at < 4, pair, mass)
    for k in range(1, nrow):
        piece = pieces[k - 1][...]
        mine = held[:, pl.ds(pl.multiple_of(side(k) * part, part), part)]
        away[k - 1][:rows, :] = lax.dot_general(piece, mine, INNER, preferred_element_type=F32)
        away[k - 1][rows:, :] = note[...]
        here = lax.dot_general(mine, piece, INNER, preferred_element_type=F32)
        for c in range(1, ncol):
            beside[c - 1][:, (k - 1) * rows : k * rows] = here[c * rows : (c + 1) * rows, :]
        local[:, group(ncol, rows, k)] = jnp.concatenate([here[:rows, :], jnp.zeros((rows, (ncol - 1) * rows), F32)], axis=1)
    local[:, group(ncol, rows, 0)] = lax.dot_general(held[:rows, :], held[...], INNER, preferred_element_type=F32)


def sum_kernel(nrow, ncol, rows, local, note, *refs):
    away, beside, (out, vectors) = refs[: nrow - 1], refs[nrow - 1 : -2], refs[-2:]
    mass = note[4:5, :1]
    vectors[:, group(ncol, rows, 0)] = note[...]
    out[:rows, group(ncol, rows, 0)] = local[:, group(ncol, rows, 0)]
    for k in range(1, nrow):
        at = group(ncol, rows, k)
        block = local[:, at] + away[k - 1][:rows, :]
        more = [beside[ncol - c - 1][:, (k - 1) * rows : k * rows] for c in range(1, ncol)]
        out[:rows, at] = block + jnp.concatenate([jnp.zeros((rows, rows), F32)] + more, axis=1)
        vectors[:, at] = away[k - 1][rows:, :]
        mass = mass + away[k - 1][rows + 4 : rows + 5, :1]
    out[rows:, :] = jnp.broadcast_to(mass, (8, out.shape[1]))


def pack_kernel(*refs):
    out, at = refs[-1], 0
    for r in refs[:-1]:
        out[at : at + r.shape[0], :] = r[...]
        at += r.shape[0]


def assemble(nrow, ncol, rows, keys, refs, held):
    for c in range(ncol):
        for n, k in enumerate(keys):
            held[pl.ds(place(nrow, ncol, rows, k, c), rows), :] = refs[c][n * rows : (n + 1) * rows, :]


def raw_gram_kernel(nrow, ncol, rows, keys, *refs):
    out, raw = refs[ncol:]
    assemble(nrow, ncol, rows, keys, refs, raw)
    out[:rows, :] = lax.dot_general(refs[0][:rows, :], raw[...], INNER, preferred_element_type=F32)
    for at in range(0, raw.shape[0], 128):
        squares = jnp.sum(jnp.square(raw[at : at + 128, :].astype(F32)), axis=1, keepdims=True)
        out[rows:, at : at + 128] = jnp.broadcast_to(lane_row(squares), (8, 128))


def normalize(raw, squares, units):
    for at in range(0, raw.shape[0], 128):
        inverse = 1.0 / jnp.sqrt(column(squares[:1, at : at + 128]))
        units[at : at + 128, :] = (raw[at : at + 128, :].astype(F32) * inverse).astype(BF16)


def unit_gram_kernel(ncol, mine, other, *refs):
    rows = mine.shape[0] - 8
    gram, inverses, squares = refs[1:4] if len(refs) > 3 else refs
    squares[...] = mine[rows:, :] + other[rows:, :]
    at = pl.multiple_of(lax.axis_index("row") * ncol * rows, 2 * rows)
    inverse = 1.0 / jnp.sqrt(column(squares[:1, pl.ds(at, 2 * rows)][:, :rows]))
    inverses[...] = jnp.broadcast_to(inverse, inverses.shape)
    gram[...] = (mine[:rows, :] + other[:rows, :]) * (inverse * (1.0 / jnp.sqrt(squares[:1, :])))
    if len(refs) > 3:
        normalize(refs[0], squares, refs[4])


def final_kernel(nrow, ncol, keys, mine, other, vectors, gram, inverses, squares, stud, scale, *refs):
    rows = stud.shape[0]
    if keys:
        out, units = refs[-2:]
        assemble(nrow, ncol, rows, keys, refs, units)
        normalize(units, squares, units)
    else:
        units, out = refs
    inverse = inverses[:, :1]
    mass = (mine[rows : rows + 1, :1] + other[rows : rows + 1, :1]) / mine.shape[1]
    outer = (column(scale[...].astype(F32)) / mass) * vectors[:1, :]
    error_b = (gram[...] - outer * (mine[:rows, :] + other[:rows, :])).astype(BF16)
    grads = 4.0 * jnp.dot(error_b, units[...], preferred_element_type=F32)
    along = 4.0 * jnp.sum(error_b.astype(F32) * gram[...], axis=1, keepdims=True)
    unit = stud[...].astype(F32) * inverse
    out[...] = (grads - along * unit) * inverse


def shards(student, teacher, scale):
    rows, half = student.shape
    nrow, ncol = lax.axis_size("row"), lax.axis_size("col")
    batch, width = rows * nrow * ncol, teacher.shape[1]
    small = batch <= 2048
    sds = jax.ShapeDtypeStruct
    scale = scale.reshape(1, rows)

    def along_row(x, k):
        return lax.ppermute(x, "row", [(i, i ^ k) for i in range(nrow)])

    def along_col(x, c):
        return lax.ppermute(x, "col", [(i, (i - c) % ncol) for i in range(ncol)])

    def other_core(x):
        return lax.ppermute(x, "sub", [(0, 1), (1, 0)])

    def with_columns(x):
        return [x if c == 0 else along_col(x, c) for c in range(ncol)]

    def pack(xs, after=()):
        if len(xs) == 1:
            return xs[0]
        return call(pack_kernel, sds((sum(x.shape[0] for x in xs), half), BF16), xs, after=after)

    cuts = call(functools.partial(cut_kernel, nrow), [sds((rows, width // 2), BF16)] * (nrow - 1), [teacher])
    others = list(range(nrow // 2, nrow)) + list(range(1, nrow // 2))
    came = {k: along_row(cuts[k - 1], k) for k in others}
    own = with_columns(teacher)
    tags = with_columns(call(tag_kernel, sds((8, 2 * rows), F32), [teacher, scale]))

    stack, keys, k = [student], [0], nrow // 2
    while k:
        stack.append(along_row(pack(stack, after=own[1:]), k))
        keys, k = keys + [n ^ k for n in keys], k // 2
    raw_refs = with_columns(pack(stack, after=list(came.values()) + tags[1:] + own[1:]))
    raw_gram, *raw = call(
        functools.partial(raw_gram_kernel, nrow, ncol, rows, keys),
        [sds((rows + 8, batch), F32)] + ([sds((batch, half), BF16)] if small else []),
        raw_refs,
        scratch=[] if small else [pltpu.VMEM((batch, half), BF16)],
    )
    gram, inverses, squares, *units = call(
        functools.partial(unit_gram_kernel, ncol),
        [sds((rows, batch), F32), sds((rows, 128), F32), sds((8, batch), F32)] + ([sds((batch, half), BF16)] if small else []),
        [raw_gram, other_core(raw_gram)] + raw,
    )

    local, note, *outs = call(
        functools.partial(gram_kernel, nrow, ncol, rows),
        [sds((rows, batch), F32), sds((8, ncol * rows), F32)]
        + [sds((rows + 8, ncol * rows), F32)] * (nrow - 1)
        + [sds((rows, (nrow - 1) * rows), F32)] * (ncol - 1),
        own + tags + [came[k] for k in range(1, nrow)],
        scratch=[pltpu.VMEM((ncol * rows, width), BF16)],
    )
    away = {k: along_row(outs[k - 1], k) for k in others}
    beside = [along_col(outs[nrow - 2 + c], -c) for c in range(1, ncol)]
    message, vectors = call(
        functools.partial(sum_kernel, nrow, ncol, rows),
        [sds((rows + 8, batch), F32), sds((8, batch), F32)],
        [local, note] + [away[k] for k in range(1, nrow)] + beside,
    )
    return call(
        functools.partial(final_kernel, nrow, ncol, None if small else keys),
        sds((rows, half), F32),
        [message, other_core(message), vectors, gram, inverses, squares, student, scale] + (units if small else raw_refs),
        scratch=[] if small else [pltpu.VMEM((batch, half), BF16)],
    )


def solution(mesh):
    spec = P(("groups", "row", "col"), "sub")
    return jax.shard_map(
        shards,
        mesh=mesh,
        in_specs=(spec, spec, P(("groups", "row", "col"))),
        out_specs=spec,
        check_vma=False,
    )
```

time: 55.5 us -> 34.4 us (0.62)
  blocking collectives: 20.6 us -> 0 us
  starting transfers between devices: 5.01 us -> 18.8 us
  waiting for transfers between devices: 21.1 us -> 11.6 us
  other arithmetic: 4.12 us -> 0 us
  Pallas kernels: 0 us -> 2.73 us
  matrix products: 1.58 us -> 0 us
  between operations: 1.44 us -> 0.1 us
    all_to_all x1 -> x0, blocking collectives: 20.6 us -> none  [shards(): lax.all_to_all(packed, 'row', 0, 0, tiled=True)]
    ppermute x2 -> x14, starting transfers between devices: 1.56 us -> 18.8 us  [the longest x8 12.4 us: along_row(): return lax.ppermute(x, 'row', [(i, i ^ k) for i in range(nrow)])]
    all_to_all x1 -> x0, waiting for transfers between devices: 8.55 us -> none  [shards(): lax.all_to_all(sent, 'row', 0, 0, tiled=True).astype(F32)]
    all_to_all x1 -> x0, starting transfers between devices: 3.45 us -> none  [shards(): lax.all_to_all(sent, 'row', 0, 0, tiled=True).astype(F32)]
    pallas_call x0 -> x9, Pallas kernels: none -> 2.73 us  [call(): pl.pallas_call(run, out_shape=out_shape, in_specs=[pl.BlockSpec(memory_sp...]
    convert_element_type x2 -> x0, other arithmetic: 1.72 us -> none  [shards(): scaled = (teacher.astype(F32) * scale.astype(F32)[:, None]).astype(BF16)]
    dot_general x3 -> x0, matrix products: 1.58 us -> none  [the longest x1 0.97 us: shards(): grads = 4.0 * jnp.dot(error_b, unit_b, preferred_element_type=F32)]
    reduce_sum x3 -> x0, other arithmetic: 1.21 us -> none  [the longest x1 0.96 us: shards(): square_part = jnp.sum(xs * xs, axis=1)]
  transfers between devices with their start and end apart: 3 -> 14, of which waited for: 3 -> 5; matrix products, arithmetic and copies ran while one was open for 1% -> 0% of each run, Pallas kernels for 0% -> 5%
where the time goes in v13:
time: 34.4 us; the launch traced here: 34.2 us
  starting transfers between devices  18.8 us (55%)
  waiting for transfers between devices  11.6 us (34%)
  Pallas kernels  2.73 us (8%)
  local copies, waits for them, and re-layouts  0.97 us (3%)
    ppermute x8, starting transfers between devices, along_row(): return lax.ppermute(x, 'row', [(i, i ^ k) for i in range(nrow)])  12.4 us
    ppermute x8, waiting for transfers between devices, along_row(): return lax.ppermute(x, 'row', [(i, i ^ k) for i in range(nrow)])  8.02 us
    ppermute x4, starting transfers between devices, along_col(): return lax.ppermute(x, 'col', [(i, (i - c) % ncol) for i in range(ncol)])  6.27 us
    pallas_call x9, Pallas kernels, call(): pl.pallas_call(run, out_shape=out_shape, in_specs=[pl.BlockSpec(memory_sp...  2.73 us
    ppermute x4, waiting for transfers between devices, along_col(): return lax.ppermute(x, 'col', [(i, (i - c) % ncol) for i in range(ncol)])  2.5 us
    ppermute x2, waiting for transfers between devices, other_core(): return lax.ppermute(x, 'sub', [(0, 1), (1, 0)])  1.08 us
    unnamed x8, local copies, waits for them, and re-layouts  0.97 us
  transfers between devices with their start and end apart: 14, of which 5 were waited for; matrix products, arithmetic and copies ran while one was open for 0% of the time, Pallas kernels for 5%

profile of v13, /device:TPU:0, one launch (start us, length us, event | category | flops | bytes accessed | tf_op | source)
XLA Modules:
  0.0 34.2 jit_solution(12283427756304097374)
XLA Ops:
  0.0 2.9 %collective-permute-start = (bf16[64,2048]{1,0:T(8,128)(2,1)}, bf16[64,2048]{1,0:T(8,128)(2,1)S(1)}, u32[]{:S(2)}, u32[]{:S(2)}) collective-permute-start(bf16[64,2048]{1,0:T(8,128)(2,1)} %refs_0_.7), channel_id=1, source_target_pairs={{0,2},{2,0},{1,3},{3,1},{4,6},{6,4},{5,7},{7,5},{8,10},{10,8},{9,1... | collective-permute-start | bytes 786440 | tf_op jit(solution)/shard_map/ppermute | solution.py:184
  2.9 2.6 %collective-permute-start.10 = (bf16[64,512]{1,0:T(8,128)(2,1)}, bf16[64,512]{1,0:T(8,128)(2,1)S(1)}, u32[]{:S(2)}, u32[]{:S(2)}) collective-permute-start(bf16[64,512]{1,0:T(8,128)(2,1)} %refs_6_.1), channel_id=1, source_target_pairs={{0,8},{4,12},{8,0},{12,4},{1,9},{5,13},{9,1},{13,5},{2,10},{6,14},... | collective-permute-start | bytes 196616 | tf_op jit(solution)/shard_map/ppermute | solution.py:181
  5.5 0.0 copy-start
  5.5 0.9 %copy-done = bf16[64,2048]{1,0:T(8,128)(2,1)S(1)} copy-done((bf16[64,2048]{1,0:T(8,128)(2,1)S(1)}, bf16[64,2048]{1,0:T(8,128)(2,1)}, u32[]{:S(2)}) %copy-start) | copy-done | bytes 262168
  6.5 0.0 copy-start.2
  6.5 1.6 %collective-permute-start.2 = (bf16[64,1024]{1,0:T(8,128)(2,1)S(1)}, bf16[64,1024]{1,0:T(8,128)(2,1)S(1)}, u32[]{:S(2)}, u32[]{:S(2)}) collective-permute-start(bf16[64,1024]{1,0:T(8,128)(2,1)S(1)} %get-tuple-element.22), channel_id=1, source_target_pairs={{0,4},{4,0},{8,12},{12,8},{1,5},{5,1},{9,13},{13,9},{2,6},{6,2},{1... | collective-permute-start | bytes 393224 | tf_op jit(solution)/shard_map/ppermute | solution.py:181
  8.2 0.3 collective-permute-start.3
  8.5 2.5 %collective-permute-start.4 = (bf16[64,1024]{1,0:T(8,128)(2,1)S(1)}, bf16[64,1024]{1,0:T(8,128)(2,1)S(1)}, u32[]{:S(2)}, u32[]{:S(2)}) collective-permute-start(bf16[64,1024]{1,0:T(8,128)(2,1)S(1)} %get-tuple-element.24), channel_id=1, source_target_pairs={{0,12},{4,8},{8,4},{12,0},{1,13},{5,9},{9,5},{13,1},{2,14},{6,10},... | collective-permute-start | bytes 393224 | tf_op jit(solution)/shard_map/ppermute | solution.py:181
  11.0 0.0 collective-permute-done.10.refs_1_
  11.0 0.0 collective-permute-done.refs_1_.refs_2_.refs_7_
  11.0 0.0 copy-done.2
  11.0 0.0 copy-start.3
  11.0 0.7 %collective-permute-start.11 = (bf16[128,512]{1,0:T(8,128)(2,1)S(1)}, bf16[128,512]{1,0:T(8,128)(2,1)S(1)}, u32[]{:S(2)}, u32[]{:S(2)}) collective-permute-start(bf16[128,512]{1,0:T(8,128)(2,1)S(1)} %shard_map.41), channel_id=1, source_target_pairs={{0,4},{4,0},{8,12},{12,8},{1,5},{5,1},{9,13},{13,9},{2,6},{6,2},{1... | collective-permute-start | bytes 393224 | tf_op jit(solution)/shard_map/ppermute | solution.py:181
  11.8 0.0 copy-done.3
  11.8 0.3 shard_map.37.refs_2_
  12.0 0.0 copy-start.1
  12.0 1.2 %collective-permute-start.1 = (f32[8,128]{1,0:T(8,128)S(1)}, f32[8,128]{1,0:T(8,128)S(1)}, u32[]{:S(2)}, u32[]{:S(2)}) collective-permute-start(f32[8,128]{1,0:T(8,128)S(1)} %shard_map.37.refs_2_), channel_id=1, source_target_pairs={{0,2},{2,0},{1,3},{3,1},{4,6},{6,4},{5,7},{7,5},{8,10},{10,8},{9,1... | collective-permute-start | bytes 12296 | tf_op jit(solution)/shard_map/ppermute | solution.py:184
  13.2 2.5 %collective-permute-done.1.refs_3_.refs_6_ = f32[8,128]{1,0:T(8,128)S(1)} collective-permute-done((f32[8,128]{1,0:T(8,128)S(1)}, f32[8,128]{1,0:T(8,128)S(1)}, u32[]{:S(2)}, u32[]{:S(2)}) %collective-permute-start.1) | collective-permute-done | bytes 4128 | tf_op jit(solution)/shard_map/ppermute | solution.py:184
  15.7 0.0 collective-permute-done.2.refs_4_.refs_5_
  15.7 4.5 %collective-permute-done.3.refs_5_.refs_3_ = bf16[64,1024]{1,0:T(8,128)(2,1)S(1)} collective-permute-done((bf16[64,1024]{1,0:T(8,128)(2,1)S(1)}, bf16[64,1024]{1,0:T(8,128)(2,1)S(1)}, u32[]{:S(2)}, u32[]{:S(2)}) %collective-permute-start.3) | collective-permute-done | bytes 131104 | tf_op jit(solution)/shard_map/ppermute | solution.py:181
  20.2 0.0 collective-permute-done.4.refs_6_.refs_4_
  20.2 0.0 collective-permute-done.11.refs_2_
  20.2 0.6 %collective-permute-start.12 = (bf16[256,512]{1,0:T(8,128)(2,1)S(1)}, bf16[256,512]{1,0:T(8,128)(2,1)S(1)}, u32[]{:S(2)}, u32[]{:S(2)}) collective-permute-start(bf16[256,512]{1,0:T(8,128)(2,1)S(1)} %shard_map.42.refs_0_), channel_id=1, source_target_pairs={{0,2},{2,0},{1,3},{3,1},{4,6},{6,4},{5,7},{7,5},{8,10},{10,8},{9,1... | collective-permute-start | bytes 786440 | tf_op jit(solution)/shard_map/ppermute | solution.py:184
  20.8 0.0 copy-done.1
  20.8 0.7 %shard_map.39 = (f32[64,512]{1,0:T(8,128)S(1)}, f32[8,128]{1,0:T(8,128)S(1)}, f32[72,128]{1,0:T(8,128)S(1)}, f32[72,128]{1,0:T(8,128)S(1)}, f32[72,128]{1,0:T(8,128)S(1)}, /*index=5*/f32[64,192]{1,0:T(8,128)S(1)}) custom-call(bf16[64,2048]{1,0:T(8,128)(2,1)S(1)} %copy-done.1, bf16[64,2048]{1,0:T(8,128)(2,1)S(1)} %collective-permute-done.refs_1_.refs_2_.refs_7_, ...), custom_call_target="tpu_custom_call" | custom-call | tf_op jit(solution)/shard_map/pallas_call | solution.py:21
  21.5 1.6 %collective-permute-start.8 = (f32[64,192]{1,0:T(8,128)S(1)}, f32[64,192]{1,0:T(8,128)S(1)}, u32[]{:S(2)}, u32[]{:S(2)}) collective-permute-start(f32[64,192]{1,0:T(8,128)S(1)} %get-tuple-element.30), channel_id=1, source_target_pairs={{0,2},{2,0},{1,3},{3,1},{4,6},{6,4},{5,7},{7,5},{8,10},{10,8},{9,1... | collective-permute-start | bytes 147464 | tf_op jit(solution)/shard_map/ppermute | solution.py:184
  23.1 2.3 %collective-permute-start.5 = (f32[72,128]{1,0:T(8,128)S(1)}, f32[72,128]{1,0:T(8,128)S(1)}, u32[]{:S(2)}, u32[]{:S(2)}) collective-permute-start(f32[72,128]{1,0:T(8,128)S(1)} %get-tuple-element.27), channel_id=1, source_target_pairs={{0,4},{4,0},{8,12},{12,8},{1,5},{5,1},{9,13},{13,9},{2,6},{6,2},{1... | collective-permute-start | bytes 110600 | tf_op jit(solution)/shard_map/ppermute | solution.py:181
  25.4 0.5 %collective-permute-start.6 = (f32[72,128]{1,0:T(8,128)S(1)}, f32[72,128]{1,0:T(8,128)S(1)}, u32[]{:S(2)}, u32[]{:S(2)}) collective-permute-start(f32[72,128]{1,0:T(8,128)S(1)} %get-tuple-element.28), channel_id=1, source_target_pairs={{0,8},{4,12},{8,0},{12,4},{1,9},{5,13},{9,1},{13,5},{2,10},{6,14},... | collective-permute-start | bytes 110600 | tf_op jit(solution)/shard_map/ppermute | solution.py:181
  25.9 1.8 %collective-permute-start.7 = (f32[72,128]{1,0:T(8,128)S(1)}, f32[72,128]{1,0:T(8,128)S(1)}, u32[]{:S(2)}, u32[]{:S(2)}) collective-permute-start(f32[72,128]{1,0:T(8,128)S(1)} %get-tuple-element.29), channel_id=1, source_target_pairs={{0,12},{4,8},{8,4},{12,0},{1,13},{5,9},{9,5},{13,1},{2,14},{6,10},... | collective-permute-start | bytes 110600 | tf_op jit(solution)/shard_map/ppermute | solution.py:181
  27.8 0.0 collective-permute-done.12.refs_1_
  27.8 0.3 shard_map.43
  28.1 0.1 collective-permute-start.13
  28.2 0.0 collective-permute-done.5.refs_2_
  28.2 2.1 %collective-permute-done.6.refs_3_ = f32[72,128]{1,0:T(8,128)S(1)} collective-permute-done((f32[72,128]{1,0:T(8,128)S(1)}, f32[72,128]{1,0:T(8,128)S(1)}, u32[]{:S(2)}, u32[]{:S(2)}) %collective-permute-start.6) | collective-permute-done | bytes 36896 | tf_op jit(solution)/shard_map/ppermute | solution.py:181
  30.3 1.4 %collective-permute-done.7.refs_4_ = f32[72,128]{1,0:T(8,128)S(1)} collective-permute-done((f32[72,128]{1,0:T(8,128)S(1)}, f32[72,128]{1,0:T(8,128)S(1)}, u32[]{:S(2)}, u32[]{:S(2)}) %collective-permute-start.7) | collective-permute-done | bytes 36896 | tf_op jit(solution)/shard_map/ppermute | solution.py:181
  31.7 0.0 collective-permute-done.8.refs_5_
  31.7 0.1 shard_map.40
  31.8 0.1 collective-permute-start.9
  31.9 0.0 collective-permute-done.13.refs_1_
  31.9 0.3 shard_map.44
  32.1 1.1 %collective-permute-done.9.refs_1_ = f32[72,512]{1,0:T(8,128)S(1)} collective-permute-done((f32[72,512]{1,0:T(8,128)S(1)}, f32[72,512]{1,0:T(8,128)S(1)}, u32[]{:S(2)}, u32[]{:S(2)}) %collective-permute-start.9) | collective-permute-done | bytes 147488 | tf_op jit(solution)/shard_map/ppermute | solution.py:187
  33.2 1.0 %shard_map.45 = f32[64,512]{1,0:T(8,128)} custom-call(f32[72,512]{1,0:T(8,128)S(1)} %get-tuple-element.31.refs_0_, f32[72,512]{1,0:T(8,128)S(1)} %collective-permute-done.9.refs_1_, f32[8,512]{1,0:T(8,128)S(1)} %get-tuple-element.32.refs_2_, f32[64,512]{1,0:T(8,128)S(1)} %get-tuple-element.35.refs_3_, f32[64,128]{1,0:T(8,128)S(1)} %get-tuple-element.36.refs_4_, ...), custom_call_target="tpu_custom_call" | custom-call | tf_op jit(solution)/shard_map/pallas_call | solution.py:21
  (3 shorter events, 0.1 us)
Async XLA Ops:
  0.0 11.0 %collective-permute-start = (bf16[64,2048]{1,0:T(8,128)(2,1)}, bf16[64,2048]{1,0:T(8,128)(2,1)S(1)}, u32[]{:S(2)}, u32[]{:S(2)}) collective-permute-start(bf16[64,2048]{1,0:T(8,128)(2,1)} %refs_0_.7), channel_id=1, source_target_pairs={{0,2},{2,0},{1,3},{3,1},{4,6},{6,4},{5,7},{7,5},{8,10},{10,8},{9,1... | collective-permute-start | bytes 786440 | tf_op jit(solution)/shard_map/ppermute | solution.py:184
  2.9 8.0 %collective-permute-start.10 = (bf16[64,512]{1,0:T(8,128)(2,1)}, bf16[64,512]{1,0:T(8,128)(2,1)S(1)}, u32[]{:S(2)}, u32[]{:S(2)}) collective-permute-start(bf16[64,512]{1,0:T(8,128)(2,1)} %refs_6_.1), channel_id=1, source_target_pairs={{0,8},{4,12},{8,0},{12,4},{1,9},{5,13},{9,1},{13,5},{2,10},{6,14},... | collective-permute-start | bytes 196616 | tf_op jit(solution)/shard_map/ppermute | solution.py:181
  5.5 0.9 %copy-start = (bf16[64,2048]{1,0:T(8,128)(2,1)S(1)}, bf16[64,2048]{1,0:T(8,128)(2,1)}, u32[]{:S(2)}) copy-start(bf16[64,2048]{1,0:T(8,128)(2,1)} %refs_0_.7) | copy-start | bytes 786436
  6.5 4.5 %copy-start.2 = (bf16[64,512]{1,0:T(8,128)(2,1)S(1)}, bf16[64,512]{1,0:T(8,128)(2,1)}, u32[]{:S(2)}) copy-start(bf16[64,512]{1,0:T(8,128)(2,1)} %refs_6_.1) | copy-start | bytes 196612
  6.5 9.2 %collective-permute-start.2 = (bf16[64,1024]{1,0:T(8,128)(2,1)S(1)}, bf16[64,1024]{1,0:T(8,128)(2,1)S(1)}, u32[]{:S(2)}, u32[]{:S(2)}) collective-permute-start(bf16[64,1024]{1,0:T(8,128)(2,1)S(1)} %get-tuple-element.22), channel_id=1, source_target_pairs={{0,4},{4,0},{8,12},{12,8},{1,5},{5,1},{9,13},{13,9},{2,6},{6,2},{1... | collective-permute-start | bytes 393224 | tf_op jit(solution)/shard_map/ppermute | solution.py:181
  8.2 12.1 %collective-permute-start.3 = (bf16[64,1024]{1,0:T(8,128)(2,1)S(1)}, bf16[64,1024]{1,0:T(8,128)(2,1)S(1)}, u32[]{:S(2)}, u32[]{:S(2)}) collective-permute-start(bf16[64,1024]{1,0:T(8,128)(2,1)S(1)} %get-tuple-element.23), channel_id=1, source_target_pairs={{0,8},{4,12},{8,0},{12,4},{1,9},{5,13},{9,1},{13,5},{2,10},{6,14},... | collective-permute-start | bytes 393224 | tf_op jit(solution)/shard_map/ppermute | solution.py:181
  8.5 11.7 %collective-permute-start.4 = (bf16[64,1024]{1,0:T(8,128)(2,1)S(1)}, bf16[64,1024]{1,0:T(8,128)(2,1)S(1)}, u32[]{:S(2)}, u32[]{:S(2)}) collective-permute-start(bf16[64,1024]{1,0:T(8,128)(2,1)S(1)} %get-tuple-element.24), channel_id=1, source_target_pairs={{0,12},{4,8},{8,4},{12,0},{1,13},{5,9},{9,5},{13,1},{2,14},{6,10},... | collective-permute-start | bytes 393224 | tf_op jit(solution)/shard_map/ppermute | solution.py:181
  11.0 0.8 %copy-start.3 = (bf16[64]{0:T(256)(128)(2,1)S(1)}, bf16[64]{0:T(256)(128)(2,1)}, u32[]{:S(2)}) copy-start(bf16[64]{0:T(256)(128)(2,1)} %param.5) | copy-start | bytes 388
  11.0 9.2 %collective-permute-start.11 = (bf16[128,512]{1,0:T(8,128)(2,1)S(1)}, bf16[128,512]{1,0:T(8,128)(2,1)S(1)}, u32[]{:S(2)}, u32[]{:S(2)}) collective-permute-start(bf16[128,512]{1,0:T(8,128)(2,1)S(1)} %shard_map.41), channel_id=1, source_target_pairs={{0,4},{4,0},{8,12},{12,8},{1,5},{5,1},{9,13},{13,9},{2,6},{6,2},{1... | collective-permute-start | bytes 393224 | tf_op jit(solution)/shard_map/ppermute | solution.py:181
  12.0 8.8 %copy-start.1 = (bf16[64,2048]{1,0:T(8,128)(2,1)S(1)}, bf16[64,2048]{1,0:T(8,128)(2,1)}, u32[]{:S(2)}) copy-start(bf16[64,2048]{1,0:T(8,128)(2,1)} %refs_0_.7) | copy-start | bytes 786436
  12.0 3.7 %collective-permute-start.1 = (f32[8,128]{1,0:T(8,128)S(1)}, f32[8,128]{1,0:T(8,128)S(1)}, u32[]{:S(2)}, u32[]{:S(2)}) collective-permute-start(f32[8,128]{1,0:T(8,128)S(1)} %shard_map.37.refs_2_), channel_id=1, source_target_pairs={{0,2},{2,0},{1,3},{3,1},{4,6},{6,4},{5,7},{7,5},{8,10},{10,8},{9,1... | collective-permute-start | bytes 12296 | tf_op jit(solution)/shard_map/ppermute | solution.py:184
  20.2 7.5 %collective-permute-start.12 = (bf16[256,512]{1,0:T(8,128)(2,1)S(1)}, bf16[256,512]{1,0:T(8,128)(2,1)S(1)}, u32[]{:S(2)}, u32[]{:S(2)}) collective-permute-start(bf16[256,512]{1,0:T(8,128)(2,1)S(1)} %shard_map.42.refs_0_), channel_id=1, source_target_pairs={{0,2},{2,0},{1,3},{3,1},{4,6},{6,4},{5,7},{7,5},{8,10},{10,8},{9,1... | collective-permute-start | bytes 786440 | tf_op jit(solution)/shard_map/ppermute | solution.py:184
  21.5 10.1 %collective-permute-start.8 = (f32[64,192]{1,0:T(8,128)S(1)}, f32[64,192]{1,0:T(8,128)S(1)}, u32[]{:S(2)}, u32[]{:S(2)}) collective-permute-start(f32[64,192]{1,0:T(8,128)S(1)} %get-tuple-element.30), channel_id=1, source_target_pairs={{0,2},{2,0},{1,3},{3,1},{4,6},{6,4},{5,7},{7,5},{8,10},{10,8},{9,1... | collective-permute-start | bytes 147464 | tf_op jit(solution)/shard_map/ppermute | solution.py:184
  23.1 5.0 %collective-permute-start.5 = (f32[72,128]{1,0:T(8,128)S(1)}, f32[72,128]{1,0:T(8,128)S(1)}, u32[]{:S(2)}, u32[]{:S(2)}) collective-permute-start(f32[72,128]{1,0:T(8,128)S(1)} %get-tuple-element.27), channel_id=1, source_target_pairs={{0,4},{4,0},{8,12},{12,8},{1,5},{5,1},{9,13},{13,9},{2,6},{6,2},{1... | collective-permute-start | bytes 110600 | tf_op jit(solution)/shard_map/ppermute | solution.py:181
  25.4 4.9 %collective-permute-start.6 = (f32[72,128]{1,0:T(8,128)S(1)}, f32[72,128]{1,0:T(8,128)S(1)}, u32[]{:S(2)}, u32[]{:S(2)}) collective-permute-start(f32[72,128]{1,0:T(8,128)S(1)} %get-tuple-element.28), channel_id=1, source_target_pairs={{0,8},{4,12},{8,0},{12,4},{1,9},{5,13},{9,1},{13,5},{2,10},{6,14},... | collective-permute-start | bytes 110600 | tf_op jit(solution)/shard_map/ppermute | solution.py:181
  25.9 5.8 %collective-permute-start.7 = (f32[72,128]{1,0:T(8,128)S(1)}, f32[72,128]{1,0:T(8,128)S(1)}, u32[]{:S(2)}, u32[]{:S(2)}) collective-permute-start(f32[72,128]{1,0:T(8,128)S(1)} %get-tuple-element.29), channel_id=1, source_target_pairs={{0,12},{4,8},{8,4},{12,0},{1,13},{5,9},{9,5},{13,1},{2,14},{6,10},... | collective-permute-start | bytes 110600 | tf_op jit(solution)/shard_map/ppermute | solution.py:181
  28.1 3.8 %collective-permute-start.13 = (f32[72,512]{1,0:T(8,128)S(1)}, f32[72,512]{1,0:T(8,128)S(1)}, u32[]{:S(2)}, u32[]{:S(2)}) collective-permute-start(f32[72,512]{1,0:T(8,128)S(1)} %get-tuple-element.33.refs_0_), channel_id=1, source_target_pairs={{0,1},{1,0},{2,3},{3,2},{4,5},{5,4},{6,7},{7,6},{8,9},{9,8},{10,11... | collective-permute-start | bytes 442376 | tf_op jit(solution)/shard_map/ppermute | solution.py:187
  31.8 1.4 %collective-permute-start.9 = (f32[72,512]{1,0:T(8,128)S(1)}, f32[72,512]{1,0:T(8,128)S(1)}, u32[]{:S(2)}, u32[]{:S(2)}) collective-permute-start(f32[72,512]{1,0:T(8,128)S(1)} %get-tuple-element.31.refs_0_), channel_id=1, source_target_pairs={{0,1},{1,0},{2,3},{3,2},{4,5},{5,4},{6,7},{7,6},{8,9},{9,8},{10,11... | collective-permute-start | bytes 442376 | tf_op jit(solution)/shard_map/ppermute | solution.py:187

commit v14 on v13

--- a/solution.py
+++ b/solution.py
@@ -119,13 +119,15 @@
 
 
 def assemble(nrow, ncol, rows, keys, refs, held):
+    half = nrow // 2
     for c in range(ncol):
         for n, k in enumerate(keys):
-            held[pl.ds(place(nrow, ncol, rows, k, c), rows), :] = refs[c][n * rows : (n + 1) * rows, :]
+            ref, at = refs[2 * c + n // half], n % half * rows
+            held[pl.ds(place(nrow, ncol, rows, k, c), rows), :] = ref[at : at + rows, :]
 
 
 def raw_gram_kernel(nrow, ncol, rows, keys, *refs):
-    out, raw = refs[ncol:]
+    out, raw = refs[2 * ncol :]
     assemble(nrow, ncol, rows, keys, refs, raw)
     out[:rows, :] = lax.dot_general(refs[0][:rows, :], raw[...], INNER, preferred_element_type=F32)
     for at in range(0, raw.shape[0], 128):
@@ -202,9 +204,15 @@
 
     stack, keys, k = [student], [0], nrow // 2
     while k:
-        stack.append(along_row(pack(stack, after=own[1:]), k))
+        joined = pack(stack, after=())
+        sent = joined
+        if k == 1:
+            first = with_columns(joined)
+            sent = call(pack_kernel, sds(joined.shape, BF16), [joined], after=first[1:] + [came[nrow - 1]])
+        stack.append(along_row(sent, k))
         keys, k = keys + [n ^ k for n in keys], k // 2
-    raw_refs = with_columns(pack(stack, after=list(came.values()) + tags[1:] + own[1:]))
+    second = with_columns(call(pack_kernel, sds(joined.shape, BF16), stack[-1:], after=list(came.values()) + tags[1:]))
+    raw_refs = [r for pair in zip(first, second) for r in pair]
     raw_gram, *raw = call(
         functools.partial(raw_gram_kernel, nrow, ncol, rows, keys),
         [sds((rows + 8, batch), F32)] + ([sds((batch, half), BF16)] if small else []),

time: 34.4 us -> 38.2 us (1.11)
  starting transfers between devices: 18.8 us -> 24.4 us
  waiting for transfers between devices: 11.6 us -> 9.87 us
    ppermute x8, starting transfers between devices: 12.4 us -> 18.5 us  [along_row(): return lax.ppermute(x, 'row', [(i, i ^ k) for i in range(nrow)])]
    ppermute x8, waiting for transfers between devices: 8.02 us -> 6.66 us  [along_row(): return lax.ppermute(x, 'row', [(i, i ^ k) for i in range(nrow)])]
    ppermute x4 -> x5, starting transfers between devices: 6.27 us -> 5.81 us  [along_col(): return lax.ppermute(x, 'col', [(i, (i - c) % ncol) for i in range(ncol)])]
    ppermute x4 -> x5, waiting for transfers between devices: 2.5 us -> 2.13 us  [along_col(): return lax.ppermute(x, 'col', [(i, (i - c) % ncol) for i in range(ncol)])]
    pallas_call x9 -> x10, Pallas kernels: 2.73 us -> 2.73 us  [call(): pl.pallas_call(run, out_shape=out_shape, in_specs=[pl.BlockSpec(memory_sp...]
  transfers between devices with their start and end apart: 14 -> 15, of which waited for: 5 -> 6; matrix products, arithmetic and copies ran while one was open for 0% -> 0% of each run, Pallas kernels for 5% -> 5%
where the time goes in v14:
time: 38.2 us; the launch traced here: 38.1 us
  starting transfers between devices  24.4 us (64%)
  waiting for transfers between devices  9.87 us (26%)
  Pallas kernels  2.73 us (7%)
  local copies, waits for them, and re-layouts  0.97 us (3%)
    ppermute x8, starting transfers between devices, along_row(): return lax.ppermute(x, 'row', [(i, i ^ k) for i in range(nrow)])  18.5 us
    ppermute x8, waiting for transfers between devices, along_row(): return lax.ppermute(x, 'row', [(i, i ^ k) for i in range(nrow)])  6.66 us
    ppermute x5, starting transfers between devices, along_col(): return lax.ppermute(x, 'col', [(i, (i - c) % ncol) for i in range(ncol)])  5.81 us
    pallas_call x10, Pallas kernels, call(): pl.pallas_call(run, out_shape=out_shape, in_specs=[pl.BlockSpec(memory_sp...  2.73 us
    ppermute x5, waiting for transfers between devices, along_col(): return lax.ppermute(x, 'col', [(i, (i - c) % ncol) for i in range(ncol)])  2.13 us
    ppermute x2, waiting for transfers between devices, other_core(): return lax.ppermute(x, 'sub', [(0, 1), (1, 0)])  1.08 us
    unnamed x8, local copies, waits for them, and re-layouts  0.97 us
  transfers between devices with their start and end apart: 15, of which 6 were waited for; matrix products, arithmetic and copies ran while one was open for 0% of the time, Pallas kernels for 5%

profile of v14, /device:TPU:0, one launch (start us, length us, event | category | flops | bytes accessed | tf_op | source)
XLA Modules:
  0.0 38.1 jit_solution(7623613088747916820)
XLA Ops:
  0.0 4.0 %collective-permute-start.10 = (bf16[64,512]{1,0:T(8,128)(2,1)}, bf16[64,512]{1,0:T(8,128)(2,1)S(1)}, u32[]{:S(2)}, u32[]{:S(2)}) collective-permute-start(bf16[64,512]{1,0:T(8,128)(2,1)} %refs_6_.1), channel_id=1, source_target_pairs={{0,8},{4,12},{8,0},{12,4},{1,9},{5,13},{9,1},{13,5},{2,10},{6,14},... | collective-permute-start | bytes 196616 | tf_op jit(solution)/shard_map/ppermute | solution.py:183
  4.0 0.0 copy-start
  4.0 0.9 %copy-done = bf16[64,2048]{1,0:T(8,128)(2,1)S(1)} copy-done((bf16[64,2048]{1,0:T(8,128)(2,1)S(1)}, bf16[64,2048]{1,0:T(8,128)(2,1)}, u32[]{:S(2)}) %copy-start) | copy-done | bytes 262168
  5.0 0.0 copy-start.2
  5.0 1.4 %collective-permute-start.4 = (bf16[64,1024]{1,0:T(8,128)(2,1)S(1)}, bf16[64,1024]{1,0:T(8,128)(2,1)S(1)}, u32[]{:S(2)}, u32[]{:S(2)}) collective-permute-start(bf16[64,1024]{1,0:T(8,128)(2,1)S(1)} %get-tuple-element.24), channel_id=1, source_target_pairs={{0,12},{4,8},{8,4},{12,0},{1,13},{5,9},{9,5},{13,1},{2,14},{6,10},... | collective-permute-start | bytes 393224 | tf_op jit(solution)/shard_map/ppermute | solution.py:183
  6.4 1.5 %collective-permute-done.10.refs_1_ = bf16[64,512]{1,0:T(8,128)(2,1)S(1)} collective-permute-done((bf16[64,512]{1,0:T(8,128)(2,1)}, bf16[64,512]{1,0:T(8,128)(2,1)S(1)}, u32[]{:S(2)}, u32[]{:S(2)}) %collective-permute-start.10) | collective-permute-done | bytes 65568 | tf_op jit(solution)/shard_map/ppermute | solution.py:183
  7.9 0.0 copy-done.2
  7.9 1.8 %collective-permute-start.11 = (bf16[128,512]{1,0:T(8,128)(2,1)S(1)}, bf16[128,512]{1,0:T(8,128)(2,1)S(1)}, u32[]{:S(2)}, u32[]{:S(2)}) collective-permute-start(bf16[128,512]{1,0:T(8,128)(2,1)S(1)} %shard_map.41.refs_0_), channel_id=1, source_target_pairs={{0,2},{2,0},{1,3},{3,1},{4,6},{6,4},{5,7},{7,5},{8,10},{10,8},{9,1... | collective-permute-start | bytes 393224 | tf_op jit(solution)/shard_map/ppermute | solution.py:186
  9.7 0.3 collective-permute-start
  10.0 3.9 %collective-permute-start.2 = (bf16[64,1024]{1,0:T(8,128)(2,1)S(1)}, bf16[64,1024]{1,0:T(8,128)(2,1)S(1)}, u32[]{:S(2)}, u32[]{:S(2)}) collective-permute-start(bf16[64,1024]{1,0:T(8,128)(2,1)S(1)} %get-tuple-element.22), channel_id=1, source_target_pairs={{0,4},{4,0},{8,12},{12,8},{1,5},{5,1},{9,13},{13,9},{2,6},{6,2},{1... | collective-permute-start | bytes 393224 | tf_op jit(solution)/shard_map/ppermute | solution.py:183
  13.9 3.3 %collective-permute-start.3 = (bf16[64,1024]{1,0:T(8,128)(2,1)S(1)}, bf16[64,1024]{1,0:T(8,128)(2,1)S(1)}, u32[]{:S(2)}, u32[]{:S(2)}) collective-permute-start(bf16[64,1024]{1,0:T(8,128)(2,1)S(1)} %get-tuple-element.23), channel_id=1, source_target_pairs={{0,8},{4,12},{8,0},{12,4},{1,9},{5,13},{9,1},{13,5},{2,10},{6,14},... | collective-permute-start | bytes 393224 | tf_op jit(solution)/shard_map/ppermute | solution.py:183
  17.2 0.0 collective-permute-done.4.refs_6_.refs_2_
  17.2 0.0 collective-permute-done.11.refs_1_.refs_2_
  17.2 0.0 copy-start.3
  17.2 1.2 %collective-permute-start.12 = (bf16[128,512]{1,0:T(8,128)(2,1)S(1)}, bf16[128,512]{1,0:T(8,128)(2,1)S(1)}, u32[]{:S(2)}, u32[]{:S(2)}) collective-permute-start(bf16[128,512]{1,0:T(8,128)(2,1)S(1)} %shard_map.42), channel_id=1, source_target_pairs={{0,4},{4,0},{8,12},{12,8},{1,5},{5,1},{9,13},{13,9},{2,6},{6,2},{1... | collective-permute-start | bytes 393224 | tf_op jit(solution)/shard_map/ppermute | solution.py:183
  18.4 0.0 copy-done.3
  18.4 0.3 shard_map.37.refs_2_
  18.7 0.0 copy-start.1
  18.7 1.6 %collective-permute-start.1 = (f32[8,128]{1,0:T(8,128)S(1)}, f32[8,128]{1,0:T(8,128)S(1)}, u32[]{:S(2)}, u32[]{:S(2)}) collective-permute-start(f32[8,128]{1,0:T(8,128)S(1)} %shard_map.37.refs_2_), channel_id=1, source_target_pairs={{0,2},{2,0},{1,3},{3,1},{4,6},{6,4},{5,7},{7,5},{8,10},{10,8},{9,1... | collective-permute-start | bytes 12296 | tf_op jit(solution)/shard_map/ppermute | solution.py:186
  20.3 2.1 %collective-permute-done.1.refs_3_.refs_4_ = f32[8,128]{1,0:T(8,128)S(1)} collective-permute-done((f32[8,128]{1,0:T(8,128)S(1)}, f32[8,128]{1,0:T(8,128)S(1)}, u32[]{:S(2)}, u32[]{:S(2)}) %collective-permute-start.1) | collective-permute-done | bytes 4128 | tf_op jit(solution)/shard_map/ppermute | solution.py:186
  22.4 0.0 collective-permute-done.2.refs_4_.refs_3_
  22.4 0.0 collective-permute-done.3.refs_5_.refs_1_
  22.4 0.1 collective-permute-done.12.refs_0_
  22.5 1.6 %collective-permute-start.13 = (bf16[128,512]{1,0:T(8,128)(2,1)S(1)}, bf16[128,512]{1,0:T(8,128)(2,1)S(1)}, u32[]{:S(2)}, u32[]{:S(2)}) collective-permute-start(bf16[128,512]{1,0:T(8,128)(2,1)S(1)} %shard_map.43.refs_1_), channel_id=1, source_target_pairs={{0,2},{2,0},{1,3},{3,1},{4,6},{6,4},{5,7},{7,5},{8,10},{10,8},{9,1... | collective-permute-start | bytes 393224 | tf_op jit(solution)/shard_map/ppermute | solution.py:186
  24.1 0.0 collective-permute-done.refs_1_
  24.1 0.0 copy-done.1
  24.1 0.7 %shard_map.39 = (f32[64,512]{1,0:T(8,128)S(1)}, f32[8,128]{1,0:T(8,128)S(1)}, f32[72,128]{1,0:T(8,128)S(1)}, f32[72,128]{1,0:T(8,128)S(1)}, f32[72,128]{1,0:T(8,128)S(1)}, /*index=5*/f32[64,192]{1,0:T(8,128)S(1)}) custom-call(bf16[64,2048]{1,0:T(8,128)(2,1)S(1)} %copy-done.1, bf16[64,2048]{1,0:T(8,128)(2,1)S(1)} %collective-permute-done.refs_1_, ...), custom_call_target="tpu_custom_call" | custom-call | tf_op jit(solution)/shard_map/pallas_call | solution.py:21
  24.8 0.6 %collective-permute-start.8 = (f32[64,192]{1,0:T(8,128)S(1)}, f32[64,192]{1,0:T(8,128)S(1)}, u32[]{:S(2)}, u32[]{:S(2)}) collective-permute-start(f32[64,192]{1,0:T(8,128)S(1)} %get-tuple-element.30), channel_id=1, source_target_pairs={{0,2},{2,0},{1,3},{3,1},{4,6},{6,4},{5,7},{7,5},{8,10},{10,8},{9,1... | collective-permute-start | bytes 147464 | tf_op jit(solution)/shard_map/ppermute | solution.py:186
  25.4 2.0 %collective-permute-start.5 = (f32[72,128]{1,0:T(8,128)S(1)}, f32[72,128]{1,0:T(8,128)S(1)}, u32[]{:S(2)}, u32[]{:S(2)}) collective-permute-start(f32[72,128]{1,0:T(8,128)S(1)} %get-tuple-element.27), channel_id=1, source_target_pairs={{0,4},{4,0},{8,12},{12,8},{1,5},{5,1},{9,13},{13,9},{2,6},{6,2},{1... | collective-permute-start | bytes 110600 | tf_op jit(solution)/shard_map/ppermute | solution.py:183
  27.4 2.4 %collective-permute-start.6 = (f32[72,128]{1,0:T(8,128)S(1)}, f32[72,128]{1,0:T(8,128)S(1)}, u32[]{:S(2)}, u32[]{:S(2)}) collective-permute-start(f32[72,128]{1,0:T(8,128)S(1)} %get-tuple-element.28), channel_id=1, source_target_pairs={{0,8},{4,12},{8,0},{12,4},{1,9},{5,13},{9,1},{13,5},{2,10},{6,14},... | collective-permute-start | bytes 110600 | tf_op jit(solution)/shard_map/ppermute | solution.py:183
  29.8 0.3 collective-permute-start.7
  30.1 0.0 collective-permute-done.13.refs_3_
  30.1 0.3 shard_map.44
  30.4 0.1 collective-permute-start.14
  30.5 0.0 collective-permute-done.5.refs_2_
  30.5 2.6 %collective-permute-done.6.refs_3_ = f32[72,128]{1,0:T(8,128)S(1)} collective-permute-done((f32[72,128]{1,0:T(8,128)S(1)}, f32[72,128]{1,0:T(8,128)S(1)}, u32[]{:S(2)}, u32[]{:S(2)}) %collective-permute-start.6) | collective-permute-done | bytes 36896 | tf_op jit(solution)/shard_map/ppermute | solution.py:183
  33.1 2.5 %collective-permute-done.7.refs_4_ = f32[72,128]{1,0:T(8,128)S(1)} collective-permute-done((f32[72,128]{1,0:T(8,128)S(1)}, f32[72,128]{1,0:T(8,128)S(1)}, u32[]{:S(2)}, u32[]{:S(2)}) %collective-permute-start.7) | collective-permute-done | bytes 36896 | tf_op jit(solution)/shard_map/ppermute | solution.py:183
  35.6 0.0 collective-permute-done.8.refs_5_
  35.6 0.1 shard_map.40
  35.7 0.1 collective-permute-start.9
  35.7 0.0 collective-permute-done.14.refs_1_
  35.7 0.3 shard_map.45
  36.0 1.1 %collective-permute-done.9.refs_1_ = f32[72,512]{1,0:T(8,128)S(1)} collective-permute-done((f32[72,512]{1,0:T(8,128)S(1)}, f32[72,512]{1,0:T(8,128)S(1)}, u32[]{:S(2)}, u32[]{:S(2)}) %collective-permute-start.9) | collective-permute-done | bytes 147488 | tf_op jit(solution)/shard_map/ppermute | solution.py:189
  37.1 1.0 %shard_map.46 = f32[64,512]{1,0:T(8,128)} custom-call(f32[72,512]{1,0:T(8,128)S(1)} %get-tuple-element.31.refs_0_, f32[72,512]{1,0:T(8,128)S(1)} %collective-permute-done.9.refs_1_, f32[8,512]{1,0:T(8,128)S(1)} %get-tuple-element.32.refs_2_, f32[64,512]{1,0:T(8,128)S(1)} %get-tuple-element.35.refs_3_, f32[64,128]{1,0:T(8,128)S(1)} %get-tuple-element.36.refs_4_, ...), custom_call_target="tpu_custom_call" | custom-call | tf_op jit(solution)/shard_map/pallas_call | solution.py:21
  (4 shorter events, 0.1 us)
Async XLA Ops:
  0.0 7.9 %collective-permute-start.10 = (bf16[64,512]{1,0:T(8,128)(2,1)}, bf16[64,512]{1,0:T(8,128)(2,1)S(1)}, u32[]{:S(2)}, u32[]{:S(2)}) collective-permute-start(bf16[64,512]{1,0:T(8,128)(2,1)} %refs_6_.1), channel_id=1, source_target_pairs={{0,8},{4,12},{8,0},{12,4},{1,9},{5,13},{9,1},{13,5},{2,10},{6,14},... | collective-permute-start | bytes 196616 | tf_op jit(solution)/shard_map/ppermute | solution.py:183
  4.0 0.9 %copy-start = (bf16[64,2048]{1,0:T(8,128)(2,1)S(1)}, bf16[64,2048]{1,0:T(8,128)(2,1)}, u32[]{:S(2)}) copy-start(bf16[64,2048]{1,0:T(8,128)(2,1)} %refs_0_.6) | copy-start | bytes 786436
  5.0 2.9 %copy-start.2 = (bf16[64,512]{1,0:T(8,128)(2,1)S(1)}, bf16[64,512]{1,0:T(8,128)(2,1)}, u32[]{:S(2)}) copy-start(bf16[64,512]{1,0:T(8,128)(2,1)} %refs_6_.1) | copy-start | bytes 196612
  5.0 12.2 %collective-permute-start.4 = (bf16[64,1024]{1,0:T(8,128)(2,1)S(1)}, bf16[64,1024]{1,0:T(8,128)(2,1)S(1)}, u32[]{:S(2)}, u32[]{:S(2)}) collective-permute-start(bf16[64,1024]{1,0:T(8,128)(2,1)S(1)} %get-tuple-element.24), channel_id=1, source_target_pairs={{0,12},{4,8},{8,4},{12,0},{1,13},{5,9},{9,5},{13,1},{2,14},{6,10},... | collective-permute-start | bytes 393224 | tf_op jit(solution)/shard_map/ppermute | solution.py:183
  7.9 9.3 %collective-permute-start.11 = (bf16[128,512]{1,0:T(8,128)(2,1)S(1)}, bf16[128,512]{1,0:T(8,128)(2,1)S(1)}, u32[]{:S(2)}, u32[]{:S(2)}) collective-permute-start(bf16[128,512]{1,0:T(8,128)(2,1)S(1)} %shard_map.41.refs_0_), channel_id=1, source_target_pairs={{0,2},{2,0},{1,3},{3,1},{4,6},{6,4},{5,7},{7,5},{8,10},{10,8},{9,1... | collective-permute-start | bytes 393224 | tf_op jit(solution)/shard_map/ppermute | solution.py:186
  9.7 14.4 %collective-permute-start = (bf16[64,2048]{1,0:T(8,128)(2,1)S(1)}, bf16[64,2048]{1,0:T(8,128)(2,1)S(1)}, u32[]{:S(2)}, u32[]{:S(2)}) collective-permute-start(bf16[64,2048]{1,0:T(8,128)(2,1)S(1)} %copy-done), channel_id=1, source_target_pairs={{0,2},{2,0},{1,3},{3,1},{4,6},{6,4},{5,7},{7,5},{8,10},{10,8},{9,1... | collective-permute-start | bytes 786440 | tf_op jit(solution)/shard_map/ppermute | solution.py:186
  10.0 12.4 %collective-permute-start.2 = (bf16[64,1024]{1,0:T(8,128)(2,1)S(1)}, bf16[64,1024]{1,0:T(8,128)(2,1)S(1)}, u32[]{:S(2)}, u32[]{:S(2)}) collective-permute-start(bf16[64,1024]{1,0:T(8,128)(2,1)S(1)} %get-tuple-element.22), channel_id=1, source_target_pairs={{0,4},{4,0},{8,12},{12,8},{1,5},{5,1},{9,13},{13,9},{2,6},{6,2},{1... | collective-permute-start | bytes 393224 | tf_op jit(solution)/shard_map/ppermute | solution.py:183
  13.9 8.5 %collective-permute-start.3 = (bf16[64,1024]{1,0:T(8,128)(2,1)S(1)}, bf16[64,1024]{1,0:T(8,128)(2,1)S(1)}, u32[]{:S(2)}, u32[]{:S(2)}) collective-permute-start(bf16[64,1024]{1,0:T(8,128)(2,1)S(1)} %get-tuple-element.23), channel_id=1, source_target_pairs={{0,8},{4,12},{8,0},{12,4},{1,9},{5,13},{9,1},{13,5},{2,10},{6,14},... | collective-permute-start | bytes 393224 | tf_op jit(solution)/shard_map/ppermute | solution.py:183
  17.2 1.2 %copy-start.3 = (bf16[64]{0:T(256)(128)(2,1)S(1)}, bf16[64]{0:T(256)(128)(2,1)}, u32[]{:S(2)}) copy-start(bf16[64]{0:T(256)(128)(2,1)} %param.5) | copy-start | bytes 388
  17.2 5.3 %collective-permute-start.12 = (bf16[128,512]{1,0:T(8,128)(2,1)S(1)}, bf16[128,512]{1,0:T(8,128)(2,1)S(1)}, u32[]{:S(2)}, u32[]{:S(2)}) collective-permute-start(bf16[128,512]{1,0:T(8,128)(2,1)S(1)} %shard_map.42), channel_id=1, source_target_pairs={{0,4},{4,0},{8,12},{12,8},{1,5},{5,1},{9,13},{13,9},{2,6},{6,2},{1... | collective-permute-start | bytes 393224 | tf_op jit(solution)/shard_map/ppermute | solution.py:183
  18.7 5.4 %copy-start.1 = (bf16[64,2048]{1,0:T(8,128)(2,1)S(1)}, bf16[64,2048]{1,0:T(8,128)(2,1)}, u32[]{:S(2)}) copy-start(bf16[64,2048]{1,0:T(8,128)(2,1)} %refs_0_.6) | copy-start | bytes 786436
  18.7 3.7 %collective-permute-start.1 = (f32[8,128]{1,0:T(8,128)S(1)}, f32[8,128]{1,0:T(8,128)S(1)}, u32[]{:S(2)}, u32[]{:S(2)}) collective-permute-start(f32[8,128]{1,0:T(8,128)S(1)} %shard_map.37.refs_2_), channel_id=1, source_target_pairs={{0,2},{2,0},{1,3},{3,1},{4,6},{6,4},{5,7},{7,5},{8,10},{10,8},{9,1... | collective-permute-start | bytes 12296 | tf_op jit(solution)/shard_map/ppermute | solution.py:186
  22.5 7.6 %collective-permute-start.13 = (bf16[128,512]{1,0:T(8,128)(2,1)S(1)}, bf16[128,512]{1,0:T(8,128)(2,1)S(1)}, u32[]{:S(2)}, u32[]{:S(2)}) collective-permute-start(bf16[128,512]{1,0:T(8,128)(2,1)S(1)} %shard_map.43.refs_1_), channel_id=1, source_target_pairs={{0,2},{2,0},{1,3},{3,1},{4,6},{6,4},{5,7},{7,5},{8,10},{10,8},{9,1... | collective-permute-start | bytes 393224 | tf_op jit(solution)/shard_map/ppermute | solution.py:186
  24.8 10.8 %collective-permute-start.8 = (f32[64,192]{1,0:T(8,128)S(1)}, f32[64,192]{1,0:T(8,128)S(1)}, u32[]{:S(2)}, u32[]{:S(2)}) collective-permute-start(f32[64,192]{1,0:T(8,128)S(1)} %get-tuple-element.30), channel_id=1, source_target_pairs={{0,2},{2,0},{1,3},{3,1},{4,6},{6,4},{5,7},{7,5},{8,10},{10,8},{9,1... | collective-permute-start | bytes 147464 | tf_op jit(solution)/shard_map/ppermute | solution.py:186
  25.4 5.1 %collective-permute-start.5 = (f32[72,128]{1,0:T(8,128)S(1)}, f32[72,128]{1,0:T(8,128)S(1)}, u32[]{:S(2)}, u32[]{:S(2)}) collective-permute-start(f32[72,128]{1,0:T(8,128)S(1)} %get-tuple-element.27), channel_id=1, source_target_pairs={{0,4},{4,0},{8,12},{12,8},{1,5},{5,1},{9,13},{13,9},{2,6},{6,2},{1... | collective-permute-start | bytes 110600 | tf_op jit(solution)/shard_map/ppermute | solution.py:183
  27.4 5.6 %collective-permute-start.6 = (f32[72,128]{1,0:T(8,128)S(1)}, f32[72,128]{1,0:T(8,128)S(1)}, u32[]{:S(2)}, u32[]{:S(2)}) collective-permute-start(f32[72,128]{1,0:T(8,128)S(1)} %get-tuple-element.28), channel_id=1, source_target_pairs={{0,8},{4,12},{8,0},{12,4},{1,9},{5,13},{9,1},{13,5},{2,10},{6,14},... | collective-permute-start | bytes 110600 | tf_op jit(solution)/shard_map/ppermute | solution.py:183
  29.8 5.8 %collective-permute-start.7 = (f32[72,128]{1,0:T(8,128)S(1)}, f32[72,128]{1,0:T(8,128)S(1)}, u32[]{:S(2)}, u32[]{:S(2)}) collective-permute-start(f32[72,128]{1,0:T(8,128)S(1)} %get-tuple-element.29), channel_id=1, source_target_pairs={{0,12},{4,8},{8,4},{12,0},{1,13},{5,9},{9,5},{13,1},{2,14},{6,10},... | collective-permute-start | bytes 110600 | tf_op jit(solution)/shard_map/ppermute | solution.py:183
  30.4 5.3 %collective-permute-start.14 = (f32[72,512]{1,0:T(8,128)S(1)}, f32[72,512]{1,0:T(8,128)S(1)}, u32[]{:S(2)}, u32[]{:S(2)}) collective-permute-start(f32[72,512]{1,0:T(8,128)S(1)} %get-tuple-element.33.refs_0_), channel_id=1, source_target_pairs={{0,1},{1,0},{2,3},{3,2},{4,5},{5,4},{6,7},{7,6},{8,9},{9,8},{10,11... | collective-permute-start | bytes 442376 | tf_op jit(solution)/shard_map/ppermute | solution.py:189
  35.7 1.4 %collective-permute-start.9 = (f32[72,512]{1,0:T(8,128)S(1)}, f32[72,512]{1,0:T(8,128)S(1)}, u32[]{:S(2)}, u32[]{:S(2)}) collective-permute-start(f32[72,512]{1,0:T(8,128)S(1)} %get-tuple-element.31.refs_0_), channel_id=1, source_target_pairs={{0,1},{1,0},{2,3},{3,2},{4,5},{5,4},{6,7},{7,6},{8,9},{9,8},{10,11... | collective-permute-start | bytes 442376 | tf_op jit(solution)/shard_map/ppermute | solution.py:189

commit v15 on v12

v15 whole, which is shorter than its diff:
```python
import functools

import jax
import jax.numpy as jnp
from jax import lax
from jax.experimental import pallas as pl
from jax.experimental.pallas import tpu as pltpu
from jax.sharding import PartitionSpec as P

F32, BF16 = jnp.float32, jnp.bfloat16
INNER = (((1,), (1,)), ((), ()))
TAIL = 16


def call(body, out_shape, operands, scratch=(), after=()):
    outs = out_shape if isinstance(out_shape, (list, tuple)) else [out_shape]
    moved = sum(x.size * x.dtype.itemsize for x in list(operands) + list(outs))

    def run(*refs):
        body(*refs[: len(operands)], *refs[len(operands) + len(after) :])

    return pl.pallas_call(
        run,
        out_shape=out_shape,
        in_specs=[pl.BlockSpec(memory_space=pltpu.VMEM)] * len(operands) + [pl.BlockSpec(memory_space=pl.ANY)] * len(after),
        out_specs=jax.tree.map(lambda _: pl.BlockSpec(memory_space=pltpu.VMEM), out_shape),
        scratch_shapes=list(scratch),
        cost_estimate=pl.CostEstimate(flops=0, bytes_accessed=0, transcendentals=0),
        compiler_params=pltpu.CompilerParams(vmem_limit_bytes=min(56 << 20, (8 << 20) + 3 * moved)),
    )(*operands, *after)


def column(row):
    shape = (row.shape[1], row.shape[1])
    eye = lax.broadcasted_iota(jnp.int32, shape, 0) == lax.broadcasted_iota(jnp.int32, shape, 1)
    return jnp.sum(jnp.where(eye, row, 0.0), axis=1, keepdims=True)


def tags_of(scales, mass):
    shape = (TAIL, scales.shape[1])
    at = lax.broadcasted_iota(jnp.int32, shape, 0)
    high = mass.astype(BF16).astype(F32)
    return jnp.where(at < 8, scales, jnp.where(at < 12, high, mass - high)).astype(BF16)


def read_tags(tags):
    tags = tags.astype(F32)
    return tags[0:1, :], tags[8:9, 0:1] + tags[12:13, 0:1]


def lane_row(col):
    shape = (col.shape[0], col.shape[0])
    eye = lax.broadcasted_iota(jnp.int32, shape, 0) == lax.broadcasted_iota(jnp.int32, shape, 1)
    return jnp.sum(jnp.where(eye, col, 0.0), axis=0, keepdims=True)


def put(held, spot, rows, ref, at):
    width = held.shape[1]
    high = rows * width // ref.shape[1]
    for n in range(ref.shape[1] // width):
        held[pl.ds(spot + n * high, high), :] = ref[at : at + high, n * width : (n + 1) * width]


def cut_kernel(nrow, teach, *outs):
    part = teach.shape[1] // nrow
    z = lax.axis_index("row")
    for k in range(nrow):
        at = pl.multiple_of((z ^ k) * part, part)
        outs[k][...] = teach[:, pl.ds(at, part)]


def tag_kernel(teach, scale, out):
    rows, width = teach.shape[0], out.shape[1]
    ts = teach[...].astype(F32)
    s = scale[...].astype(F32)
    mass = jnp.sum(jnp.square(column(s)) * jnp.sum(ts * ts, axis=1, keepdims=True), keepdims=True)
    tags = tags_of(jnp.concatenate([s, s], axis=1), mass)
    out[...] = jnp.concatenate([tags] * (width // (2 * rows)), axis=1)


def late_kernel(rows, tags, *refs):
    out = refs[-1]
    for n, ref in enumerate(refs[:-1]):
        put(out, n * rows, rows, ref, 0)
    out[(len(refs) - 1) * rows :, :] = tags[...]


def pack_kernel(*refs):
    out, at = refs[-1], 0
    for r in refs[:-1]:
        out[at : at + r.shape[0], :] = r[...]
        at += r.shape[0]


def place(nrow, ncol, rows, k, c):
    return pl.multiple_of(((lax.axis_index("row") ^ k) * ncol + c) * rows, rows)


def group(ncol, rows, k):
    at = (lax.axis_index("row") ^ k) * ncol * rows
    return pl.ds(pl.multiple_of(at, 2 * rows), ncol * rows)


def gram_kernel(nrow, ncol, rows, order, *refs):
    outs, held, left = refs[2 * ncol : 2 * ncol + nrow], refs[-2], refs[-1]
    for c in range(ncol):
        put(held, place(nrow, ncol, rows, 0, c), rows, refs[2 * c], 0)
        for n, k in enumerate([k for k in order if k]):
            put(held, place(nrow, ncol, rows, k, c), rows, refs[2 * c + 1], n * rows)
    for n, k in enumerate(order):
        left[n * rows : (n + 1) * rows, :] = held[pl.ds(place(nrow, ncol, rows, k, 0), rows), :]
    sub = rows // 2
    at = lax.broadcasted_iota(jnp.int32, (sub, 2 * rows), 0)
    lane = lax.broadcasted_iota(jnp.int32, (sub, 2 * rows), 1)
    note, mass = jnp.zeros((sub, 2 * rows), F32), jnp.zeros((1, 1), F32)
    for c in range(ncol):
        scales, part = read_tags(refs[2 * c + 1][(nrow - 1) * rows :, : 2 * rows])
        turned = jnp.concatenate([scales[:, sub:], scales[:, :sub]], axis=1)
        note = jnp.where(at == 2 * c, scales, jnp.where(at == 2 * c + 1, turned, note))
        mass = mass + part
    high = mass.astype(BF16).astype(F32)
    note = jnp.where(at < sub // 2, note, jnp.where(at < sub * 3 // 4, high, mass - high))
    per = max(1, 2048 * rows * nrow // held.shape[0] // rows // 8)
    for first in range(0, nrow, per):
        last = min(first + per, nrow)
        gram = lax.dot_general(left[first * rows : last * rows, :], held[...], INNER, preferred_element_type=F32)
        for n in range(first, last):
            out = outs[order[n]]
            out[...] = gram[(n - first) * rows : (n - first + 1) * rows, :].astype(out.dtype)
            spot = pl.ds(pl.multiple_of(place(nrow, ncol, rows, order[n], 0), 2 * rows), 2 * rows)
            seen = out[sub:, spot].astype(F32)
            out[sub:, spot] = jnp.where(lane < sub, note, seen).astype(out.dtype)


def sum_kernel(nrow, ncol, order, *refs):
    parts, (out, vectors) = [refs[order.index(k)] for k in range(nrow)], refs[-2:]
    rows = parts[0].shape[0]
    sub = rows // 2
    total = parts[0][...].astype(F32)
    for r in parts[1:]:
        total = total + r[...].astype(F32)
    out[:rows, :] = total
    own = group(ncol, rows, 0)
    mirror = jnp.transpose(out[:sub, own])[sub : 2 * sub, :]
    out[sub:rows, own] = jnp.concatenate([mirror, out[sub:rows, own][:, sub:]], axis=1)
    mass = jnp.zeros((1, 1), F32)
    for k, part in enumerate(parts):
        note = part[sub:, own].astype(F32)[:, :sub]
        mass = mass + note[sub // 2 : sub // 2 + 1, :1] + note[sub * 3 // 4 : sub * 3 // 4 + 1, :1]
        line = jnp.concatenate([note[n : n + 1, :] for n in range(2 * ncol)], axis=1)
        vectors[:, group(ncol, rows, k)] = jnp.broadcast_to(line, (8, ncol * rows))
    out[rows:, :] = jnp.broadcast_to(mass, (8, out.shape[1]))


def assemble(nrow, ncol, rows, keys, refs, held):
    for c in range(ncol):
        for n, k in enumerate(keys):
            held[pl.ds(place(nrow, ncol, rows, k, c), rows), :] = refs[c][n * rows : (n + 1) * rows, :]


def raw_gram_kernel(nrow, ncol, rows, keys, *refs):
    out, raw = refs[ncol:]
    assemble(nrow, ncol, rows, keys, refs, raw)
    out[:rows, :] = lax.dot_general(refs[0][:rows, :], raw[...], INNER, preferred_element_type=F32)
    for at in range(0, raw.shape[0], 128):
        squares = jnp.sum(jnp.square(raw[at : at + 128, :].astype(F32)), axis=1, keepdims=True)
        out[rows:, at : at + 128] = jnp.broadcast_to(lane_row(squares), (8, 128))


def normalize(raw, squares, units):
    for at in range(0, raw.shape[0], 128):
        inverse = 1.0 / jnp.sqrt(column(squares[:1, at : at + 128]))
        units[at : at + 128, :] = (raw[at : at + 128, :].astype(F32) * inverse).astype(BF16)


def unit_gram_kernel(ncol, mine, other, *refs):
    rows = mine.shape[0] - 8
    gram, inverses, squares = refs[1:4] if len(refs) > 3 else refs
    squares[...] = mine[rows:, :] + other[rows:, :]
    at = pl.multiple_of(lax.axis_index("row") * ncol * rows, 2 * rows)
    inverse = 1.0 / jnp.sqrt(column(squares[:1, pl.ds(at, 2 * rows)][:, :rows]))
    inverses[...] = jnp.broadcast_to(inverse, inverses.shape)
    gram[...] = (mine[:rows, :] + other[:rows, :]) * (inverse * (1.0 / jnp.sqrt(squares[:1, :])))
    if len(refs) > 3:
        normalize(refs[0], squares, refs[4])


def final_kernel(nrow, ncol, keys, mine, other, vectors, gram, inverses, squares, stud, scale, *refs):
    rows = stud.shape[0]
    if keys:
        out, units = refs[-2:]
        assemble(nrow, ncol, rows, keys, refs, units)
        normalize(units, squares, units)
    else:
        units, out = refs
    inverse = inverses[:, :1]
    mass = (mine[rows : rows + 1, :1] + other[rows : rows + 1, :1]) / mine.shape[1]
    outer = (column(scale[...].astype(F32)) / mass) * vectors[:1, :]
    error_b = (gram[...] - outer * (mine[:rows, :] + other[:rows, :])).astype(BF16)
    grads = 4.0 * jnp.dot(error_b, units[...], preferred_element_type=F32)
    along = 4.0 * jnp.sum(error_b.astype(F32) * gram[...], axis=1, keepdims=True)
    unit = stud[...].astype(F32) * inverse
    out[...] = (grads - along * unit) * inverse


def shards(student, teacher, scale):
    rows, half = student.shape
    nrow, ncol = lax.axis_size("row"), lax.axis_size("col")
    batch = rows * nrow * ncol
    part = teacher.shape[1] // nrow
    small = batch <= 2048
    sds = jax.ShapeDtypeStruct
    scale = scale.reshape(1, rows)

    def along_row(x, k):
        return lax.ppermute(x, "row", [(i, i ^ k) for i in range(nrow)])

    def along_col(x, c):
        return lax.ppermute(x, "col", [(i, (i - c) % ncol) for i in range(ncol)])

    def other_core(x):
        return lax.ppermute(x, "sub", [(0, 1), (1, 0)])

    def pack(xs, after=()):
        shape = (sum(x.shape[0] for x in xs), half)
        return call(pack_kernel, sds(shape, BF16), xs, after=after)

    def with_columns(x):
        return [x if c == 0 else along_col(x, c) for c in range(ncol)]

    middle = nrow // 2
    order = list(range(middle, nrow)) + list(range(middle))
    cuts = call(functools.partial(cut_kernel, nrow), [sds((rows, part), BF16)] * nrow, [teacher])
    came = {k: along_row(cuts[k], k) for k in order if k}
    swapped = along_row(student, middle)
    tags = call(tag_kernel, sds((TAIL, part), BF16), [teacher, scale], after=[came[n] for n in ()])
    own = with_columns(cuts[0])
    others = [k for k in order if k]
    late = call(
        functools.partial(late_kernel, rows),
        sds(((nrow - 1) * rows + TAIL, part), BF16),
        [tags] + [came[k] for k in others],
        after=own[1:2] + [swapped],
    )
    late = with_columns(late)
    partial = call(
        functools.partial(gram_kernel, nrow, ncol, rows, order),
        [sds((rows, batch), BF16 if k else F32) for k in range(nrow)],
        [r for pair in zip(own, late) for r in pair],
        scratch=[pltpu.VMEM((batch, part), BF16), pltpu.VMEM((nrow * rows, part), BF16)],
    )
    returned = {k: along_row(partial[k], k) if k else partial[0] for k in order}

    stack, keys, k = [student], [0], middle
    while k:
        joined = pack(stack, after=late[:1] if k == 1 else ()) if k < middle else student
        stack.append(swapped if k == middle else along_row(joined, k))
        keys, k = keys + [n ^ k for n in keys], k // 2
    raw_refs = with_columns(pack(stack, after=[partial[0]]))
    raw_gram, *raw = call(
        functools.partial(raw_gram_kernel, nrow, ncol, rows, keys),
        [sds((rows + 8, batch), F32)] + ([sds((batch, half), BF16)] if small else []),
        raw_refs,
        scratch=[] if small else [pltpu.VMEM((batch, half), BF16)],
    )
    gram, inverses, squares, *units = call(
        functools.partial(unit_gram_kernel, ncol),
        [sds((rows, batch), F32), sds((rows, 128), F32), sds((8, batch), F32)] + ([sds((batch, half), BF16)] if small else []),
        [raw_gram, other_core(raw_gram)] + raw,
    )
    message, vectors = call(
        functools.partial(sum_kernel, nrow, ncol, order),
        [sds((rows + 8, batch), F32), sds((8, batch), F32)],
        [returned[k] for k in order],
    )
    return call(
        functools.partial(final_kernel, nrow, ncol, None if small else keys),
        sds((rows, half), F32),
        [message, other_core(message), vectors, gram, inverses, squares, student, scale] + (units if small else raw_refs),
        scratch=[] if small else [pltpu.VMEM((batch, half), BF16)],
    )


def solution(mesh):
    spec = P(("groups", "row", "col"), "sub")
    return jax.shard_map(
        shards,
        mesh=mesh,
        in_specs=(spec, spec, P(("groups", "row", "col"))),
        out_specs=spec,
        check_vma=False,
    )
```

time: 36.7 us -> 34.1 us (0.929)
  waiting for transfers between devices: 15 us -> 12 us
  starting transfers between devices: 16.9 us -> 18.4 us
  local copies, waits for them, and re-layouts: 2.11 us -> 0.96 us
    ppermute x7 -> x8, starting transfers between devices: 11.3 us -> 13.8 us  [along_row(): return lax.ppermute(x, 'row', [(i, i ^ k) for i in range(nrow)])]
    ppermute x7 -> x8, waiting for transfers between devices: 8.85 us -> 7.3 us  [along_row(): return lax.ppermute(x, 'row', [(i, i ^ k) for i in range(nrow)])]
    ppermute x6 -> x3, starting transfers between devices: 5.61 us -> 4.46 us  [along_col(): return lax.ppermute(x, 'col', [(i, (i - c) % ncol) for i in range(ncol)])]
    unnamed x6, local copies, waits for them, and re-layouts: 2.11 us -> 0.96 us
    ppermute x6 -> x3, waiting for transfers between devices: 4.56 us -> 3.62 us  [along_col(): return lax.ppermute(x, 'col', [(i, (i - c) % ncol) for i in range(ncol)])]
    ppermute x1 -> x2, waiting for transfers between devices: 1.57 us -> 1.08 us  [other_core(): return lax.ppermute(x, 'sub', [(0, 1), (1, 0)])]
    pallas_call x12 -> x10, Pallas kernels: 2.43 us -> 2.54 us  [call(): pl.pallas_call(run, out_shape=out_shape, in_specs=[pl.BlockSpec(memory_sp...]
  transfers between devices with their start and end apart: 14 -> 13, of which waited for: 8 -> 8; matrix products, arithmetic and copies ran while one was open for 0% -> 0% of each run, Pallas kernels for 3% -> 4%
where the time goes in v15:
time: 34.1 us; the launch traced here: 34 us
  starting transfers between devices  18.4 us (54%)
  waiting for transfers between devices  12 us (35%)
  Pallas kernels  2.54 us (7%)
  local copies, waits for them, and re-layouts  0.96 us (3%)
    ppermute x8, starting transfers between devices, along_row(): return lax.ppermute(x, 'row', [(i, i ^ k) for i in range(nrow)])  13.8 us
    ppermute x8, waiting for transfers between devices, along_row(): return lax.ppermute(x, 'row', [(i, i ^ k) for i in range(nrow)])  7.3 us
    ppermute x3, starting transfers between devices, along_col(): return lax.ppermute(x, 'col', [(i, (i - c) % ncol) for i in range(ncol)])  4.46 us
    ppermute x3, waiting for transfers between devices, along_col(): return lax.ppermute(x, 'col', [(i, (i - c) % ncol) for i in range(ncol)])  3.62 us
    pallas_call x10, Pallas kernels, call(): pl.pallas_call(run, out_shape=out_shape, in_specs=[pl.BlockSpec(memory_sp...  2.54 us
    ppermute x2, waiting for transfers between devices, other_core(): return lax.ppermute(x, 'sub', [(0, 1), (1, 0)])  1.08 us
    unnamed x6, local copies, waits for them, and re-layouts  0.96 us
  transfers between devices with their start and end apart: 13, of which 8 were waited for; matrix products, arithmetic and copies ran while one was open for 0% of the time, Pallas kernels for 4%

profile of v15, /device:TPU:0, one launch (start us, length us, event | category | flops | bytes accessed | tf_op | source)
XLA Modules:
  0.0 34.0 jit_solution(10620120619741187630)
XLA Ops:
  0.0 4.0 %collective-permute-start.4 = (bf16[64,512]{1,0:T(8,128)(2,1)}, bf16[64,512]{1,0:T(8,128)(2,1)S(1)}, u32[]{:S(2)}, u32[]{:S(2)}) collective-permute-start(bf16[64,512]{1,0:T(8,128)(2,1)} %refs_6_.1), channel_id=1, source_target_pairs={{0,8},{4,12},{8,0},{12,4},{1,9},{5,13},{9,1},{13,5},{2,10},{6,14},... | collective-permute-start | bytes 196616 | tf_op jit(solution)/shard_map/ppermute | solution.py:216
  4.0 0.0 copy-start
  4.0 0.9 %copy-done = bf16[64,2048]{1,0:T(8,128)(2,1)S(1)} copy-done((bf16[64,2048]{1,0:T(8,128)(2,1)S(1)}, bf16[64,2048]{1,0:T(8,128)(2,1)}, u32[]{:S(2)}) %copy-start) | copy-done | bytes 262168
  5.0 0.1 collective-permute-start
  5.1 3.9 %collective-permute-start.1 = (bf16[64,512]{1,0:T(8,128)(2,1)S(1)}, bf16[64,512]{1,0:T(8,128)(2,1)S(1)}, u32[]{:S(2)}, u32[]{:S(2)}) collective-permute-start(bf16[64,512]{1,0:T(8,128)(2,1)S(1)} %get-tuple-element.23), channel_id=1, source_target_pairs={{0,12},{4,8},{8,4},{12,0},{1,13},{5,9},{9,5},{13,1},{2,14},{6,10},... | collective-permute-start | bytes 196616 | tf_op jit(solution)/shard_map/ppermute | solution.py:216
  9.0 0.0 collective-permute-start.2
  9.0 0.0 copy-start.2
  9.0 1.5 %collective-permute-start.3 = (bf16[64,512]{1,0:T(8,128)(2,1)S(1)}, bf16[64,512]{1,0:T(8,128)(2,1)S(1)}, u32[]{:S(2)}, u32[]{:S(2)}) collective-permute-start(bf16[64,512]{1,0:T(8,128)(2,1)S(1)} %get-tuple-element.21.refs_0_), channel_id=1, source_target_pairs={{0,2},{2,0},{1,3},{3,1},{4,6},{6,4},{5,7},{7,5},{8,10},{10,8},{9,1... | collective-permute-start | bytes 196616 | tf_op jit(solution)/shard_map/ppermute | solution.py:219
  10.5 0.0 copy-done.2
  10.5 0.3 shard_map.38.refs_0_
  10.8 0.0 copy-start.1
  10.8 0.0 collective-permute-done.4.refs_5_.refs_1_
  10.8 2.3 %collective-permute-done.refs_1_ = bf16[64,512]{1,0:T(8,128)(2,1)S(1)} collective-permute-done((bf16[64,512]{1,0:T(8,128)(2,1)S(1)}, bf16[64,512]{1,0:T(8,128)(2,1)S(1)}, u32[]{:S(2)}, u32[]{:S(2)}) %collective-permute-start) | collective-permute-done | bytes 65568 | tf_op jit(solution)/shard_map/ppermute | solution.py:216
  13.1 0.0 collective-permute-done.1.refs_2_
  13.1 0.6 %collective-permute-done.2.refs_3_ = bf16[64,512]{1,0:T(8,128)(2,1)S(1)} collective-permute-done((bf16[64,512]{1,0:T(8,128)(2,1)S(1)}, bf16[64,512]{1,0:T(8,128)(2,1)S(1)}, u32[]{:S(2)}, u32[]{:S(2)}) %collective-permute-start.2) | collective-permute-done | bytes 65568 | tf_op jit(solution)/shard_map/ppermute | solution.py:216
  13.7 0.0 collective-permute-done.3.refs_4_.refs_2_
  13.8 1.6 %collective-permute-start.5 = (bf16[208,512]{1,0:T(8,128)(2,1)S(1)}, bf16[208,512]{1,0:T(8,128)(2,1)S(1)}, u32[]{:S(2)}, u32[]{:S(2)}) collective-permute-start(bf16[208,512]{1,0:T(8,128)(2,1)S(1)} %shard_map.39.refs_1_.refs_2_), channel_id=1, source_target_pairs={{0,2},{2,0},{1,3},{3,1},{4,6},{6,4},{5,7},{7,5},{8,10},{10,8},{9,1... | collective-permute-start | bytes 638984 | tf_op jit(solution)/shard_map/ppermute | solution.py:219
  15.3 0.0 copy-done.1
  15.3 1.6 %collective-permute-start.10 = (bf16[128,512]{1,0:T(8,128)(2,1)S(1)}, bf16[128,512]{1,0:T(8,128)(2,1)S(1)}, u32[]{:S(2)}, u32[]{:S(2)}) collective-permute-start(bf16[128,512]{1,0:T(8,128)(2,1)S(1)} %shard_map.42), channel_id=1, source_target_pairs={{0,4},{4,0},{8,12},{12,8},{1,5},{5,1},{9,13},{13,9},{2,6},{6,2},{1... | collective-permute-start | bytes 393224 | tf_op jit(solution)/shard_map/ppermute | solution.py:216
  17.0 2.7 %collective-permute-done.5.refs_3_ = bf16[208,512]{1,0:T(8,128)(2,1)S(1)} collective-permute-done((bf16[208,512]{1,0:T(8,128)(2,1)S(1)}, bf16[208,512]{1,0:T(8,128)(2,1)S(1)}, u32[]{:S(2)}, u32[]{:S(2)}) %collective-permute-start.5) | collective-permute-done | bytes 213024 | tf_op jit(solution)/shard_map/ppermute | solution.py:219
  19.7 0.5 %shard_map.40 = (f32[64,512]{1,0:T(8,128)S(1)}, bf16[64,512]{1,0:T(8,128)(2,1)S(1)}, bf16[64,512]{1,0:T(8,128)(2,1)S(1)}, bf16[64,512]{1,0:T(8,128)(2,1)S(1)}) custom-call(bf16[64,512]{1,0:T(8,128)(2,1)S(1)} %get-tuple-element.21.refs_0_, bf16[208,512]{1,0:T(8,128)(2,1)S(1)} %shard_map.39.refs_1_.refs_2_, ...), custom_call_target="tpu_custom_call" | custom-call | tf_op jit(solution)/shard_map/pallas_call | solution.py:22
  20.2 0.2 collective-permute-done.10.refs_2_
  20.4 1.4 %collective-permute-start.11 = (bf16[256,512]{1,0:T(8,128)(2,1)S(1)}, bf16[256,512]{1,0:T(8,128)(2,1)S(1)}, u32[]{:S(2)}, u32[]{:S(2)}) collective-permute-start(bf16[256,512]{1,0:T(8,128)(2,1)S(1)} %shard_map.43.refs_0_), channel_id=1, source_target_pairs={{0,2},{2,0},{1,3},{3,1},{4,6},{6,4},{5,7},{7,5},{8,10},{10,8},{9,1... | collective-permute-start | bytes 786440 | tf_op jit(solution)/shard_map/ppermute | solution.py:219
  21.8 3.6 %collective-permute-start.6 = (bf16[64,512]{1,0:T(8,128)(2,1)S(1)}, bf16[64,512]{1,0:T(8,128)(2,1)S(1)}, u32[]{:S(2)}, u32[]{:S(2)}) collective-permute-start(bf16[64,512]{1,0:T(8,128)(2,1)S(1)} %get-tuple-element.25), channel_id=1, source_target_pairs={{0,8},{4,12},{8,0},{12,4},{1,9},{5,13},{9,1},{13,5},{2,10},{6,14},... | collective-permute-start | bytes 196616 | tf_op jit(solution)/shard_map/ppermute | solution.py:216
  25.4 0.4 %collective-permute-start.7 = (bf16[64,512]{1,0:T(8,128)(2,1)S(1)}, bf16[64,512]{1,0:T(8,128)(2,1)S(1)}, u32[]{:S(2)}, u32[]{:S(2)}) collective-permute-start(bf16[64,512]{1,0:T(8,128)(2,1)S(1)} %get-tuple-element.26), channel_id=1, source_target_pairs={{0,12},{4,8},{8,4},{12,0},{1,13},{5,9},{9,5},{13,1},{2,14},{6,10},... | collective-permute-start | bytes 196616 | tf_op jit(solution)/shard_map/ppermute | solution.py:216
  25.8 0.1 collective-permute-start.8
  25.9 0.9 %collective-permute-done.11.refs_1_ = bf16[256,512]{1,0:T(8,128)(2,1)S(1)} collective-permute-done((bf16[256,512]{1,0:T(8,128)(2,1)S(1)}, bf16[256,512]{1,0:T(8,128)(2,1)S(1)}, u32[]{:S(2)}, u32[]{:S(2)}) %collective-permute-start.11) | collective-permute-done | bytes 262176 | tf_op jit(solution)/shard_map/ppermute | solution.py:219
  26.8 0.3 shard_map.44
  27.2 0.1 collective-permute-start.12
  27.2 1.8 %collective-permute-done.6.refs_0_ = bf16[64,512]{1,0:T(8,128)(2,1)S(1)} collective-permute-done((bf16[64,512]{1,0:T(8,128)(2,1)S(1)}, bf16[64,512]{1,0:T(8,128)(2,1)S(1)}, u32[]{:S(2)}, u32[]{:S(2)}) %collective-permute-start.6) | collective-permute-done | bytes 65568 | tf_op jit(solution)/shard_map/ppermute | solution.py:216
  29.0 2.4 %collective-permute-done.7.refs_1_ = bf16[64,512]{1,0:T(8,128)(2,1)S(1)} collective-permute-done((bf16[64,512]{1,0:T(8,128)(2,1)S(1)}, bf16[64,512]{1,0:T(8,128)(2,1)S(1)}, u32[]{:S(2)}, u32[]{:S(2)}) %collective-permute-start.7) | collective-permute-done | bytes 65568 | tf_op jit(solution)/shard_map/ppermute | solution.py:216
  31.4 0.0 collective-permute-done.8.refs_3_
  31.4 0.1 shard_map.41
  31.5 0.1 collective-permute-start.9
  31.6 0.0 collective-permute-done.12.refs_1_
  31.6 0.3 shard_map.45
  31.9 1.1 %collective-permute-done.9.refs_1_ = f32[72,512]{1,0:T(8,128)S(1)} collective-permute-done((f32[72,512]{1,0:T(8,128)S(1)}, f32[72,512]{1,0:T(8,128)S(1)}, u32[]{:S(2)}, u32[]{:S(2)}) %collective-permute-start.9) | collective-permute-done | bytes 147488 | tf_op jit(solution)/shard_map/ppermute | solution.py:222
  33.0 1.0 %shard_map.46 = f32[64,512]{1,0:T(8,128)} custom-call(f32[72,512]{1,0:T(8,128)S(1)} %get-tuple-element.29.refs_0_, f32[72,512]{1,0:T(8,128)S(1)} %collective-permute-done.9.refs_1_, f32[8,512]{1,0:T(8,128)S(1)} %get-tuple-element.30.refs_2_, f32[64,512]{1,0:T(8,128)S(1)} %get-tuple-element.33.refs_3_, f32[64,128]{1,0:T(8,128)S(1)} %get-tuple-element.34.refs_4_, ...), custom_call_target="tpu_custom_call" | custom-call | tf_op jit(solution)/shard_map/pallas_call | solution.py:22
  (4 shorter events, 0.1 us)
Async XLA Ops:
  0.0 10.8 %collective-permute-start.4 = (bf16[64,512]{1,0:T(8,128)(2,1)}, bf16[64,512]{1,0:T(8,128)(2,1)S(1)}, u32[]{:S(2)}, u32[]{:S(2)}) collective-permute-start(bf16[64,512]{1,0:T(8,128)(2,1)} %refs_6_.1), channel_id=1, source_target_pairs={{0,8},{4,12},{8,0},{12,4},{1,9},{5,13},{9,1},{13,5},{2,10},{6,14},... | collective-permute-start | bytes 196616 | tf_op jit(solution)/shard_map/ppermute | solution.py:216
  4.0 0.9 %copy-start = (bf16[64,2048]{1,0:T(8,128)(2,1)S(1)}, bf16[64,2048]{1,0:T(8,128)(2,1)}, u32[]{:S(2)}) copy-start(bf16[64,2048]{1,0:T(8,128)(2,1)} %refs_0_.5) | copy-start | bytes 786436
  5.0 8.1 %collective-permute-start = (bf16[64,512]{1,0:T(8,128)(2,1)S(1)}, bf16[64,512]{1,0:T(8,128)(2,1)S(1)}, u32[]{:S(2)}, u32[]{:S(2)}) collective-permute-start(bf16[64,512]{1,0:T(8,128)(2,1)S(1)} %get-tuple-element.22), channel_id=1, source_target_pairs={{0,8},{4,12},{8,0},{12,4},{1,9},{5,13},{9,1},{13,5},{2,10},{6,14},... | collective-permute-start | bytes 196616 | tf_op jit(solution)/shard_map/ppermute | solution.py:216
  5.1 8.0 %collective-permute-start.1 = (bf16[64,512]{1,0:T(8,128)(2,1)S(1)}, bf16[64,512]{1,0:T(8,128)(2,1)S(1)}, u32[]{:S(2)}, u32[]{:S(2)}) collective-permute-start(bf16[64,512]{1,0:T(8,128)(2,1)S(1)} %get-tuple-element.23), channel_id=1, source_target_pairs={{0,12},{4,8},{8,4},{12,0},{1,13},{5,9},{9,5},{13,1},{2,14},{6,10},... | collective-permute-start | bytes 196616 | tf_op jit(solution)/shard_map/ppermute | solution.py:216
  9.0 4.7 %collective-permute-start.2 = (bf16[64,512]{1,0:T(8,128)(2,1)S(1)}, bf16[64,512]{1,0:T(8,128)(2,1)S(1)}, u32[]{:S(2)}, u32[]{:S(2)}) collective-permute-start(bf16[64,512]{1,0:T(8,128)(2,1)S(1)} %get-tuple-element.24), channel_id=1, source_target_pairs={{0,4},{4,0},{8,12},{12,8},{1,5},{5,1},{9,13},{13,9},{2,6},{6,2},{1... | collective-permute-start | bytes 196616 | tf_op jit(solution)/shard_map/ppermute | solution.py:216
  9.0 1.5 %copy-start.2 = (bf16[64]{0:T(256)(128)(2,1)S(1)}, bf16[64]{0:T(256)(128)(2,1)}, u32[]{:S(2)}) copy-start(bf16[64]{0:T(256)(128)(2,1)} %param.5) | copy-start | bytes 388
  9.0 4.7 %collective-permute-start.3 = (bf16[64,512]{1,0:T(8,128)(2,1)S(1)}, bf16[64,512]{1,0:T(8,128)(2,1)S(1)}, u32[]{:S(2)}, u32[]{:S(2)}) collective-permute-start(bf16[64,512]{1,0:T(8,128)(2,1)S(1)} %get-tuple-element.21.refs_0_), channel_id=1, source_target_pairs={{0,2},{2,0},{1,3},{3,1},{4,6},{6,4},{5,7},{7,5},{8,10},{10,8},{9,1... | collective-permute-start | bytes 196616 | tf_op jit(solution)/shard_map/ppermute | solution.py:219
  10.8 4.5 %copy-start.1 = (bf16[64,512]{1,0:T(8,128)(2,1)S(1)}, bf16[64,512]{1,0:T(8,128)(2,1)}, u32[]{:S(2)}) copy-start(bf16[64,512]{1,0:T(8,128)(2,1)} %refs_6_.1) | copy-start | bytes 196612
  13.8 5.9 %collective-permute-start.5 = (bf16[208,512]{1,0:T(8,128)(2,1)S(1)}, bf16[208,512]{1,0:T(8,128)(2,1)S(1)}, u32[]{:S(2)}, u32[]{:S(2)}) collective-permute-start(bf16[208,512]{1,0:T(8,128)(2,1)S(1)} %shard_map.39.refs_1_.refs_2_), channel_id=1, source_target_pairs={{0,2},{2,0},{1,3},{3,1},{4,6},{6,4},{5,7},{7,5},{8,10},{10,8},{9,1... | collective-permute-start | bytes 638984 | tf_op jit(solution)/shard_map/ppermute | solution.py:219
  15.3 5.0 %collective-permute-start.10 = (bf16[128,512]{1,0:T(8,128)(2,1)S(1)}, bf16[128,512]{1,0:T(8,128)(2,1)S(1)}, u32[]{:S(2)}, u32[]{:S(2)}) collective-permute-start(bf16[128,512]{1,0:T(8,128)(2,1)S(1)} %shard_map.42), channel_id=1, source_target_pairs={{0,4},{4,0},{8,12},{12,8},{1,5},{5,1},{9,13},{13,9},{2,6},{6,2},{1... | collective-permute-start | bytes 393224 | tf_op jit(solution)/shard_map/ppermute | solution.py:216
  20.4 6.4 %collective-permute-start.11 = (bf16[256,512]{1,0:T(8,128)(2,1)S(1)}, bf16[256,512]{1,0:T(8,128)(2,1)S(1)}, u32[]{:S(2)}, u32[]{:S(2)}) collective-permute-start(bf16[256,512]{1,0:T(8,128)(2,1)S(1)} %shard_map.43.refs_0_), channel_id=1, source_target_pairs={{0,2},{2,0},{1,3},{3,1},{4,6},{6,4},{5,7},{7,5},{8,10},{10,8},{9,1... | collective-permute-start | bytes 786440 | tf_op jit(solution)/shard_map/ppermute | solution.py:219
  21.8 7.2 %collective-permute-start.6 = (bf16[64,512]{1,0:T(8,128)(2,1)S(1)}, bf16[64,512]{1,0:T(8,128)(2,1)S(1)}, u32[]{:S(2)}, u32[]{:S(2)}) collective-permute-start(bf16[64,512]{1,0:T(8,128)(2,1)S(1)} %get-tuple-element.25), channel_id=1, source_target_pairs={{0,8},{4,12},{8,0},{12,4},{1,9},{5,13},{9,1},{13,5},{2,10},{6,14},... | collective-permute-start | bytes 196616 | tf_op jit(solution)/shard_map/ppermute | solution.py:216
  25.4 6.1 %collective-permute-start.7 = (bf16[64,512]{1,0:T(8,128)(2,1)S(1)}, bf16[64,512]{1,0:T(8,128)(2,1)S(1)}, u32[]{:S(2)}, u32[]{:S(2)}) collective-permute-start(bf16[64,512]{1,0:T(8,128)(2,1)S(1)} %get-tuple-element.26), channel_id=1, source_target_pairs={{0,12},{4,8},{8,4},{12,0},{1,13},{5,9},{9,5},{13,1},{2,14},{6,10},... | collective-permute-start | bytes 196616 | tf_op jit(solution)/shard_map/ppermute | solution.py:216
  25.8 5.6 %collective-permute-start.8 = (bf16[64,512]{1,0:T(8,128)(2,1)S(1)}, bf16[64,512]{1,0:T(8,128)(2,1)S(1)}, u32[]{:S(2)}, u32[]{:S(2)}) collective-permute-start(bf16[64,512]{1,0:T(8,128)(2,1)S(1)} %get-tuple-element.28), channel_id=1, source_target_pairs={{0,4},{4,0},{8,12},{12,8},{1,5},{5,1},{9,13},{13,9},{2,6},{6,2},{1... | collective-permute-start | bytes 196616 | tf_op jit(solution)/shard_map/ppermute | solution.py:216
  27.2 4.5 %collective-permute-start.12 = (f32[72,512]{1,0:T(8,128)S(1)}, f32[72,512]{1,0:T(8,128)S(1)}, u32[]{:S(2)}, u32[]{:S(2)}) collective-permute-start(f32[72,512]{1,0:T(8,128)S(1)} %get-tuple-element.31.refs_0_), channel_id=1, source_target_pairs={{0,1},{1,0},{2,3},{3,2},{4,5},{5,4},{6,7},{7,6},{8,9},{9,8},{10,11... | collective-permute-start | bytes 442376 | tf_op jit(solution)/shard_map/ppermute | solution.py:222
  31.5 1.4 %collective-permute-start.9 = (f32[72,512]{1,0:T(8,128)S(1)}, f32[72,512]{1,0:T(8,128)S(1)}, u32[]{:S(2)}, u32[]{:S(2)}) collective-permute-start(f32[72,512]{1,0:T(8,128)S(1)} %get-tuple-element.29.refs_0_), channel_id=1, source_target_pairs={{0,1},{1,0},{2,3},{3,2},{4,5},{5,4},{6,7},{7,6},{8,9},{9,8},{10,11... | collective-permute-start | bytes 442376 | tf_op jit(solution)/shard_map/ppermute | solution.py:222

commit v16 on v15

--- a/solution.py
+++ b/solution.py
@@ -69,7 +69,8 @@
         outs[k][...] = teach[:, pl.ds(at, part)]
 
 
-def tag_kernel(teach, scale, out):
+def tag_kernel(teach, scale, cut, out, own):
+    own[...] = cut[...]
     rows, width = teach.shape[0], out.shape[1]
     ts = teach[...].astype(F32)
     s = scale[...].astype(F32)
@@ -78,13 +79,6 @@
     out[...] = jnp.concatenate([tags] * (width // (2 * rows)), axis=1)
 
 
-def late_kernel(rows, tags, *refs):
-    out = refs[-1]
-    for n, ref in enumerate(refs[:-1]):
-        put(out, n * rows, rows, ref, 0)
-    out[(len(refs) - 1) * rows :, :] = tags[...]
-
-
 def pack_kernel(*refs):
     out, at = refs[-1], 0
     for r in refs[:-1]:
@@ -102,11 +96,11 @@
 
 
 def gram_kernel(nrow, ncol, rows, order, *refs):
-    outs, held, left = refs[2 * ncol : 2 * ncol + nrow], refs[-2], refs[-1]
-    for c in range(ncol):
-        put(held, place(nrow, ncol, rows, 0, c), rows, refs[2 * c], 0)
-        for n, k in enumerate([k for k in order if k]):
-            put(held, place(nrow, ncol, rows, k, c), rows, refs[2 * c + 1], n * rows)
+    count = nrow * ncol
+    outs, held, left = refs[count : count + nrow], refs[-2], refs[-1]
+    for n, k in enumerate(order):
+        for c in range(ncol):
+            put(held, place(nrow, ncol, rows, k, c), rows, refs[n * ncol + c], 0)
     for n, k in enumerate(order):
         left[n * rows : (n + 1) * rows, :] = held[pl.ds(place(nrow, ncol, rows, k, 0), rows), :]
     sub = rows // 2
@@ -114,7 +108,7 @@
     lane = lax.broadcasted_iota(jnp.int32, (sub, 2 * rows), 1)
     note, mass = jnp.zeros((sub, 2 * rows), F32), jnp.zeros((1, 1), F32)
     for c in range(ncol):
-        scales, part = read_tags(refs[2 * c + 1][(nrow - 1) * rows :, : 2 * rows])
+        scales, part = read_tags(refs[order.index(1) * ncol + c][rows:, : 2 * rows])
         turned = jnp.concatenate([scales[:, sub:], scales[:, :sub]], axis=1)
         note = jnp.where(at == 2 * c, scales, jnp.where(at == 2 * c + 1, turned, note))
         mass = mass + part
@@ -233,27 +227,24 @@
     cuts = call(functools.partial(cut_kernel, nrow), [sds((rows, part), BF16)] * nrow, [teacher])
     came = {k: along_row(cuts[k], k) for k in order if k}
     swapped = along_row(student, middle)
-    tags = call(tag_kernel, sds((TAIL, part), BF16), [teacher, scale], after=[came[n] for n in ()])
-    own = with_columns(cuts[0])
-    others = [k for k in order if k]
-    late = call(
-        functools.partial(late_kernel, rows),
-        sds(((nrow - 1) * rows + TAIL, part), BF16),
-        [tags] + [came[k] for k in others],
-        after=own[1:2] + [swapped],
-    )
-    late = with_columns(late)
+    tags, own = call(tag_kernel, [sds((TAIL, part), BF16), sds((rows, part), BF16)], [teacher, scale, cuts[0]])
+    columns = {}
+    for k in order:
+        piece = came[k] if k else own
+        if k == 1:
+            piece = call(pack_kernel, sds((rows + TAIL, part), BF16), [piece, tags])
+        columns[k] = with_columns(piece)
     partial = call(
         functools.partial(gram_kernel, nrow, ncol, rows, order),
         [sds((rows, batch), BF16 if k else F32) for k in range(nrow)],
-        [r for pair in zip(own, late) for r in pair],
+        [columns[k][c] for k in order for c in range(ncol)],
         scratch=[pltpu.VMEM((batch, part), BF16), pltpu.VMEM((nrow * rows, part), BF16)],
     )
     returned = {k: along_row(partial[k], k) if k else partial[0] for k in order}
 
     stack, keys, k = [student], [0], middle
     while k:
-        joined = pack(stack, after=late[:1] if k == 1 else ()) if k < middle else student
+        joined = pack(stack, after=columns[middle][1:2] + columns[0][1:2] + list(came.values()) if k == 1 else ()) if k < middle else student
         stack.append(swapped if k == middle else along_row(joined, k))
         keys, k = keys + [n ^ k for n in keys], k // 2
     raw_refs = with_columns(pack(stack, after=[partial[0]]))

time: 34.1 us -> 35.4 us (1.038)
  local copies, waits for them, and re-layouts: 0.96 us -> 1.61 us
  starting transfers between devices: 18.4 us -> 18.9 us
    ppermute x3 -> x5, waiting for transfers between devices: 3.62 us -> 7.48 us  [along_col(): return lax.ppermute(x, 'col', [(i, (i - c) % ncol) for i in range(ncol)])]
    ppermute x8, waiting for transfers between devices: 7.3 us -> 3.54 us  [along_row(): return lax.ppermute(x, 'row', [(i, i ^ k) for i in range(nrow)])]
    ppermute x3 -> x5, starting transfers between devices: 4.46 us -> 5.12 us  [along_col(): return lax.ppermute(x, 'col', [(i, (i - c) % ncol) for i in range(ncol)])]
    unnamed x6 -> x8, local copies, waits for them, and re-layouts: 0.96 us -> 1.61 us
  transfers between devices with their start and end apart: 13 -> 15, of which waited for: 8 -> 8; matrix products, arithmetic and copies ran while one was open for 0% -> 0% of each run, Pallas kernels for 4% -> 4%
where the time goes in v16:
time: 35.4 us; the launch traced here: 35.2 us
  starting transfers between devices  18.9 us (53%)
  waiting for transfers between devices  12.1 us (34%)
  Pallas kernels  2.54 us (7%)
  local copies, waits for them, and re-layouts  1.61 us (5%)
    ppermute x8, starting transfers between devices, along_row(): return lax.ppermute(x, 'row', [(i, i ^ k) for i in range(nrow)])  13.6 us
    ppermute x5, waiting for transfers between devices, along_col(): return lax.ppermute(x, 'col', [(i, (i - c) % ncol) for i in range(ncol)])  7.48 us
    ppermute x5, starting transfers between devices, along_col(): return lax.ppermute(x, 'col', [(i, (i - c) % ncol) for i in range(ncol)])  5.12 us
    ppermute x8, waiting for transfers between devices, along_row(): return lax.ppermute(x, 'row', [(i, i ^ k) for i in range(nrow)])  3.54 us
    pallas_call x10, Pallas kernels, call(): pl.pallas_call(run, out_shape=out_shape, in_specs=[pl.BlockSpec(memory_sp...  2.54 us
    unnamed x8, local copies, waits for them, and re-layouts  1.61 us
    ppermute x2, waiting for transfers between devices, other_core(): return lax.ppermute(x, 'sub', [(0, 1), (1, 0)])  1.08 us
  transfers between devices with their start and end apart: 15, of which 8 were waited for; matrix products, arithmetic and copies ran while one was open for 0% of the time, Pallas kernels for 4%

profile of v16, /device:TPU:0, one launch (start us, length us, event | category | flops | bytes accessed | tf_op | source)
XLA Modules:
  0.0 35.2 jit_solution(15782656568496894086)
XLA Ops:
  0.0 0.0 copy-start
  0.0 0.9 %copy-done = bf16[64,2048]{1,0:T(8,128)(2,1)S(1)} copy-done((bf16[64,2048]{1,0:T(8,128)(2,1)S(1)}, bf16[64,2048]{1,0:T(8,128)(2,1)}, u32[]{:S(2)}) %copy-start) | copy-done | bytes 262168
  1.0 0.0 copy-start.1
  1.0 4.1 %collective-permute-start = (bf16[64,512]{1,0:T(8,128)(2,1)S(1)}, bf16[64,512]{1,0:T(8,128)(2,1)S(1)}, u32[]{:S(2)}, u32[]{:S(2)}) collective-permute-start(bf16[64,512]{1,0:T(8,128)(2,1)S(1)} %get-tuple-element.23), channel_id=1, source_target_pairs={{0,8},{4,12},{8,0},{12,4},{1,9},{5,13},{9,1},{13,5},{2,10},{6,14},... | collective-permute-start | bytes 196616 | tf_op jit(solution)/shard_map/ppermute | solution.py:210
  5.1 0.1 collective-permute-start.11
  5.2 3.9 %collective-permute-start.2 = (bf16[64,512]{1,0:T(8,128)(2,1)S(1)}, bf16[64,512]{1,0:T(8,128)(2,1)S(1)}, u32[]{:S(2)}, u32[]{:S(2)}) collective-permute-start(bf16[64,512]{1,0:T(8,128)(2,1)S(1)} %get-tuple-element.24), channel_id=1, source_target_pairs={{0,12},{4,8},{8,4},{12,0},{1,13},{5,9},{9,5},{13,1},{2,14},{6,10},... | collective-permute-start | bytes 196616 | tf_op jit(solution)/shard_map/ppermute | solution.py:210
  9.0 0.0 collective-permute-start.5
  9.0 0.0 copy-start.3
  9.0 0.0 copy-done.1
  9.0 0.7 %copy-done.3 = bf16[64]{0:T(256)(128)(2,1)S(1)} copy-done((bf16[64]{0:T(256)(128)(2,1)S(1)}, bf16[64]{0:T(256)(128)(2,1)}, u32[]{:S(2)}) %copy-start.3) | copy-done | bytes 152
  9.7 0.0 copy-start.2
  9.7 0.3 shard_map.38
  9.9 1.6 %collective-permute-start.4 = (bf16[64,512]{1,0:T(8,128)(2,1)S(1)}, bf16[64,512]{1,0:T(8,128)(2,1)S(1)}, u32[]{:S(2)}, u32[]{:S(2)}) collective-permute-start(bf16[64,512]{1,0:T(8,128)(2,1)S(1)} %get-tuple-element.26.refs_4_), channel_id=1, source_target_pairs={{0,2},{2,0},{1,3},{3,1},{4,6},{6,4},{5,7},{7,5},{8,10},{10,8},{9,1... | collective-permute-start | bytes 196616 | tf_op jit(solution)/shard_map/ppermute | solution.py:213
  11.5 0.0 collective-permute-done.refs_0_.refs_4_
  11.5 0.5 %collective-permute-start.1 = (bf16[64,512]{1,0:T(8,128)(2,1)S(1)}, bf16[64,512]{1,0:T(8,128)(2,1)S(1)}, u32[]{:S(2)}, u32[]{:S(2)}) collective-permute-start(bf16[64,512]{1,0:T(8,128)(2,1)S(1)} %collective-permute-done.refs_0_.refs_4_), channel_id=1, source_target_pairs={{0,2},{2,0},{1,3},{3,1},{4,6},{6,4},{5,7},{7,5},{8,10},{10,8},{9,1... | collective-permute-start | bytes 196616 | tf_op jit(solution)/shard_map/ppermute | solution.py:213
  12.0 1.6 %collective-permute-done.11.refs_1_ = bf16[64,512]{1,0:T(8,128)(2,1)S(1)} collective-permute-done((bf16[64,512]{1,0:T(8,128)(2,1)}, bf16[64,512]{1,0:T(8,128)(2,1)S(1)}, u32[]{:S(2)}, u32[]{:S(2)}) %collective-permute-start.11) | collective-permute-done | bytes 65568 | tf_op jit(solution)/shard_map/ppermute | solution.py:210
  13.6 0.0 collective-permute-done.2.refs_2_.refs_5_
  13.7 0.4 %collective-permute-done.5.refs_0_.refs_6_ = bf16[64,512]{1,0:T(8,128)(2,1)S(1)} collective-permute-done((bf16[64,512]{1,0:T(8,128)(2,1)S(1)}, bf16[64,512]{1,0:T(8,128)(2,1)S(1)}, u32[]{:S(2)}, u32[]{:S(2)}) %collective-permute-start.5) | collective-permute-done | bytes 65568 | tf_op jit(solution)/shard_map/ppermute | solution.py:210
  14.0 0.3 collective-permute-done.4.refs_5_.refs_3_
  14.3 1.5 %collective-permute-done.1.refs_1_.refs_2_ = bf16[64,512]{1,0:T(8,128)(2,1)S(1)} collective-permute-done((bf16[64,512]{1,0:T(8,128)(2,1)S(1)}, bf16[64,512]{1,0:T(8,128)(2,1)S(1)}, u32[]{:S(2)}, u32[]{:S(2)}) %collective-permute-start.1) | collective-permute-done | bytes 65568 | tf_op jit(solution)/shard_map/ppermute | solution.py:213
  15.8 0.0 copy-done.2
  15.8 2.1 %collective-permute-start.12 = (bf16[128,512]{1,0:T(8,128)(2,1)S(1)}, bf16[128,512]{1,0:T(8,128)(2,1)S(1)}, u32[]{:S(2)}, u32[]{:S(2)}) collective-permute-start(bf16[128,512]{1,0:T(8,128)(2,1)S(1)} %shard_map.42), channel_id=1, source_target_pairs={{0,4},{4,0},{8,12},{12,8},{1,5},{5,1},{9,13},{13,9},{2,6},{6,2},{1... | collective-permute-start | bytes 393224 | tf_op jit(solution)/shard_map/ppermute | solution.py:210
  17.9 0.7 %collective-permute-start.6 = (bf16[80,512]{1,0:T(8,128)(2,1)S(1)}, bf16[80,512]{1,0:T(8,128)(2,1)S(1)}, u32[]{:S(2)}, u32[]{:S(2)}) collective-permute-start(bf16[80,512]{1,0:T(8,128)(2,1)S(1)} %shard_map.39.refs_6_), channel_id=1, source_target_pairs={{0,2},{2,0},{1,3},{3,1},{4,6},{6,4},{5,7},{7,5},{8,10},{10,8},{9,1... | collective-permute-start | bytes 245768 | tf_op jit(solution)/shard_map/ppermute | solution.py:213
  18.6 1.3 %collective-permute-start.3 = (bf16[64,512]{1,0:T(8,128)(2,1)S(1)}, bf16[64,512]{1,0:T(8,128)(2,1)S(1)}, u32[]{:S(2)}, u32[]{:S(2)}) collective-permute-start(bf16[64,512]{1,0:T(8,128)(2,1)S(1)} %collective-permute-done.2.refs_2_.refs_5_), channel_id=1, source_target_pairs={{0,2},{2,0},{1,3},{3,1},{4,6},{6,4},{5,7},{7,5},{8,10},{10,8},{9,1... | collective-permute-start | bytes 196616 | tf_op jit(solution)/shard_map/ppermute | solution.py:213
  19.9 3.8 %collective-permute-done.3.refs_3_ = bf16[64,512]{1,0:T(8,128)(2,1)S(1)} collective-permute-done((bf16[64,512]{1,0:T(8,128)(2,1)S(1)}, bf16[64,512]{1,0:T(8,128)(2,1)S(1)}, u32[]{:S(2)}, u32[]{:S(2)}) %collective-permute-start.3) | collective-permute-done | bytes 65568 | tf_op jit(solution)/shard_map/ppermute | solution.py:213
  23.7 0.0 collective-permute-done.6.refs_7_
  23.7 0.5 %shard_map.40 = (f32[64,512]{1,0:T(8,128)S(1)}, bf16[64,512]{1,0:T(8,128)(2,1)S(1)}, bf16[64,512]{1,0:T(8,128)(2,1)S(1)}, bf16[64,512]{1,0:T(8,128)(2,1)S(1)}) custom-call(bf16[64,512]{1,0:T(8,128)(2,1)S(1)} %collective-permute-done.refs_0_.refs_4_, bf16[64,512]{1,0:T(8,128)(2,1)S(1)} %collective-permute-done.1.refs_1_.refs_2_, ...), custom_call_target="tpu_custom_call" | custom-call | tf_op jit(solution)/shard_map/pallas_call | solution.py:22
  24.2 0.0 collective-permute-done.12.refs_2_
  24.3 1.0 %collective-permute-start.13 = (bf16[256,512]{1,0:T(8,128)(2,1)S(1)}, bf16[256,512]{1,0:T(8,128)(2,1)S(1)}, u32[]{:S(2)}, u32[]{:S(2)}) collective-permute-start(bf16[256,512]{1,0:T(8,128)(2,1)S(1)} %shard_map.43.refs_0_), channel_id=1, source_target_pairs={{0,2},{2,0},{1,3},{3,1},{4,6},{6,4},{5,7},{7,5},{8,10},{10,8},{9,1... | collective-permute-start | bytes 786440 | tf_op jit(solution)/shard_map/ppermute | solution.py:213
  25.3 1.3 %collective-permute-start.7 = (bf16[64,512]{1,0:T(8,128)(2,1)S(1)}, bf16[64,512]{1,0:T(8,128)(2,1)S(1)}, u32[]{:S(2)}, u32[]{:S(2)}) collective-permute-start(bf16[64,512]{1,0:T(8,128)(2,1)S(1)} %get-tuple-element.29), channel_id=1, source_target_pairs={{0,8},{4,12},{8,0},{12,4},{1,9},{5,13},{9,1},{13,5},{2,10},{6,14},... | collective-permute-start | bytes 196616 | tf_op jit(solution)/shard_map/ppermute | solution.py:210
  26.6 1.0 %collective-permute-start.8 = (bf16[64,512]{1,0:T(8,128)(2,1)S(1)}, bf16[64,512]{1,0:T(8,128)(2,1)S(1)}, u32[]{:S(2)}, u32[]{:S(2)}) collective-permute-start(bf16[64,512]{1,0:T(8,128)(2,1)S(1)} %get-tuple-element.30), channel_id=1, source_target_pairs={{0,12},{4,8},{8,4},{12,0},{1,13},{5,9},{9,5},{13,1},{2,14},{6,10},... | collective-permute-start | bytes 196616 | tf_op jit(solution)/shard_map/ppermute | solution.py:210
  27.6 1.1 %collective-permute-start.9 = (bf16[64,512]{1,0:T(8,128)(2,1)S(1)}, bf16[64,512]{1,0:T(8,128)(2,1)S(1)}, u32[]{:S(2)}, u32[]{:S(2)}) collective-permute-start(bf16[64,512]{1,0:T(8,128)(2,1)S(1)} %get-tuple-element.32), channel_id=1, source_target_pairs={{0,4},{4,0},{8,12},{12,8},{1,5},{5,1},{9,13},{13,9},{2,6},{6,2},{1... | collective-permute-start | bytes 196616 | tf_op jit(solution)/shard_map/ppermute | solution.py:210
  28.7 1.9 %collective-permute-done.13.refs_1_ = bf16[256,512]{1,0:T(8,128)(2,1)S(1)} collective-permute-done((bf16[256,512]{1,0:T(8,128)(2,1)S(1)}, bf16[256,512]{1,0:T(8,128)(2,1)S(1)}, u32[]{:S(2)}, u32[]{:S(2)}) %collective-permute-start.13) | collective-permute-done | bytes 262176 | tf_op jit(solution)/shard_map/ppermute | solution.py:213
  30.7 0.3 shard_map.44
  31.0 0.1 collective-permute-start.14
  31.1 0.0 collective-permute-done.7.refs_0_
  31.1 1.6 %collective-permute-done.8.refs_1_ = bf16[64,512]{1,0:T(8,128)(2,1)S(1)} collective-permute-done((bf16[64,512]{1,0:T(8,128)(2,1)S(1)}, bf16[64,512]{1,0:T(8,128)(2,1)S(1)}, u32[]{:S(2)}, u32[]{:S(2)}) %collective-permute-start.8) | collective-permute-done | bytes 65568 | tf_op jit(solution)/shard_map/ppermute | solution.py:210
  32.7 0.0 collective-permute-done.9.refs_3_
  32.7 0.1 shard_map.41
  32.8 0.1 collective-permute-start.10
  32.9 0.0 collective-permute-done.14.refs_1_
  32.9 0.3 shard_map.45
  33.1 1.1 %collective-permute-done.10.refs_1_ = f32[72,512]{1,0:T(8,128)S(1)} collective-permute-done((f32[72,512]{1,0:T(8,128)S(1)}, f32[72,512]{1,0:T(8,128)S(1)}, u32[]{:S(2)}, u32[]{:S(2)}) %collective-permute-start.10) | collective-permute-done | bytes 147488 | tf_op jit(solution)/shard_map/ppermute | solution.py:216
  34.2 1.0 %shard_map.46 = f32[64,512]{1,0:T(8,128)} custom-call(f32[72,512]{1,0:T(8,128)S(1)} %get-tuple-element.33.refs_0_, f32[72,512]{1,0:T(8,128)S(1)} %collective-permute-done.10.refs_1_, f32[8,512]{1,0:T(8,128)S(1)} %get-tuple-element.34.refs_2_, f32[64,512]{1,0:T(8,128)S(1)} %get-tuple-element.37.refs_3_, f32[64,128]{1,0:T(8,128)S(1)} %get-tuple-element.38.refs_4_, ...), custom_call_target="tpu_custom_call" | custom-call | tf_op jit(solution)/shard_map/pallas_call | solution.py:22
  (4 shorter events, 0.1 us)
Async XLA Ops:
  0.0 0.9 %copy-start = (bf16[64,2048]{1,0:T(8,128)(2,1)S(1)}, bf16[64,2048]{1,0:T(8,128)(2,1)}, u32[]{:S(2)}) copy-start(bf16[64,2048]{1,0:T(8,128)(2,1)} %refs_0_.5) | copy-start | bytes 786436
  1.0 8.1 %copy-start.1 = (bf16[64,2048]{1,0:T(8,128)(2,1)S(1)}, bf16[64,2048]{1,0:T(8,128)(2,1)}, u32[]{:S(2)}) copy-start(bf16[64,2048]{1,0:T(8,128)(2,1)} %refs_0_.5) | copy-start | bytes 786436
  1.0 10.5 %collective-permute-start = (bf16[64,512]{1,0:T(8,128)(2,1)S(1)}, bf16[64,512]{1,0:T(8,128)(2,1)S(1)}, u32[]{:S(2)}, u32[]{:S(2)}) collective-permute-start(bf16[64,512]{1,0:T(8,128)(2,1)S(1)} %get-tuple-element.23), channel_id=1, source_target_pairs={{0,8},{4,12},{8,0},{12,4},{1,9},{5,13},{9,1},{13,5},{2,10},{6,14},... | collective-permute-start | bytes 196616 | tf_op jit(solution)/shard_map/ppermute | solution.py:210
  5.1 8.6 %collective-permute-start.11 = (bf16[64,512]{1,0:T(8,128)(2,1)}, bf16[64,512]{1,0:T(8,128)(2,1)S(1)}, u32[]{:S(2)}, u32[]{:S(2)}) collective-permute-start(bf16[64,512]{1,0:T(8,128)(2,1)} %refs_6_.1), channel_id=1, source_target_pairs={{0,8},{4,12},{8,0},{12,4},{1,9},{5,13},{9,1},{13,5},{2,10},{6,14},... | collective-permute-start | bytes 196616 | tf_op jit(solution)/shard_map/ppermute | solution.py:210
  5.2 8.5 %collective-permute-start.2 = (bf16[64,512]{1,0:T(8,128)(2,1)S(1)}, bf16[64,512]{1,0:T(8,128)(2,1)S(1)}, u32[]{:S(2)}, u32[]{:S(2)}) collective-permute-start(bf16[64,512]{1,0:T(8,128)(2,1)S(1)} %get-tuple-element.24), channel_id=1, source_target_pairs={{0,12},{4,8},{8,4},{12,0},{1,13},{5,9},{9,5},{13,1},{2,14},{6,10},... | collective-permute-start | bytes 196616 | tf_op jit(solution)/shard_map/ppermute | solution.py:210
  9.0 5.0 %collective-permute-start.5 = (bf16[64,512]{1,0:T(8,128)(2,1)S(1)}, bf16[64,512]{1,0:T(8,128)(2,1)S(1)}, u32[]{:S(2)}, u32[]{:S(2)}) collective-permute-start(bf16[64,512]{1,0:T(8,128)(2,1)S(1)} %get-tuple-element.27), channel_id=1, source_target_pairs={{0,4},{4,0},{8,12},{12,8},{1,5},{5,1},{9,13},{13,9},{2,6},{6,2},{1... | collective-permute-start | bytes 196616 | tf_op jit(solution)/shard_map/ppermute | solution.py:210
  9.0 0.7 %copy-start.3 = (bf16[64]{0:T(256)(128)(2,1)S(1)}, bf16[64]{0:T(256)(128)(2,1)}, u32[]{:S(2)}) copy-start(bf16[64]{0:T(256)(128)(2,1)} %param.5) | copy-start | bytes 388
  9.7 6.1 %copy-start.2 = (bf16[64,512]{1,0:T(8,128)(2,1)S(1)}, bf16[64,512]{1,0:T(8,128)(2,1)}, u32[]{:S(2)}) copy-start(bf16[64,512]{1,0:T(8,128)(2,1)} %refs_6_.1) | copy-start | bytes 196612
  9.9 4.3 %collective-permute-start.4 = (bf16[64,512]{1,0:T(8,128)(2,1)S(1)}, bf16[64,512]{1,0:T(8,128)(2,1)S(1)}, u32[]{:S(2)}, u32[]{:S(2)}) collective-permute-start(bf16[64,512]{1,0:T(8,128)(2,1)S(1)} %get-tuple-element.26.refs_4_), channel_id=1, source_target_pairs={{0,2},{2,0},{1,3},{3,1},{4,6},{6,4},{5,7},{7,5},{8,10},{10,8},{9,1... | collective-permute-start | bytes 196616 | tf_op jit(solution)/shard_map/ppermute | solution.py:213
  11.5 4.3 %collective-permute-start.1 = (bf16[64,512]{1,0:T(8,128)(2,1)S(1)}, bf16[64,512]{1,0:T(8,128)(2,1)S(1)}, u32[]{:S(2)}, u32[]{:S(2)}) collective-permute-start(bf16[64,512]{1,0:T(8,128)(2,1)S(1)} %collective-permute-done.refs_0_.refs_4_), channel_id=1, source_target_pairs={{0,2},{2,0},{1,3},{3,1},{4,6},{6,4},{5,7},{7,5},{8,10},{10,8},{9,1... | collective-permute-start | bytes 196616 | tf_op jit(solution)/shard_map/ppermute | solution.py:213
  15.8 8.4 %collective-permute-start.12 = (bf16[128,512]{1,0:T(8,128)(2,1)S(1)}, bf16[128,512]{1,0:T(8,128)(2,1)S(1)}, u32[]{:S(2)}, u32[]{:S(2)}) collective-permute-start(bf16[128,512]{1,0:T(8,128)(2,1)S(1)} %shard_map.42), channel_id=1, source_target_pairs={{0,4},{4,0},{8,12},{12,8},{1,5},{5,1},{9,13},{13,9},{2,6},{6,2},{1... | collective-permute-start | bytes 393224 | tf_op jit(solution)/shard_map/ppermute | solution.py:210
  17.9 5.8 %collective-permute-start.6 = (bf16[80,512]{1,0:T(8,128)(2,1)S(1)}, bf16[80,512]{1,0:T(8,128)(2,1)S(1)}, u32[]{:S(2)}, u32[]{:S(2)}) collective-permute-start(bf16[80,512]{1,0:T(8,128)(2,1)S(1)} %shard_map.39.refs_6_), channel_id=1, source_target_pairs={{0,2},{2,0},{1,3},{3,1},{4,6},{6,4},{5,7},{7,5},{8,10},{10,8},{9,1... | collective-permute-start | bytes 245768 | tf_op jit(solution)/shard_map/ppermute | solution.py:213
  18.6 5.1 %collective-permute-start.3 = (bf16[64,512]{1,0:T(8,128)(2,1)S(1)}, bf16[64,512]{1,0:T(8,128)(2,1)S(1)}, u32[]{:S(2)}, u32[]{:S(2)}) collective-permute-start(bf16[64,512]{1,0:T(8,128)(2,1)S(1)} %collective-permute-done.2.refs_2_.refs_5_), channel_id=1, source_target_pairs={{0,2},{2,0},{1,3},{3,1},{4,6},{6,4},{5,7},{7,5},{8,10},{10,8},{9,1... | collective-permute-start | bytes 196616 | tf_op jit(solution)/shard_map/ppermute | solution.py:213
  24.3 6.4 %collective-permute-start.13 = (bf16[256,512]{1,0:T(8,128)(2,1)S(1)}, bf16[256,512]{1,0:T(8,128)(2,1)S(1)}, u32[]{:S(2)}, u32[]{:S(2)}) collective-permute-start(bf16[256,512]{1,0:T(8,128)(2,1)S(1)} %shard_map.43.refs_0_), channel_id=1, source_target_pairs={{0,2},{2,0},{1,3},{3,1},{4,6},{6,4},{5,7},{7,5},{8,10},{10,8},{9,1... | collective-permute-start | bytes 786440 | tf_op jit(solution)/shard_map/ppermute | solution.py:213
  25.3 5.8 %collective-permute-start.7 = (bf16[64,512]{1,0:T(8,128)(2,1)S(1)}, bf16[64,512]{1,0:T(8,128)(2,1)S(1)}, u32[]{:S(2)}, u32[]{:S(2)}) collective-permute-start(bf16[64,512]{1,0:T(8,128)(2,1)S(1)} %get-tuple-element.29), channel_id=1, source_target_pairs={{0,8},{4,12},{8,0},{12,4},{1,9},{5,13},{9,1},{13,5},{2,10},{6,14},... | collective-permute-start | bytes 196616 | tf_op jit(solution)/shard_map/ppermute | solution.py:210
  26.6 6.1 %collective-permute-start.8 = (bf16[64,512]{1,0:T(8,128)(2,1)S(1)}, bf16[64,512]{1,0:T(8,128)(2,1)S(1)}, u32[]{:S(2)}, u32[]{:S(2)}) collective-permute-start(bf16[64,512]{1,0:T(8,128)(2,1)S(1)} %get-tuple-element.30), channel_id=1, source_target_pairs={{0,12},{4,8},{8,4},{12,0},{1,13},{5,9},{9,5},{13,1},{2,14},{6,10},... | collective-permute-start | bytes 196616 | tf_op jit(solution)/shard_map/ppermute | solution.py:210
  27.6 5.0 %collective-permute-start.9 = (bf16[64,512]{1,0:T(8,128)(2,1)S(1)}, bf16[64,512]{1,0:T(8,128)(2,1)S(1)}, u32[]{:S(2)}, u32[]{:S(2)}) collective-permute-start(bf16[64,512]{1,0:T(8,128)(2,1)S(1)} %get-tuple-element.32), channel_id=1, source_target_pairs={{0,4},{4,0},{8,12},{12,8},{1,5},{5,1},{9,13},{13,9},{2,6},{6,2},{1... | collective-permute-start | bytes 196616 | tf_op jit(solution)/shard_map/ppermute | solution.py:210
  31.0 1.8 %collective-permute-start.14 = (f32[72,512]{1,0:T(8,128)S(1)}, f32[72,512]{1,0:T(8,128)S(1)}, u32[]{:S(2)}, u32[]{:S(2)}) collective-permute-start(f32[72,512]{1,0:T(8,128)S(1)} %get-tuple-element.35.refs_0_), channel_id=1, source_target_pairs={{0,1},{1,0},{2,3},{3,2},{4,5},{5,4},{6,7},{7,6},{8,9},{9,8},{10,11... | collective-permute-start | bytes 442376 | tf_op jit(solution)/shard_map/ppermute | solution.py:216
  32.8 1.4 %collective-permute-start.10 = (f32[72,512]{1,0:T(8,128)S(1)}, f32[72,512]{1,0:T(8,128)S(1)}, u32[]{:S(2)}, u32[]{:S(2)}) collective-permute-start(f32[72,512]{1,0:T(8,128)S(1)} %get-tuple-element.33.refs_0_), channel_id=1, source_target_pairs={{0,1},{1,0},{2,3},{3,2},{4,5},{5,4},{6,7},{7,6},{8,9},{9,8},{10,11... | collective-permute-start | bytes 442376 | tf_op jit(solution)/shard_map/ppermute | solution.py:216

commit v17 on v8

--- a/solution.py
+++ b/solution.py
@@ -111,8 +111,9 @@
     return pl.multiple_of(((lax.axis_index("row") ^ k) * ncol + c) * rows, rows)
 
 
-def group_spot(nrow, ncol, rows, k):
-    return pl.multiple_of((lax.axis_index("row") ^ k) * ncol * rows, 2 * rows)
+def group(ncol, rows, k):
+    at = (lax.axis_index("row") ^ k) * ncol * rows
+    return pl.ds(pl.multiple_of(at, 2 * rows), ncol * rows)
 
 
 def gram_kernel(nrow, ncol, rows, order, *refs):
@@ -142,7 +143,7 @@
         for n in range(first, last):
             out = outs[order[n]]
             out[...] = gram[(n - first) * rows : (n - first + 1) * rows, :].astype(out.dtype)
-            spot = pl.ds(group_spot(nrow, ncol, rows, order[n]), 2 * rows)
+            spot = pl.ds(pl.multiple_of(place(nrow, ncol, rows, order[n], 0), 2 * rows), 2 * rows)
             seen = out[sub:, spot].astype(F32)
             out[sub:, spot] = jnp.where(lane < sub, note, seen).astype(out.dtype)
 
@@ -165,7 +166,7 @@
         out[rows:, at : at + 128] = jnp.broadcast_to(lane_row(squares), (8, 128))
 
 
-def message_kernel(nrow, ncol, order, raw_gram, *refs):
+def sum_kernel(nrow, ncol, order, *refs):
     parts, (out, vectors) = [refs[order.index(k)] for k in range(nrow)], refs[-2:]
     rows = parts[0].shape[0]
     sub = rows // 2
@@ -173,7 +174,7 @@
     for r in parts[1:]:
         total = total + r[...].astype(F32)
     out[:rows, :] = total
-    own = pl.ds(group_spot(nrow, ncol, rows, 0), 2 * rows)
+    own = group(ncol, rows, 0)
     mirror = jnp.transpose(out[:sub, own])[sub : 2 * sub, :]
     out[sub:rows, own] = jnp.concatenate([mirror, out[sub:rows, own][:, sub:]], axis=1)
     mass = jnp.zeros((1, 1), F32)
@@ -181,34 +182,44 @@
         note = part[sub:, own].astype(F32)[:, :sub]
         mass = mass + note[sub // 2 : sub // 2 + 1, :1] + note[sub * 3 // 4 : sub * 3 // 4 + 1, :1]
         line = jnp.concatenate([note[n : n + 1, :] for n in range(2 * ncol)], axis=1)
-        vectors[:, pl.ds(group_spot(nrow, ncol, rows, k), ncol * rows)] = jnp.broadcast_to(line, (8, ncol * rows))
-    out[rows : 2 * rows + 8, :] = raw_gram[...]
-    out[2 * rows + 8 :, :] = jnp.broadcast_to(mass, (8, out.shape[1]))
-
-
-def final_kernel(nrow, ncol, keys, mine, other, vectors, stud, scale, *refs):
+        vectors[:, group(ncol, rows, k)] = jnp.broadcast_to(line, (8, ncol * rows))
+    out[rows:, :] = jnp.broadcast_to(mass, (8, out.shape[1]))
+
+
+def normalize(raw, squares, units):
+    for at in range(0, raw.shape[0], 128):
+        inverse = 1.0 / jnp.sqrt(column(squares[:1, at : at + 128]))
+        units[at : at + 128, :] = (raw[at : at + 128, :].astype(F32) * inverse).astype(BF16)
+
+
+def unit_gram_kernel(ncol, mine, other, *refs):
+    rows = mine.shape[0] - 8
+    gram, inverses, squares = refs[1:4] if len(refs) > 3 else refs
+    squares[...] = mine[rows:, :] + other[rows:, :]
+    at = pl.multiple_of(lax.axis_index("row") * ncol * rows, 2 * rows)
+    inverse = 1.0 / jnp.sqrt(column(squares[:1, pl.ds(at, 2 * rows)][:, :rows]))
+    inverses[...] = jnp.broadcast_to(inverse, inverses.shape)
+    gram[...] = (mine[:rows, :] + other[:rows, :]) * (inverse * (1.0 / jnp.sqrt(squares[:1, :])))
+    if len(refs) > 3:
+        normalize(refs[0], squares, refs[4])
+
+
+def final_kernel(nrow, ncol, keys, mine, other, vectors, gram, inverses, squares, stud, scale, *refs):
     rows = stud.shape[0]
     if keys:
-        out, raw, units = refs[-3:]
-        assemble(nrow, ncol, rows, keys, refs, raw)
+        out, units = refs[-2:]
+        assemble(nrow, ncol, rows, keys, refs[:-2], units)
+        normalize(units, squares, units)
     else:
-        raw, out, units = refs
-    batch = mine.shape[1]
-    squares = mine[2 * rows : 2 * rows + 8, :] + other[2 * rows : 2 * rows + 8, :]
-    for at in range(0, batch, 128):
-        norm = jnp.sqrt(column(squares[:1, at : at + 128]))
-        units[at : at + 128, :] = (raw[at : at + 128, :].astype(F32) / norm).astype(BF16)
-    at = pl.ds(group_spot(nrow, ncol, rows, 0), 2 * rows)
-    own = (mine[2 * rows : 2 * rows + 8, at] + other[2 * rows : 2 * rows + 8, at])[:1, :rows]
-    norm = jnp.sqrt(column(own))
-    mass = (mine[2 * rows + 8 : 2 * rows + 9, :1] + other[2 * rows + 8 : 2 * rows + 9, :1]) / batch
-    gram = (mine[rows : 2 * rows, :] + other[rows : 2 * rows, :]) / (norm * jnp.sqrt(squares[:1, :]))
-    outer = column(scale[...].astype(F32)) * vectors[:1, :]
-    error_b = (gram - outer * (mine[:rows, :] + other[:rows, :]) / mass).astype(BF16)
+        units, out = refs
+    inverse = inverses[:, :1]
+    mass = (mine[rows : rows + 1, :1] + other[rows : rows + 1, :1]) / mine.shape[1]
+    outer = (column(scale[...].astype(F32)) / mass) * vectors[:1, :]
+    error_b = (gram[...] - outer * (mine[:rows, :] + other[:rows, :])).astype(BF16)
     grads = 4.0 * jnp.dot(error_b, units[...], preferred_element_type=F32)
-    along = 4.0 * jnp.sum(error_b.astype(F32) * gram, axis=1, keepdims=True)
-    unit = stud[...].astype(F32) / norm
-    out[...] = (grads - along * unit) / norm
+    along = 4.0 * jnp.sum(error_b.astype(F32) * gram[...], axis=1, keepdims=True)
+    unit = stud[...].astype(F32) * inverse
+    out[...] = (grads - along * unit) * inverse
 
 
 def shards(student, teacher, scale):
@@ -276,22 +287,27 @@
     raw_keys = [[0], [1, middle] + got_keys]
     sources = [columns[0], with_columns(rest)]
     raw_refs = [x[c] for c in range(ncol) for x in sources]
-    raw_gram, *all_raw = call(
+    raw_gram, *raw = call(
         functools.partial(raw_gram_kernel, nrow, ncol, rows, raw_keys),
         [sds((rows + 8, batch), F32)] + ([sds((batch, half), BF16)] if small else []),
         raw_refs,
         scratch=[] if small else [pltpu.VMEM((batch, half), BF16)],
     )
+    gram, inverses, squares, *units = call(
+        functools.partial(unit_gram_kernel, ncol),
+        [sds((rows, batch), F32), sds((rows, 128), F32), sds((8, batch), F32)] + ([sds((batch, half), BF16)] if small else []),
+        [raw_gram, other_core(raw_gram)] + raw,
+    )
     message, vectors = call(
-        functools.partial(message_kernel, nrow, ncol, order),
-        [sds((2 * rows + 16, batch), F32), sds((8, batch), F32)],
-        [raw_gram] + [returned[k] for k in order],
+        functools.partial(sum_kernel, nrow, ncol, order),
+        [sds((rows + 8, batch), F32), sds((8, batch), F32)],
+        [returned[k] for k in order],
     )
     return call(
         functools.partial(final_kernel, nrow, ncol, None if small else raw_keys),
         sds((rows, half), F32),
-        [message, other_core(message), vectors, student, scale] + (all_raw if small else raw_refs),
-        scratch=([] if small else [pltpu.VMEM((batch, half), BF16)]) + [pltpu.VMEM((batch, half), BF16)],
+        [message, other_core(message), vectors, gram, inverses, squares, student, scale] + (units if small else raw_refs),
+        scratch=[] if small else [pltpu.VMEM((batch, half), BF16)],
     )
 
 

time: 32.6 us -> 33.1 us (1.015)
  starting transfers between devices: 15 us -> 15.4 us
    ppermute x7, waiting for transfers between devices: 7.18 us -> 7.72 us  [along_row(): return lax.ppermute(x, 'row', [(i, i ^ k) for i in range(nrow)])]
    ppermute x1 -> x2, waiting for transfers between devices: 1.57 us -> 1.07 us  [other_core(): return lax.ppermute(x, 'sub', [(0, 1), (1, 0)])]
    ppermute x7, starting transfers between devices: 9.23 us -> 9.61 us  [along_row(): return lax.ppermute(x, 'row', [(i, i ^ k) for i in range(nrow)])]
    pallas_call x11 -> x12, Pallas kernels: 2.4 us -> 2.55 us  [call(): pl.pallas_call(run, out_shape=out_shape, in_specs=[pl.BlockSpec(memory_sp...]
  transfers between devices with their start and end apart: 13 -> 14, of which waited for: 11 -> 10; matrix products, arithmetic and copies ran while one was open for 0% -> 0% of each run, Pallas kernels for 4% -> 5%
where the time goes in v17:
time: 33.1 us; the launch traced here: 32.9 us
  starting transfers between devices  15.4 us (47%)
  waiting for transfers between devices  13 us (39%)
  Pallas kernels  2.55 us (8%)
  local copies, waits for them, and re-layouts  1.8 us (5%)
    ppermute x7, starting transfers between devices, along_row(): return lax.ppermute(x, 'row', [(i, i ^ k) for i in range(nrow)])  9.61 us
    ppermute x7, waiting for transfers between devices, along_row(): return lax.ppermute(x, 'row', [(i, i ^ k) for i in range(nrow)])  7.72 us
    ppermute x5, starting transfers between devices, along_col(): return lax.ppermute(x, 'col', [(i, (i - c) % ncol) for i in range(ncol)])  5.69 us
    ppermute x5, waiting for transfers between devices, along_col(): return lax.ppermute(x, 'col', [(i, (i - c) % ncol) for i in range(ncol)])  4.24 us
    pallas_call x12, Pallas kernels, call(): pl.pallas_call(run, out_shape=out_shape, in_specs=[pl.BlockSpec(memory_sp...  2.55 us
    unnamed x10, local copies, waits for them, and re-layouts  1.8 us
    ppermute x2, waiting for transfers between devices, other_core(): return lax.ppermute(x, 'sub', [(0, 1), (1, 0)])  1.07 us
  transfers between devices with their start and end apart: 14, of which 10 were waited for; matrix products, arithmetic and copies ran while one was open for 0% of the time, Pallas kernels for 5%

profile of v17, /device:TPU:0, one launch (start us, length us, event | category | flops | bytes accessed | tf_op | source)
XLA Modules:
  0.0 32.9 jit_solution(5497451670496916795)
XLA Ops:
  0.0 0.0 copy-start
  0.0 0.9 %copy-done = bf16[64,2048]{1,0:T(8,128)(2,1)S(1)} copy-done((bf16[64,2048]{1,0:T(8,128)(2,1)S(1)}, bf16[64,2048]{1,0:T(8,128)(2,1)}, u32[]{:S(2)}) %copy-start) | copy-done | bytes 262168
  1.0 0.0 copy-start.1
  1.0 5.1 %collective-permute-start.2 = (bf16[64,512]{1,0:T(8,128)(2,1)S(1)}, bf16[64,512]{1,0:T(8,128)(2,1)S(1)}, u32[]{:S(2)}, u32[]{:S(2)}) collective-permute-start(bf16[64,512]{1,0:T(8,128)(2,1)S(1)} %get-tuple-element.25), channel_id=1, source_target_pairs={{0,12},{4,8},{8,4},{12,0},{1,13},{5,9},{9,5},{13,1},{2,14},{6,10},... | collective-permute-start | bytes 196616 | tf_op jit(solution)/shard_map/ppermute | solution.py:235
  6.1 0.0 copy-start.2
  6.1 0.8 %copy-done.2 = bf16[64,512]{1,0:T(8,128)(2,1)S(1)} copy-done((bf16[64,512]{1,0:T(8,128)(2,1)S(1)}, bf16[64,512]{1,0:T(8,128)(2,1)}, u32[]{:S(2)}) %copy-start.2) | copy-done | bytes 65560
  6.9 0.1 collective-permute-start
  7.0 0.0 copy-start.4
  7.0 0.6 %collective-permute-start.5 = (bf16[128,512]{1,0:T(8,128)(2,1)S(1)}, bf16[128,512]{1,0:T(8,128)(2,1)S(1)}, u32[]{:S(2)}, u32[]{:S(2)}) collective-permute-start(bf16[128,512]{1,0:T(8,128)(2,1)S(1)} %get-tuple-element.26), channel_id=1, source_target_pairs={{0,4},{4,0},{8,12},{12,8},{1,5},{5,1},{9,13},{13,9},{2,6},{6,2},{1... | collective-permute-start | bytes 393224 | tf_op jit(solution)/shard_map/ppermute | solution.py:235
  7.6 1.0 %collective-permute-done.2.refs_3_.refs_2_ = bf16[64,512]{1,0:T(8,128)(2,1)S(1)} collective-permute-done((bf16[64,512]{1,0:T(8,128)(2,1)S(1)}, bf16[64,512]{1,0:T(8,128)(2,1)S(1)}, u32[]{:S(2)}, u32[]{:S(2)}) %collective-permute-start.2) | collective-permute-done | bytes 65568 | tf_op jit(solution)/shard_map/ppermute | solution.py:235
  8.6 0.0 copy-done.1
  8.6 0.0 copy-done.4
  8.6 0.3 shard_map.40.refs_4_.refs_0_
  8.8 1.6 %collective-permute-start.4 = (bf16[144,512]{1,0:T(8,128)(2,1)S(1)}, bf16[144,512]{1,0:T(8,128)(2,1)S(1)}, u32[]{:S(2)}, u32[]{:S(2)}) collective-permute-start(bf16[144,512]{1,0:T(8,128)(2,1)S(1)} %shard_map.40.refs_4_.refs_0_), channel_id=1, source_target_pairs={{0,2},{2,0},{1,3},{3,1},{4,6},{6,4},{5,7},{7,5},{8,10},{10,8},{9,1... | collective-permute-start | bytes 442376 | tf_op jit(solution)/shard_map/ppermute | solution.py:238
  10.4 0.5 %collective-permute-start.3 = (bf16[64,512]{1,0:T(8,128)(2,1)S(1)}, bf16[64,512]{1,0:T(8,128)(2,1)S(1)}, u32[]{:S(2)}, u32[]{:S(2)}) collective-permute-start(bf16[64,512]{1,0:T(8,128)(2,1)S(1)} %collective-permute-done.2.refs_3_.refs_2_), channel_id=1, source_target_pairs={{0,2},{2,0},{1,3},{3,1},{4,6},{6,4},{5,7},{7,5},{8,10},{10,8},{9,1... | collective-permute-start | bytes 196616 | tf_op jit(solution)/shard_map/ppermute | solution.py:238
  10.9 3.8 %collective-permute-done.refs_0_.refs_1_ = bf16[128,512]{1,0:T(8,128)(2,1)S(1)} collective-permute-done((bf16[128,512]{1,0:T(8,128)(2,1)S(1)}, bf16[128,512]{1,0:T(8,128)(2,1)S(1)}, u32[]{:S(2)}, u32[]{:S(2)}) %collective-permute-start) | collective-permute-done | bytes 131104 | tf_op jit(solution)/shard_map/ppermute | solution.py:235
  14.8 1.4 %collective-permute-start.1 = (bf16[64,512]{1,0:T(8,128)(2,1)S(1)}, bf16[64,512]{1,0:T(8,128)(2,1)S(1)}, u32[]{:S(2)}, u32[]{:S(2)}) collective-permute-start(bf16[64,512]{1,0:T(8,128)(2,1)S(1)} %shard_map.39.refs_0_), channel_id=1, source_target_pairs={{0,2},{2,0},{1,3},{3,1},{4,6},{6,4},{5,7},{7,5},{8,10},{10,8},{9,1... | collective-permute-start | bytes 196616 | tf_op jit(solution)/shard_map/ppermute | solution.py:238
  16.2 0.0 collective-permute-done.5.refs_0_
  16.2 0.6 %collective-permute-start.6 = (bf16[64,512]{1,0:T(8,128)(2,1)S(1)}, bf16[64,512]{1,0:T(8,128)(2,1)S(1)}, u32[]{:S(2)}, u32[]{:S(2)}) collective-permute-start(bf16[64,512]{1,0:T(8,128)(2,1)S(1)} %shard_map.41.refs_6_), channel_id=1, source_target_pairs={{0,2},{2,0},{1,3},{3,1},{4,6},{6,4},{5,7},{7,5},{8,10},{10,8},{9,1... | collective-permute-start | bytes 196616 | tf_op jit(solution)/shard_map/ppermute | solution.py:238
  16.9 0.4 %collective-permute-start.11 = (bf16[64,512]{1,0:T(8,128)(2,1)S(1)}, bf16[64,512]{1,0:T(8,128)(2,1)S(1)}, u32[]{:S(2)}, u32[]{:S(2)}) collective-permute-start(bf16[64,512]{1,0:T(8,128)(2,1)S(1)} %shard_map.44), channel_id=1, source_target_pairs={{0,4},{4,0},{8,12},{12,8},{1,5},{5,1},{9,13},{13,9},{2,6},{6,2},{1... | collective-permute-start | bytes 196616 | tf_op jit(solution)/shard_map/ppermute | solution.py:235
  17.3 0.0 collective-permute-done.3.refs_3_
  17.3 2.3 %collective-permute-done.1.refs_1_ = bf16[64,512]{1,0:T(8,128)(2,1)S(1)} collective-permute-done((bf16[64,512]{1,0:T(8,128)(2,1)S(1)}, bf16[64,512]{1,0:T(8,128)(2,1)S(1)}, u32[]{:S(2)}, u32[]{:S(2)}) %collective-permute-start.1) | collective-permute-done | bytes 65568 | tf_op jit(solution)/shard_map/ppermute | solution.py:238
  19.6 1.0 %collective-permute-done.6.refs_7_ = bf16[64,512]{1,0:T(8,128)(2,1)S(1)} collective-permute-done((bf16[64,512]{1,0:T(8,128)(2,1)S(1)}, bf16[64,512]{1,0:T(8,128)(2,1)S(1)}, u32[]{:S(2)}, u32[]{:S(2)}) %collective-permute-start.6) | collective-permute-done | bytes 65568 | tf_op jit(solution)/shard_map/ppermute | solution.py:238
  20.6 0.0 collective-permute-done.4.refs_5_.refs_2_
  20.6 0.5 %shard_map.42 = (f32[64,512]{1,0:T(8,128)S(1)}, bf16[64,512]{1,0:T(8,128)(2,1)S(1)}, bf16[64,512]{1,0:T(8,128)(2,1)S(1)}, bf16[64,512]{1,0:T(8,128)(2,1)S(1)}) custom-call(bf16[64,512]{1,0:T(8,128)(2,1)S(1)} %shard_map.39.refs_0_, bf16[64,512]{1,0:T(8,128)(2,1)S(1)} %collective-permute-done.1.refs_1_, ...), custom_call_target="tpu_custom_call" | custom-call | tf_op jit(solution)/shard_map/pallas_call | solution.py:22
  21.1 0.1 collective-permute-done.11.refs_2_
  21.2 1.5 %collective-permute-start.12 = (bf16[192,512]{1,0:T(8,128)(2,1)S(1)}, bf16[192,512]{1,0:T(8,128)(2,1)S(1)}, u32[]{:S(2)}, u32[]{:S(2)}) collective-permute-start(bf16[192,512]{1,0:T(8,128)(2,1)S(1)} %shard_map.45.refs_1_), channel_id=1, source_target_pairs={{0,2},{2,0},{1,3},{3,1},{4,6},{6,4},{5,7},{7,5},{8,10},{10,8},{9,1... | collective-permute-start | bytes 589832 | tf_op jit(solution)/shard_map/ppermute | solution.py:238
  22.7 1.3 %collective-permute-start.7 = (bf16[64,512]{1,0:T(8,128)(2,1)S(1)}, bf16[64,512]{1,0:T(8,128)(2,1)S(1)}, u32[]{:S(2)}, u32[]{:S(2)}) collective-permute-start(bf16[64,512]{1,0:T(8,128)(2,1)S(1)} %get-tuple-element.27), channel_id=1, source_target_pairs={{0,8},{4,12},{8,0},{12,4},{1,9},{5,13},{9,1},{13,5},{2,10},{6,14},... | collective-permute-start | bytes 196616 | tf_op jit(solution)/shard_map/ppermute | solution.py:235
  23.9 1.5 %collective-permute-start.8 = (bf16[64,512]{1,0:T(8,128)(2,1)S(1)}, bf16[64,512]{1,0:T(8,128)(2,1)S(1)}, u32[]{:S(2)}, u32[]{:S(2)}) collective-permute-start(bf16[64,512]{1,0:T(8,128)(2,1)S(1)} %get-tuple-element.28), channel_id=1, source_target_pairs={{0,12},{4,8},{8,4},{12,0},{1,13},{5,9},{9,5},{13,1},{2,14},{6,10},... | collective-permute-start | bytes 196616 | tf_op jit(solution)/shard_map/ppermute | solution.py:235
  25.4 0.8 %collective-permute-start.9 = (bf16[64,512]{1,0:T(8,128)(2,1)S(1)}, bf16[64,512]{1,0:T(8,128)(2,1)S(1)}, u32[]{:S(2)}, u32[]{:S(2)}) collective-permute-start(bf16[64,512]{1,0:T(8,128)(2,1)S(1)} %get-tuple-element.30), channel_id=1, source_target_pairs={{0,4},{4,0},{8,12},{12,8},{1,5},{5,1},{9,13},{13,9},{2,6},{6,2},{1... | collective-permute-start | bytes 196616 | tf_op jit(solution)/shard_map/ppermute | solution.py:235
  26.2 0.9 %collective-permute-done.12.refs_3_ = bf16[192,512]{1,0:T(8,128)(2,1)S(1)} collective-permute-done((bf16[192,512]{1,0:T(8,128)(2,1)S(1)}, bf16[192,512]{1,0:T(8,128)(2,1)S(1)}, u32[]{:S(2)}, u32[]{:S(2)}) %collective-permute-start.12) | collective-permute-done | bytes 196640 | tf_op jit(solution)/shard_map/ppermute | solution.py:238
  27.1 0.3 shard_map.46
  27.4 0.1 collective-permute-start.13
  27.5 1.1 %collective-permute-done.7.refs_0_ = bf16[64,512]{1,0:T(8,128)(2,1)S(1)} collective-permute-done((bf16[64,512]{1,0:T(8,128)(2,1)S(1)}, bf16[64,512]{1,0:T(8,128)(2,1)S(1)}, u32[]{:S(2)}, u32[]{:S(2)}) %collective-permute-start.7) | collective-permute-done | bytes 65568 | tf_op jit(solution)/shard_map/ppermute | solution.py:235
  28.6 1.5 %collective-permute-done.8.refs_1_ = bf16[64,512]{1,0:T(8,128)(2,1)S(1)} collective-permute-done((bf16[64,512]{1,0:T(8,128)(2,1)S(1)}, bf16[64,512]{1,0:T(8,128)(2,1)S(1)}, u32[]{:S(2)}, u32[]{:S(2)}) %collective-permute-start.8) | collective-permute-done | bytes 65568 | tf_op jit(solution)/shard_map/ppermute | solution.py:235
  30.2 0.2 collective-permute-done.9.refs_3_
  30.4 0.1 shard_map.43
  30.5 0.1 collective-permute-start.10
  30.6 0.0 collective-permute-done.13.refs_1_
  30.6 0.0 copy-start.3
  30.6 0.3 shard_map.47
  30.9 1.1 %collective-permute-done.10.refs_1_ = f32[72,512]{1,0:T(8,128)S(1)} collective-permute-done((f32[72,512]{1,0:T(8,128)S(1)}, f32[72,512]{1,0:T(8,128)S(1)}, u32[]{:S(2)}, u32[]{:S(2)}) %collective-permute-start.10) | collective-permute-done | bytes 147488 | tf_op jit(solution)/shard_map/ppermute | solution.py:241
  31.9 0.0 copy-done.3
  31.9 1.0 %shard_map.48 = f32[64,512]{1,0:T(8,128)} custom-call(f32[72,512]{1,0:T(8,128)S(1)} %get-tuple-element.31.refs_0_, f32[72,512]{1,0:T(8,128)S(1)} %collective-permute-done.10.refs_1_, f32[8,512]{1,0:T(8,128)S(1)} %get-tuple-element.32.refs_2_, f32[64,512]{1,0:T(8,128)S(1)} %get-tuple-element.35.refs_3_, f32[64,128]{1,0:T(8,128)S(1)} %get-tuple-element.36.refs_4_, ...), custom_call_target="tpu_custom_call" | custom-call | tf_op jit(solution)/shard_map/pallas_call | solution.py:22
  (6 shorter events, 0.1 us)
Async XLA Ops:
  0.0 0.9 %copy-start = (bf16[64,2048]{1,0:T(8,128)(2,1)S(1)}, bf16[64,2048]{1,0:T(8,128)(2,1)}, u32[]{:S(2)}) copy-start(bf16[64,2048]{1,0:T(8,128)(2,1)} %refs_0_.5) | copy-start | bytes 786436
  1.0 7.6 %copy-start.1 = (bf16[64,2048]{1,0:T(8,128)(2,1)S(1)}, bf16[64,2048]{1,0:T(8,128)(2,1)}, u32[]{:S(2)}) copy-start(bf16[64,2048]{1,0:T(8,128)(2,1)} %refs_0_.5) | copy-start | bytes 786436
  1.0 7.6 %collective-permute-start.2 = (bf16[64,512]{1,0:T(8,128)(2,1)S(1)}, bf16[64,512]{1,0:T(8,128)(2,1)S(1)}, u32[]{:S(2)}, u32[]{:S(2)}) collective-permute-start(bf16[64,512]{1,0:T(8,128)(2,1)S(1)} %get-tuple-element.25), channel_id=1, source_target_pairs={{0,12},{4,8},{8,4},{12,0},{1,13},{5,9},{9,5},{13,1},{2,14},{6,10},... | collective-permute-start | bytes 196616 | tf_op jit(solution)/shard_map/ppermute | solution.py:235
  6.1 0.8 %copy-start.2 = (bf16[64,512]{1,0:T(8,128)(2,1)S(1)}, bf16[64,512]{1,0:T(8,128)(2,1)}, u32[]{:S(2)}) copy-start(bf16[64,512]{1,0:T(8,128)(2,1)} %refs_6_.1) | copy-start | bytes 196612
  6.9 7.8 %collective-permute-start = (bf16[128,512]{1,0:T(8,128)(2,1)S(1)}, bf16[128,512]{1,0:T(8,128)(2,1)S(1)}, u32[]{:S(2)}, u32[]{:S(2)}) collective-permute-start(bf16[128,512]{1,0:T(8,128)(2,1)S(1)} %get-tuple-element.24), channel_id=1, source_target_pairs={{0,8},{4,12},{8,0},{12,4},{1,9},{5,13},{9,1},{13,5},{2,10},{6,14},... | collective-permute-start | bytes 393224 | tf_op jit(solution)/shard_map/ppermute | solution.py:235
  7.0 1.5 %copy-start.4 = (bf16[64]{0:T(256)(128)(2,1)S(1)}, bf16[64]{0:T(256)(128)(2,1)}, u32[]{:S(2)}) copy-start(bf16[64]{0:T(256)(128)(2,1)} %param.5) | copy-start | bytes 388
  7.0 9.2 %collective-permute-start.5 = (bf16[128,512]{1,0:T(8,128)(2,1)S(1)}, bf16[128,512]{1,0:T(8,128)(2,1)S(1)}, u32[]{:S(2)}, u32[]{:S(2)}) collective-permute-start(bf16[128,512]{1,0:T(8,128)(2,1)S(1)} %get-tuple-element.26), channel_id=1, source_target_pairs={{0,4},{4,0},{8,12},{12,8},{1,5},{5,1},{9,13},{13,9},{2,6},{6,2},{1... | collective-permute-start | bytes 393224 | tf_op jit(solution)/shard_map/ppermute | solution.py:235
  8.8 11.7 %collective-permute-start.4 = (bf16[144,512]{1,0:T(8,128)(2,1)S(1)}, bf16[144,512]{1,0:T(8,128)(2,1)S(1)}, u32[]{:S(2)}, u32[]{:S(2)}) collective-permute-start(bf16[144,512]{1,0:T(8,128)(2,1)S(1)} %shard_map.40.refs_4_.refs_0_), channel_id=1, source_target_pairs={{0,2},{2,0},{1,3},{3,1},{4,6},{6,4},{5,7},{7,5},{8,10},{10,8},{9,1... | collective-permute-start | bytes 442376 | tf_op jit(solution)/shard_map/ppermute | solution.py:238
  10.4 6.8 %collective-permute-start.3 = (bf16[64,512]{1,0:T(8,128)(2,1)S(1)}, bf16[64,512]{1,0:T(8,128)(2,1)S(1)}, u32[]{:S(2)}, u32[]{:S(2)}) collective-permute-start(bf16[64,512]{1,0:T(8,128)(2,1)S(1)} %collective-permute-done.2.refs_3_.refs_2_), channel_id=1, source_target_pairs={{0,2},{2,0},{1,3},{3,1},{4,6},{6,4},{5,7},{7,5},{8,10},{10,8},{9,1... | collective-permute-start | bytes 196616 | tf_op jit(solution)/shard_map/ppermute | solution.py:238
  14.8 4.8 %collective-permute-start.1 = (bf16[64,512]{1,0:T(8,128)(2,1)S(1)}, bf16[64,512]{1,0:T(8,128)(2,1)S(1)}, u32[]{:S(2)}, u32[]{:S(2)}) collective-permute-start(bf16[64,512]{1,0:T(8,128)(2,1)S(1)} %shard_map.39.refs_0_), channel_id=1, source_target_pairs={{0,2},{2,0},{1,3},{3,1},{4,6},{6,4},{5,7},{7,5},{8,10},{10,8},{9,1... | collective-permute-start | bytes 196616 | tf_op jit(solution)/shard_map/ppermute | solution.py:238
  16.2 4.3 %collective-permute-start.6 = (bf16[64,512]{1,0:T(8,128)(2,1)S(1)}, bf16[64,512]{1,0:T(8,128)(2,1)S(1)}, u32[]{:S(2)}, u32[]{:S(2)}) collective-permute-start(bf16[64,512]{1,0:T(8,128)(2,1)S(1)} %shard_map.41.refs_6_), channel_id=1, source_target_pairs={{0,2},{2,0},{1,3},{3,1},{4,6},{6,4},{5,7},{7,5},{8,10},{10,8},{9,1... | collective-permute-start | bytes 196616 | tf_op jit(solution)/shard_map/ppermute | solution.py:238
  16.9 4.3 %collective-permute-start.11 = (bf16[64,512]{1,0:T(8,128)(2,1)S(1)}, bf16[64,512]{1,0:T(8,128)(2,1)S(1)}, u32[]{:S(2)}, u32[]{:S(2)}) collective-permute-start(bf16[64,512]{1,0:T(8,128)(2,1)S(1)} %shard_map.44), channel_id=1, source_target_pairs={{0,4},{4,0},{8,12},{12,8},{1,5},{5,1},{9,13},{13,9},{2,6},{6,2},{1... | collective-permute-start | bytes 196616 | tf_op jit(solution)/shard_map/ppermute | solution.py:235
  21.2 5.9 %collective-permute-start.12 = (bf16[192,512]{1,0:T(8,128)(2,1)S(1)}, bf16[192,512]{1,0:T(8,128)(2,1)S(1)}, u32[]{:S(2)}, u32[]{:S(2)}) collective-permute-start(bf16[192,512]{1,0:T(8,128)(2,1)S(1)} %shard_map.45.refs_1_), channel_id=1, source_target_pairs={{0,2},{2,0},{1,3},{3,1},{4,6},{6,4},{5,7},{7,5},{8,10},{10,8},{9,1... | collective-permute-start | bytes 589832 | tf_op jit(solution)/shard_map/ppermute | solution.py:238
  22.7 6.0 %collective-permute-start.7 = (bf16[64,512]{1,0:T(8,128)(2,1)S(1)}, bf16[64,512]{1,0:T(8,128)(2,1)S(1)}, u32[]{:S(2)}, u32[]{:S(2)}) collective-permute-start(bf16[64,512]{1,0:T(8,128)(2,1)S(1)} %get-tuple-element.27), channel_id=1, source_target_pairs={{0,8},{4,12},{8,0},{12,4},{1,9},{5,13},{9,1},{13,5},{2,10},{6,14},... | collective-permute-start | bytes 196616 | tf_op jit(solution)/shard_map/ppermute | solution.py:235
  23.9 6.2 %collective-permute-start.8 = (bf16[64,512]{1,0:T(8,128)(2,1)S(1)}, bf16[64,512]{1,0:T(8,128)(2,1)S(1)}, u32[]{:S(2)}, u32[]{:S(2)}) collective-permute-start(bf16[64,512]{1,0:T(8,128)(2,1)S(1)} %get-tuple-element.28), channel_id=1, source_target_pairs={{0,12},{4,8},{8,4},{12,0},{1,13},{5,9},{9,5},{13,1},{2,14},{6,10},... | collective-permute-start | bytes 196616 | tf_op jit(solution)/shard_map/ppermute | solution.py:235
  25.4 5.0 %collective-permute-start.9 = (bf16[64,512]{1,0:T(8,128)(2,1)S(1)}, bf16[64,512]{1,0:T(8,128)(2,1)S(1)}, u32[]{:S(2)}, u32[]{:S(2)}) collective-permute-start(bf16[64,512]{1,0:T(8,128)(2,1)S(1)} %get-tuple-element.30), channel_id=1, source_target_pairs={{0,4},{4,0},{8,12},{12,8},{1,5},{5,1},{9,13},{13,9},{2,6},{6,2},{1... | collective-permute-start | bytes 196616 | tf_op jit(solution)/shard_map/ppermute | solution.py:235
  27.4 3.1 %collective-permute-start.13 = (f32[72,512]{1,0:T(8,128)S(1)}, f32[72,512]{1,0:T(8,128)S(1)}, u32[]{:S(2)}, u32[]{:S(2)}) collective-permute-start(f32[72,512]{1,0:T(8,128)S(1)} %get-tuple-element.33.refs_0_), channel_id=1, source_target_pairs={{0,1},{1,0},{2,3},{3,2},{4,5},{5,4},{6,7},{7,6},{8,9},{9,8},{10,11... | collective-permute-start | bytes 442376 | tf_op jit(solution)/shard_map/ppermute | solution.py:241
  30.5 1.4 %collective-permute-start.10 = (f32[72,512]{1,0:T(8,128)S(1)}, f32[72,512]{1,0:T(8,128)S(1)}, u32[]{:S(2)}, u32[]{:S(2)}) collective-permute-start(f32[72,512]{1,0:T(8,128)S(1)} %get-tuple-element.31.refs_0_), channel_id=1, source_target_pairs={{0,1},{1,0},{2,3},{3,2},{4,5},{5,4},{6,7},{7,6},{8,9},{9,8},{10,11... | collective-permute-start | bytes 442376 | tf_op jit(solution)/shard_map/ppermute | solution.py:241
  30.6 1.4 %copy-start.3 = (bf16[64,512]{1,0:T(8,128)(2,1)S(1)}, bf16[64,512]{1,0:T(8,128)(2,1)}, u32[]{:S(2)}) copy-start(bf16[64,512]{1,0:T(8,128)(2,1)} %refs_6_.1) | copy-start | bytes 196612

commit v18 on v17

--- a/solution.py
+++ b/solution.py
@@ -116,36 +116,71 @@
     return pl.ds(pl.multiple_of(at, 2 * rows), ncol * rows)
 
 
+def note_of(scales, mass):
+    shape = (32, scales.shape[1])
+    at = lax.broadcasted_iota(jnp.int32, shape, 0)
+    high = mass.astype(BF16).astype(F32)
+    return jnp.where(at < 16, scales, jnp.where(at < 24, high, mass - high))
+
+
+def read_note(note):
+    note = note.astype(F32)
+    return note[0:1, :], note[16:17, :1] + note[24:25, :1]
+
+
 def gram_kernel(nrow, ncol, rows, order, *refs):
     count = nrow * ncol
-    outs, held, left = refs[count : count + nrow], refs[-2], refs[-1]
+    kept, given, held, left = refs[count:]
     own = order.index(0) * ncol
     for n, k in enumerate(order):
         for c in range(ncol):
             put(held, place(nrow, ncol, rows, k, c), rows, refs[n * ncol + c], 0 if k else rows + TAIL)
+    sub, batch = rows // 2, held.shape[0]
+    total = nrow * sub
+    core = lax.axis_index("sub")
     for n, k in enumerate(order):
-        left[n * rows : (n + 1) * rows, :] = held[pl.ds(place(nrow, ncol, rows, k, 0), rows), :]
-    sub = rows // 2
-    at = lax.broadcasted_iota(jnp.int32, (sub, 2 * rows), 0)
-    lane = lax.broadcasted_iota(jnp.int32, (sub, 2 * rows), 1)
-    note, mass = jnp.zeros((sub, 2 * rows), F32), jnp.zeros((1, 1), F32)
-    for c in range(ncol):
-        scales, part = read_tags(refs[own + c][rows : rows + TAIL, : 2 * rows])
-        turned = jnp.concatenate([scales[:, sub:], scales[:, :sub]], axis=1)
-        note = jnp.where(at == 2 * c, scales, jnp.where(at == 2 * c + 1, turned, note))
-        mass = mass + part
-    high = mass.astype(BF16).astype(F32)
-    note = jnp.where(at < sub // 2, note, jnp.where(at < sub * 3 // 4, high, mass - high))
-    per = max(1, 2048 * rows * nrow // held.shape[0] // rows // 8)
-    for first in range(0, nrow, per):
-        last = min(first + per, nrow)
-        gram = lax.dot_general(left[first * rows : last * rows, :], held[...], INNER, preferred_element_type=F32)
-        for n in range(first, last):
-            out = outs[order[n]]
-            out[...] = gram[(n - first) * rows : (n - first + 1) * rows, :].astype(out.dtype)
-            spot = pl.ds(pl.multiple_of(place(nrow, ncol, rows, order[n], 0), 2 * rows), 2 * rows)
-            seen = out[sub:, spot].astype(F32)
-            out[sub:, spot] = jnp.where(lane < sub, note, seen).astype(out.dtype)
+        for first, which in ((0, 1 - core), (total, core)):
+            at = pl.multiple_of(place(nrow, ncol, rows, k, 0) + which * sub, sub)
+            left[first + n * sub : first + (n + 1) * sub, :] = held[pl.ds(at, sub), :]
+    lane = lax.broadcasted_iota(jnp.int32, (1, 2 * rows), 1)
+    line, mass = [], jnp.zeros((1, 1), F32)
+    for c in range(0, ncol, 2):
+        pair = [read_tags(refs[own + d][rows : rows + TAIL, : 2 * rows]) for d in (c, c + 1)]
+        line.append(jnp.where(lane < rows, pair[0][0], pair[1][0]))
+        mass = mass + pair[0][1] + pair[1][1]
+    note = note_of(jnp.concatenate(line, axis=1) if len(line) > 1 else line[0], mass)
+    given[:, :batch] = lax.dot_general(left[:total, :], held[...], INNER, preferred_element_type=F32).astype(BF16)
+    given[:sub, batch:] = note.astype(BF16)
+    given[sub:, batch:] = jnp.zeros((total - sub, ncol * rows), BF16)
+    kept[:, :batch] = lax.dot_general(left[total:, :], held[...], INNER, preferred_element_type=F32).astype(kept.dtype)
+    kept[:sub, batch:] = note.astype(kept.dtype)
+
+
+def fold_kernel(order, batch, kept, came, *outs):
+    sub = outs[0].shape[0]
+    (scales, mass), (_, more) = read_note(kept[:sub, batch:]), read_note(came[:sub, batch:])
+    note = note_of(scales, mass + more)
+    for n, k in enumerate(order):
+        at = slice(n * sub, (n + 1) * sub)
+        outs[k][:, :batch] = (kept[at, :batch].astype(F32) + came[at, :batch].astype(F32)).astype(outs[k].dtype)
+        outs[k][:, batch:] = note.astype(outs[k].dtype)
+
+
+def teach_kernel(nrow, ncol, rows, *refs):
+    parts, (scale, out, vectors) = refs[:nrow], refs[nrow:]
+    sub, batch = out.shape
+    total, mass = parts[0][:, :batch].astype(F32), jnp.zeros((1, 1), F32)
+    for k, part in enumerate(parts):
+        scales, more = read_note(part[:, batch:])
+        mass = mass + more
+        vectors[:, group(ncol, rows, k)] = jnp.broadcast_to(scales, (8, ncol * rows))
+        if k:
+            total = total + part[:, :batch].astype(F32)
+    shape = (sub, rows)
+    first = lax.axis_index("sub") * sub
+    eye = lax.broadcasted_iota(jnp.int32, shape, 0) + first == lax.broadcasted_iota(jnp.int32, shape, 1)
+    s = jnp.sum(jnp.where(eye, scale[...].astype(F32), 0.0), axis=1, keepdims=True)
+    out[...] = (s / (mass / batch)) * vectors[:1, :] * total
 
 
 def assemble(nrow, ncol, rows, keys, refs, held):
@@ -164,26 +199,6 @@
     for at in range(0, raw.shape[0], 128):
         squares = jnp.sum(jnp.square(raw[at : at + 128, :].astype(F32)), axis=1, keepdims=True)
         out[rows:, at : at + 128] = jnp.broadcast_to(lane_row(squares), (8, 128))
-
-
-def sum_kernel(nrow, ncol, order, *refs):
-    parts, (out, vectors) = [refs[order.index(k)] for k in range(nrow)], refs[-2:]
-    rows = parts[0].shape[0]
-    sub = rows // 2
-    total = parts[0][...].astype(F32)
-    for r in parts[1:]:
-        total = total + r[...].astype(F32)
-    out[:rows, :] = total
-    own = group(ncol, rows, 0)
-    mirror = jnp.transpose(out[:sub, own])[sub : 2 * sub, :]
-    out[sub:rows, own] = jnp.concatenate([mirror, out[sub:rows, own][:, sub:]], axis=1)
-    mass = jnp.zeros((1, 1), F32)
-    for k, part in enumerate(parts):
-        note = part[sub:, own].astype(F32)[:, :sub]
-        mass = mass + note[sub // 2 : sub // 2 + 1, :1] + note[sub * 3 // 4 : sub * 3 // 4 + 1, :1]
-        line = jnp.concatenate([note[n : n + 1, :] for n in range(2 * ncol)], axis=1)
-        vectors[:, group(ncol, rows, k)] = jnp.broadcast_to(line, (8, ncol * rows))
-    out[rows:, :] = jnp.broadcast_to(mass, (8, out.shape[1]))
 
 
 def normalize(raw, squares, units):
@@ -204,18 +219,20 @@
         normalize(refs[0], squares, refs[4])
 
 
-def final_kernel(nrow, ncol, keys, mine, other, vectors, gram, inverses, squares, stud, scale, *refs):
+def final_kernel(nrow, ncol, keys, mine, other, gram, inverses, squares, stud, *refs):
     rows = stud.shape[0]
     if keys:
-        out, units = refs[-2:]
-        assemble(nrow, ncol, rows, keys, refs[:-2], units)
+        out, teach, units = refs[-3:]
+        assemble(nrow, ncol, rows, keys, refs[:-3], units)
         normalize(units, squares, units)
     else:
-        units, out = refs
+        units, out, teach = refs
+    sub = rows // 2
+    core = lax.axis_index("sub")
+    teach[pl.ds(pl.multiple_of(core * sub, sub), sub), :] = mine[...]
+    teach[pl.ds(pl.multiple_of((1 - core) * sub, sub), sub), :] = other[...]
+    error_b = (gram[...] - teach[...]).astype(BF16)
     inverse = inverses[:, :1]
-    mass = (mine[rows : rows + 1, :1] + other[rows : rows + 1, :1]) / mine.shape[1]
-    outer = (column(scale[...].astype(F32)) / mass) * vectors[:1, :]
-    error_b = (gram[...] - outer * (mine[:rows, :] + other[:rows, :])).astype(BF16)
     grads = 4.0 * jnp.dot(error_b, units[...], preferred_element_type=F32)
     along = 4.0 * jnp.sum(error_b.astype(F32) * gram[...], axis=1, keepdims=True)
     unit = stud[...].astype(F32) * inverse
@@ -266,11 +283,17 @@
         if k in riders:
             piece = call(functools.partial(take_kernel, rows), sds((rows, part), BF16), [piece])
         columns[k] = with_columns(piece)
-    partial = call(
+    extra = batch + ncol * rows
+    kept, given = call(
         functools.partial(gram_kernel, nrow, ncol, rows, order),
-        [sds((rows, batch), BF16 if k else F32) for k in range(nrow)],
+        [sds((nrow * rows // 2, extra), F32 if small else BF16), sds((nrow * rows // 2, extra), BF16)],
         [columns[k][c] for k in order for c in range(ncol)],
         scratch=[pltpu.VMEM((batch, part), BF16), pltpu.VMEM((nrow * rows, part), BF16)],
+    )
+    partial = call(
+        functools.partial(fold_kernel, order, batch),
+        [sds((rows // 2, extra), BF16 if k else F32) for k in range(nrow)],
+        [kept, other_core(given)],
     )
     returned = {k: along_row(partial[k], k) if k else partial[0] for k in order}
 
@@ -283,7 +306,7 @@
         got_keys += [n ^ k for n in keys[first:]]
         stack, spans, keys = stack + got[-1:], spans + [(0, len(keys) * rows)], keys + [n ^ k for n in keys]
         k //= 2
-    rest = pack([near, far] + got, [(0, rows)] * 2 + [(0, g.shape[0]) for g in got], after=[partial[0]])
+    rest = pack([near, far] + got, [(0, rows)] * 2 + [(0, g.shape[0]) for g in got], after=[kept])
     raw_keys = [[0], [1, middle] + got_keys]
     sources = [columns[0], with_columns(rest)]
     raw_refs = [x[c] for c in range(ncol) for x in sources]
@@ -291,6 +314,7 @@
         functools.partial(raw_gram_kernel, nrow, ncol, rows, raw_keys),
         [sds((rows + 8, batch), F32)] + ([sds((batch, half), BF16)] if small else []),
         raw_refs,
+        after=[returned[k] for k in order if k],
         scratch=[] if small else [pltpu.VMEM((batch, half), BF16)],
     )
     gram, inverses, squares, *units = call(
@@ -298,16 +322,17 @@
         [sds((rows, batch), F32), sds((rows, 128), F32), sds((8, batch), F32)] + ([sds((batch, half), BF16)] if small else []),
         [raw_gram, other_core(raw_gram)] + raw,
     )
-    message, vectors = call(
-        functools.partial(sum_kernel, nrow, ncol, order),
-        [sds((rows + 8, batch), F32), sds((8, batch), F32)],
-        [returned[k] for k in order],
+    taught = call(
+        functools.partial(teach_kernel, nrow, ncol, rows),
+        sds((rows // 2, batch), F32),
+        [returned[k] for k in range(nrow)] + [scale],
+        scratch=[pltpu.VMEM((8, batch), F32)],
     )
     return call(
         functools.partial(final_kernel, nrow, ncol, None if small else raw_keys),
         sds((rows, half), F32),
-        [message, other_core(message), vectors, gram, inverses, squares, student, scale] + (units if small else raw_refs),
-        scratch=[] if small else [pltpu.VMEM((batch, half), BF16)],
+        [taught, other_core(taught), gram, inverses, squares, student] + (units if small else raw_refs),
+        scratch=[pltpu.VMEM((rows, batch), F32)] + ([] if small else [pltpu.VMEM((batch, half), BF16)]),
     )
 
 

time: 33.1 us -> 35.6 us (1.076)
  starting transfers between devices: 15.4 us -> 16.9 us
  local copies, waits for them, and re-layouts: 1.8 us -> 2.36 us
  waiting for transfers between devices: 13 us -> 13.4 us
    ppermute x7, starting transfers between devices: 9.61 us -> 10.6 us  [along_row(): return lax.ppermute(x, 'row', [(i, i ^ k) for i in range(nrow)])]
    unnamed x10, local copies, waits for them, and re-layouts: 1.8 us -> 2.36 us
    ppermute x2 -> x3, starting transfers between devices: 0.14 us -> 0.7 us  [other_core(): return lax.ppermute(x, 'sub', [(0, 1), (1, 0)])]
    ppermute x2 -> x3, waiting for transfers between devices: 1.07 us -> 0.64 us  [other_core(): return lax.ppermute(x, 'sub', [(0, 1), (1, 0)])]
    ppermute x5, waiting for transfers between devices: 4.24 us -> 4.67 us  [along_col(): return lax.ppermute(x, 'col', [(i, (i - c) % ncol) for i in range(ncol)])]
    ppermute x7, waiting for transfers between devices: 7.72 us -> 8.13 us  [along_row(): return lax.ppermute(x, 'row', [(i, i ^ k) for i in range(nrow)])]
    pallas_call x12 -> x13, Pallas kernels: 2.55 us -> 2.53 us  [call(): pl.pallas_call(run, out_shape=out_shape, in_specs=[pl.BlockSpec(memory_sp...]
  transfers between devices with their start and end apart: 14 -> 15, of which waited for: 10 -> 8; matrix products, arithmetic and copies ran while one was open for 0% -> 0% of each run, Pallas kernels for 5% -> 4%
where the time goes in v18:
time: 35.6 us; the launch traced here: 35.4 us
  starting transfers between devices  16.9 us (47%)
  waiting for transfers between devices  13.4 us (38%)
  Pallas kernels  2.53 us (7%)
  local copies, waits for them, and re-layouts  2.36 us (7%)
    ppermute x7, starting transfers between devices, along_row(): return lax.ppermute(x, 'row', [(i, i ^ k) for i in range(nrow)])  10.6 us
    ppermute x7, waiting for transfers between devices, along_row(): return lax.ppermute(x, 'row', [(i, i ^ k) for i in range(nrow)])  8.13 us
    ppermute x5, starting transfers between devices, along_col(): return lax.ppermute(x, 'col', [(i, (i - c) % ncol) for i in range(ncol)])  5.65 us
    ppermute x5, waiting for transfers between devices, along_col(): return lax.ppermute(x, 'col', [(i, (i - c) % ncol) for i in range(ncol)])  4.67 us
    pallas_call x13, Pallas kernels, call(): pl.pallas_call(run, out_shape=out_shape, in_specs=[pl.BlockSpec(memory_sp...  2.53 us
    unnamed x10, local copies, waits for them, and re-layouts  2.36 us
  transfers between devices with their start and end apart: 15, of which 8 were waited for; matrix products, arithmetic and copies ran while one was open for 0% of the time, Pallas kernels for 4%

profile of v18, /device:TPU:0, one launch (start us, length us, event | category | flops | bytes accessed | tf_op | source)
XLA Modules:
  0.0 35.4 jit_solution(8567479051317090077)
XLA Ops:
  0.0 0.0 copy-start
  0.0 0.9 %copy-done = bf16[64,2048]{1,0:T(8,128)(2,1)S(1)} copy-done((bf16[64,2048]{1,0:T(8,128)(2,1)S(1)}, bf16[64,2048]{1,0:T(8,128)(2,1)}, u32[]{:S(2)}) %copy-start) | copy-done | bytes 262168
  1.0 0.0 copy-start.1
  1.0 5.1 %collective-permute-start.2 = (bf16[64,512]{1,0:T(8,128)(2,1)S(1)}, bf16[64,512]{1,0:T(8,128)(2,1)S(1)}, u32[]{:S(2)}, u32[]{:S(2)}) collective-permute-start(bf16[64,512]{1,0:T(8,128)(2,1)S(1)} %get-tuple-element.25), channel_id=1, source_target_pairs={{0,12},{4,8},{8,4},{12,0},{1,13},{5,9},{9,5},{13,1},{2,14},{6,10},... | collective-permute-start | bytes 196616 | tf_op jit(solution)/shard_map/ppermute | solution.py:252
  6.1 0.0 copy-start.2
  6.1 0.8 %copy-done.2 = bf16[64,512]{1,0:T(8,128)(2,1)S(1)} copy-done((bf16[64,512]{1,0:T(8,128)(2,1)S(1)}, bf16[64,512]{1,0:T(8,128)(2,1)}, u32[]{:S(2)}) %copy-start.2) | copy-done | bytes 65560
  6.9 0.1 collective-permute-start
  7.0 0.0 copy-start.4
  7.0 0.6 %collective-permute-start.5 = (bf16[128,512]{1,0:T(8,128)(2,1)S(1)}, bf16[128,512]{1,0:T(8,128)(2,1)S(1)}, u32[]{:S(2)}, u32[]{:S(2)}) collective-permute-start(bf16[128,512]{1,0:T(8,128)(2,1)S(1)} %get-tuple-element.26), channel_id=1, source_target_pairs={{0,4},{4,0},{8,12},{12,8},{1,5},{5,1},{9,13},{13,9},{2,6},{6,2},{1... | collective-permute-start | bytes 393224 | tf_op jit(solution)/shard_map/ppermute | solution.py:252
  7.6 1.0 %collective-permute-done.2.refs_3_.refs_2_ = bf16[64,512]{1,0:T(8,128)(2,1)S(1)} collective-permute-done((bf16[64,512]{1,0:T(8,128)(2,1)S(1)}, bf16[64,512]{1,0:T(8,128)(2,1)S(1)}, u32[]{:S(2)}, u32[]{:S(2)}) %collective-permute-start.2) | collective-permute-done | bytes 65568 | tf_op jit(solution)/shard_map/ppermute | solution.py:252
  8.6 0.0 copy-done.1
  8.6 0.0 copy-done.4
  8.6 0.3 shard_map.40.refs_4_.refs_0_
  8.8 1.6 %collective-permute-start.4 = (bf16[144,512]{1,0:T(8,128)(2,1)S(1)}, bf16[144,512]{1,0:T(8,128)(2,1)S(1)}, u32[]{:S(2)}, u32[]{:S(2)}) collective-permute-start(bf16[144,512]{1,0:T(8,128)(2,1)S(1)} %shard_map.40.refs_4_.refs_0_), channel_id=1, source_target_pairs={{0,2},{2,0},{1,3},{3,1},{4,6},{6,4},{5,7},{7,5},{8,10},{10,8},{9,1... | collective-permute-start | bytes 442376 | tf_op jit(solution)/shard_map/ppermute | solution.py:255
  10.4 0.5 %collective-permute-start.3 = (bf16[64,512]{1,0:T(8,128)(2,1)S(1)}, bf16[64,512]{1,0:T(8,128)(2,1)S(1)}, u32[]{:S(2)}, u32[]{:S(2)}) collective-permute-start(bf16[64,512]{1,0:T(8,128)(2,1)S(1)} %collective-permute-done.2.refs_3_.refs_2_), channel_id=1, source_target_pairs={{0,2},{2,0},{1,3},{3,1},{4,6},{6,4},{5,7},{7,5},{8,10},{10,8},{9,1... | collective-permute-start | bytes 196616 | tf_op jit(solution)/shard_map/ppermute | solution.py:255
  10.9 3.8 %collective-permute-done.refs_0_.refs_1_ = bf16[128,512]{1,0:T(8,128)(2,1)S(1)} collective-permute-done((bf16[128,512]{1,0:T(8,128)(2,1)S(1)}, bf16[128,512]{1,0:T(8,128)(2,1)S(1)}, u32[]{:S(2)}, u32[]{:S(2)}) %collective-permute-start) | collective-permute-done | bytes 131104 | tf_op jit(solution)/shard_map/ppermute | solution.py:252
  14.8 1.4 %collective-permute-start.1 = (bf16[64,512]{1,0:T(8,128)(2,1)S(1)}, bf16[64,512]{1,0:T(8,128)(2,1)S(1)}, u32[]{:S(2)}, u32[]{:S(2)}) collective-permute-start(bf16[64,512]{1,0:T(8,128)(2,1)S(1)} %shard_map.39.refs_0_), channel_id=1, source_target_pairs={{0,2},{2,0},{1,3},{3,1},{4,6},{6,4},{5,7},{7,5},{8,10},{10,8},{9,1... | collective-permute-start | bytes 196616 | tf_op jit(solution)/shard_map/ppermute | solution.py:255
  16.2 0.0 collective-permute-done.5.refs_0_
  16.2 0.6 %collective-permute-start.6 = (bf16[64,512]{1,0:T(8,128)(2,1)S(1)}, bf16[64,512]{1,0:T(8,128)(2,1)S(1)}, u32[]{:S(2)}, u32[]{:S(2)}) collective-permute-start(bf16[64,512]{1,0:T(8,128)(2,1)S(1)} %shard_map.41.refs_6_), channel_id=1, source_target_pairs={{0,2},{2,0},{1,3},{3,1},{4,6},{6,4},{5,7},{7,5},{8,10},{10,8},{9,1... | collective-permute-start | bytes 196616 | tf_op jit(solution)/shard_map/ppermute | solution.py:255
  16.9 0.4 %collective-permute-start.12 = (bf16[64,512]{1,0:T(8,128)(2,1)S(1)}, bf16[64,512]{1,0:T(8,128)(2,1)S(1)}, u32[]{:S(2)}, u32[]{:S(2)}) collective-permute-start(bf16[64,512]{1,0:T(8,128)(2,1)S(1)} %shard_map.45), channel_id=1, source_target_pairs={{0,4},{4,0},{8,12},{12,8},{1,5},{5,1},{9,13},{13,9},{2,6},{6,2},{1... | collective-permute-start | bytes 196616 | tf_op jit(solution)/shard_map/ppermute | solution.py:252
  17.3 0.0 collective-permute-done.3.refs_3_
  17.3 2.3 %collective-permute-done.1.refs_1_ = bf16[64,512]{1,0:T(8,128)(2,1)S(1)} collective-permute-done((bf16[64,512]{1,0:T(8,128)(2,1)S(1)}, bf16[64,512]{1,0:T(8,128)(2,1)S(1)}, u32[]{:S(2)}, u32[]{:S(2)}) %collective-permute-start.1) | collective-permute-done | bytes 65568 | tf_op jit(solution)/shard_map/ppermute | solution.py:255
  19.6 1.0 %collective-permute-done.6.refs_7_ = bf16[64,512]{1,0:T(8,128)(2,1)S(1)} collective-permute-done((bf16[64,512]{1,0:T(8,128)(2,1)S(1)}, bf16[64,512]{1,0:T(8,128)(2,1)S(1)}, u32[]{:S(2)}, u32[]{:S(2)}) %collective-permute-start.6) | collective-permute-done | bytes 65568 | tf_op jit(solution)/shard_map/ppermute | solution.py:255
  20.6 0.0 collective-permute-done.4.refs_5_.refs_2_
  20.6 0.5 %shard_map.42 = (f32[128,640]{1,0:T(8,128)S(1)}, bf16[128,640]{1,0:T(8,128)(2,1)S(1)}) custom-call(bf16[64,512]{1,0:T(8,128)(2,1)S(1)} %shard_map.39.refs_0_, bf16[64,512]{1,0:T(8,128)(2,1)S(1)} %collective-permute-done.1.refs_1_, bf16[64,512]{1,0:T(8,128)(2,1)S(1)} %collective-permute-done.2.refs_3_.refs_2_, ...), custom_call_target="tpu_custom_call" | custom-call | tf_op jit(solution)/shard_map/pallas_call | solution.py:22
  21.1 0.1 collective-permute-start.7
  21.2 0.0 collective-permute-done.12.refs_2_
  21.2 1.5 %collective-permute-start.13 = (bf16[192,512]{1,0:T(8,128)(2,1)S(1)}, bf16[192,512]{1,0:T(8,128)(2,1)S(1)}, u32[]{:S(2)}, u32[]{:S(2)}) collective-permute-start(bf16[192,512]{1,0:T(8,128)(2,1)S(1)} %shard_map.46.refs_1_), channel_id=1, source_target_pairs={{0,2},{2,0},{1,3},{3,1},{4,6},{6,4},{5,7},{7,5},{8,10},{10,8},{9,1... | collective-permute-start | bytes 589832 | tf_op jit(solution)/shard_map/ppermute | solution.py:255
  22.7 0.0 collective-permute-done.7.refs_1_
  22.7 0.1 collective-permute-start.8
  22.8 3.3 %collective-permute-start.9 = (bf16[32,640]{1,0:T(8,128)(2,1)S(1)}, bf16[32,640]{1,0:T(8,128)(2,1)S(1)}, u32[]{:S(2)}, u32[]{:S(2)}) collective-permute-start(bf16[32,640]{1,0:T(8,128)(2,1)S(1)} %get-tuple-element.31), channel_id=1, source_target_pairs={{0,8},{4,12},{8,0},{12,4},{1,9},{5,13},{9,1},{13,5},{2,10},{6,14},... | collective-permute-start | bytes 122888 | tf_op jit(solution)/shard_map/ppermute | solution.py:252
  26.1 1.1 %collective-permute-start.10 = (bf16[32,640]{1,0:T(8,128)(2,1)S(1)}, bf16[32,640]{1,0:T(8,128)(2,1)S(1)}, u32[]{:S(2)}, u32[]{:S(2)}) collective-permute-start(bf16[32,640]{1,0:T(8,128)(2,1)S(1)} %get-tuple-element.32), channel_id=1, source_target_pairs={{0,12},{4,8},{8,4},{12,0},{1,13},{5,9},{9,5},{13,1},{2,14},{6,10},... | collective-permute-start | bytes 122888 | tf_op jit(solution)/shard_map/ppermute | solution.py:252
  27.2 1.4 %collective-permute-done.13.refs_3_ = bf16[192,512]{1,0:T(8,128)(2,1)S(1)} collective-permute-done((bf16[192,512]{1,0:T(8,128)(2,1)S(1)}, bf16[192,512]{1,0:T(8,128)(2,1)S(1)}, u32[]{:S(2)}, u32[]{:S(2)}) %collective-permute-start.13) | collective-permute-done | bytes 196640 | tf_op jit(solution)/shard_map/ppermute | solution.py:255
  28.6 0.0 collective-permute-done.8.refs_1_.refs_6_
  28.6 0.2 collective-permute-done.9.refs_2_.refs_4_
  28.8 3.1 %collective-permute-done.10.refs_3_.refs_5_ = bf16[32,640]{1,0:T(8,128)(2,1)S(1)} collective-permute-done((bf16[32,640]{1,0:T(8,128)(2,1)S(1)}, bf16[32,640]{1,0:T(8,128)(2,1)S(1)}, u32[]{:S(2)}, u32[]{:S(2)}) %collective-permute-start.10) | collective-permute-done | bytes 40992 | tf_op jit(solution)/shard_map/ppermute | solution.py:252
  31.9 0.3 shard_map.47
  32.2 0.1 collective-permute-start.14
  32.3 0.2 shard_map.44.refs_0_
  32.5 0.6 %collective-permute-start.11 = (f32[32,512]{1,0:T(8,128)S(1)}, f32[32,512]{1,0:T(8,128)S(1)}, u32[]{:S(2)}, u32[]{:S(2)}) collective-permute-start(f32[32,512]{1,0:T(8,128)S(1)} %shard_map.44.refs_0_), channel_id=1, source_target_pairs={{0,1},{1,0},{2,3},{3,2},{4,5},{5,4},{6,7},{7,6},{8,9},{9,8},{10,11... | collective-permute-start | bytes 196616 | tf_op jit(solution)/shard_map/ppermute | solution.py:258
  33.0 0.6 %collective-permute-done.14.refs_1_ = f32[72,512]{1,0:T(8,128)S(1)} collective-permute-done((f32[72,512]{1,0:T(8,128)S(1)}, f32[72,512]{1,0:T(8,128)S(1)}, u32[]{:S(2)}, u32[]{:S(2)}) %collective-permute-start.14) | collective-permute-done | bytes 147488 | tf_op jit(solution)/shard_map/ppermute | solution.py:258
  33.6 0.0 copy-start.3
  33.6 0.3 shard_map.48
  33.9 0.0 collective-permute-done.11.refs_1_
  33.9 0.6 %copy-done.3 = bf16[64,512]{1,0:T(8,128)(2,1)S(1)} copy-done((bf16[64,512]{1,0:T(8,128)(2,1)S(1)}, bf16[64,512]{1,0:T(8,128)(2,1)}, u32[]{:S(2)}) %copy-start.3) | copy-done | bytes 65560
  34.5 0.9 %shard_map.49 = f32[64,512]{1,0:T(8,128)} custom-call(f32[32,512]{1,0:T(8,128)S(1)} %shard_map.44.refs_0_, f32[32,512]{1,0:T(8,128)S(1)} %collective-permute-done.11.refs_1_, f32[64,512]{1,0:T(8,128)S(1)} %get-tuple-element.35.refs_2_, f32[64,128]{1,0:T(8,128)S(1)} %get-tuple-element.36.refs_3_, f32[8,512]{1,0:T(8,128)S(1)} %get-tuple-element.37.refs_4_, ...), custom_call_target="tpu_custom_call" | custom-call | tf_op jit(solution)/shard_map/pallas_call | solution.py:22
  (7 shorter events, 0.1 us)
Async XLA Ops:
  0.0 0.9 %copy-start = (bf16[64,2048]{1,0:T(8,128)(2,1)S(1)}, bf16[64,2048]{1,0:T(8,128)(2,1)}, u32[]{:S(2)}) copy-start(bf16[64,2048]{1,0:T(8,128)(2,1)} %refs_0_.5) | copy-start | bytes 786436
  1.0 7.6 %copy-start.1 = (bf16[64,2048]{1,0:T(8,128)(2,1)S(1)}, bf16[64,2048]{1,0:T(8,128)(2,1)}, u32[]{:S(2)}) copy-start(bf16[64,2048]{1,0:T(8,128)(2,1)} %refs_0_.5) | copy-start | bytes 786436
  1.0 7.6 %collective-permute-start.2 = (bf16[64,512]{1,0:T(8,128)(2,1)S(1)}, bf16[64,512]{1,0:T(8,128)(2,1)S(1)}, u32[]{:S(2)}, u32[]{:S(2)}) collective-permute-start(bf16[64,512]{1,0:T(8,128)(2,1)S(1)} %get-tuple-element.25), channel_id=1, source_target_pairs={{0,12},{4,8},{8,4},{12,0},{1,13},{5,9},{9,5},{13,1},{2,14},{6,10},... | collective-permute-start | bytes 196616 | tf_op jit(solution)/shard_map/ppermute | solution.py:252
  6.1 0.8 %copy-start.2 = (bf16[64,512]{1,0:T(8,128)(2,1)S(1)}, bf16[64,512]{1,0:T(8,128)(2,1)}, u32[]{:S(2)}) copy-start(bf16[64,512]{1,0:T(8,128)(2,1)} %refs_5_.1) | copy-start | bytes 196612
  6.9 7.8 %collective-permute-start = (bf16[128,512]{1,0:T(8,128)(2,1)S(1)}, bf16[128,512]{1,0:T(8,128)(2,1)S(1)}, u32[]{:S(2)}, u32[]{:S(2)}) collective-permute-start(bf16[128,512]{1,0:T(8,128)(2,1)S(1)} %get-tuple-element.24), channel_id=1, source_target_pairs={{0,8},{4,12},{8,0},{12,4},{1,9},{5,13},{9,1},{13,5},{2,10},{6,14},... | collective-permute-start | bytes 393224 | tf_op jit(solution)/shard_map/ppermute | solution.py:252
  7.0 1.5 %copy-start.4 = (bf16[64]{0:T(256)(128)(2,1)S(1)}, bf16[64]{0:T(256)(128)(2,1)}, u32[]{:S(2)}) copy-start(bf16[64]{0:T(256)(128)(2,1)} %param.5) | copy-start | bytes 388
  7.0 9.2 %collective-permute-start.5 = (bf16[128,512]{1,0:T(8,128)(2,1)S(1)}, bf16[128,512]{1,0:T(8,128)(2,1)S(1)}, u32[]{:S(2)}, u32[]{:S(2)}) collective-permute-start(bf16[128,512]{1,0:T(8,128)(2,1)S(1)} %get-tuple-element.26), channel_id=1, source_target_pairs={{0,4},{4,0},{8,12},{12,8},{1,5},{5,1},{9,13},{13,9},{2,6},{6,2},{1... | collective-permute-start | bytes 393224 | tf_op jit(solution)/shard_map/ppermute | solution.py:252
  8.8 11.7 %collective-permute-start.4 = (bf16[144,512]{1,0:T(8,128)(2,1)S(1)}, bf16[144,512]{1,0:T(8,128)(2,1)S(1)}, u32[]{:S(2)}, u32[]{:S(2)}) collective-permute-start(bf16[144,512]{1,0:T(8,128)(2,1)S(1)} %shard_map.40.refs_4_.refs_0_), channel_id=1, source_target_pairs={{0,2},{2,0},{1,3},{3,1},{4,6},{6,4},{5,7},{7,5},{8,10},{10,8},{9,1... | collective-permute-start | bytes 442376 | tf_op jit(solution)/shard_map/ppermute | solution.py:255
  10.4 6.8 %collective-permute-start.3 = (bf16[64,512]{1,0:T(8,128)(2,1)S(1)}, bf16[64,512]{1,0:T(8,128)(2,1)S(1)}, u32[]{:S(2)}, u32[]{:S(2)}) collective-permute-start(bf16[64,512]{1,0:T(8,128)(2,1)S(1)} %collective-permute-done.2.refs_3_.refs_2_), channel_id=1, source_target_pairs={{0,2},{2,0},{1,3},{3,1},{4,6},{6,4},{5,7},{7,5},{8,10},{10,8},{9,1... | collective-permute-start | bytes 196616 | tf_op jit(solution)/shard_map/ppermute | solution.py:255
  14.8 4.8 %collective-permute-start.1 = (bf16[64,512]{1,0:T(8,128)(2,1)S(1)}, bf16[64,512]{1,0:T(8,128)(2,1)S(1)}, u32[]{:S(2)}, u32[]{:S(2)}) collective-permute-start(bf16[64,512]{1,0:T(8,128)(2,1)S(1)} %shard_map.39.refs_0_), channel_id=1, source_target_pairs={{0,2},{2,0},{1,3},{3,1},{4,6},{6,4},{5,7},{7,5},{8,10},{10,8},{9,1... | collective-permute-start | bytes 196616 | tf_op jit(solution)/shard_map/ppermute | solution.py:255
  16.2 4.3 %collective-permute-start.6 = (bf16[64,512]{1,0:T(8,128)(2,1)S(1)}, bf16[64,512]{1,0:T(8,128)(2,1)S(1)}, u32[]{:S(2)}, u32[]{:S(2)}) collective-permute-start(bf16[64,512]{1,0:T(8,128)(2,1)S(1)} %shard_map.41.refs_6_), channel_id=1, source_target_pairs={{0,2},{2,0},{1,3},{3,1},{4,6},{6,4},{5,7},{7,5},{8,10},{10,8},{9,1... | collective-permute-start | bytes 196616 | tf_op jit(solution)/shard_map/ppermute | solution.py:255
  16.9 4.3 %collective-permute-start.12 = (bf16[64,512]{1,0:T(8,128)(2,1)S(1)}, bf16[64,512]{1,0:T(8,128)(2,1)S(1)}, u32[]{:S(2)}, u32[]{:S(2)}) collective-permute-start(bf16[64,512]{1,0:T(8,128)(2,1)S(1)} %shard_map.45), channel_id=1, source_target_pairs={{0,4},{4,0},{8,12},{12,8},{1,5},{5,1},{9,13},{13,9},{2,6},{6,2},{1... | collective-permute-start | bytes 196616 | tf_op jit(solution)/shard_map/ppermute | solution.py:252
  21.1 1.6 %collective-permute-start.7 = (bf16[128,640]{1,0:T(8,128)(2,1)S(1)}, bf16[128,640]{1,0:T(8,128)(2,1)S(1)}, u32[]{:S(2)}, u32[]{:S(2)}) collective-permute-start(bf16[128,640]{1,0:T(8,128)(2,1)S(1)} %get-tuple-element.28), channel_id=1, source_target_pairs={{0,1},{1,0},{2,3},{3,2},{4,5},{5,4},{6,7},{7,6},{8,9},{9,8},{10,11... | collective-permute-start | bytes 491528 | tf_op jit(solution)/shard_map/ppermute | solution.py:258
  21.2 7.4 %collective-permute-start.13 = (bf16[192,512]{1,0:T(8,128)(2,1)S(1)}, bf16[192,512]{1,0:T(8,128)(2,1)S(1)}, u32[]{:S(2)}, u32[]{:S(2)}) collective-permute-start(bf16[192,512]{1,0:T(8,128)(2,1)S(1)} %shard_map.46.refs_1_), channel_id=1, source_target_pairs={{0,2},{2,0},{1,3},{3,1},{4,6},{6,4},{5,7},{7,5},{8,10},{10,8},{9,1... | collective-permute-start | bytes 589832 | tf_op jit(solution)/shard_map/ppermute | solution.py:255
  22.7 5.8 %collective-permute-start.8 = (bf16[32,640]{1,0:T(8,128)(2,1)S(1)}, bf16[32,640]{1,0:T(8,128)(2,1)S(1)}, u32[]{:S(2)}, u32[]{:S(2)}) collective-permute-start(bf16[32,640]{1,0:T(8,128)(2,1)S(1)} %get-tuple-element.30), channel_id=1, source_target_pairs={{0,4},{4,0},{8,12},{12,8},{1,5},{5,1},{9,13},{13,9},{2,6},{6,2},{1... | collective-permute-start | bytes 122888 | tf_op jit(solution)/shard_map/ppermute | solution.py:252
  22.8 6.0 %collective-permute-start.9 = (bf16[32,640]{1,0:T(8,128)(2,1)S(1)}, bf16[32,640]{1,0:T(8,128)(2,1)S(1)}, u32[]{:S(2)}, u32[]{:S(2)}) collective-permute-start(bf16[32,640]{1,0:T(8,128)(2,1)S(1)} %get-tuple-element.31), channel_id=1, source_target_pairs={{0,8},{4,12},{8,0},{12,4},{1,9},{5,13},{9,1},{13,5},{2,10},{6,14},... | collective-permute-start | bytes 122888 | tf_op jit(solution)/shard_map/ppermute | solution.py:252
  26.1 5.8 %collective-permute-start.10 = (bf16[32,640]{1,0:T(8,128)(2,1)S(1)}, bf16[32,640]{1,0:T(8,128)(2,1)S(1)}, u32[]{:S(2)}, u32[]{:S(2)}) collective-permute-start(bf16[32,640]{1,0:T(8,128)(2,1)S(1)} %get-tuple-element.32), channel_id=1, source_target_pairs={{0,12},{4,8},{8,4},{12,0},{1,13},{5,9},{9,5},{13,1},{2,14},{6,10},... | collective-permute-start | bytes 122888 | tf_op jit(solution)/shard_map/ppermute | solution.py:252
  32.2 1.4 %collective-permute-start.14 = (f32[72,512]{1,0:T(8,128)S(1)}, f32[72,512]{1,0:T(8,128)S(1)}, u32[]{:S(2)}, u32[]{:S(2)}) collective-permute-start(f32[72,512]{1,0:T(8,128)S(1)} %get-tuple-element.33.refs_0_), channel_id=1, source_target_pairs={{0,1},{1,0},{2,3},{3,2},{4,5},{5,4},{6,7},{7,6},{8,9},{9,8},{10,11... | collective-permute-start | bytes 442376 | tf_op jit(solution)/shard_map/ppermute | solution.py:258
  32.5 1.5 %collective-permute-start.11 = (f32[32,512]{1,0:T(8,128)S(1)}, f32[32,512]{1,0:T(8,128)S(1)}, u32[]{:S(2)}, u32[]{:S(2)}) collective-permute-start(f32[32,512]{1,0:T(8,128)S(1)} %shard_map.44.refs_0_), channel_id=1, source_target_pairs={{0,1},{1,0},{2,3},{3,2},{4,5},{5,4},{6,7},{7,6},{8,9},{9,8},{10,11... | collective-permute-start | bytes 196616 | tf_op jit(solution)/shard_map/ppermute | solution.py:258
  33.6 0.8 %copy-start.3 = (bf16[64,512]{1,0:T(8,128)(2,1)S(1)}, bf16[64,512]{1,0:T(8,128)(2,1)}, u32[]{:S(2)}) copy-start(bf16[64,512]{1,0:T(8,128)(2,1)} %refs_5_.1) | copy-start | bytes 196612

commit v19 on v17

--- a/solution.py
+++ b/solution.py
@@ -283,14 +283,16 @@
         got_keys += [n ^ k for n in keys[first:]]
         stack, spans, keys = stack + got[-1:], spans + [(0, len(keys) * rows)], keys + [n ^ k for n in keys]
         k //= 2
-    rest = pack([near, far] + got, [(0, rows)] * 2 + [(0, g.shape[0]) for g in got], after=[partial[0]])
-    raw_keys = [[0], [1, middle] + got_keys]
-    sources = [columns[0], with_columns(rest)]
+    two = pack([near, far], [(0, rows)] * 2)
+    rest = pack(got, [(0, g.shape[0]) for g in got], after=[partial[0]])
+    raw_keys = [[0], [1, middle], got_keys]
+    sources = [columns[0], with_columns(two), with_columns(rest)]
     raw_refs = [x[c] for c in range(ncol) for x in sources]
     raw_gram, *raw = call(
         functools.partial(raw_gram_kernel, nrow, ncol, rows, raw_keys),
         [sds((rows + 8, batch), F32)] + ([sds((batch, half), BF16)] if small else []),
         raw_refs,
+        after=[returned[k] for k in order if k],
         scratch=[] if small else [pltpu.VMEM((batch, half), BF16)],
     )
     gram, inverses, squares, *units = call(

time: 33.1 us -> 33.6 us (1.015)
  waiting for transfers between devices: 13 us -> 11.3 us
  starting transfers between devices: 15.4 us -> 17 us
  local copies, waits for them, and re-layouts: 1.8 us -> 2.32 us
    ppermute x5 -> x6, starting transfers between devices: 5.69 us -> 7.05 us  [along_col(): return lax.ppermute(x, 'col', [(i, (i - c) % ncol) for i in range(ncol)])]
    ppermute x5 -> x6, waiting for transfers between devices: 4.24 us -> 3.16 us  [along_col(): return lax.ppermute(x, 'col', [(i, (i - c) % ncol) for i in range(ncol)])]
    unnamed x10, local copies, waits for them, and re-layouts: 1.8 us -> 2.32 us
    ppermute x2, starting transfers between devices: 0.14 us -> 0.63 us  [other_core(): return lax.ppermute(x, 'sub', [(0, 1), (1, 0)])]
    pallas_call x12 -> x13, Pallas kernels: 2.55 us -> 2.55 us  [call(): pl.pallas_call(run, out_shape=out_shape, in_specs=[pl.BlockSpec(memory_sp...]
  transfers between devices with their start and end apart: 14 -> 15, of which waited for: 10 -> 9; matrix products, arithmetic and copies ran while one was open for 0% -> 0% of each run, Pallas kernels for 5% -> 4%
where the time goes in v19:
time: 33.6 us; the launch traced here: 33.3 us
  starting transfers between devices  17 us (51%)
  waiting for transfers between devices  11.3 us (34%)
  Pallas kernels  2.55 us (8%)
  local copies, waits for them, and re-layouts  2.32 us (7%)
    ppermute x7, starting transfers between devices, along_row(): return lax.ppermute(x, 'row', [(i, i ^ k) for i in range(nrow)])  9.37 us
    ppermute x7, waiting for transfers between devices, along_row(): return lax.ppermute(x, 'row', [(i, i ^ k) for i in range(nrow)])  7.44 us
    ppermute x6, starting transfers between devices, along_col(): return lax.ppermute(x, 'col', [(i, (i - c) % ncol) for i in range(ncol)])  7.05 us
    ppermute x6, waiting for transfers between devices, along_col(): return lax.ppermute(x, 'col', [(i, (i - c) % ncol) for i in range(ncol)])  3.16 us
    pallas_call x13, Pallas kernels, call(): pl.pallas_call(run, out_shape=out_shape, in_specs=[pl.BlockSpec(memory_sp...  2.55 us
    unnamed x10, local copies, waits for them, and re-layouts  2.32 us
    ppermute x2, waiting for transfers between devices, other_core(): return lax.ppermute(x, 'sub', [(0, 1), (1, 0)])  0.74 us
  transfers between devices with their start and end apart: 15, of which 9 were waited for; matrix products, arithmetic and copies ran while one was open for 0% of the time, Pallas kernels for 4%

profile of v19, /device:TPU:0, one launch (start us, length us, event | category | flops | bytes accessed | tf_op | source)
XLA Modules:
  0.0 33.3 jit_solution(9467661208102519413)
XLA Ops:
  0.0 0.0 copy-start
  0.0 0.9 %copy-done = bf16[64,2048]{1,0:T(8,128)(2,1)S(1)} copy-done((bf16[64,2048]{1,0:T(8,128)(2,1)S(1)}, bf16[64,2048]{1,0:T(8,128)(2,1)}, u32[]{:S(2)}) %copy-start) | copy-done | bytes 262168
  1.0 0.0 copy-start.1
  1.0 5.1 %collective-permute-start.2 = (bf16[64,512]{1,0:T(8,128)(2,1)S(1)}, bf16[64,512]{1,0:T(8,128)(2,1)S(1)}, u32[]{:S(2)}, u32[]{:S(2)}) collective-permute-start(bf16[64,512]{1,0:T(8,128)(2,1)S(1)} %get-tuple-element.25), channel_id=1, source_target_pairs={{0,12},{4,8},{8,4},{12,0},{1,13},{5,9},{9,5},{13,1},{2,14},{6,10},... | collective-permute-start | bytes 196616 | tf_op jit(solution)/shard_map/ppermute | solution.py:235
  6.1 0.0 copy-start.2
  6.1 0.8 %copy-done.2 = bf16[64,512]{1,0:T(8,128)(2,1)S(1)} copy-done((bf16[64,512]{1,0:T(8,128)(2,1)S(1)}, bf16[64,512]{1,0:T(8,128)(2,1)}, u32[]{:S(2)}) %copy-start.2) | copy-done | bytes 65560
  6.9 0.1 collective-permute-start
  7.0 0.0 copy-start.4
  7.0 0.6 %collective-permute-start.5 = (bf16[128,512]{1,0:T(8,128)(2,1)S(1)}, bf16[128,512]{1,0:T(8,128)(2,1)S(1)}, u32[]{:S(2)}, u32[]{:S(2)}) collective-permute-start(bf16[128,512]{1,0:T(8,128)(2,1)S(1)} %get-tuple-element.26), channel_id=1, source_target_pairs={{0,4},{4,0},{8,12},{12,8},{1,5},{5,1},{9,13},{13,9},{2,6},{6,2},{1... | collective-permute-start | bytes 393224 | tf_op jit(solution)/shard_map/ppermute | solution.py:235
  7.6 1.0 %collective-permute-done.2.refs_3_.refs_2_ = bf16[64,512]{1,0:T(8,128)(2,1)S(1)} collective-permute-done((bf16[64,512]{1,0:T(8,128)(2,1)S(1)}, bf16[64,512]{1,0:T(8,128)(2,1)S(1)}, u32[]{:S(2)}, u32[]{:S(2)}) %collective-permute-start.2) | collective-permute-done | bytes 65568 | tf_op jit(solution)/shard_map/ppermute | solution.py:235
  8.6 0.0 copy-done.1
  8.6 0.0 copy-done.4
  8.6 0.3 shard_map.40.refs_4_.refs_0_
  8.8 1.6 %collective-permute-start.4 = (bf16[144,512]{1,0:T(8,128)(2,1)S(1)}, bf16[144,512]{1,0:T(8,128)(2,1)S(1)}, u32[]{:S(2)}, u32[]{:S(2)}) collective-permute-start(bf16[144,512]{1,0:T(8,128)(2,1)S(1)} %shard_map.40.refs_4_.refs_0_), channel_id=1, source_target_pairs={{0,2},{2,0},{1,3},{3,1},{4,6},{6,4},{5,7},{7,5},{8,10},{10,8},{9,1... | collective-permute-start | bytes 442376 | tf_op jit(solution)/shard_map/ppermute | solution.py:238
  10.4 0.5 %collective-permute-start.3 = (bf16[64,512]{1,0:T(8,128)(2,1)S(1)}, bf16[64,512]{1,0:T(8,128)(2,1)S(1)}, u32[]{:S(2)}, u32[]{:S(2)}) collective-permute-start(bf16[64,512]{1,0:T(8,128)(2,1)S(1)} %collective-permute-done.2.refs_3_.refs_2_), channel_id=1, source_target_pairs={{0,2},{2,0},{1,3},{3,1},{4,6},{6,4},{5,7},{7,5},{8,10},{10,8},{9,1... | collective-permute-start | bytes 196616 | tf_op jit(solution)/shard_map/ppermute | solution.py:238
  10.9 3.8 %collective-permute-done.refs_0_.refs_1_ = bf16[128,512]{1,0:T(8,128)(2,1)S(1)} collective-permute-done((bf16[128,512]{1,0:T(8,128)(2,1)S(1)}, bf16[128,512]{1,0:T(8,128)(2,1)S(1)}, u32[]{:S(2)}, u32[]{:S(2)}) %collective-permute-start) | collective-permute-done | bytes 131104 | tf_op jit(solution)/shard_map/ppermute | solution.py:235
  14.8 1.4 %collective-permute-start.1 = (bf16[64,512]{1,0:T(8,128)(2,1)S(1)}, bf16[64,512]{1,0:T(8,128)(2,1)S(1)}, u32[]{:S(2)}, u32[]{:S(2)}) collective-permute-start(bf16[64,512]{1,0:T(8,128)(2,1)S(1)} %shard_map.39.refs_0_), channel_id=1, source_target_pairs={{0,2},{2,0},{1,3},{3,1},{4,6},{6,4},{5,7},{7,5},{8,10},{10,8},{9,1... | collective-permute-start | bytes 196616 | tf_op jit(solution)/shard_map/ppermute | solution.py:238
  16.2 0.0 collective-permute-done.5.refs_0_
  16.2 0.6 %collective-permute-start.6 = (bf16[64,512]{1,0:T(8,128)(2,1)S(1)}, bf16[64,512]{1,0:T(8,128)(2,1)S(1)}, u32[]{:S(2)}, u32[]{:S(2)}) collective-permute-start(bf16[64,512]{1,0:T(8,128)(2,1)S(1)} %shard_map.41.refs_6_), channel_id=1, source_target_pairs={{0,2},{2,0},{1,3},{3,1},{4,6},{6,4},{5,7},{7,5},{8,10},{10,8},{9,1... | collective-permute-start | bytes 196616 | tf_op jit(solution)/shard_map/ppermute | solution.py:238
  16.9 1.5 %collective-permute-start.12 = (bf16[128,512]{1,0:T(8,128)(2,1)S(1)}, bf16[128,512]{1,0:T(8,128)(2,1)S(1)}, u32[]{:S(2)}, u32[]{:S(2)}) collective-permute-start(bf16[128,512]{1,0:T(8,128)(2,1)S(1)} %shard_map.44.refs_1_), channel_id=1, source_target_pairs={{0,2},{2,0},{1,3},{3,1},{4,6},{6,4},{5,7},{7,5},{8,10},{10,8},{9,1... | collective-permute-start | bytes 393224 | tf_op jit(solution)/shard_map/ppermute | solution.py:238
  18.4 0.0 collective-permute-done.3.refs_3_
  18.4 0.1 collective-permute-start.11
  18.5 1.1 %collective-permute-done.1.refs_1_ = bf16[64,512]{1,0:T(8,128)(2,1)S(1)} collective-permute-done((bf16[64,512]{1,0:T(8,128)(2,1)S(1)}, bf16[64,512]{1,0:T(8,128)(2,1)S(1)}, u32[]{:S(2)}, u32[]{:S(2)}) %collective-permute-start.1) | collective-permute-done | bytes 65568 | tf_op jit(solution)/shard_map/ppermute | solution.py:238
  19.6 1.7 %collective-permute-done.6.refs_7_ = bf16[64,512]{1,0:T(8,128)(2,1)S(1)} collective-permute-done((bf16[64,512]{1,0:T(8,128)(2,1)S(1)}, bf16[64,512]{1,0:T(8,128)(2,1)S(1)}, u32[]{:S(2)}, u32[]{:S(2)}) %collective-permute-start.6) | collective-permute-done | bytes 65568 | tf_op jit(solution)/shard_map/ppermute | solution.py:238
  21.3 0.0 collective-permute-done.4.refs_5_.refs_3_
  21.3 0.5 %shard_map.42 = (f32[64,512]{1,0:T(8,128)S(1)}, bf16[64,512]{1,0:T(8,128)(2,1)S(1)}, bf16[64,512]{1,0:T(8,128)(2,1)S(1)}, bf16[64,512]{1,0:T(8,128)(2,1)S(1)}) custom-call(bf16[64,512]{1,0:T(8,128)(2,1)S(1)} %shard_map.39.refs_0_, bf16[64,512]{1,0:T(8,128)(2,1)S(1)} %collective-permute-done.1.refs_1_, ...), custom_call_target="tpu_custom_call" | custom-call | tf_op jit(solution)/shard_map/pallas_call | solution.py:22
  21.8 0.5 %collective-permute-start.7 = (bf16[64,512]{1,0:T(8,128)(2,1)S(1)}, bf16[64,512]{1,0:T(8,128)(2,1)S(1)}, u32[]{:S(2)}, u32[]{:S(2)}) collective-permute-start(bf16[64,512]{1,0:T(8,128)(2,1)S(1)} %get-tuple-element.27), channel_id=1, source_target_pairs={{0,8},{4,12},{8,0},{12,4},{1,9},{5,13},{9,1},{13,5},{2,10},{6,14},... | collective-permute-start | bytes 196616 | tf_op jit(solution)/shard_map/ppermute | solution.py:235
  22.4 2.3 %collective-permute-start.8 = (bf16[64,512]{1,0:T(8,128)(2,1)S(1)}, bf16[64,512]{1,0:T(8,128)(2,1)S(1)}, u32[]{:S(2)}, u32[]{:S(2)}) collective-permute-start(bf16[64,512]{1,0:T(8,128)(2,1)S(1)} %get-tuple-element.28), channel_id=1, source_target_pairs={{0,12},{4,8},{8,4},{12,0},{1,13},{5,9},{9,5},{13,1},{2,14},{6,10},... | collective-permute-start | bytes 196616 | tf_op jit(solution)/shard_map/ppermute | solution.py:235
  24.7 0.7 %collective-permute-start.9 = (bf16[64,512]{1,0:T(8,128)(2,1)S(1)}, bf16[64,512]{1,0:T(8,128)(2,1)S(1)}, u32[]{:S(2)}, u32[]{:S(2)}) collective-permute-start(bf16[64,512]{1,0:T(8,128)(2,1)S(1)} %get-tuple-element.30), channel_id=1, source_target_pairs={{0,4},{4,0},{8,12},{12,8},{1,5},{5,1},{9,13},{13,9},{2,6},{6,2},{1... | collective-permute-start | bytes 196616 | tf_op jit(solution)/shard_map/ppermute | solution.py:235
  25.4 0.0 collective-permute-done.11.refs_0_
  25.4 1.4 %collective-permute-start.13 = (bf16[64,512]{1,0:T(8,128)(2,1)S(1)}, bf16[64,512]{1,0:T(8,128)(2,1)S(1)}, u32[]{:S(2)}, u32[]{:S(2)}) collective-permute-start(bf16[64,512]{1,0:T(8,128)(2,1)S(1)} %shard_map.46.refs_2_), channel_id=1, source_target_pairs={{0,2},{2,0},{1,3},{3,1},{4,6},{6,4},{5,7},{7,5},{8,10},{10,8},{9,1... | collective-permute-start | bytes 196616 | tf_op jit(solution)/shard_map/ppermute | solution.py:238
  26.8 0.0 collective-permute-done.12.refs_4_
  26.8 2.0 %collective-permute-done.7.refs_0_.refs_6_ = bf16[64,512]{1,0:T(8,128)(2,1)S(1)} collective-permute-done((bf16[64,512]{1,0:T(8,128)(2,1)S(1)}, bf16[64,512]{1,0:T(8,128)(2,1)S(1)}, u32[]{:S(2)}, u32[]{:S(2)}) %collective-permute-start.7) | collective-permute-done | bytes 65568 | tf_op jit(solution)/shard_map/ppermute | solution.py:235
  28.7 0.0 collective-permute-done.8.refs_1_.refs_7_
  28.7 0.7 %collective-permute-done.9.refs_3_.refs_8_ = bf16[64,512]{1,0:T(8,128)(2,1)S(1)} collective-permute-done((bf16[64,512]{1,0:T(8,128)(2,1)S(1)}, bf16[64,512]{1,0:T(8,128)(2,1)S(1)}, u32[]{:S(2)}, u32[]{:S(2)}) %collective-permute-start.9) | collective-permute-done | bytes 65568 | tf_op jit(solution)/shard_map/ppermute | solution.py:235
  29.4 0.3 %collective-permute-done.13.refs_5_ = bf16[64,512]{1,0:T(8,128)(2,1)S(1)} collective-permute-done((bf16[64,512]{1,0:T(8,128)(2,1)S(1)}, bf16[64,512]{1,0:T(8,128)(2,1)S(1)}, u32[]{:S(2)}, u32[]{:S(2)}) %collective-permute-start.13) | collective-permute-done | bytes 65568 | tf_op jit(solution)/shard_map/ppermute | solution.py:238
  29.7 0.3 shard_map.47
  30.1 0.1 collective-permute-start.14
  30.1 0.1 shard_map.43
  30.2 0.6 %collective-permute-start.10 = (f32[72,512]{1,0:T(8,128)S(1)}, f32[72,512]{1,0:T(8,128)S(1)}, u32[]{:S(2)}, u32[]{:S(2)}) collective-permute-start(f32[72,512]{1,0:T(8,128)S(1)} %get-tuple-element.31.refs_0_), channel_id=1, source_target_pairs={{0,1},{1,0},{2,3},{3,2},{4,5},{5,4},{6,7},{7,6},{8,9},{9,8},{10,11... | collective-permute-start | bytes 442376 | tf_op jit(solution)/shard_map/ppermute | solution.py:241
  30.8 0.7 %collective-permute-done.14.refs_1_ = f32[72,512]{1,0:T(8,128)S(1)} collective-permute-done((f32[72,512]{1,0:T(8,128)S(1)}, f32[72,512]{1,0:T(8,128)S(1)}, u32[]{:S(2)}, u32[]{:S(2)}) %collective-permute-start.14) | collective-permute-done | bytes 147488 | tf_op jit(solution)/shard_map/ppermute | solution.py:241
  31.5 0.0 copy-start.3
  31.5 0.3 shard_map.48
  31.8 0.1 collective-permute-done.10.refs_1_
  31.8 0.5 %copy-done.3 = bf16[64,512]{1,0:T(8,128)(2,1)S(1)} copy-done((bf16[64,512]{1,0:T(8,128)(2,1)S(1)}, bf16[64,512]{1,0:T(8,128)(2,1)}, u32[]{:S(2)}) %copy-start.3) | copy-done | bytes 65560
  32.3 1.0 %shard_map.49 = f32[64,512]{1,0:T(8,128)} custom-call(f32[72,512]{1,0:T(8,128)S(1)} %get-tuple-element.31.refs_0_, f32[72,512]{1,0:T(8,128)S(1)} %collective-permute-done.10.refs_1_, f32[8,512]{1,0:T(8,128)S(1)} %get-tuple-element.32.refs_2_, f32[64,512]{1,0:T(8,128)S(1)} %get-tuple-element.35.refs_3_, f32[64,128]{1,0:T(8,128)S(1)} %get-tuple-element.36.refs_4_, ...), custom_call_target="tpu_custom_call" | custom-call | tf_op jit(solution)/shard_map/pallas_call | solution.py:22
  (7 shorter events, 0.1 us)
Async XLA Ops:
  0.0 0.9 %copy-start = (bf16[64,2048]{1,0:T(8,128)(2,1)S(1)}, bf16[64,2048]{1,0:T(8,128)(2,1)}, u32[]{:S(2)}) copy-start(bf16[64,2048]{1,0:T(8,128)(2,1)} %refs_0_.5) | copy-start | bytes 786436
  1.0 7.6 %copy-start.1 = (bf16[64,2048]{1,0:T(8,128)(2,1)S(1)}, bf16[64,2048]{1,0:T(8,128)(2,1)}, u32[]{:S(2)}) copy-start(bf16[64,2048]{1,0:T(8,128)(2,1)} %refs_0_.5) | copy-start | bytes 786436
  1.0 7.6 %collective-permute-start.2 = (bf16[64,512]{1,0:T(8,128)(2,1)S(1)}, bf16[64,512]{1,0:T(8,128)(2,1)S(1)}, u32[]{:S(2)}, u32[]{:S(2)}) collective-permute-start(bf16[64,512]{1,0:T(8,128)(2,1)S(1)} %get-tuple-element.25), channel_id=1, source_target_pairs={{0,12},{4,8},{8,4},{12,0},{1,13},{5,9},{9,5},{13,1},{2,14},{6,10},... | collective-permute-start | bytes 196616 | tf_op jit(solution)/shard_map/ppermute | solution.py:235
  6.1 0.8 %copy-start.2 = (bf16[64,512]{1,0:T(8,128)(2,1)S(1)}, bf16[64,512]{1,0:T(8,128)(2,1)}, u32[]{:S(2)}) copy-start(bf16[64,512]{1,0:T(8,128)(2,1)} %refs_6_.1) | copy-start | bytes 196612
  6.9 7.8 %collective-permute-start = (bf16[128,512]{1,0:T(8,128)(2,1)S(1)}, bf16[128,512]{1,0:T(8,128)(2,1)S(1)}, u32[]{:S(2)}, u32[]{:S(2)}) collective-permute-start(bf16[128,512]{1,0:T(8,128)(2,1)S(1)} %get-tuple-element.24), channel_id=1, source_target_pairs={{0,8},{4,12},{8,0},{12,4},{1,9},{5,13},{9,1},{13,5},{2,10},{6,14},... | collective-permute-start | bytes 393224 | tf_op jit(solution)/shard_map/ppermute | solution.py:235
  7.0 1.5 %copy-start.4 = (bf16[64]{0:T(256)(128)(2,1)S(1)}, bf16[64]{0:T(256)(128)(2,1)}, u32[]{:S(2)}) copy-start(bf16[64]{0:T(256)(128)(2,1)} %param.5) | copy-start | bytes 388
  7.0 9.2 %collective-permute-start.5 = (bf16[128,512]{1,0:T(8,128)(2,1)S(1)}, bf16[128,512]{1,0:T(8,128)(2,1)S(1)}, u32[]{:S(2)}, u32[]{:S(2)}) collective-permute-start(bf16[128,512]{1,0:T(8,128)(2,1)S(1)} %get-tuple-element.26), channel_id=1, source_target_pairs={{0,4},{4,0},{8,12},{12,8},{1,5},{5,1},{9,13},{13,9},{2,6},{6,2},{1... | collective-permute-start | bytes 393224 | tf_op jit(solution)/shard_map/ppermute | solution.py:235
  8.8 12.5 %collective-permute-start.4 = (bf16[144,512]{1,0:T(8,128)(2,1)S(1)}, bf16[144,512]{1,0:T(8,128)(2,1)S(1)}, u32[]{:S(2)}, u32[]{:S(2)}) collective-permute-start(bf16[144,512]{1,0:T(8,128)(2,1)S(1)} %shard_map.40.refs_4_.refs_0_), channel_id=1, source_target_pairs={{0,2},{2,0},{1,3},{3,1},{4,6},{6,4},{5,7},{7,5},{8,10},{10,8},{9,1... | collective-permute-start | bytes 442376 | tf_op jit(solution)/shard_map/ppermute | solution.py:238
  10.4 8.0 %collective-permute-start.3 = (bf16[64,512]{1,0:T(8,128)(2,1)S(1)}, bf16[64,512]{1,0:T(8,128)(2,1)S(1)}, u32[]{:S(2)}, u32[]{:S(2)}) collective-permute-start(bf16[64,512]{1,0:T(8,128)(2,1)S(1)} %collective-permute-done.2.refs_3_.refs_2_), channel_id=1, source_target_pairs={{0,2},{2,0},{1,3},{3,1},{4,6},{6,4},{5,7},{7,5},{8,10},{10,8},{9,1... | collective-permute-start | bytes 196616 | tf_op jit(solution)/shard_map/ppermute | solution.py:238
  14.8 4.8 %collective-permute-start.1 = (bf16[64,512]{1,0:T(8,128)(2,1)S(1)}, bf16[64,512]{1,0:T(8,128)(2,1)S(1)}, u32[]{:S(2)}, u32[]{:S(2)}) collective-permute-start(bf16[64,512]{1,0:T(8,128)(2,1)S(1)} %shard_map.39.refs_0_), channel_id=1, source_target_pairs={{0,2},{2,0},{1,3},{3,1},{4,6},{6,4},{5,7},{7,5},{8,10},{10,8},{9,1... | collective-permute-start | bytes 196616 | tf_op jit(solution)/shard_map/ppermute | solution.py:238
  16.2 5.1 %collective-permute-start.6 = (bf16[64,512]{1,0:T(8,128)(2,1)S(1)}, bf16[64,512]{1,0:T(8,128)(2,1)S(1)}, u32[]{:S(2)}, u32[]{:S(2)}) collective-permute-start(bf16[64,512]{1,0:T(8,128)(2,1)S(1)} %shard_map.41.refs_6_), channel_id=1, source_target_pairs={{0,2},{2,0},{1,3},{3,1},{4,6},{6,4},{5,7},{7,5},{8,10},{10,8},{9,1... | collective-permute-start | bytes 196616 | tf_op jit(solution)/shard_map/ppermute | solution.py:238
  16.9 9.9 %collective-permute-start.12 = (bf16[128,512]{1,0:T(8,128)(2,1)S(1)}, bf16[128,512]{1,0:T(8,128)(2,1)S(1)}, u32[]{:S(2)}, u32[]{:S(2)}) collective-permute-start(bf16[128,512]{1,0:T(8,128)(2,1)S(1)} %shard_map.44.refs_1_), channel_id=1, source_target_pairs={{0,2},{2,0},{1,3},{3,1},{4,6},{6,4},{5,7},{7,5},{8,10},{10,8},{9,1... | collective-permute-start | bytes 393224 | tf_op jit(solution)/shard_map/ppermute | solution.py:238
  18.4 7.0 %collective-permute-start.11 = (bf16[64,512]{1,0:T(8,128)(2,1)S(1)}, bf16[64,512]{1,0:T(8,128)(2,1)S(1)}, u32[]{:S(2)}, u32[]{:S(2)}) collective-permute-start(bf16[64,512]{1,0:T(8,128)(2,1)S(1)} %shard_map.45), channel_id=1, source_target_pairs={{0,4},{4,0},{8,12},{12,8},{1,5},{5,1},{9,13},{13,9},{2,6},{6,2},{1... | collective-permute-start | bytes 196616 | tf_op jit(solution)/shard_map/ppermute | solution.py:235
  21.8 6.9 %collective-permute-start.7 = (bf16[64,512]{1,0:T(8,128)(2,1)S(1)}, bf16[64,512]{1,0:T(8,128)(2,1)S(1)}, u32[]{:S(2)}, u32[]{:S(2)}) collective-permute-start(bf16[64,512]{1,0:T(8,128)(2,1)S(1)} %get-tuple-element.27), channel_id=1, source_target_pairs={{0,8},{4,12},{8,0},{12,4},{1,9},{5,13},{9,1},{13,5},{2,10},{6,14},... | collective-permute-start | bytes 196616 | tf_op jit(solution)/shard_map/ppermute | solution.py:235
  22.4 6.4 %collective-permute-start.8 = (bf16[64,512]{1,0:T(8,128)(2,1)S(1)}, bf16[64,512]{1,0:T(8,128)(2,1)S(1)}, u32[]{:S(2)}, u32[]{:S(2)}) collective-permute-start(bf16[64,512]{1,0:T(8,128)(2,1)S(1)} %get-tuple-element.28), channel_id=1, source_target_pairs={{0,12},{4,8},{8,4},{12,0},{1,13},{5,9},{9,5},{13,1},{2,14},{6,10},... | collective-permute-start | bytes 196616 | tf_op jit(solution)/shard_map/ppermute | solution.py:235
  24.7 4.7 %collective-permute-start.9 = (bf16[64,512]{1,0:T(8,128)(2,1)S(1)}, bf16[64,512]{1,0:T(8,128)(2,1)S(1)}, u32[]{:S(2)}, u32[]{:S(2)}) collective-permute-start(bf16[64,512]{1,0:T(8,128)(2,1)S(1)} %get-tuple-element.30), channel_id=1, source_target_pairs={{0,4},{4,0},{8,12},{12,8},{1,5},{5,1},{9,13},{13,9},{2,6},{6,2},{1... | collective-permute-start | bytes 196616 | tf_op jit(solution)/shard_map/ppermute | solution.py:235
  25.4 4.3 %collective-permute-start.13 = (bf16[64,512]{1,0:T(8,128)(2,1)S(1)}, bf16[64,512]{1,0:T(8,128)(2,1)S(1)}, u32[]{:S(2)}, u32[]{:S(2)}) collective-permute-start(bf16[64,512]{1,0:T(8,128)(2,1)S(1)} %shard_map.46.refs_2_), channel_id=1, source_target_pairs={{0,2},{2,0},{1,3},{3,1},{4,6},{6,4},{5,7},{7,5},{8,10},{10,8},{9,1... | collective-permute-start | bytes 196616 | tf_op jit(solution)/shard_map/ppermute | solution.py:238
  30.1 1.4 %collective-permute-start.14 = (f32[72,512]{1,0:T(8,128)S(1)}, f32[72,512]{1,0:T(8,128)S(1)}, u32[]{:S(2)}, u32[]{:S(2)}) collective-permute-start(f32[72,512]{1,0:T(8,128)S(1)} %get-tuple-element.33.refs_0_), channel_id=1, source_target_pairs={{0,1},{1,0},{2,3},{3,2},{4,5},{5,4},{6,7},{7,6},{8,9},{9,8},{10,11... | collective-permute-start | bytes 442376 | tf_op jit(solution)/shard_map/ppermute | solution.py:241
  30.2 1.6 %collective-permute-start.10 = (f32[72,512]{1,0:T(8,128)S(1)}, f32[72,512]{1,0:T(8,128)S(1)}, u32[]{:S(2)}, u32[]{:S(2)}) collective-permute-start(f32[72,512]{1,0:T(8,128)S(1)} %get-tuple-element.31.refs_0_), channel_id=1, source_target_pairs={{0,1},{1,0},{2,3},{3,2},{4,5},{5,4},{6,7},{7,6},{8,9},{9,8},{10,11... | collective-permute-start | bytes 442376 | tf_op jit(solution)/shard_map/ppermute | solution.py:241
  31.5 0.8 %copy-start.3 = (bf16[64,512]{1,0:T(8,128)(2,1)S(1)}, bf16[64,512]{1,0:T(8,128)(2,1)}, u32[]{:S(2)}) copy-start(bf16[64,512]{1,0:T(8,128)(2,1)} %refs_6_.1) | copy-start | bytes 196612

commit v20 on v8

--- a/solution.py
+++ b/solution.py
@@ -77,11 +77,10 @@
         outs[k - 1][...] = teach[:, pl.ds(at, part)]
 
 
-def ride_kernel(stud, *refs):
-    rows, count = stud.shape[0], len(refs) // 2
-    for piece, out in zip(refs[:count], refs[count:]):
-        out[:rows, :] = stud[...]
-        wide(out, rows, piece)
+def ride_kernel(stud, piece, out):
+    rows = stud.shape[0]
+    out[:rows, :] = stud[...]
+    wide(out, rows, piece[...])
 
 
 def own_kernel(nrow, teach, stud, scale, out):
@@ -240,9 +239,13 @@
     order = list(range(middle, nrow)) + list(range(middle))
     riders = (1, middle)
     cuts = call(functools.partial(cut_kernel, nrow), [sds((rows, part), BF16)] * (nrow - 1), [teacher])
-    ridden = call(ride_kernel, [sds((rows + high, half), BF16)] * 2, [student] + [cuts[k - 1] for k in riders])
-    leaving = dict(enumerate(cuts, 1)) | dict(zip(riders, ridden))
-    came = {k: along_row(leaving[k], k) for k in order if k}
+    came = {}
+    for k in order:
+        if k:
+            leaving = cuts[k - 1]
+            if k in riders:
+                leaving = call(ride_kernel, sds((rows + high, half), BF16), [student, leaving])
+            came[k] = along_row(leaving, k)
     own = call(
         functools.partial(own_kernel, nrow),
         sds((rows + TAIL + high, half), BF16),

time: 32.6 us -> 33.6 us (1.031)
  starting transfers between devices: 15 us -> 16.5 us
  local copies, waits for them, and re-layouts: 1.8 us -> 0.96 us
    ppermute x7, starting transfers between devices: 9.23 us -> 10.7 us  [along_row(): return lax.ppermute(x, 'row', [(i, i ^ k) for i in range(nrow)])]
    unnamed x10 -> x8, local copies, waits for them, and re-layouts: 1.8 us -> 0.96 us
    ppermute x7, waiting for transfers between devices: 7.18 us -> 7.98 us  [along_row(): return lax.ppermute(x, 'row', [(i, i ^ k) for i in range(nrow)])]
    ppermute x5, waiting for transfers between devices: 4.39 us -> 3.9 us  [along_col(): return lax.ppermute(x, 'col', [(i, (i - c) % ncol) for i in range(ncol)])]
    pallas_call x11 -> x12, Pallas kernels: 2.4 us -> 2.4 us  [call(): pl.pallas_call(run, out_shape=out_shape, in_specs=[pl.BlockSpec(memory_sp...]
  transfers between devices with their start and end apart: 13 -> 13, of which waited for: 11 -> 9; matrix products, arithmetic and copies ran while one was open for 0% -> 0% of each run, Pallas kernels for 4% -> 3%
where the time goes in v20:
time: 33.6 us; the launch traced here: 33.4 us
  starting transfers between devices  16.5 us (49%)
  waiting for transfers between devices  13.4 us (40%)
  Pallas kernels  2.4 us (7%)
  local copies, waits for them, and re-layouts  0.96 us (3%)
    ppermute x7, starting transfers between devices, along_row(): return lax.ppermute(x, 'row', [(i, i ^ k) for i in range(nrow)])  10.7 us
    ppermute x7, waiting for transfers between devices, along_row(): return lax.ppermute(x, 'row', [(i, i ^ k) for i in range(nrow)])  7.98 us
    ppermute x5, starting transfers between devices, along_col(): return lax.ppermute(x, 'col', [(i, (i - c) % ncol) for i in range(ncol)])  5.72 us
    ppermute x5, waiting for transfers between devices, along_col(): return lax.ppermute(x, 'col', [(i, (i - c) % ncol) for i in range(ncol)])  3.9 us
    pallas_call x12, Pallas kernels, call(): pl.pallas_call(run, out_shape=out_shape, in_specs=[pl.BlockSpec(memory_sp...  2.4 us
    ppermute x1, waiting for transfers between devices, other_core(): return lax.ppermute(x, 'sub', [(0, 1), (1, 0)])  1.57 us
    unnamed x8, local copies, waits for them, and re-layouts  0.96 us
  transfers between devices with their start and end apart: 13, of which 9 were waited for; matrix products, arithmetic and copies ran while one was open for 0% of the time, Pallas kernels for 3%

profile of v20, /device:TPU:0, one launch (start us, length us, event | category | flops | bytes accessed | tf_op | source)
XLA Modules:
  0.0 33.4 jit_solution(10848880061763172201)
XLA Ops:
  0.0 0.0 copy-start
  0.0 0.9 %copy-done = bf16[64,2048]{1,0:T(8,128)(2,1)S(1)} copy-done((bf16[64,2048]{1,0:T(8,128)(2,1)S(1)}, bf16[64,2048]{1,0:T(8,128)(2,1)}, u32[]{:S(2)}) %copy-start) | copy-done | bytes 262168
  1.0 0.0 copy-start.2
  1.0 5.1 %collective-permute-start = (bf16[64,512]{1,0:T(8,128)(2,1)S(1)}, bf16[64,512]{1,0:T(8,128)(2,1)S(1)}, u32[]{:S(2)}, u32[]{:S(2)}) collective-permute-start(bf16[64,512]{1,0:T(8,128)(2,1)S(1)} %get-tuple-element.16), channel_id=1, source_target_pairs={{0,12},{4,8},{8,4},{12,0},{1,13},{5,9},{9,5},{13,1},{2,14},{6,10},... | collective-permute-start | bytes 196616 | tf_op jit(solution)/shard_map/ppermute | solution.py:223
  6.1 0.0 copy-done.2
  6.1 0.0 copy-start.1
  6.1 0.1 collective-permute-start.2
  6.2 0.0 copy-start.3
  6.2 1.4 %collective-permute-start.1 = (bf16[128,512]{1,0:T(8,128)(2,1)S(1)}, bf16[128,512]{1,0:T(8,128)(2,1)S(1)}, u32[]{:S(2)}, u32[]{:S(2)}) collective-permute-start(bf16[128,512]{1,0:T(8,128)(2,1)S(1)} %shard_map.39), channel_id=1, source_target_pairs={{0,4},{4,0},{8,12},{12,8},{1,5},{5,1},{9,13},{13,9},{2,6},{6,2},{1... | collective-permute-start | bytes 393224 | tf_op jit(solution)/shard_map/ppermute | solution.py:223
  7.6 1.0 %collective-permute-done.refs_3_.refs_2_ = bf16[64,512]{1,0:T(8,128)(2,1)S(1)} collective-permute-done((bf16[64,512]{1,0:T(8,128)(2,1)S(1)}, bf16[64,512]{1,0:T(8,128)(2,1)S(1)}, u32[]{:S(2)}, u32[]{:S(2)}) %collective-permute-start) | collective-permute-done | bytes 65568 | tf_op jit(solution)/shard_map/ppermute | solution.py:223
  8.6 0.0 copy-done.1
  8.6 0.0 copy-done.3
  8.6 0.3 shard_map.38.refs_4_.refs_0_
  8.9 2.0 %collective-permute-start.6 = (bf16[144,512]{1,0:T(8,128)(2,1)S(1)}, bf16[144,512]{1,0:T(8,128)(2,1)S(1)}, u32[]{:S(2)}, u32[]{:S(2)}) collective-permute-start(bf16[144,512]{1,0:T(8,128)(2,1)S(1)} %shard_map.38.refs_4_.refs_0_), channel_id=1, source_target_pairs={{0,2},{2,0},{1,3},{3,1},{4,6},{6,4},{5,7},{7,5},{8,10},{10,8},{9,1... | collective-permute-start | bytes 442376 | tf_op jit(solution)/shard_map/ppermute | solution.py:226
  10.9 0.1 collective-permute-start.5
  10.9 3.5 %collective-permute-done.2.refs_0_.refs_1_ = bf16[128,512]{1,0:T(8,128)(2,1)S(1)} collective-permute-done((bf16[128,512]{1,0:T(8,128)(2,1)S(1)}, bf16[128,512]{1,0:T(8,128)(2,1)S(1)}, u32[]{:S(2)}, u32[]{:S(2)}) %collective-permute-start.2) | collective-permute-done | bytes 131104 | tf_op jit(solution)/shard_map/ppermute | solution.py:223
  14.5 1.5 %collective-permute-start.4 = (bf16[64,512]{1,0:T(8,128)(2,1)S(1)}, bf16[64,512]{1,0:T(8,128)(2,1)S(1)}, u32[]{:S(2)}, u32[]{:S(2)}) collective-permute-start(bf16[64,512]{1,0:T(8,128)(2,1)S(1)} %shard_map.42.refs_0_), channel_id=1, source_target_pairs={{0,2},{2,0},{1,3},{3,1},{4,6},{6,4},{5,7},{7,5},{8,10},{10,8},{9,1... | collective-permute-start | bytes 196616 | tf_op jit(solution)/shard_map/ppermute | solution.py:226
  16.0 0.0 collective-permute-done.1.refs_0_
  16.0 0.6 %collective-permute-start.7 = (bf16[64,512]{1,0:T(8,128)(2,1)S(1)}, bf16[64,512]{1,0:T(8,128)(2,1)S(1)}, u32[]{:S(2)}, u32[]{:S(2)}) collective-permute-start(bf16[64,512]{1,0:T(8,128)(2,1)S(1)} %shard_map.43.refs_6_), channel_id=1, source_target_pairs={{0,2},{2,0},{1,3},{3,1},{4,6},{6,4},{5,7},{7,5},{8,10},{10,8},{9,1... | collective-permute-start | bytes 196616 | tf_op jit(solution)/shard_map/ppermute | solution.py:226
  16.6 0.7 %collective-permute-start.3 = (bf16[64,512]{1,0:T(8,128)(2,1)S(1)}, bf16[64,512]{1,0:T(8,128)(2,1)S(1)}, u32[]{:S(2)}, u32[]{:S(2)}) collective-permute-start(bf16[64,512]{1,0:T(8,128)(2,1)S(1)} %shard_map.41), channel_id=1, source_target_pairs={{0,4},{4,0},{8,12},{12,8},{1,5},{5,1},{9,13},{13,9},{2,6},{6,2},{1... | collective-permute-start | bytes 196616 | tf_op jit(solution)/shard_map/ppermute | solution.py:223
  17.3 0.0 collective-permute-done.5.refs_3_
  17.3 1.9 %collective-permute-done.4.refs_1_ = bf16[64,512]{1,0:T(8,128)(2,1)S(1)} collective-permute-done((bf16[64,512]{1,0:T(8,128)(2,1)S(1)}, bf16[64,512]{1,0:T(8,128)(2,1)S(1)}, u32[]{:S(2)}, u32[]{:S(2)}) %collective-permute-start.4) | collective-permute-done | bytes 65568 | tf_op jit(solution)/shard_map/ppermute | solution.py:226
  19.3 1.1 %collective-permute-done.7.refs_7_ = bf16[64,512]{1,0:T(8,128)(2,1)S(1)} collective-permute-done((bf16[64,512]{1,0:T(8,128)(2,1)S(1)}, bf16[64,512]{1,0:T(8,128)(2,1)S(1)}, u32[]{:S(2)}, u32[]{:S(2)}) %collective-permute-start.7) | collective-permute-done | bytes 65568 | tf_op jit(solution)/shard_map/ppermute | solution.py:226
  20.3 0.0 collective-permute-done.6.refs_5_.refs_2_
  20.3 0.5 %shard_map.44 = (f32[64,512]{1,0:T(8,128)S(1)}, bf16[64,512]{1,0:T(8,128)(2,1)S(1)}, bf16[64,512]{1,0:T(8,128)(2,1)S(1)}, bf16[64,512]{1,0:T(8,128)(2,1)S(1)}) custom-call(bf16[64,512]{1,0:T(8,128)(2,1)S(1)} %shard_map.42.refs_0_, bf16[64,512]{1,0:T(8,128)(2,1)S(1)} %collective-permute-done.4.refs_1_, ...), custom_call_target="tpu_custom_call" | custom-call | tf_op jit(solution)/shard_map/pallas_call | solution.py:22
  20.9 0.0 collective-permute-done.3.refs_2_
  20.9 1.5 %collective-permute-start.8 = (bf16[192,512]{1,0:T(8,128)(2,1)S(1)}, bf16[192,512]{1,0:T(8,128)(2,1)S(1)}, u32[]{:S(2)}, u32[]{:S(2)}) collective-permute-start(bf16[192,512]{1,0:T(8,128)(2,1)S(1)} %shard_map.45.refs_1_), channel_id=1, source_target_pairs={{0,2},{2,0},{1,3},{3,1},{4,6},{6,4},{5,7},{7,5},{8,10},{10,8},{9,1... | collective-permute-start | bytes 589832 | tf_op jit(solution)/shard_map/ppermute | solution.py:226
  22.5 1.3 %collective-permute-start.9 = (bf16[64,512]{1,0:T(8,128)(2,1)S(1)}, bf16[64,512]{1,0:T(8,128)(2,1)S(1)}, u32[]{:S(2)}, u32[]{:S(2)}) collective-permute-start(bf16[64,512]{1,0:T(8,128)(2,1)S(1)} %get-tuple-element.21), channel_id=1, source_target_pairs={{0,8},{4,12},{8,0},{12,4},{1,9},{5,13},{9,1},{13,5},{2,10},{6,14},... | collective-permute-start | bytes 196616 | tf_op jit(solution)/shard_map/ppermute | solution.py:223
  23.8 1.8 %collective-permute-start.10 = (bf16[64,512]{1,0:T(8,128)(2,1)S(1)}, bf16[64,512]{1,0:T(8,128)(2,1)S(1)}, u32[]{:S(2)}, u32[]{:S(2)}) collective-permute-start(bf16[64,512]{1,0:T(8,128)(2,1)S(1)} %get-tuple-element.22), channel_id=1, source_target_pairs={{0,12},{4,8},{8,4},{12,0},{1,13},{5,9},{9,5},{13,1},{2,14},{6,10},... | collective-permute-start | bytes 196616 | tf_op jit(solution)/shard_map/ppermute | solution.py:223
  25.6 0.3 %collective-permute-start.11 = (bf16[64,512]{1,0:T(8,128)(2,1)S(1)}, bf16[64,512]{1,0:T(8,128)(2,1)S(1)}, u32[]{:S(2)}, u32[]{:S(2)}) collective-permute-start(bf16[64,512]{1,0:T(8,128)(2,1)S(1)} %get-tuple-element.23), channel_id=1, source_target_pairs={{0,4},{4,0},{8,12},{12,8},{1,5},{5,1},{9,13},{13,9},{2,6},{6,2},{1... | collective-permute-start | bytes 196616 | tf_op jit(solution)/shard_map/ppermute | solution.py:223
  25.9 0.9 %collective-permute-done.8.refs_3_ = bf16[192,512]{1,0:T(8,128)(2,1)S(1)} collective-permute-done((bf16[192,512]{1,0:T(8,128)(2,1)S(1)}, bf16[192,512]{1,0:T(8,128)(2,1)S(1)}, u32[]{:S(2)}, u32[]{:S(2)}) %collective-permute-start.8) | collective-permute-done | bytes 196640 | tf_op jit(solution)/shard_map/ppermute | solution.py:226
  26.8 0.3 shard_map.46
  27.1 1.6 %collective-permute-done.9.refs_1_ = bf16[64,512]{1,0:T(8,128)(2,1)S(1)} collective-permute-done((bf16[64,512]{1,0:T(8,128)(2,1)S(1)}, bf16[64,512]{1,0:T(8,128)(2,1)S(1)}, u32[]{:S(2)}, u32[]{:S(2)}) %collective-permute-start.9) | collective-permute-done | bytes 65568 | tf_op jit(solution)/shard_map/ppermute | solution.py:223
  28.7 1.3 %collective-permute-done.10.refs_2_ = bf16[64,512]{1,0:T(8,128)(2,1)S(1)} collective-permute-done((bf16[64,512]{1,0:T(8,128)(2,1)S(1)}, bf16[64,512]{1,0:T(8,128)(2,1)S(1)}, u32[]{:S(2)}, u32[]{:S(2)}) %collective-permute-start.10) | collective-permute-done | bytes 65568 | tf_op jit(solution)/shard_map/ppermute | solution.py:223
  30.0 0.6 %collective-permute-done.11.refs_4_ = bf16[64,512]{1,0:T(8,128)(2,1)S(1)} collective-permute-done((bf16[64,512]{1,0:T(8,128)(2,1)S(1)}, bf16[64,512]{1,0:T(8,128)(2,1)S(1)}, u32[]{:S(2)}, u32[]{:S(2)}) %collective-permute-start.11) | collective-permute-done | bytes 65568 | tf_op jit(solution)/shard_map/ppermute | solution.py:223
  30.6 0.1 shard_map.47
  30.7 0.1 collective-permute-start.12
  30.7 1.6 %collective-permute-done.12.refs_1_ = f32[144,512]{1,0:T(8,128)S(1)} collective-permute-done((f32[144,512]{1,0:T(8,128)S(1)}, f32[144,512]{1,0:T(8,128)S(1)}, u32[]{:S(2)}, u32[]{:S(2)}) %collective-permute-start.12) | collective-permute-done | bytes 294944 | tf_op jit(solution)/shard_map/ppermute | solution.py:229
  32.3 1.1 %shard_map.48 = f32[64,512]{1,0:T(8,128)} custom-call(f32[144,512]{1,0:T(8,128)S(1)} %get-tuple-element.24.refs_0_, f32[144,512]{1,0:T(8,128)S(1)} %collective-permute-done.12.refs_1_, f32[8,512]{1,0:T(8,128)S(1)} %get-tuple-element.25.refs_2_, bf16[64,512]{1,0:T(8,128)(2,1)S(1)} %copy-done.2, bf16[1,64]{1,0:T(2,128)(2,1)S(1)} %bitcast.2, ...), custom_call_target="tpu_custom_call" | custom-call | tf_op jit(solution)/shard_map/pallas_call | solution.py:22
  (7 shorter events, 0.1 us)
Async XLA Ops:
  0.0 0.9 %copy-start = (bf16[64,2048]{1,0:T(8,128)(2,1)S(1)}, bf16[64,2048]{1,0:T(8,128)(2,1)}, u32[]{:S(2)}) copy-start(bf16[64,2048]{1,0:T(8,128)(2,1)} %refs_0_.5) | copy-start | bytes 786436
  1.0 5.1 %copy-start.2 = (bf16[64,512]{1,0:T(8,128)(2,1)S(1)}, bf16[64,512]{1,0:T(8,128)(2,1)}, u32[]{:S(2)}) copy-start(bf16[64,512]{1,0:T(8,128)(2,1)} %refs_3_.1) | copy-start | bytes 196612
  1.0 7.6 %collective-permute-start = (bf16[64,512]{1,0:T(8,128)(2,1)S(1)}, bf16[64,512]{1,0:T(8,128)(2,1)S(1)}, u32[]{:S(2)}, u32[]{:S(2)}) collective-permute-start(bf16[64,512]{1,0:T(8,128)(2,1)S(1)} %get-tuple-element.16), channel_id=1, source_target_pairs={{0,12},{4,8},{8,4},{12,0},{1,13},{5,9},{9,5},{13,1},{2,14},{6,10},... | collective-permute-start | bytes 196616 | tf_op jit(solution)/shard_map/ppermute | solution.py:223
  6.1 2.5 %copy-start.1 = (bf16[64,2048]{1,0:T(8,128)(2,1)S(1)}, bf16[64,2048]{1,0:T(8,128)(2,1)}, u32[]{:S(2)}) copy-start(bf16[64,2048]{1,0:T(8,128)(2,1)} %refs_0_.5) | copy-start | bytes 786436
  6.1 8.4 %collective-permute-start.2 = (bf16[128,512]{1,0:T(8,128)(2,1)S(1)}, bf16[128,512]{1,0:T(8,128)(2,1)S(1)}, u32[]{:S(2)}, u32[]{:S(2)}) collective-permute-start(bf16[128,512]{1,0:T(8,128)(2,1)S(1)} %shard_map.40), channel_id=1, source_target_pairs={{0,8},{4,12},{8,0},{12,4},{1,9},{5,13},{9,1},{13,5},{2,10},{6,14},... | collective-permute-start | bytes 393224 | tf_op jit(solution)/shard_map/ppermute | solution.py:223
  6.2 2.4 %copy-start.3 = (bf16[64]{0:T(256)(128)(2,1)S(1)}, bf16[64]{0:T(256)(128)(2,1)}, u32[]{:S(2)}) copy-start(bf16[64]{0:T(256)(128)(2,1)} %param.5) | copy-start | bytes 388
  6.2 9.8 %collective-permute-start.1 = (bf16[128,512]{1,0:T(8,128)(2,1)S(1)}, bf16[128,512]{1,0:T(8,128)(2,1)S(1)}, u32[]{:S(2)}, u32[]{:S(2)}) collective-permute-start(bf16[128,512]{1,0:T(8,128)(2,1)S(1)} %shard_map.39), channel_id=1, source_target_pairs={{0,4},{4,0},{8,12},{12,8},{1,5},{5,1},{9,13},{13,9},{2,6},{6,2},{1... | collective-permute-start | bytes 393224 | tf_op jit(solution)/shard_map/ppermute | solution.py:223
  8.9 11.5 %collective-permute-start.6 = (bf16[144,512]{1,0:T(8,128)(2,1)S(1)}, bf16[144,512]{1,0:T(8,128)(2,1)S(1)}, u32[]{:S(2)}, u32[]{:S(2)}) collective-permute-start(bf16[144,512]{1,0:T(8,128)(2,1)S(1)} %shard_map.38.refs_4_.refs_0_), channel_id=1, source_target_pairs={{0,2},{2,0},{1,3},{3,1},{4,6},{6,4},{5,7},{7,5},{8,10},{10,8},{9,1... | collective-permute-start | bytes 442376 | tf_op jit(solution)/shard_map/ppermute | solution.py:226
  10.9 6.4 %collective-permute-start.5 = (bf16[64,512]{1,0:T(8,128)(2,1)S(1)}, bf16[64,512]{1,0:T(8,128)(2,1)S(1)}, u32[]{:S(2)}, u32[]{:S(2)}) collective-permute-start(bf16[64,512]{1,0:T(8,128)(2,1)S(1)} %collective-permute-done.refs_3_.refs_2_), channel_id=1, source_target_pairs={{0,2},{2,0},{1,3},{3,1},{4,6},{6,4},{5,7},{7,5},{8,10},{10,8},{9,1... | collective-permute-start | bytes 196616 | tf_op jit(solution)/shard_map/ppermute | solution.py:226
  14.5 4.7 %collective-permute-start.4 = (bf16[64,512]{1,0:T(8,128)(2,1)S(1)}, bf16[64,512]{1,0:T(8,128)(2,1)S(1)}, u32[]{:S(2)}, u32[]{:S(2)}) collective-permute-start(bf16[64,512]{1,0:T(8,128)(2,1)S(1)} %shard_map.42.refs_0_), channel_id=1, source_target_pairs={{0,2},{2,0},{1,3},{3,1},{4,6},{6,4},{5,7},{7,5},{8,10},{10,8},{9,1... | collective-permute-start | bytes 196616 | tf_op jit(solution)/shard_map/ppermute | solution.py:226
  16.0 4.3 %collective-permute-start.7 = (bf16[64,512]{1,0:T(8,128)(2,1)S(1)}, bf16[64,512]{1,0:T(8,128)(2,1)S(1)}, u32[]{:S(2)}, u32[]{:S(2)}) collective-permute-start(bf16[64,512]{1,0:T(8,128)(2,1)S(1)} %shard_map.43.refs_6_), channel_id=1, source_target_pairs={{0,2},{2,0},{1,3},{3,1},{4,6},{6,4},{5,7},{7,5},{8,10},{10,8},{9,1... | collective-permute-start | bytes 196616 | tf_op jit(solution)/shard_map/ppermute | solution.py:226
  16.6 4.3 %collective-permute-start.3 = (bf16[64,512]{1,0:T(8,128)(2,1)S(1)}, bf16[64,512]{1,0:T(8,128)(2,1)S(1)}, u32[]{:S(2)}, u32[]{:S(2)}) collective-permute-start(bf16[64,512]{1,0:T(8,128)(2,1)S(1)} %shard_map.41), channel_id=1, source_target_pairs={{0,4},{4,0},{8,12},{12,8},{1,5},{5,1},{9,13},{13,9},{2,6},{6,2},{1... | collective-permute-start | bytes 196616 | tf_op jit(solution)/shard_map/ppermute | solution.py:223
  20.9 5.9 %collective-permute-start.8 = (bf16[192,512]{1,0:T(8,128)(2,1)S(1)}, bf16[192,512]{1,0:T(8,128)(2,1)S(1)}, u32[]{:S(2)}, u32[]{:S(2)}) collective-permute-start(bf16[192,512]{1,0:T(8,128)(2,1)S(1)} %shard_map.45.refs_1_), channel_id=1, source_target_pairs={{0,2},{2,0},{1,3},{3,1},{4,6},{6,4},{5,7},{7,5},{8,10},{10,8},{9,1... | collective-permute-start | bytes 589832 | tf_op jit(solution)/shard_map/ppermute | solution.py:226
  22.5 6.2 %collective-permute-start.9 = (bf16[64,512]{1,0:T(8,128)(2,1)S(1)}, bf16[64,512]{1,0:T(8,128)(2,1)S(1)}, u32[]{:S(2)}, u32[]{:S(2)}) collective-permute-start(bf16[64,512]{1,0:T(8,128)(2,1)S(1)} %get-tuple-element.21), channel_id=1, source_target_pairs={{0,8},{4,12},{8,0},{12,4},{1,9},{5,13},{9,1},{13,5},{2,10},{6,14},... | collective-permute-start | bytes 196616 | tf_op jit(solution)/shard_map/ppermute | solution.py:223
  23.8 6.2 %collective-permute-start.10 = (bf16[64,512]{1,0:T(8,128)(2,1)S(1)}, bf16[64,512]{1,0:T(8,128)(2,1)S(1)}, u32[]{:S(2)}, u32[]{:S(2)}) collective-permute-start(bf16[64,512]{1,0:T(8,128)(2,1)S(1)} %get-tuple-element.22), channel_id=1, source_target_pairs={{0,12},{4,8},{8,4},{12,0},{1,13},{5,9},{9,5},{13,1},{2,14},{6,10},... | collective-permute-start | bytes 196616 | tf_op jit(solution)/shard_map/ppermute | solution.py:223
  25.6 5.0 %collective-permute-start.11 = (bf16[64,512]{1,0:T(8,128)(2,1)S(1)}, bf16[64,512]{1,0:T(8,128)(2,1)S(1)}, u32[]{:S(2)}, u32[]{:S(2)}) collective-permute-start(bf16[64,512]{1,0:T(8,128)(2,1)S(1)} %get-tuple-element.23), channel_id=1, source_target_pairs={{0,4},{4,0},{8,12},{12,8},{1,5},{5,1},{9,13},{13,9},{2,6},{6,2},{1... | collective-permute-start | bytes 196616 | tf_op jit(solution)/shard_map/ppermute | solution.py:223
  30.7 1.7 %collective-permute-start.12 = (f32[144,512]{1,0:T(8,128)S(1)}, f32[144,512]{1,0:T(8,128)S(1)}, u32[]{:S(2)}, u32[]{:S(2)}) collective-permute-start(f32[144,512]{1,0:T(8,128)S(1)} %get-tuple-element.24.refs_0_), channel_id=1, source_target_pairs={{0,1},{1,0},{2,3},{3,2},{4,5},{5,4},{6,7},{7,6},{8,9},{9,8},{10,11... | collective-permute-start | bytes 884744 | tf_op jit(solution)/shard_map/ppermute | solution.py:229

commit v21 on v20

--- a/solution.py
+++ b/solution.py
@@ -252,12 +252,14 @@
         [teacher, student, scale],
         after=[came[nrow - 1]],
     )
-    columns = {0: with_columns(own)}
+    columns, taken = {0: with_columns(own)}, ()
     for k in range(1, nrow):
         piece = came[k]
         if k in riders:
-            piece = call(functools.partial(take_kernel, rows), sds((rows, part), BF16), [piece])
+            piece = call(functools.partial(take_kernel, rows), sds((rows, part), BF16), [piece], after=taken)
         columns[k] = with_columns(piece)
+        if k == 1:
+            taken = columns[k][1:2]
     partial = call(
         functools.partial(gram_kernel, nrow, ncol, rows, order),
         [sds((rows, batch), BF16 if k else F32) for k in range(nrow)],

time: 33.6 us -> 38.5 us (1.15)
  waiting for transfers between devices: 13.4 us -> 17.9 us
  local copies, waits for them, and re-layouts: 0.96 us -> 1.78 us
    ppermute x5, waiting for transfers between devices: 3.9 us -> 6.86 us  [along_col(): return lax.ppermute(x, 'col', [(i, (i - c) % ncol) for i in range(ncol)])]
    ppermute x7, waiting for transfers between devices: 7.98 us -> 9.45 us  [along_row(): return lax.ppermute(x, 'row', [(i, i ^ k) for i in range(nrow)])]
    unnamed x8, local copies, waits for them, and re-layouts: 0.96 us -> 1.78 us
  transfers between devices with their start and end apart: 13 -> 13, of which waited for: 9 -> 8; matrix products, arithmetic and copies ran while one was open for 0% -> 0% of each run, Pallas kernels for 3% -> 3%
where the time goes in v21:
time: 38.5 us; the launch traced here: 38.3 us
  waiting for transfers between devices  17.9 us (46%)
  starting transfers between devices  16.2 us (42%)
  Pallas kernels  2.4 us (6%)
  local copies, waits for them, and re-layouts  1.78 us (5%)
    ppermute x7, starting transfers between devices, along_row(): return lax.ppermute(x, 'row', [(i, i ^ k) for i in range(nrow)])  10.4 us
    ppermute x7, waiting for transfers between devices, along_row(): return lax.ppermute(x, 'row', [(i, i ^ k) for i in range(nrow)])  9.45 us
    ppermute x5, waiting for transfers between devices, along_col(): return lax.ppermute(x, 'col', [(i, (i - c) % ncol) for i in range(ncol)])  6.86 us
    ppermute x5, starting transfers between devices, along_col(): return lax.ppermute(x, 'col', [(i, (i - c) % ncol) for i in range(ncol)])  5.66 us
    pallas_call x12, Pallas kernels, call(): pl.pallas_call(run, out_shape=out_shape, in_specs=[pl.BlockSpec(memory_sp...  2.4 us
    unnamed x8, local copies, waits for them, and re-layouts  1.78 us
    ppermute x1, waiting for transfers between devices, other_core(): return lax.ppermute(x, 'sub', [(0, 1), (1, 0)])  1.57 us
  transfers between devices with their start and end apart: 13, of which 8 were waited for; matrix products, arithmetic and copies ran while one was open for 0% of the time, Pallas kernels for 3%

profile of v21, /device:TPU:0, one launch (start us, length us, event | category | flops | bytes accessed | tf_op | source)
XLA Modules:
  0.0 38.3 jit_solution(10940938665861279622)
XLA Ops:
  0.0 0.0 copy-start
  0.0 0.9 %copy-done = bf16[64,2048]{1,0:T(8,128)(2,1)S(1)} copy-done((bf16[64,2048]{1,0:T(8,128)(2,1)S(1)}, bf16[64,2048]{1,0:T(8,128)(2,1)}, u32[]{:S(2)}) %copy-start) | copy-done | bytes 262168
  1.0 0.0 copy-start.2
  1.0 0.8 %copy-done.2 = bf16[64,512]{1,0:T(8,128)(2,1)S(1)} copy-done((bf16[64,512]{1,0:T(8,128)(2,1)S(1)}, bf16[64,512]{1,0:T(8,128)(2,1)}, u32[]{:S(2)}) %copy-start.2) | copy-done | bytes 65560
  1.8 0.0 copy-start.1
  1.8 3.1 %collective-permute-start.1 = (bf16[128,512]{1,0:T(8,128)(2,1)S(1)}, bf16[128,512]{1,0:T(8,128)(2,1)S(1)}, u32[]{:S(2)}, u32[]{:S(2)}) collective-permute-start(bf16[128,512]{1,0:T(8,128)(2,1)S(1)} %shard_map.39), channel_id=1, source_target_pairs={{0,4},{4,0},{8,12},{12,8},{1,5},{5,1},{9,13},{13,9},{2,6},{6,2},{1... | collective-permute-start | bytes 393224 | tf_op jit(solution)/shard_map/ppermute | solution.py:223
  4.9 2.5 %collective-permute-start = (bf16[64,512]{1,0:T(8,128)(2,1)S(1)}, bf16[64,512]{1,0:T(8,128)(2,1)S(1)}, u32[]{:S(2)}, u32[]{:S(2)}) collective-permute-start(bf16[64,512]{1,0:T(8,128)(2,1)S(1)} %get-tuple-element.16), channel_id=1, source_target_pairs={{0,12},{4,8},{8,4},{12,0},{1,13},{5,9},{9,5},{13,1},{2,14},{6,10},... | collective-permute-start | bytes 196616 | tf_op jit(solution)/shard_map/ppermute | solution.py:223
  7.4 0.0 copy-start.3
  7.4 0.2 collective-permute-start.2
  7.6 5.7 %collective-permute-done.refs_3_.refs_2_ = bf16[64,512]{1,0:T(8,128)(2,1)S(1)} collective-permute-done((bf16[64,512]{1,0:T(8,128)(2,1)S(1)}, bf16[64,512]{1,0:T(8,128)(2,1)S(1)}, u32[]{:S(2)}, u32[]{:S(2)}) %collective-permute-start) | collective-permute-done | bytes 65568 | tf_op jit(solution)/shard_map/ppermute | solution.py:223
  13.2 0.0 copy-done.1
  13.2 0.0 copy-done.3
  13.2 0.3 shard_map.38.refs_4_.refs_0_
  13.5 1.6 %collective-permute-start.7 = (bf16[144,512]{1,0:T(8,128)(2,1)S(1)}, bf16[144,512]{1,0:T(8,128)(2,1)S(1)}, u32[]{:S(2)}, u32[]{:S(2)}) collective-permute-start(bf16[144,512]{1,0:T(8,128)(2,1)S(1)} %shard_map.38.refs_4_.refs_0_), channel_id=1, source_target_pairs={{0,2},{2,0},{1,3},{3,1},{4,6},{6,4},{5,7},{7,5},{8,10},{10,8},{9,1... | collective-permute-start | bytes 442376 | tf_op jit(solution)/shard_map/ppermute | solution.py:226
  15.1 0.0 collective-permute-done.1.refs_0_
  15.1 0.6 %collective-permute-start.4 = (bf16[64,512]{1,0:T(8,128)(2,1)S(1)}, bf16[64,512]{1,0:T(8,128)(2,1)S(1)}, u32[]{:S(2)}, u32[]{:S(2)}) collective-permute-start(bf16[64,512]{1,0:T(8,128)(2,1)S(1)} %shard_map.42.refs_6_), channel_id=1, source_target_pairs={{0,2},{2,0},{1,3},{3,1},{4,6},{6,4},{5,7},{7,5},{8,10},{10,8},{9,1... | collective-permute-start | bytes 196616 | tf_op jit(solution)/shard_map/ppermute | solution.py:226
  15.7 1.5 %collective-permute-start.6 = (bf16[64,512]{1,0:T(8,128)(2,1)S(1)}, bf16[64,512]{1,0:T(8,128)(2,1)S(1)}, u32[]{:S(2)}, u32[]{:S(2)}) collective-permute-start(bf16[64,512]{1,0:T(8,128)(2,1)S(1)} %collective-permute-done.refs_3_.refs_2_), channel_id=1, source_target_pairs={{0,2},{2,0},{1,3},{3,1},{4,6},{6,4},{5,7},{7,5},{8,10},{10,8},{9,1... | collective-permute-start | bytes 196616 | tf_op jit(solution)/shard_map/ppermute | solution.py:226
  17.2 0.0 collective-permute-done.2.refs_0_.refs_1_
  17.2 2.9 %collective-permute-done.4.refs_1_.refs_7_ = bf16[64,512]{1,0:T(8,128)(2,1)S(1)} collective-permute-done((bf16[64,512]{1,0:T(8,128)(2,1)S(1)}, bf16[64,512]{1,0:T(8,128)(2,1)S(1)}, u32[]{:S(2)}, u32[]{:S(2)}) %collective-permute-start.4) | collective-permute-done | bytes 65568 | tf_op jit(solution)/shard_map/ppermute | solution.py:226
  20.0 1.5 %collective-permute-start.5 = (bf16[64,512]{1,0:T(8,128)(2,1)S(1)}, bf16[64,512]{1,0:T(8,128)(2,1)S(1)}, u32[]{:S(2)}, u32[]{:S(2)}) collective-permute-start(bf16[64,512]{1,0:T(8,128)(2,1)S(1)} %shard_map.43.refs_0_), channel_id=1, source_target_pairs={{0,2},{2,0},{1,3},{3,1},{4,6},{6,4},{5,7},{7,5},{8,10},{10,8},{9,1... | collective-permute-start | bytes 196616 | tf_op jit(solution)/shard_map/ppermute | solution.py:226
  21.5 1.2 %collective-permute-start.3 = (bf16[64,512]{1,0:T(8,128)(2,1)S(1)}, bf16[64,512]{1,0:T(8,128)(2,1)S(1)}, u32[]{:S(2)}, u32[]{:S(2)}) collective-permute-start(bf16[64,512]{1,0:T(8,128)(2,1)S(1)} %shard_map.41), channel_id=1, source_target_pairs={{0,4},{4,0},{8,12},{12,8},{1,5},{5,1},{9,13},{13,9},{2,6},{6,2},{1... | collective-permute-start | bytes 196616 | tf_op jit(solution)/shard_map/ppermute | solution.py:223
  22.7 0.0 collective-permute-done.6.refs_3_
  22.7 0.0 collective-permute-done.7.refs_5_.refs_2_
  22.8 2.3 %collective-permute-done.5.refs_1_ = bf16[64,512]{1,0:T(8,128)(2,1)S(1)} collective-permute-done((bf16[64,512]{1,0:T(8,128)(2,1)S(1)}, bf16[64,512]{1,0:T(8,128)(2,1)S(1)}, u32[]{:S(2)}, u32[]{:S(2)}) %collective-permute-start.5) | collective-permute-done | bytes 65568 | tf_op jit(solution)/shard_map/ppermute | solution.py:226
  25.0 0.5 %shard_map.44 = (f32[64,512]{1,0:T(8,128)S(1)}, bf16[64,512]{1,0:T(8,128)(2,1)S(1)}, bf16[64,512]{1,0:T(8,128)(2,1)S(1)}, bf16[64,512]{1,0:T(8,128)(2,1)S(1)}) custom-call(bf16[64,512]{1,0:T(8,128)(2,1)S(1)} %shard_map.43.refs_0_, bf16[64,512]{1,0:T(8,128)(2,1)S(1)} %collective-permute-done.5.refs_1_, ...), custom_call_target="tpu_custom_call" | custom-call | tf_op jit(solution)/shard_map/pallas_call | solution.py:22
  25.5 1.0 %collective-permute-done.3.refs_2_ = bf16[64,512]{1,0:T(8,128)(2,1)S(1)} collective-permute-done((bf16[64,512]{1,0:T(8,128)(2,1)S(1)}, bf16[64,512]{1,0:T(8,128)(2,1)S(1)}, u32[]{:S(2)}, u32[]{:S(2)}) %collective-permute-start.3) | collective-permute-done | bytes 65568 | tf_op jit(solution)/shard_map/ppermute | solution.py:223
  26.6 0.5 %collective-permute-start.8 = (bf16[192,512]{1,0:T(8,128)(2,1)S(1)}, bf16[192,512]{1,0:T(8,128)(2,1)S(1)}, u32[]{:S(2)}, u32[]{:S(2)}) collective-permute-start(bf16[192,512]{1,0:T(8,128)(2,1)S(1)} %shard_map.45.refs_1_), channel_id=1, source_target_pairs={{0,2},{2,0},{1,3},{3,1},{4,6},{6,4},{5,7},{7,5},{8,10},{10,8},{9,1... | collective-permute-start | bytes 589832 | tf_op jit(solution)/shard_map/ppermute | solution.py:226
  27.1 2.2 %collective-permute-start.9 = (bf16[64,512]{1,0:T(8,128)(2,1)S(1)}, bf16[64,512]{1,0:T(8,128)(2,1)S(1)}, u32[]{:S(2)}, u32[]{:S(2)}) collective-permute-start(bf16[64,512]{1,0:T(8,128)(2,1)S(1)} %get-tuple-element.21), channel_id=1, source_target_pairs={{0,8},{4,12},{8,0},{12,4},{1,9},{5,13},{9,1},{13,5},{2,10},{6,14},... | collective-permute-start | bytes 196616 | tf_op jit(solution)/shard_map/ppermute | solution.py:223
  29.3 1.1 %collective-permute-start.10 = (bf16[64,512]{1,0:T(8,128)(2,1)S(1)}, bf16[64,512]{1,0:T(8,128)(2,1)S(1)}, u32[]{:S(2)}, u32[]{:S(2)}) collective-permute-start(bf16[64,512]{1,0:T(8,128)(2,1)S(1)} %get-tuple-element.22), channel_id=1, source_target_pairs={{0,12},{4,8},{8,4},{12,0},{1,13},{5,9},{9,5},{13,1},{2,14},{6,10},... | collective-permute-start | bytes 196616 | tf_op jit(solution)/shard_map/ppermute | solution.py:223
  30.5 0.2 collective-permute-start.11
  30.6 1.7 %collective-permute-done.8.refs_3_ = bf16[192,512]{1,0:T(8,128)(2,1)S(1)} collective-permute-done((bf16[192,512]{1,0:T(8,128)(2,1)S(1)}, bf16[192,512]{1,0:T(8,128)(2,1)S(1)}, u32[]{:S(2)}, u32[]{:S(2)}) %collective-permute-start.8) | collective-permute-done | bytes 196640 | tf_op jit(solution)/shard_map/ppermute | solution.py:226
  32.3 0.3 shard_map.46
  32.7 0.3 collective-permute-done.9.refs_1_
  33.0 2.4 %collective-permute-done.10.refs_2_ = bf16[64,512]{1,0:T(8,128)(2,1)S(1)} collective-permute-done((bf16[64,512]{1,0:T(8,128)(2,1)S(1)}, bf16[64,512]{1,0:T(8,128)(2,1)S(1)}, u32[]{:S(2)}, u32[]{:S(2)}) %collective-permute-start.10) | collective-permute-done | bytes 65568 | tf_op jit(solution)/shard_map/ppermute | solution.py:223
  35.4 0.0 collective-permute-done.11.refs_4_
  35.4 0.1 shard_map.47
  35.5 0.1 collective-permute-start.12
  35.6 1.6 %collective-permute-done.12.refs_1_ = f32[144,512]{1,0:T(8,128)S(1)} collective-permute-done((f32[144,512]{1,0:T(8,128)S(1)}, f32[144,512]{1,0:T(8,128)S(1)}, u32[]{:S(2)}, u32[]{:S(2)}) %collective-permute-start.12) | collective-permute-done | bytes 294944 | tf_op jit(solution)/shard_map/ppermute | solution.py:229
  37.2 1.1 %shard_map.48 = f32[64,512]{1,0:T(8,128)} custom-call(f32[144,512]{1,0:T(8,128)S(1)} %get-tuple-element.24.refs_0_, f32[144,512]{1,0:T(8,128)S(1)} %collective-permute-done.12.refs_1_, f32[8,512]{1,0:T(8,128)S(1)} %get-tuple-element.25.refs_2_, bf16[64,512]{1,0:T(8,128)(2,1)S(1)} %copy-done.2, bf16[1,64]{1,0:T(2,128)(2,1)S(1)} %bitcast.2, ...), custom_call_target="tpu_custom_call" | custom-call | tf_op jit(solution)/shard_map/pallas_call | solution.py:22
  (7 shorter events, 0.1 us)
Async XLA Ops:
  0.0 0.9 %copy-start = (bf16[64,2048]{1,0:T(8,128)(2,1)S(1)}, bf16[64,2048]{1,0:T(8,128)(2,1)}, u32[]{:S(2)}) copy-start(bf16[64,2048]{1,0:T(8,128)(2,1)} %refs_0_.5) | copy-start | bytes 786436
  1.0 0.8 %copy-start.2 = (bf16[64,512]{1,0:T(8,128)(2,1)S(1)}, bf16[64,512]{1,0:T(8,128)(2,1)}, u32[]{:S(2)}) copy-start(bf16[64,512]{1,0:T(8,128)(2,1)} %refs_3_.1) | copy-start | bytes 196612
  1.8 11.4 %copy-start.1 = (bf16[64,2048]{1,0:T(8,128)(2,1)S(1)}, bf16[64,2048]{1,0:T(8,128)(2,1)}, u32[]{:S(2)}) copy-start(bf16[64,2048]{1,0:T(8,128)(2,1)} %refs_0_.5) | copy-start | bytes 786436
  1.8 13.3 %collective-permute-start.1 = (bf16[128,512]{1,0:T(8,128)(2,1)S(1)}, bf16[128,512]{1,0:T(8,128)(2,1)S(1)}, u32[]{:S(2)}, u32[]{:S(2)}) collective-permute-start(bf16[128,512]{1,0:T(8,128)(2,1)S(1)} %shard_map.39), channel_id=1, source_target_pairs={{0,4},{4,0},{8,12},{12,8},{1,5},{5,1},{9,13},{13,9},{2,6},{6,2},{1... | collective-permute-start | bytes 393224 | tf_op jit(solution)/shard_map/ppermute | solution.py:223
  4.9 8.3 %collective-permute-start = (bf16[64,512]{1,0:T(8,128)(2,1)S(1)}, bf16[64,512]{1,0:T(8,128)(2,1)S(1)}, u32[]{:S(2)}, u32[]{:S(2)}) collective-permute-start(bf16[64,512]{1,0:T(8,128)(2,1)S(1)} %get-tuple-element.16), channel_id=1, source_target_pairs={{0,12},{4,8},{8,4},{12,0},{1,13},{5,9},{9,5},{13,1},{2,14},{6,10},... | collective-permute-start | bytes 196616 | tf_op jit(solution)/shard_map/ppermute | solution.py:223
  7.4 5.9 %copy-start.3 = (bf16[64]{0:T(256)(128)(2,1)S(1)}, bf16[64]{0:T(256)(128)(2,1)}, u32[]{:S(2)}) copy-start(bf16[64]{0:T(256)(128)(2,1)} %param.5) | copy-start | bytes 388
  7.4 9.8 %collective-permute-start.2 = (bf16[128,512]{1,0:T(8,128)(2,1)S(1)}, bf16[128,512]{1,0:T(8,128)(2,1)S(1)}, u32[]{:S(2)}, u32[]{:S(2)}) collective-permute-start(bf16[128,512]{1,0:T(8,128)(2,1)S(1)} %shard_map.40), channel_id=1, source_target_pairs={{0,8},{4,12},{8,0},{12,4},{1,9},{5,13},{9,1},{13,5},{2,10},{6,14},... | collective-permute-start | bytes 393224 | tf_op jit(solution)/shard_map/ppermute | solution.py:223
  13.5 9.2 %collective-permute-start.7 = (bf16[144,512]{1,0:T(8,128)(2,1)S(1)}, bf16[144,512]{1,0:T(8,128)(2,1)S(1)}, u32[]{:S(2)}, u32[]{:S(2)}) collective-permute-start(bf16[144,512]{1,0:T(8,128)(2,1)S(1)} %shard_map.38.refs_4_.refs_0_), channel_id=1, source_target_pairs={{0,2},{2,0},{1,3},{3,1},{4,6},{6,4},{5,7},{7,5},{8,10},{10,8},{9,1... | collective-permute-start | bytes 442376 | tf_op jit(solution)/shard_map/ppermute | solution.py:226
  15.1 5.0 %collective-permute-start.4 = (bf16[64,512]{1,0:T(8,128)(2,1)S(1)}, bf16[64,512]{1,0:T(8,128)(2,1)S(1)}, u32[]{:S(2)}, u32[]{:S(2)}) collective-permute-start(bf16[64,512]{1,0:T(8,128)(2,1)S(1)} %shard_map.42.refs_6_), channel_id=1, source_target_pairs={{0,2},{2,0},{1,3},{3,1},{4,6},{6,4},{5,7},{7,5},{8,10},{10,8},{9,1... | collective-permute-start | bytes 196616 | tf_op jit(solution)/shard_map/ppermute | solution.py:226
  15.7 7.1 %collective-permute-start.6 = (bf16[64,512]{1,0:T(8,128)(2,1)S(1)}, bf16[64,512]{1,0:T(8,128)(2,1)S(1)}, u32[]{:S(2)}, u32[]{:S(2)}) collective-permute-start(bf16[64,512]{1,0:T(8,128)(2,1)S(1)} %collective-permute-done.refs_3_.refs_2_), channel_id=1, source_target_pairs={{0,2},{2,0},{1,3},{3,1},{4,6},{6,4},{5,7},{7,5},{8,10},{10,8},{9,1... | collective-permute-start | bytes 196616 | tf_op jit(solution)/shard_map/ppermute | solution.py:226
  20.0 5.0 %collective-permute-start.5 = (bf16[64,512]{1,0:T(8,128)(2,1)S(1)}, bf16[64,512]{1,0:T(8,128)(2,1)S(1)}, u32[]{:S(2)}, u32[]{:S(2)}) collective-permute-start(bf16[64,512]{1,0:T(8,128)(2,1)S(1)} %shard_map.43.refs_0_), channel_id=1, source_target_pairs={{0,2},{2,0},{1,3},{3,1},{4,6},{6,4},{5,7},{7,5},{8,10},{10,8},{9,1... | collective-permute-start | bytes 196616 | tf_op jit(solution)/shard_map/ppermute | solution.py:226
  21.5 5.0 %collective-permute-start.3 = (bf16[64,512]{1,0:T(8,128)(2,1)S(1)}, bf16[64,512]{1,0:T(8,128)(2,1)S(1)}, u32[]{:S(2)}, u32[]{:S(2)}) collective-permute-start(bf16[64,512]{1,0:T(8,128)(2,1)S(1)} %shard_map.41), channel_id=1, source_target_pairs={{0,4},{4,0},{8,12},{12,8},{1,5},{5,1},{9,13},{13,9},{2,6},{6,2},{1... | collective-permute-start | bytes 196616 | tf_op jit(solution)/shard_map/ppermute | solution.py:223
  26.6 5.7 %collective-permute-start.8 = (bf16[192,512]{1,0:T(8,128)(2,1)S(1)}, bf16[192,512]{1,0:T(8,128)(2,1)S(1)}, u32[]{:S(2)}, u32[]{:S(2)}) collective-permute-start(bf16[192,512]{1,0:T(8,128)(2,1)S(1)} %shard_map.45.refs_1_), channel_id=1, source_target_pairs={{0,2},{2,0},{1,3},{3,1},{4,6},{6,4},{5,7},{7,5},{8,10},{10,8},{9,1... | collective-permute-start | bytes 589832 | tf_op jit(solution)/shard_map/ppermute | solution.py:226
  27.1 5.9 %collective-permute-start.9 = (bf16[64,512]{1,0:T(8,128)(2,1)S(1)}, bf16[64,512]{1,0:T(8,128)(2,1)S(1)}, u32[]{:S(2)}, u32[]{:S(2)}) collective-permute-start(bf16[64,512]{1,0:T(8,128)(2,1)S(1)} %get-tuple-element.21), channel_id=1, source_target_pairs={{0,8},{4,12},{8,0},{12,4},{1,9},{5,13},{9,1},{13,5},{2,10},{6,14},... | collective-permute-start | bytes 196616 | tf_op jit(solution)/shard_map/ppermute | solution.py:223
  29.3 6.1 %collective-permute-start.10 = (bf16[64,512]{1,0:T(8,128)(2,1)S(1)}, bf16[64,512]{1,0:T(8,128)(2,1)S(1)}, u32[]{:S(2)}, u32[]{:S(2)}) collective-permute-start(bf16[64,512]{1,0:T(8,128)(2,1)S(1)} %get-tuple-element.22), channel_id=1, source_target_pairs={{0,12},{4,8},{8,4},{12,0},{1,13},{5,9},{9,5},{13,1},{2,14},{6,10},... | collective-permute-start | bytes 196616 | tf_op jit(solution)/shard_map/ppermute | solution.py:223
  30.5 5.0 %collective-permute-start.11 = (bf16[64,512]{1,0:T(8,128)(2,1)S(1)}, bf16[64,512]{1,0:T(8,128)(2,1)S(1)}, u32[]{:S(2)}, u32[]{:S(2)}) collective-permute-start(bf16[64,512]{1,0:T(8,128)(2,1)S(1)} %get-tuple-element.23), channel_id=1, source_target_pairs={{0,4},{4,0},{8,12},{12,8},{1,5},{5,1},{9,13},{13,9},{2,6},{6,2},{1... | collective-permute-start | bytes 196616 | tf_op jit(solution)/shard_map/ppermute | solution.py:223
  35.5 1.7 %collective-permute-start.12 = (f32[144,512]{1,0:T(8,128)S(1)}, f32[144,512]{1,0:T(8,128)S(1)}, u32[]{:S(2)}, u32[]{:S(2)}) collective-permute-start(f32[144,512]{1,0:T(8,128)S(1)} %get-tuple-element.24.refs_0_), channel_id=1, source_target_pairs={{0,1},{1,0},{2,3},{3,2},{4,5},{5,4},{6,7},{7,6},{8,9},{9,8},{10,11... | collective-permute-start | bytes 884744 | tf_op jit(solution)/shard_map/ppermute | solution.py:229

commit v22 on v8

--- a/solution.py
+++ b/solution.py
@@ -96,8 +96,9 @@
     wide(out, rows + TAIL, teach[:, pl.ds(pl.multiple_of(lax.axis_index("row") * part, part), part)])
 
 
-def take_kernel(rows, ref, out):
-    put(out, 0, rows, ref, rows)
+def take_kernel(rows, near, far, out):
+    put(out, 0, rows, near, rows)
+    put(out, rows, rows, far, rows)
 
 
 def pack_kernel(spans, *refs):
@@ -121,7 +122,7 @@
     own = order.index(0) * ncol
     for n, k in enumerate(order):
         for c in range(ncol):
-            put(held, place(nrow, ncol, rows, k, c), rows, refs[n * ncol + c], 0 if k else rows + TAIL)
+            put(held, place(nrow, ncol, rows, k, c), rows, refs[n * ncol + c], {0: rows + TAIL, nrow // 2: rows}.get(k, 0))
     for n, k in enumerate(order):
         left[n * rows : (n + 1) * rows, :] = held[pl.ds(place(nrow, ncol, rows, k, 0), rows), :]
     sub = rows // 2
@@ -250,11 +251,10 @@
         after=[came[nrow - 1]],
     )
     columns = {0: with_columns(own)}
+    pair = call(functools.partial(take_kernel, rows), sds((2 * rows, part), BF16), [came[k] for k in riders])
+    pair = with_columns(pair)
     for k in range(1, nrow):
-        piece = came[k]
-        if k in riders:
-            piece = call(functools.partial(take_kernel, rows), sds((rows, part), BF16), [piece])
-        columns[k] = with_columns(piece)
+        columns[k] = pair if k in riders else with_columns(came[k])
     partial = call(
         functools.partial(gram_kernel, nrow, ncol, rows, order),
         [sds((rows, batch), BF16 if k else F32) for k in range(nrow)],

time: 32.6 us -> 38.3 us (1.17)
  waiting for transfers between devices: 13.1 us -> 16.6 us
  starting transfers between devices: 15 us -> 17.2 us
    ppermute x7, waiting for transfers between devices: 7.18 us -> 12.1 us  [along_row(): return lax.ppermute(x, 'row', [(i, i ^ k) for i in range(nrow)])]
    ppermute x7, starting transfers between devices: 9.23 us -> 11.9 us  [along_row(): return lax.ppermute(x, 'row', [(i, i ^ k) for i in range(nrow)])]
    ppermute x5 -> x4, waiting for transfers between devices: 4.39 us -> 2.95 us  [along_col(): return lax.ppermute(x, 'col', [(i, (i - c) % ncol) for i in range(ncol)])]
    ppermute x5 -> x4, starting transfers between devices: 5.68 us -> 5.2 us  [along_col(): return lax.ppermute(x, 'col', [(i, (i - c) % ncol) for i in range(ncol)])]
    pallas_call x11 -> x10, Pallas kernels: 2.4 us -> 2.41 us  [call(): pl.pallas_call(run, out_shape=out_shape, in_specs=[pl.BlockSpec(memory_sp...]
  transfers between devices with their start and end apart: 13 -> 12, of which waited for: 11 -> 5; matrix products, arithmetic and copies ran while one was open for 0% -> 0% of each run, Pallas kernels for 4% -> 3%
where the time goes in v22:
time: 38.3 us; the launch traced here: 38.1 us
  starting transfers between devices  17.2 us (45%)
  waiting for transfers between devices  16.6 us (43%)
  Pallas kernels  2.41 us (6%)
  local copies, waits for them, and re-layouts  1.83 us (5%)
    ppermute x7, waiting for transfers between devices, along_row(): return lax.ppermute(x, 'row', [(i, i ^ k) for i in range(nrow)])  12.1 us
    ppermute x7, starting transfers between devices, along_row(): return lax.ppermute(x, 'row', [(i, i ^ k) for i in range(nrow)])  11.9 us
    ppermute x4, starting transfers between devices, along_col(): return lax.ppermute(x, 'col', [(i, (i - c) % ncol) for i in range(ncol)])  5.2 us
    ppermute x4, waiting for transfers between devices, along_col(): return lax.ppermute(x, 'col', [(i, (i - c) % ncol) for i in range(ncol)])  2.95 us
    pallas_call x10, Pallas kernels, call(): pl.pallas_call(run, out_shape=out_shape, in_specs=[pl.BlockSpec(memory_sp...  2.41 us
    unnamed x10, local copies, waits for them, and re-layouts  1.83 us
    ppermute x1, waiting for transfers between devices, other_core(): return lax.ppermute(x, 'sub', [(0, 1), (1, 0)])  1.57 us
  transfers between devices with their start and end apart: 12, of which 5 were waited for; matrix products, arithmetic and copies ran while one was open for 0% of the time, Pallas kernels for 3%

profile of v22, /device:TPU:0, one launch (start us, length us, event | category | flops | bytes accessed | tf_op | source)
XLA Modules:
  0.0 38.1 jit_solution(8046679960063499955)
XLA Ops:
  0.0 0.0 copy-start
  0.0 0.9 %copy-done = bf16[64,2048]{1,0:T(8,128)(2,1)S(1)} copy-done((bf16[64,2048]{1,0:T(8,128)(2,1)S(1)}, bf16[64,2048]{1,0:T(8,128)(2,1)}, u32[]{:S(2)}) %copy-start) | copy-done | bytes 262168
  1.0 0.0 copy-start.1
  1.0 0.0 copy-start.2
  1.0 0.9 %copy-done.2 = bf16[64,512]{1,0:T(8,128)(2,1)S(1)} copy-done((bf16[64,512]{1,0:T(8,128)(2,1)S(1)}, bf16[64,512]{1,0:T(8,128)(2,1)}, u32[]{:S(2)}) %copy-start.2) | copy-done | bytes 65560
  1.9 3.1 %collective-permute-start.1 = (bf16[128,512]{1,0:T(8,128)(2,1)S(1)}, bf16[128,512]{1,0:T(8,128)(2,1)S(1)}, u32[]{:S(2)}, u32[]{:S(2)}) collective-permute-start(bf16[128,512]{1,0:T(8,128)(2,1)S(1)} %get-tuple-element.21), channel_id=1, source_target_pairs={{0,4},{4,0},{8,12},{12,8},{1,5},{5,1},{9,13},{13,9},{2,6},{6,2},{1... | collective-permute-start | bytes 393224 | tf_op jit(solution)/shard_map/ppermute | solution.py:225
  5.0 2.6 %collective-permute-start.2 = (bf16[128,512]{1,0:T(8,128)(2,1)S(1)}, bf16[128,512]{1,0:T(8,128)(2,1)S(1)}, u32[]{:S(2)}, u32[]{:S(2)}) collective-permute-start(bf16[128,512]{1,0:T(8,128)(2,1)S(1)} %get-tuple-element.22), channel_id=1, source_target_pairs={{0,8},{4,12},{8,0},{12,4},{1,9},{5,13},{9,1},{13,5},{2,10},{6,14},... | collective-permute-start | bytes 393224 | tf_op jit(solution)/shard_map/ppermute | solution.py:225
  7.6 0.0 copy-start.4
  7.6 0.0 collective-permute-start
  7.6 7.4 %collective-permute-done.refs_3_.refs_2_ = bf16[64,512]{1,0:T(8,128)(2,1)S(1)} collective-permute-done((bf16[64,512]{1,0:T(8,128)(2,1)S(1)}, bf16[64,512]{1,0:T(8,128)(2,1)S(1)}, u32[]{:S(2)}, u32[]{:S(2)}) %collective-permute-start) | collective-permute-done | bytes 65568 | tf_op jit(solution)/shard_map/ppermute | solution.py:225
  15.0 0.0 copy-done.1
  15.0 0.0 copy-done.4
  15.0 0.3 shard_map.38.refs_4_.refs_0_
  15.2 1.6 %collective-permute-start.6 = (bf16[144,512]{1,0:T(8,128)(2,1)S(1)}, bf16[144,512]{1,0:T(8,128)(2,1)S(1)}, u32[]{:S(2)}, u32[]{:S(2)}) collective-permute-start(bf16[144,512]{1,0:T(8,128)(2,1)S(1)} %shard_map.38.refs_4_.refs_0_), channel_id=1, source_target_pairs={{0,2},{2,0},{1,3},{3,1},{4,6},{6,4},{5,7},{7,5},{8,10},{10,8},{9,1... | collective-permute-start | bytes 442376 | tf_op jit(solution)/shard_map/ppermute | solution.py:228
  16.8 0.0 collective-permute-done.1.refs_0_
  16.8 0.0 collective-permute-done.2.refs_0_.refs_1_
  16.8 0.6 %collective-permute-start.4 = (bf16[128,512]{1,0:T(8,128)(2,1)S(1)}, bf16[128,512]{1,0:T(8,128)(2,1)S(1)}, u32[]{:S(2)}, u32[]{:S(2)}) collective-permute-start(bf16[128,512]{1,0:T(8,128)(2,1)S(1)} %shard_map.41.refs_0_.refs_6_), channel_id=1, source_target_pairs={{0,2},{2,0},{1,3},{3,1},{4,6},{6,4},{5,7},{7,5},{8,10},{10,8},{9,1... | collective-permute-start | bytes 393224 | tf_op jit(solution)/shard_map/ppermute | solution.py:228
  17.4 1.5 %collective-permute-start.5 = (bf16[64,512]{1,0:T(8,128)(2,1)S(1)}, bf16[64,512]{1,0:T(8,128)(2,1)S(1)}, u32[]{:S(2)}, u32[]{:S(2)}) collective-permute-start(bf16[64,512]{1,0:T(8,128)(2,1)S(1)} %collective-permute-done.refs_3_.refs_2_), channel_id=1, source_target_pairs={{0,2},{2,0},{1,3},{3,1},{4,6},{6,4},{5,7},{7,5},{8,10},{10,8},{9,1... | collective-permute-start | bytes 196616 | tf_op jit(solution)/shard_map/ppermute | solution.py:228
  18.9 2.1 %collective-permute-start.3 = (bf16[64,512]{1,0:T(8,128)(2,1)S(1)}, bf16[64,512]{1,0:T(8,128)(2,1)S(1)}, u32[]{:S(2)}, u32[]{:S(2)}) collective-permute-start(bf16[64,512]{1,0:T(8,128)(2,1)S(1)} %shard_map.40), channel_id=1, source_target_pairs={{0,4},{4,0},{8,12},{12,8},{1,5},{5,1},{9,13},{13,9},{2,6},{6,2},{1... | collective-permute-start | bytes 196616 | tf_op jit(solution)/shard_map/ppermute | solution.py:225
  21.0 2.9 %collective-permute-done.5.refs_3_ = bf16[64,512]{1,0:T(8,128)(2,1)S(1)} collective-permute-done((bf16[64,512]{1,0:T(8,128)(2,1)S(1)}, bf16[64,512]{1,0:T(8,128)(2,1)S(1)}, u32[]{:S(2)}, u32[]{:S(2)}) %collective-permute-start.5) | collective-permute-done | bytes 65568 | tf_op jit(solution)/shard_map/ppermute | solution.py:228
  23.9 0.0 collective-permute-done.6.refs_5_.refs_2_
  23.9 0.0 collective-permute-done.4.refs_1_.refs_7_
  23.9 0.5 %shard_map.42 = (f32[64,512]{1,0:T(8,128)S(1)}, bf16[64,512]{1,0:T(8,128)(2,1)S(1)}, bf16[64,512]{1,0:T(8,128)(2,1)S(1)}, bf16[64,512]{1,0:T(8,128)(2,1)S(1)}) custom-call(bf16[128,512]{1,0:T(8,128)(2,1)S(1)} %shard_map.41.refs_0_.refs_6_, bf16[128,512]{1,0:T(8,128)(2,1)S(1)} %collective-permute-done.4.refs_1_.refs_7_, ...), custom_call_target="tpu_custom_call" | custom-call | tf_op jit(solution)/shard_map/pallas_call | solution.py:22
  24.5 0.0 collective-permute-done.3.refs_2_
  24.5 1.6 %collective-permute-start.7 = (bf16[192,512]{1,0:T(8,128)(2,1)S(1)}, bf16[192,512]{1,0:T(8,128)(2,1)S(1)}, u32[]{:S(2)}, u32[]{:S(2)}) collective-permute-start(bf16[192,512]{1,0:T(8,128)(2,1)S(1)} %shard_map.43.refs_1_), channel_id=1, source_target_pairs={{0,2},{2,0},{1,3},{3,1},{4,6},{6,4},{5,7},{7,5},{8,10},{10,8},{9,1... | collective-permute-start | bytes 589832 | tf_op jit(solution)/shard_map/ppermute | solution.py:228
  26.1 3.0 %collective-permute-start.8 = (bf16[64,512]{1,0:T(8,128)(2,1)S(1)}, bf16[64,512]{1,0:T(8,128)(2,1)S(1)}, u32[]{:S(2)}, u32[]{:S(2)}) collective-permute-start(bf16[64,512]{1,0:T(8,128)(2,1)S(1)} %get-tuple-element.25), channel_id=1, source_target_pairs={{0,8},{4,12},{8,0},{12,4},{1,9},{5,13},{9,1},{13,5},{2,10},{6,14},... | collective-permute-start | bytes 196616 | tf_op jit(solution)/shard_map/ppermute | solution.py:225
  29.1 1.2 %collective-permute-start.9 = (bf16[64,512]{1,0:T(8,128)(2,1)S(1)}, bf16[64,512]{1,0:T(8,128)(2,1)S(1)}, u32[]{:S(2)}, u32[]{:S(2)}) collective-permute-start(bf16[64,512]{1,0:T(8,128)(2,1)S(1)} %get-tuple-element.26), channel_id=1, source_target_pairs={{0,12},{4,8},{8,4},{12,0},{1,13},{5,9},{9,5},{13,1},{2,14},{6,10},... | collective-permute-start | bytes 196616 | tf_op jit(solution)/shard_map/ppermute | solution.py:225
  30.2 0.0 collective-permute-start.10
  30.2 0.0 collective-permute-done.7.refs_3_
  30.3 0.3 shard_map.44
  30.6 1.6 %collective-permute-done.8.refs_1_ = bf16[64,512]{1,0:T(8,128)(2,1)S(1)} collective-permute-done((bf16[64,512]{1,0:T(8,128)(2,1)S(1)}, bf16[64,512]{1,0:T(8,128)(2,1)S(1)}, u32[]{:S(2)}, u32[]{:S(2)}) %collective-permute-start.8) | collective-permute-done | bytes 65568 | tf_op jit(solution)/shard_map/ppermute | solution.py:225
  32.2 3.1 %collective-permute-done.9.refs_2_ = bf16[64,512]{1,0:T(8,128)(2,1)S(1)} collective-permute-done((bf16[64,512]{1,0:T(8,128)(2,1)S(1)}, bf16[64,512]{1,0:T(8,128)(2,1)S(1)}, u32[]{:S(2)}, u32[]{:S(2)}) %collective-permute-start.9) | collective-permute-done | bytes 65568 | tf_op jit(solution)/shard_map/ppermute | solution.py:225
  35.2 0.0 collective-permute-done.10.refs_4_
  35.2 0.0 copy-start.3
  35.2 0.1 shard_map.45
  35.3 0.1 collective-permute-start.11
  35.4 1.6 %collective-permute-done.11.refs_1_ = f32[144,512]{1,0:T(8,128)S(1)} collective-permute-done((f32[144,512]{1,0:T(8,128)S(1)}, f32[144,512]{1,0:T(8,128)S(1)}, u32[]{:S(2)}, u32[]{:S(2)}) %collective-permute-start.11) | collective-permute-done | bytes 294944 | tf_op jit(solution)/shard_map/ppermute | solution.py:231
  37.0 0.0 copy-done.3
  37.0 1.1 %shard_map.46 = f32[64,512]{1,0:T(8,128)} custom-call(f32[144,512]{1,0:T(8,128)S(1)} %get-tuple-element.28.refs_0_, f32[144,512]{1,0:T(8,128)S(1)} %collective-permute-done.11.refs_1_, f32[8,512]{1,0:T(8,128)S(1)} %get-tuple-element.29.refs_2_, bf16[64,512]{1,0:T(8,128)(2,1)S(1)} %copy-done.3, bf16[1,64]{1,0:T(2,128)(2,1)S(1)} %bitcast.2, ...), custom_call_target="tpu_custom_call" | custom-call | tf_op jit(solution)/shard_map/pallas_call | solution.py:22
  (5 shorter events, 0.1 us)
Async XLA Ops:
  0.0 0.9 %copy-start = (bf16[64,2048]{1,0:T(8,128)(2,1)S(1)}, bf16[64,2048]{1,0:T(8,128)(2,1)}, u32[]{:S(2)}) copy-start(bf16[64,2048]{1,0:T(8,128)(2,1)} %refs_0_.4) | copy-start | bytes 786436
  1.0 14.0 %copy-start.1 = (bf16[64,2048]{1,0:T(8,128)(2,1)S(1)}, bf16[64,2048]{1,0:T(8,128)(2,1)}, u32[]{:S(2)}) copy-start(bf16[64,2048]{1,0:T(8,128)(2,1)} %refs_0_.4) | copy-start | bytes 786436
  1.0 0.9 %copy-start.2 = (bf16[64,512]{1,0:T(8,128)(2,1)S(1)}, bf16[64,512]{1,0:T(8,128)(2,1)}, u32[]{:S(2)}) copy-start(bf16[64,512]{1,0:T(8,128)(2,1)} %refs_3_.1) | copy-start | bytes 196612
  1.9 14.9 %collective-permute-start.1 = (bf16[128,512]{1,0:T(8,128)(2,1)S(1)}, bf16[128,512]{1,0:T(8,128)(2,1)S(1)}, u32[]{:S(2)}, u32[]{:S(2)}) collective-permute-start(bf16[128,512]{1,0:T(8,128)(2,1)S(1)} %get-tuple-element.21), channel_id=1, source_target_pairs={{0,4},{4,0},{8,12},{12,8},{1,5},{5,1},{9,13},{13,9},{2,6},{6,2},{1... | collective-permute-start | bytes 393224 | tf_op jit(solution)/shard_map/ppermute | solution.py:225
  5.0 11.8 %collective-permute-start.2 = (bf16[128,512]{1,0:T(8,128)(2,1)S(1)}, bf16[128,512]{1,0:T(8,128)(2,1)S(1)}, u32[]{:S(2)}, u32[]{:S(2)}) collective-permute-start(bf16[128,512]{1,0:T(8,128)(2,1)S(1)} %get-tuple-element.22), channel_id=1, source_target_pairs={{0,8},{4,12},{8,0},{12,4},{1,9},{5,13},{9,1},{13,5},{2,10},{6,14},... | collective-permute-start | bytes 393224 | tf_op jit(solution)/shard_map/ppermute | solution.py:225
  7.6 7.4 %copy-start.4 = (bf16[64]{0:T(256)(128)(2,1)S(1)}, bf16[64]{0:T(256)(128)(2,1)}, u32[]{:S(2)}) copy-start(bf16[64]{0:T(256)(128)(2,1)} %param.5) | copy-start | bytes 388
  7.6 7.4 %collective-permute-start = (bf16[64,512]{1,0:T(8,128)(2,1)S(1)}, bf16[64,512]{1,0:T(8,128)(2,1)S(1)}, u32[]{:S(2)}, u32[]{:S(2)}) collective-permute-start(bf16[64,512]{1,0:T(8,128)(2,1)S(1)} %get-tuple-element.18), channel_id=1, source_target_pairs={{0,12},{4,8},{8,4},{12,0},{1,13},{5,9},{9,5},{13,1},{2,14},{6,10},... | collective-permute-start | bytes 196616 | tf_op jit(solution)/shard_map/ppermute | solution.py:225
  15.2 8.7 %collective-permute-start.6 = (bf16[144,512]{1,0:T(8,128)(2,1)S(1)}, bf16[144,512]{1,0:T(8,128)(2,1)S(1)}, u32[]{:S(2)}, u32[]{:S(2)}) collective-permute-start(bf16[144,512]{1,0:T(8,128)(2,1)S(1)} %shard_map.38.refs_4_.refs_0_), channel_id=1, source_target_pairs={{0,2},{2,0},{1,3},{3,1},{4,6},{6,4},{5,7},{7,5},{8,10},{10,8},{9,1... | collective-permute-start | bytes 442376 | tf_op jit(solution)/shard_map/ppermute | solution.py:228
  16.8 7.1 %collective-permute-start.4 = (bf16[128,512]{1,0:T(8,128)(2,1)S(1)}, bf16[128,512]{1,0:T(8,128)(2,1)S(1)}, u32[]{:S(2)}, u32[]{:S(2)}) collective-permute-start(bf16[128,512]{1,0:T(8,128)(2,1)S(1)} %shard_map.41.refs_0_.refs_6_), channel_id=1, source_target_pairs={{0,2},{2,0},{1,3},{3,1},{4,6},{6,4},{5,7},{7,5},{8,10},{10,8},{9,1... | collective-permute-start | bytes 393224 | tf_op jit(solution)/shard_map/ppermute | solution.py:228
  17.4 6.5 %collective-permute-start.5 = (bf16[64,512]{1,0:T(8,128)(2,1)S(1)}, bf16[64,512]{1,0:T(8,128)(2,1)S(1)}, u32[]{:S(2)}, u32[]{:S(2)}) collective-permute-start(bf16[64,512]{1,0:T(8,128)(2,1)S(1)} %collective-permute-done.refs_3_.refs_2_), channel_id=1, source_target_pairs={{0,2},{2,0},{1,3},{3,1},{4,6},{6,4},{5,7},{7,5},{8,10},{10,8},{9,1... | collective-permute-start | bytes 196616 | tf_op jit(solution)/shard_map/ppermute | solution.py:228
  18.9 5.6 %collective-permute-start.3 = (bf16[64,512]{1,0:T(8,128)(2,1)S(1)}, bf16[64,512]{1,0:T(8,128)(2,1)S(1)}, u32[]{:S(2)}, u32[]{:S(2)}) collective-permute-start(bf16[64,512]{1,0:T(8,128)(2,1)S(1)} %shard_map.40), channel_id=1, source_target_pairs={{0,4},{4,0},{8,12},{12,8},{1,5},{5,1},{9,13},{13,9},{2,6},{6,2},{1... | collective-permute-start | bytes 196616 | tf_op jit(solution)/shard_map/ppermute | solution.py:225
  24.5 5.7 %collective-permute-start.7 = (bf16[192,512]{1,0:T(8,128)(2,1)S(1)}, bf16[192,512]{1,0:T(8,128)(2,1)S(1)}, u32[]{:S(2)}, u32[]{:S(2)}) collective-permute-start(bf16[192,512]{1,0:T(8,128)(2,1)S(1)} %shard_map.43.refs_1_), channel_id=1, source_target_pairs={{0,2},{2,0},{1,3},{3,1},{4,6},{6,4},{5,7},{7,5},{8,10},{10,8},{9,1... | collective-permute-start | bytes 589832 | tf_op jit(solution)/shard_map/ppermute | solution.py:228
  26.1 6.1 %collective-permute-start.8 = (bf16[64,512]{1,0:T(8,128)(2,1)S(1)}, bf16[64,512]{1,0:T(8,128)(2,1)S(1)}, u32[]{:S(2)}, u32[]{:S(2)}) collective-permute-start(bf16[64,512]{1,0:T(8,128)(2,1)S(1)} %get-tuple-element.25), channel_id=1, source_target_pairs={{0,8},{4,12},{8,0},{12,4},{1,9},{5,13},{9,1},{13,5},{2,10},{6,14},... | collective-permute-start | bytes 196616 | tf_op jit(solution)/shard_map/ppermute | solution.py:225
  29.1 6.1 %collective-permute-start.9 = (bf16[64,512]{1,0:T(8,128)(2,1)S(1)}, bf16[64,512]{1,0:T(8,128)(2,1)S(1)}, u32[]{:S(2)}, u32[]{:S(2)}) collective-permute-start(bf16[64,512]{1,0:T(8,128)(2,1)S(1)} %get-tuple-element.26), channel_id=1, source_target_pairs={{0,12},{4,8},{8,4},{12,0},{1,13},{5,9},{9,5},{13,1},{2,14},{6,10},... | collective-permute-start | bytes 196616 | tf_op jit(solution)/shard_map/ppermute | solution.py:225
  30.2 5.0 %collective-permute-start.10 = (bf16[64,512]{1,0:T(8,128)(2,1)S(1)}, bf16[64,512]{1,0:T(8,128)(2,1)S(1)}, u32[]{:S(2)}, u32[]{:S(2)}) collective-permute-start(bf16[64,512]{1,0:T(8,128)(2,1)S(1)} %get-tuple-element.27), channel_id=1, source_target_pairs={{0,4},{4,0},{8,12},{12,8},{1,5},{5,1},{9,13},{13,9},{2,6},{6,2},{1... | collective-permute-start | bytes 196616 | tf_op jit(solution)/shard_map/ppermute | solution.py:225
  35.2 1.8 %copy-start.3 = (bf16[64,512]{1,0:T(8,128)(2,1)S(1)}, bf16[64,512]{1,0:T(8,128)(2,1)}, u32[]{:S(2)}) copy-start(bf16[64,512]{1,0:T(8,128)(2,1)} %refs_3_.1) | copy-start | bytes 196612
  35.3 1.7 %collective-permute-start.11 = (f32[144,512]{1,0:T(8,128)S(1)}, f32[144,512]{1,0:T(8,128)S(1)}, u32[]{:S(2)}, u32[]{:S(2)}) collective-permute-start(f32[144,512]{1,0:T(8,128)S(1)} %get-tuple-element.28.refs_0_), channel_id=1, source_target_pairs={{0,1},{1,0},{2,3},{3,2},{4,5},{5,4},{6,7},{7,6},{8,9},{9,8},{10,11... | collective-permute-start | bytes 884744 | tf_op jit(solution)/shard_map/ppermute | solution.py:231

commit v23 on v22

--- a/solution.py
+++ b/solution.py
@@ -248,7 +248,7 @@
         functools.partial(own_kernel, nrow),
         sds((rows + TAIL + high, half), BF16),
         [teacher, student, scale],
-        after=[came[nrow - 1]],
+        after=[],
     )
     columns = {0: with_columns(own)}
     pair = call(functools.partial(take_kernel, rows), sds((2 * rows, part), BF16), [came[k] for k in riders])

time: 38.3 us -> 34.2 us (0.89)
  waiting for transfers between devices: 16.6 us -> 14.2 us
  starting transfers between devices: 17.2 us -> 15.6 us
    ppermute x7, waiting for transfers between devices: 12.1 us -> 8.05 us  [along_row(): return lax.ppermute(x, 'row', [(i, i ^ k) for i in range(nrow)])]
    ppermute x4, waiting for transfers between devices: 2.95 us -> 4.54 us  [along_col(): return lax.ppermute(x, 'col', [(i, (i - c) % ncol) for i in range(ncol)])]
    ppermute x7, starting transfers between devices: 11.9 us -> 10.4 us  [along_row(): return lax.ppermute(x, 'row', [(i, i ^ k) for i in range(nrow)])]
  transfers between devices with their start and end apart: 12 -> 12, of which waited for: 5 -> 8; matrix products, arithmetic and copies ran while one was open for 0% -> 0% of each run, Pallas kernels for 3% -> 3%
where the time goes in v23:
time: 34.2 us; the launch traced here: 34.1 us
  starting transfers between devices  15.6 us (46%)
  waiting for transfers between devices  14.2 us (42%)
  Pallas kernels  2.41 us (7%)
  local copies, waits for them, and re-layouts  1.83 us (5%)
    ppermute x7, starting transfers between devices, along_row(): return lax.ppermute(x, 'row', [(i, i ^ k) for i in range(nrow)])  10.4 us
    ppermute x7, waiting for transfers between devices, along_row(): return lax.ppermute(x, 'row', [(i, i ^ k) for i in range(nrow)])  8.05 us
    ppermute x4, starting transfers between devices, along_col(): return lax.ppermute(x, 'col', [(i, (i - c) % ncol) for i in range(ncol)])  5.08 us
    ppermute x4, waiting for transfers between devices, along_col(): return lax.ppermute(x, 'col', [(i, (i - c) % ncol) for i in range(ncol)])  4.54 us
    pallas_call x10, Pallas kernels, call(): pl.pallas_call(run, out_shape=out_shape, in_specs=[pl.BlockSpec(memory_sp...  2.41 us
    unnamed x10, local copies, waits for them, and re-layouts  1.83 us
    ppermute x1, waiting for transfers between devices, other_core(): return lax.ppermute(x, 'sub', [(0, 1), (1, 0)])  1.57 us
  transfers between devices with their start and end apart: 12, of which 8 were waited for; matrix products, arithmetic and copies ran while one was open for 0% of the time, Pallas kernels for 3%

profile of v23, /device:TPU:0, one launch (start us, length us, event | category | flops | bytes accessed | tf_op | source)
XLA Modules:
  0.0 34.1 jit_solution(16860402675384608320)
XLA Ops:
  0.0 0.0 copy-start
  0.0 0.9 %copy-done = bf16[64,2048]{1,0:T(8,128)(2,1)S(1)} copy-done((bf16[64,2048]{1,0:T(8,128)(2,1)S(1)}, bf16[64,2048]{1,0:T(8,128)(2,1)}, u32[]{:S(2)}) %copy-start) | copy-done | bytes 262168
  1.0 0.0 copy-start.1
  1.0 0.0 copy-start.2
  1.0 0.9 %copy-done.2 = bf16[64,512]{1,0:T(8,128)(2,1)S(1)} copy-done((bf16[64,512]{1,0:T(8,128)(2,1)S(1)}, bf16[64,512]{1,0:T(8,128)(2,1)}, u32[]{:S(2)}) %copy-start.2) | copy-done | bytes 65560
  1.9 0.0 copy-start.3
  1.9 3.1 %collective-permute-start = (bf16[128,512]{1,0:T(8,128)(2,1)S(1)}, bf16[128,512]{1,0:T(8,128)(2,1)S(1)}, u32[]{:S(2)}, u32[]{:S(2)}) collective-permute-start(bf16[128,512]{1,0:T(8,128)(2,1)S(1)} %get-tuple-element.20), channel_id=1, source_target_pairs={{0,4},{4,0},{8,12},{12,8},{1,5},{5,1},{9,13},{13,9},{2,6},{6,2},{1... | collective-permute-start | bytes 393224 | tf_op jit(solution)/shard_map/ppermute | solution.py:225
  5.0 0.0 copy-start.4
  5.0 2.6 %collective-permute-start.1 = (bf16[128,512]{1,0:T(8,128)(2,1)S(1)}, bf16[128,512]{1,0:T(8,128)(2,1)S(1)}, u32[]{:S(2)}, u32[]{:S(2)}) collective-permute-start(bf16[128,512]{1,0:T(8,128)(2,1)S(1)} %get-tuple-element.21), channel_id=1, source_target_pairs={{0,8},{4,12},{8,0},{12,4},{1,9},{5,13},{9,1},{13,5},{2,10},{6,14},... | collective-permute-start | bytes 393224 | tf_op jit(solution)/shard_map/ppermute | solution.py:225
  7.6 0.0 copy-done.1
  7.6 0.0 copy-done.3
  7.6 0.0 copy-done.4
  7.6 0.3 shard_map.37.refs_4_.refs_0_
  7.8 1.6 %collective-permute-start.6 = (bf16[144,512]{1,0:T(8,128)(2,1)S(1)}, bf16[144,512]{1,0:T(8,128)(2,1)S(1)}, u32[]{:S(2)}, u32[]{:S(2)}) collective-permute-start(bf16[144,512]{1,0:T(8,128)(2,1)S(1)} %shard_map.37.refs_4_.refs_0_), channel_id=1, source_target_pairs={{0,2},{2,0},{1,3},{3,1},{4,6},{6,4},{5,7},{7,5},{8,10},{10,8},{9,1... | collective-permute-start | bytes 442376 | tf_op jit(solution)/shard_map/ppermute | solution.py:228
  9.4 0.5 %collective-permute-start.4 = (bf16[64,512]{1,0:T(8,128)(2,1)S(1)}, bf16[64,512]{1,0:T(8,128)(2,1)S(1)}, u32[]{:S(2)}, u32[]{:S(2)}) collective-permute-start(bf16[64,512]{1,0:T(8,128)(2,1)S(1)} %get-tuple-element.22), channel_id=1, source_target_pairs={{0,12},{4,8},{8,4},{12,0},{1,13},{5,9},{9,5},{13,1},{2,14},{6,10},... | collective-permute-start | bytes 196616 | tf_op jit(solution)/shard_map/ppermute | solution.py:225
  9.9 0.4 %collective-permute-done.refs_0_ = bf16[128,512]{1,0:T(8,128)(2,1)S(1)} collective-permute-done((bf16[128,512]{1,0:T(8,128)(2,1)S(1)}, bf16[128,512]{1,0:T(8,128)(2,1)S(1)}, u32[]{:S(2)}, u32[]{:S(2)}) %collective-permute-start) | collective-permute-done | bytes 131104 | tf_op jit(solution)/shard_map/ppermute | solution.py:225
  10.3 5.4 %collective-permute-done.1.refs_0_.refs_1_ = bf16[128,512]{1,0:T(8,128)(2,1)S(1)} collective-permute-done((bf16[128,512]{1,0:T(8,128)(2,1)S(1)}, bf16[128,512]{1,0:T(8,128)(2,1)S(1)}, u32[]{:S(2)}, u32[]{:S(2)}) %collective-permute-start.1) | collective-permute-done | bytes 131104 | tf_op jit(solution)/shard_map/ppermute | solution.py:225
  15.7 1.6 %collective-permute-start.3 = (bf16[128,512]{1,0:T(8,128)(2,1)S(1)}, bf16[128,512]{1,0:T(8,128)(2,1)S(1)}, u32[]{:S(2)}, u32[]{:S(2)}) collective-permute-start(bf16[128,512]{1,0:T(8,128)(2,1)S(1)} %shard_map.41.refs_0_.refs_6_), channel_id=1, source_target_pairs={{0,2},{2,0},{1,3},{3,1},{4,6},{6,4},{5,7},{7,5},{8,10},{10,8},{9,1... | collective-permute-start | bytes 393224 | tf_op jit(solution)/shard_map/ppermute | solution.py:228
  17.4 0.0 collective-permute-done.4.refs_2_
  17.4 0.5 %collective-permute-start.5 = (bf16[64,512]{1,0:T(8,128)(2,1)S(1)}, bf16[64,512]{1,0:T(8,128)(2,1)S(1)}, u32[]{:S(2)}, u32[]{:S(2)}) collective-permute-start(bf16[64,512]{1,0:T(8,128)(2,1)S(1)} %collective-permute-done.4.refs_2_), channel_id=1, source_target_pairs={{0,2},{2,0},{1,3},{3,1},{4,6},{6,4},{5,7},{7,5},{8,10},{10,8},{9,1... | collective-permute-start | bytes 196616 | tf_op jit(solution)/shard_map/ppermute | solution.py:228
  17.8 0.7 %collective-permute-start.2 = (bf16[64,512]{1,0:T(8,128)(2,1)S(1)}, bf16[64,512]{1,0:T(8,128)(2,1)S(1)}, u32[]{:S(2)}, u32[]{:S(2)}) collective-permute-start(bf16[64,512]{1,0:T(8,128)(2,1)S(1)} %shard_map.40), channel_id=1, source_target_pairs={{0,4},{4,0},{8,12},{12,8},{1,5},{5,1},{9,13},{13,9},{2,6},{6,2},{1... | collective-permute-start | bytes 196616 | tf_op jit(solution)/shard_map/ppermute | solution.py:225
  18.5 3.7 %collective-permute-done.5.refs_3_ = bf16[64,512]{1,0:T(8,128)(2,1)S(1)} collective-permute-done((bf16[64,512]{1,0:T(8,128)(2,1)S(1)}, bf16[64,512]{1,0:T(8,128)(2,1)S(1)}, u32[]{:S(2)}, u32[]{:S(2)}) %collective-permute-start.5) | collective-permute-done | bytes 65568 | tf_op jit(solution)/shard_map/ppermute | solution.py:228
  22.3 0.0 collective-permute-done.6.refs_5_.refs_2_
  22.3 0.0 collective-permute-done.3.refs_1_.refs_7_
  22.3 0.5 %shard_map.42 = (f32[64,512]{1,0:T(8,128)S(1)}, bf16[64,512]{1,0:T(8,128)(2,1)S(1)}, bf16[64,512]{1,0:T(8,128)(2,1)S(1)}, bf16[64,512]{1,0:T(8,128)(2,1)S(1)}) custom-call(bf16[128,512]{1,0:T(8,128)(2,1)S(1)} %shard_map.41.refs_0_.refs_6_, bf16[128,512]{1,0:T(8,128)(2,1)S(1)} %collective-permute-done.3.refs_1_.refs_7_, ...), custom_call_target="tpu_custom_call" | custom-call | tf_op jit(solution)/shard_map/pallas_call | solution.py:22
  22.8 0.0 collective-permute-done.2.refs_2_
  22.9 1.4 %collective-permute-start.7 = (bf16[192,512]{1,0:T(8,128)(2,1)S(1)}, bf16[192,512]{1,0:T(8,128)(2,1)S(1)}, u32[]{:S(2)}, u32[]{:S(2)}) collective-permute-start(bf16[192,512]{1,0:T(8,128)(2,1)S(1)} %shard_map.43.refs_1_), channel_id=1, source_target_pairs={{0,2},{2,0},{1,3},{3,1},{4,6},{6,4},{5,7},{7,5},{8,10},{10,8},{9,1... | collective-permute-start | bytes 589832 | tf_op jit(solution)/shard_map/ppermute | solution.py:228
  24.3 0.5 %collective-permute-start.8 = (bf16[64,512]{1,0:T(8,128)(2,1)S(1)}, bf16[64,512]{1,0:T(8,128)(2,1)S(1)}, u32[]{:S(2)}, u32[]{:S(2)}) collective-permute-start(bf16[64,512]{1,0:T(8,128)(2,1)S(1)} %get-tuple-element.25), channel_id=1, source_target_pairs={{0,8},{4,12},{8,0},{12,4},{1,9},{5,13},{9,1},{13,5},{2,10},{6,14},... | collective-permute-start | bytes 196616 | tf_op jit(solution)/shard_map/ppermute | solution.py:225
  24.8 1.5 %collective-permute-start.9 = (bf16[64,512]{1,0:T(8,128)(2,1)S(1)}, bf16[64,512]{1,0:T(8,128)(2,1)S(1)}, u32[]{:S(2)}, u32[]{:S(2)}) collective-permute-start(bf16[64,512]{1,0:T(8,128)(2,1)S(1)} %get-tuple-element.26), channel_id=1, source_target_pairs={{0,12},{4,8},{8,4},{12,0},{1,13},{5,9},{9,5},{13,1},{2,14},{6,10},... | collective-permute-start | bytes 196616 | tf_op jit(solution)/shard_map/ppermute | solution.py:225
  26.2 1.6 %collective-permute-start.10 = (bf16[64,512]{1,0:T(8,128)(2,1)S(1)}, bf16[64,512]{1,0:T(8,128)(2,1)S(1)}, u32[]{:S(2)}, u32[]{:S(2)}) collective-permute-start(bf16[64,512]{1,0:T(8,128)(2,1)S(1)} %get-tuple-element.27), channel_id=1, source_target_pairs={{0,4},{4,0},{8,12},{12,8},{1,5},{5,1},{9,13},{13,9},{2,6},{6,2},{1... | collective-permute-start | bytes 196616 | tf_op jit(solution)/shard_map/ppermute | solution.py:225
  27.8 0.8 %collective-permute-done.7.refs_3_ = bf16[192,512]{1,0:T(8,128)(2,1)S(1)} collective-permute-done((bf16[192,512]{1,0:T(8,128)(2,1)S(1)}, bf16[192,512]{1,0:T(8,128)(2,1)S(1)}, u32[]{:S(2)}, u32[]{:S(2)}) %collective-permute-start.7) | collective-permute-done | bytes 196640 | tf_op jit(solution)/shard_map/ppermute | solution.py:228
  28.6 0.3 shard_map.44
  28.9 0.6 %collective-permute-done.8.refs_1_ = bf16[64,512]{1,0:T(8,128)(2,1)S(1)} collective-permute-done((bf16[64,512]{1,0:T(8,128)(2,1)S(1)}, bf16[64,512]{1,0:T(8,128)(2,1)S(1)}, u32[]{:S(2)}, u32[]{:S(2)}) %collective-permute-start.8) | collective-permute-done | bytes 65568 | tf_op jit(solution)/shard_map/ppermute | solution.py:225
  29.5 1.5 %collective-permute-done.9.refs_2_ = bf16[64,512]{1,0:T(8,128)(2,1)S(1)} collective-permute-done((bf16[64,512]{1,0:T(8,128)(2,1)S(1)}, bf16[64,512]{1,0:T(8,128)(2,1)S(1)}, u32[]{:S(2)}, u32[]{:S(2)}) %collective-permute-start.9) | collective-permute-done | bytes 65568 | tf_op jit(solution)/shard_map/ppermute | solution.py:225
  31.0 0.2 collective-permute-done.10.refs_4_
  31.2 0.1 shard_map.45
  31.3 0.1 collective-permute-start.11
  31.4 1.6 %collective-permute-done.11.refs_1_ = f32[144,512]{1,0:T(8,128)S(1)} collective-permute-done((f32[144,512]{1,0:T(8,128)S(1)}, f32[144,512]{1,0:T(8,128)S(1)}, u32[]{:S(2)}, u32[]{:S(2)}) %collective-permute-start.11) | collective-permute-done | bytes 294944 | tf_op jit(solution)/shard_map/ppermute | solution.py:231
  33.0 1.1 %shard_map.46 = f32[64,512]{1,0:T(8,128)} custom-call(f32[144,512]{1,0:T(8,128)S(1)} %get-tuple-element.28.refs_0_, f32[144,512]{1,0:T(8,128)S(1)} %collective-permute-done.11.refs_1_, f32[8,512]{1,0:T(8,128)S(1)} %get-tuple-element.29.refs_2_, bf16[64,512]{1,0:T(8,128)(2,1)S(1)} %copy-done.3, bf16[1,64]{1,0:T(2,128)(2,1)S(1)} %bitcast.2, ...), custom_call_target="tpu_custom_call" | custom-call | tf_op jit(solution)/shard_map/pallas_call | solution.py:22
  (5 shorter events, 0.1 us)
Async XLA Ops:
  0.0 0.9 %copy-start = (bf16[64,2048]{1,0:T(8,128)(2,1)S(1)}, bf16[64,2048]{1,0:T(8,128)(2,1)}, u32[]{:S(2)}) copy-start(bf16[64,2048]{1,0:T(8,128)(2,1)} %refs_0_.4) | copy-start | bytes 786436
  1.0 6.6 %copy-start.1 = (bf16[64,2048]{1,0:T(8,128)(2,1)S(1)}, bf16[64,2048]{1,0:T(8,128)(2,1)}, u32[]{:S(2)}) copy-start(bf16[64,2048]{1,0:T(8,128)(2,1)} %refs_0_.4) | copy-start | bytes 786436
  1.0 0.9 %copy-start.2 = (bf16[64,512]{1,0:T(8,128)(2,1)S(1)}, bf16[64,512]{1,0:T(8,128)(2,1)}, u32[]{:S(2)}) copy-start(bf16[64,512]{1,0:T(8,128)(2,1)} %refs_3_.1) | copy-start | bytes 196612
  1.9 5.7 %copy-start.3 = (bf16[64,512]{1,0:T(8,128)(2,1)S(1)}, bf16[64,512]{1,0:T(8,128)(2,1)}, u32[]{:S(2)}) copy-start(bf16[64,512]{1,0:T(8,128)(2,1)} %refs_3_.1) | copy-start | bytes 196612
  1.9 8.4 %collective-permute-start = (bf16[128,512]{1,0:T(8,128)(2,1)S(1)}, bf16[128,512]{1,0:T(8,128)(2,1)S(1)}, u32[]{:S(2)}, u32[]{:S(2)}) collective-permute-start(bf16[128,512]{1,0:T(8,128)(2,1)S(1)} %get-tuple-element.20), channel_id=1, source_target_pairs={{0,4},{4,0},{8,12},{12,8},{1,5},{5,1},{9,13},{13,9},{2,6},{6,2},{1... | collective-permute-start | bytes 393224 | tf_op jit(solution)/shard_map/ppermute | solution.py:225
  5.0 2.6 %copy-start.4 = (bf16[64]{0:T(256)(128)(2,1)S(1)}, bf16[64]{0:T(256)(128)(2,1)}, u32[]{:S(2)}) copy-start(bf16[64]{0:T(256)(128)(2,1)} %param.5) | copy-start | bytes 388
  5.0 10.7 %collective-permute-start.1 = (bf16[128,512]{1,0:T(8,128)(2,1)S(1)}, bf16[128,512]{1,0:T(8,128)(2,1)S(1)}, u32[]{:S(2)}, u32[]{:S(2)}) collective-permute-start(bf16[128,512]{1,0:T(8,128)(2,1)S(1)} %get-tuple-element.21), channel_id=1, source_target_pairs={{0,8},{4,12},{8,0},{12,4},{1,9},{5,13},{9,1},{13,5},{2,10},{6,14},... | collective-permute-start | bytes 393224 | tf_op jit(solution)/shard_map/ppermute | solution.py:225
  7.8 14.4 %collective-permute-start.6 = (bf16[144,512]{1,0:T(8,128)(2,1)S(1)}, bf16[144,512]{1,0:T(8,128)(2,1)S(1)}, u32[]{:S(2)}, u32[]{:S(2)}) collective-permute-start(bf16[144,512]{1,0:T(8,128)(2,1)S(1)} %shard_map.37.refs_4_.refs_0_), channel_id=1, source_target_pairs={{0,2},{2,0},{1,3},{3,1},{4,6},{6,4},{5,7},{7,5},{8,10},{10,8},{9,1... | collective-permute-start | bytes 442376 | tf_op jit(solution)/shard_map/ppermute | solution.py:228
  9.4 8.0 %collective-permute-start.4 = (bf16[64,512]{1,0:T(8,128)(2,1)S(1)}, bf16[64,512]{1,0:T(8,128)(2,1)S(1)}, u32[]{:S(2)}, u32[]{:S(2)}) collective-permute-start(bf16[64,512]{1,0:T(8,128)(2,1)S(1)} %get-tuple-element.22), channel_id=1, source_target_pairs={{0,12},{4,8},{8,4},{12,0},{1,13},{5,9},{9,5},{13,1},{2,14},{6,10},... | collective-permute-start | bytes 196616 | tf_op jit(solution)/shard_map/ppermute | solution.py:225
  15.7 6.6 %collective-permute-start.3 = (bf16[128,512]{1,0:T(8,128)(2,1)S(1)}, bf16[128,512]{1,0:T(8,128)(2,1)S(1)}, u32[]{:S(2)}, u32[]{:S(2)}) collective-permute-start(bf16[128,512]{1,0:T(8,128)(2,1)S(1)} %shard_map.41.refs_0_.refs_6_), channel_id=1, source_target_pairs={{0,2},{2,0},{1,3},{3,1},{4,6},{6,4},{5,7},{7,5},{8,10},{10,8},{9,1... | collective-permute-start | bytes 393224 | tf_op jit(solution)/shard_map/ppermute | solution.py:228
  17.4 4.9 %collective-permute-start.5 = (bf16[64,512]{1,0:T(8,128)(2,1)S(1)}, bf16[64,512]{1,0:T(8,128)(2,1)S(1)}, u32[]{:S(2)}, u32[]{:S(2)}) collective-permute-start(bf16[64,512]{1,0:T(8,128)(2,1)S(1)} %collective-permute-done.4.refs_2_), channel_id=1, source_target_pairs={{0,2},{2,0},{1,3},{3,1},{4,6},{6,4},{5,7},{7,5},{8,10},{10,8},{9,1... | collective-permute-start | bytes 196616 | tf_op jit(solution)/shard_map/ppermute | solution.py:228
  17.8 5.0 %collective-permute-start.2 = (bf16[64,512]{1,0:T(8,128)(2,1)S(1)}, bf16[64,512]{1,0:T(8,128)(2,1)S(1)}, u32[]{:S(2)}, u32[]{:S(2)}) collective-permute-start(bf16[64,512]{1,0:T(8,128)(2,1)S(1)} %shard_map.40), channel_id=1, source_target_pairs={{0,4},{4,0},{8,12},{12,8},{1,5},{5,1},{9,13},{13,9},{2,6},{6,2},{1... | collective-permute-start | bytes 196616 | tf_op jit(solution)/shard_map/ppermute | solution.py:225
  22.9 5.7 %collective-permute-start.7 = (bf16[192,512]{1,0:T(8,128)(2,1)S(1)}, bf16[192,512]{1,0:T(8,128)(2,1)S(1)}, u32[]{:S(2)}, u32[]{:S(2)}) collective-permute-start(bf16[192,512]{1,0:T(8,128)(2,1)S(1)} %shard_map.43.refs_1_), channel_id=1, source_target_pairs={{0,2},{2,0},{1,3},{3,1},{4,6},{6,4},{5,7},{7,5},{8,10},{10,8},{9,1... | collective-permute-start | bytes 589832 | tf_op jit(solution)/shard_map/ppermute | solution.py:228
  24.3 5.2 %collective-permute-start.8 = (bf16[64,512]{1,0:T(8,128)(2,1)S(1)}, bf16[64,512]{1,0:T(8,128)(2,1)S(1)}, u32[]{:S(2)}, u32[]{:S(2)}) collective-permute-start(bf16[64,512]{1,0:T(8,128)(2,1)S(1)} %get-tuple-element.25), channel_id=1, source_target_pairs={{0,8},{4,12},{8,0},{12,4},{1,9},{5,13},{9,1},{13,5},{2,10},{6,14},... | collective-permute-start | bytes 196616 | tf_op jit(solution)/shard_map/ppermute | solution.py:225
  24.8 6.2 %collective-permute-start.9 = (bf16[64,512]{1,0:T(8,128)(2,1)S(1)}, bf16[64,512]{1,0:T(8,128)(2,1)S(1)}, u32[]{:S(2)}, u32[]{:S(2)}) collective-permute-start(bf16[64,512]{1,0:T(8,128)(2,1)S(1)} %get-tuple-element.26), channel_id=1, source_target_pairs={{0,12},{4,8},{8,4},{12,0},{1,13},{5,9},{9,5},{13,1},{2,14},{6,10},... | collective-permute-start | bytes 196616 | tf_op jit(solution)/shard_map/ppermute | solution.py:225
  26.2 5.0 %collective-permute-start.10 = (bf16[64,512]{1,0:T(8,128)(2,1)S(1)}, bf16[64,512]{1,0:T(8,128)(2,1)S(1)}, u32[]{:S(2)}, u32[]{:S(2)}) collective-permute-start(bf16[64,512]{1,0:T(8,128)(2,1)S(1)} %get-tuple-element.27), channel_id=1, source_target_pairs={{0,4},{4,0},{8,12},{12,8},{1,5},{5,1},{9,13},{13,9},{2,6},{6,2},{1... | collective-permute-start | bytes 196616 | tf_op jit(solution)/shard_map/ppermute | solution.py:225
  31.3 1.7 %collective-permute-start.11 = (f32[144,512]{1,0:T(8,128)S(1)}, f32[144,512]{1,0:T(8,128)S(1)}, u32[]{:S(2)}, u32[]{:S(2)}) collective-permute-start(f32[144,512]{1,0:T(8,128)S(1)} %get-tuple-element.28.refs_0_), channel_id=1, source_target_pairs={{0,1},{1,0},{2,3},{3,2},{4,5},{5,4},{6,7},{7,6},{8,9},{9,8},{10,11... | collective-permute-start | bytes 884744 | tf_op jit(solution)/shard_map/ppermute | solution.py:231

commit v24 on v8

--- a/solution.py
+++ b/solution.py
@@ -196,19 +196,19 @@
     batch = mine.shape[1]
     squares = mine[2 * rows : 2 * rows + 8, :] + other[2 * rows : 2 * rows + 8, :]
     for at in range(0, batch, 128):
-        norm = jnp.sqrt(column(squares[:1, at : at + 128]))
-        units[at : at + 128, :] = (raw[at : at + 128, :].astype(F32) / norm).astype(BF16)
+        inverse = 1.0 / jnp.sqrt(column(squares[:1, at : at + 128]))
+        units[at : at + 128, :] = (raw[at : at + 128, :].astype(F32) * inverse).astype(BF16)
     at = pl.ds(group_spot(nrow, ncol, rows, 0), 2 * rows)
     own = (mine[2 * rows : 2 * rows + 8, at] + other[2 * rows : 2 * rows + 8, at])[:1, :rows]
-    norm = jnp.sqrt(column(own))
+    inverse = 1.0 / jnp.sqrt(column(own))
     mass = (mine[2 * rows + 8 : 2 * rows + 9, :1] + other[2 * rows + 8 : 2 * rows + 9, :1]) / batch
-    gram = (mine[rows : 2 * rows, :] + other[rows : 2 * rows, :]) / (norm * jnp.sqrt(squares[:1, :]))
-    outer = column(scale[...].astype(F32)) * vectors[:1, :]
-    error_b = (gram - outer * (mine[:rows, :] + other[:rows, :]) / mass).astype(BF16)
+    gram = (mine[rows : 2 * rows, :] + other[rows : 2 * rows, :]) * (inverse * (1.0 / jnp.sqrt(squares[:1, :])))
+    outer = (column(scale[...].astype(F32)) / mass) * vectors[:1, :]
+    error_b = (gram - outer * (mine[:rows, :] + other[:rows, :])).astype(BF16)
     grads = 4.0 * jnp.dot(error_b, units[...], preferred_element_type=F32)
     along = 4.0 * jnp.sum(error_b.astype(F32) * gram, axis=1, keepdims=True)
-    unit = stud[...].astype(F32) / norm
-    out[...] = (grads - along * unit) / norm
+    unit = stud[...].astype(F32) * inverse
+    out[...] = (grads - along * unit) * inverse
 
 
 def shards(student, teacher, scale):
@@ -282,10 +282,11 @@
         raw_refs,
         scratch=[] if small else [pltpu.VMEM((batch, half), BF16)],
     )
+    far_first = sorted(order, reverse=True)
     message, vectors = call(
-        functools.partial(message_kernel, nrow, ncol, order),
+        functools.partial(message_kernel, nrow, ncol, far_first),
         [sds((2 * rows + 16, batch), F32), sds((8, batch), F32)],
-        [raw_gram] + [returned[k] for k in order],
+        [raw_gram] + [returned[k] for k in far_first],
     )
     return call(
         functools.partial(final_kernel, nrow, ncol, None if small else raw_keys),

time: 32.6 us -> 32.8 us (level)
  starting transfers between devices: 15 us -> 15.9 us
  waiting for transfers between devices: 13.1 us -> 12.4 us
    ppermute x7, starting transfers between devices: 9.23 us -> 10.1 us  [along_row(): return lax.ppermute(x, 'row', [(i, i ^ k) for i in range(nrow)])]
    ppermute x5, waiting for transfers between devices: 4.39 us -> 3.49 us  [along_col(): return lax.ppermute(x, 'col', [(i, (i - c) % ncol) for i in range(ncol)])]
  transfers between devices with their start and end apart: 13 -> 13, of which waited for: 11 -> 10; matrix products, arithmetic and copies ran while one was open for 0% -> 0% of each run, Pallas kernels for 4% -> 4%
where the time goes in v24:
time: 32.8 us; the launch traced here: 32.6 us
  starting transfers between devices  15.9 us (48%)
  waiting for transfers between devices  12.4 us (38%)
  Pallas kernels  2.42 us (7%)
  local copies, waits for them, and re-layouts  1.8 us (5%)
    ppermute x7, starting transfers between devices, along_row(): return lax.ppermute(x, 'row', [(i, i ^ k) for i in range(nrow)])  10.1 us
    ppermute x7, waiting for transfers between devices, along_row(): return lax.ppermute(x, 'row', [(i, i ^ k) for i in range(nrow)])  7.33 us
    ppermute x5, starting transfers between devices, along_col(): return lax.ppermute(x, 'col', [(i, (i - c) % ncol) for i in range(ncol)])  5.68 us
    ppermute x5, waiting for transfers between devices, along_col(): return lax.ppermute(x, 'col', [(i, (i - c) % ncol) for i in range(ncol)])  3.49 us
    pallas_call x11, Pallas kernels, call(): pl.pallas_call(run, out_shape=out_shape, in_specs=[pl.BlockSpec(memory_sp...  2.42 us
    unnamed x10, local copies, waits for them, and re-layouts  1.8 us
    ppermute x1, waiting for transfers between devices, other_core(): return lax.ppermute(x, 'sub', [(0, 1), (1, 0)])  1.57 us
  transfers between devices with their start and end apart: 13, of which 10 were waited for; matrix products, arithmetic and copies ran while one was open for 0% of the time, Pallas kernels for 4%

profile of v24, /device:TPU:0, one launch (start us, length us, event | category | flops | bytes accessed | tf_op | source)
XLA Modules:
  0.0 32.6 jit_solution(10350733812221505561)
XLA Ops:
  0.0 0.0 copy-start
  0.0 0.9 %copy-done = bf16[64,2048]{1,0:T(8,128)(2,1)S(1)} copy-done((bf16[64,2048]{1,0:T(8,128)(2,1)S(1)}, bf16[64,2048]{1,0:T(8,128)(2,1)}, u32[]{:S(2)}) %copy-start) | copy-done | bytes 262168
  1.0 0.0 copy-start.1
  1.0 5.1 %collective-permute-start = (bf16[64,512]{1,0:T(8,128)(2,1)S(1)}, bf16[64,512]{1,0:T(8,128)(2,1)S(1)}, u32[]{:S(2)}, u32[]{:S(2)}) collective-permute-start(bf16[64,512]{1,0:T(8,128)(2,1)S(1)} %get-tuple-element.18), channel_id=1, source_target_pairs={{0,12},{4,8},{8,4},{12,0},{1,13},{5,9},{9,5},{13,1},{2,14},{6,10},... | collective-permute-start | bytes 196616 | tf_op jit(solution)/shard_map/ppermute | solution.py:224
  6.1 0.0 copy-start.2
  6.1 0.8 %copy-done.2 = bf16[64,512]{1,0:T(8,128)(2,1)S(1)} copy-done((bf16[64,512]{1,0:T(8,128)(2,1)S(1)}, bf16[64,512]{1,0:T(8,128)(2,1)}, u32[]{:S(2)}) %copy-start.2) | copy-done | bytes 65560
  6.9 0.1 collective-permute-start.1
  7.0 0.0 copy-start.4
  7.0 0.6 %collective-permute-start.2 = (bf16[128,512]{1,0:T(8,128)(2,1)S(1)}, bf16[128,512]{1,0:T(8,128)(2,1)S(1)}, u32[]{:S(2)}, u32[]{:S(2)}) collective-permute-start(bf16[128,512]{1,0:T(8,128)(2,1)S(1)} %get-tuple-element.22), channel_id=1, source_target_pairs={{0,8},{4,12},{8,0},{12,4},{1,9},{5,13},{9,1},{13,5},{2,10},{6,14},... | collective-permute-start | bytes 393224 | tf_op jit(solution)/shard_map/ppermute | solution.py:224
  7.6 1.1 %collective-permute-done.refs_3_.refs_2_ = bf16[64,512]{1,0:T(8,128)(2,1)S(1)} collective-permute-done((bf16[64,512]{1,0:T(8,128)(2,1)S(1)}, bf16[64,512]{1,0:T(8,128)(2,1)S(1)}, u32[]{:S(2)}, u32[]{:S(2)}) %collective-permute-start) | collective-permute-done | bytes 65568 | tf_op jit(solution)/shard_map/ppermute | solution.py:224
  8.7 0.0 copy-done.1
  8.7 0.0 copy-done.4
  8.7 0.3 shard_map.38.refs_4_.refs_0_
  9.0 1.9 %collective-permute-start.6 = (bf16[144,512]{1,0:T(8,128)(2,1)S(1)}, bf16[144,512]{1,0:T(8,128)(2,1)S(1)}, u32[]{:S(2)}, u32[]{:S(2)}) collective-permute-start(bf16[144,512]{1,0:T(8,128)(2,1)S(1)} %shard_map.38.refs_4_.refs_0_), channel_id=1, source_target_pairs={{0,2},{2,0},{1,3},{3,1},{4,6},{6,4},{5,7},{7,5},{8,10},{10,8},{9,1... | collective-permute-start | bytes 442376 | tf_op jit(solution)/shard_map/ppermute | solution.py:227
  10.9 0.2 collective-permute-start.5
  11.1 2.2 %collective-permute-done.1.refs_0_ = bf16[128,512]{1,0:T(8,128)(2,1)S(1)} collective-permute-done((bf16[128,512]{1,0:T(8,128)(2,1)S(1)}, bf16[128,512]{1,0:T(8,128)(2,1)S(1)}, u32[]{:S(2)}, u32[]{:S(2)}) %collective-permute-start.1) | collective-permute-done | bytes 131104 | tf_op jit(solution)/shard_map/ppermute | solution.py:224
  13.3 1.5 %collective-permute-start.7 = (bf16[64,512]{1,0:T(8,128)(2,1)S(1)}, bf16[64,512]{1,0:T(8,128)(2,1)S(1)}, u32[]{:S(2)}, u32[]{:S(2)}) collective-permute-start(bf16[64,512]{1,0:T(8,128)(2,1)S(1)} %shard_map.42.refs_6_), channel_id=1, source_target_pairs={{0,2},{2,0},{1,3},{3,1},{4,6},{6,4},{5,7},{7,5},{8,10},{10,8},{9,1... | collective-permute-start | bytes 196616 | tf_op jit(solution)/shard_map/ppermute | solution.py:227
  14.8 1.0 %collective-permute-done.2.refs_0_.refs_1_ = bf16[128,512]{1,0:T(8,128)(2,1)S(1)} collective-permute-done((bf16[128,512]{1,0:T(8,128)(2,1)S(1)}, bf16[128,512]{1,0:T(8,128)(2,1)S(1)}, u32[]{:S(2)}, u32[]{:S(2)}) %collective-permute-start.2) | collective-permute-done | bytes 131104 | tf_op jit(solution)/shard_map/ppermute | solution.py:224
  15.8 1.5 %collective-permute-start.4 = (bf16[64,512]{1,0:T(8,128)(2,1)S(1)}, bf16[64,512]{1,0:T(8,128)(2,1)S(1)}, u32[]{:S(2)}, u32[]{:S(2)}) collective-permute-start(bf16[64,512]{1,0:T(8,128)(2,1)S(1)} %shard_map.41.refs_0_), channel_id=1, source_target_pairs={{0,2},{2,0},{1,3},{3,1},{4,6},{6,4},{5,7},{7,5},{8,10},{10,8},{9,1... | collective-permute-start | bytes 196616 | tf_op jit(solution)/shard_map/ppermute | solution.py:227
  17.3 0.0 collective-permute-start.3
  17.3 0.0 collective-permute-done.5.refs_3_
  17.3 0.6 %collective-permute-done.7.refs_7_ = bf16[64,512]{1,0:T(8,128)(2,1)S(1)} collective-permute-done((bf16[64,512]{1,0:T(8,128)(2,1)S(1)}, bf16[64,512]{1,0:T(8,128)(2,1)S(1)}, u32[]{:S(2)}, u32[]{:S(2)}) %collective-permute-start.7) | collective-permute-done | bytes 65568 | tf_op jit(solution)/shard_map/ppermute | solution.py:227
  17.9 2.2 %collective-permute-done.4.refs_1_ = bf16[64,512]{1,0:T(8,128)(2,1)S(1)} collective-permute-done((bf16[64,512]{1,0:T(8,128)(2,1)S(1)}, bf16[64,512]{1,0:T(8,128)(2,1)S(1)}, u32[]{:S(2)}, u32[]{:S(2)}) %collective-permute-start.4) | collective-permute-done | bytes 65568 | tf_op jit(solution)/shard_map/ppermute | solution.py:227
  20.1 0.0 collective-permute-done.6.refs_5_.refs_2_
  20.1 0.5 %shard_map.43 = (f32[64,512]{1,0:T(8,128)S(1)}, bf16[64,512]{1,0:T(8,128)(2,1)S(1)}, bf16[64,512]{1,0:T(8,128)(2,1)S(1)}, bf16[64,512]{1,0:T(8,128)(2,1)S(1)}) custom-call(bf16[64,512]{1,0:T(8,128)(2,1)S(1)} %shard_map.41.refs_0_, bf16[64,512]{1,0:T(8,128)(2,1)S(1)} %collective-permute-done.4.refs_1_, ...), custom_call_target="tpu_custom_call" | custom-call | tf_op jit(solution)/shard_map/pallas_call | solution.py:22
  20.6 1.0 %collective-permute-done.3.refs_2_ = bf16[64,512]{1,0:T(8,128)(2,1)S(1)} collective-permute-done((bf16[64,512]{1,0:T(8,128)(2,1)S(1)}, bf16[64,512]{1,0:T(8,128)(2,1)S(1)}, u32[]{:S(2)}, u32[]{:S(2)}) %collective-permute-start.3) | collective-permute-done | bytes 65568 | tf_op jit(solution)/shard_map/ppermute | solution.py:224
  21.6 0.6 %collective-permute-start.8 = (bf16[192,512]{1,0:T(8,128)(2,1)S(1)}, bf16[192,512]{1,0:T(8,128)(2,1)S(1)}, u32[]{:S(2)}, u32[]{:S(2)}) collective-permute-start(bf16[192,512]{1,0:T(8,128)(2,1)S(1)} %shard_map.44.refs_1_), channel_id=1, source_target_pairs={{0,2},{2,0},{1,3},{3,1},{4,6},{6,4},{5,7},{7,5},{8,10},{10,8},{9,1... | collective-permute-start | bytes 589832 | tf_op jit(solution)/shard_map/ppermute | solution.py:227
  22.2 2.1 %collective-permute-start.9 = (bf16[64,512]{1,0:T(8,128)(2,1)S(1)}, bf16[64,512]{1,0:T(8,128)(2,1)S(1)}, u32[]{:S(2)}, u32[]{:S(2)}) collective-permute-start(bf16[64,512]{1,0:T(8,128)(2,1)S(1)} %get-tuple-element.25), channel_id=1, source_target_pairs={{0,12},{4,8},{8,4},{12,0},{1,13},{5,9},{9,5},{13,1},{2,14},{6,10},... | collective-permute-start | bytes 196616 | tf_op jit(solution)/shard_map/ppermute | solution.py:224
  24.3 0.0 collective-permute-start.10
  24.3 2.3 %collective-permute-start.11 = (bf16[64,512]{1,0:T(8,128)(2,1)S(1)}, bf16[64,512]{1,0:T(8,128)(2,1)S(1)}, u32[]{:S(2)}, u32[]{:S(2)}) collective-permute-start(bf16[64,512]{1,0:T(8,128)(2,1)S(1)} %get-tuple-element.27), channel_id=1, source_target_pairs={{0,4},{4,0},{8,12},{12,8},{1,5},{5,1},{9,13},{13,9},{2,6},{6,2},{1... | collective-permute-start | bytes 196616 | tf_op jit(solution)/shard_map/ppermute | solution.py:224
  26.6 0.7 %collective-permute-done.8.refs_3_ = bf16[192,512]{1,0:T(8,128)(2,1)S(1)} collective-permute-done((bf16[192,512]{1,0:T(8,128)(2,1)S(1)}, bf16[192,512]{1,0:T(8,128)(2,1)S(1)}, u32[]{:S(2)}, u32[]{:S(2)}) %collective-permute-start.8) | collective-permute-done | bytes 196640 | tf_op jit(solution)/shard_map/ppermute | solution.py:227
  27.3 0.3 %shard_map.45 = (f32[72,512]{1,0:T(8,128)S(1)}, bf16[512,512]{1,0:T(8,128)(2,1)S(1)}) custom-call(bf16[144,512]{1,0:T(8,128)(2,1)S(1)} %shard_map.38.refs_4_.refs_0_, bf16[192,512]{1,0:T(8,128)(2,1)S(1)} %shard_map.44.refs_1_, bf16[144,512]{1,0:T(8,128)(2,1)S(1)} %collective-permute-done.6.refs_5_.refs_2_, bf16[192,512]{1,0:T(8,128)(2,1)S(1)} %collective-permute-done.8.refs_3_), custom_call_target="tpu_custom_call" | custom-call | tf_op jit(solution)/shard_map/pallas_call | solution.py:22
  27.7 0.6 %collective-permute-done.9.refs_1_ = bf16[64,512]{1,0:T(8,128)(2,1)S(1)} collective-permute-done((bf16[64,512]{1,0:T(8,128)(2,1)S(1)}, bf16[64,512]{1,0:T(8,128)(2,1)S(1)}, u32[]{:S(2)}, u32[]{:S(2)}) %collective-permute-start.9) | collective-permute-done | bytes 65568 | tf_op jit(solution)/shard_map/ppermute | solution.py:224
  28.3 1.4 %collective-permute-done.10.refs_2_ = bf16[64,512]{1,0:T(8,128)(2,1)S(1)} collective-permute-done((bf16[64,512]{1,0:T(8,128)(2,1)S(1)}, bf16[64,512]{1,0:T(8,128)(2,1)S(1)}, u32[]{:S(2)}, u32[]{:S(2)}) %collective-permute-start.10) | collective-permute-done | bytes 65568 | tf_op jit(solution)/shard_map/ppermute | solution.py:224
  29.7 0.0 collective-permute-done.11.refs_3_
  29.7 0.0 copy-start.3
  29.7 0.1 shard_map.46
  29.8 0.1 collective-permute-start.12
  29.9 1.6 %collective-permute-done.12.refs_1_ = f32[144,512]{1,0:T(8,128)S(1)} collective-permute-done((f32[144,512]{1,0:T(8,128)S(1)}, f32[144,512]{1,0:T(8,128)S(1)}, u32[]{:S(2)}, u32[]{:S(2)}) %collective-permute-start.12) | collective-permute-done | bytes 294944 | tf_op jit(solution)/shard_map/ppermute | solution.py:230
  31.4 0.0 copy-done.3
  31.4 1.1 %shard_map.47 = f32[64,512]{1,0:T(8,128)} custom-call(f32[144,512]{1,0:T(8,128)S(1)} %get-tuple-element.28.refs_0_, f32[144,512]{1,0:T(8,128)S(1)} %collective-permute-done.12.refs_1_, f32[8,512]{1,0:T(8,128)S(1)} %get-tuple-element.29.refs_2_, bf16[64,512]{1,0:T(8,128)(2,1)S(1)} %copy-done.3, bf16[1,64]{1,0:T(2,128)(2,1)S(1)} %bitcast.2, ...), custom_call_target="tpu_custom_call" | custom-call | tf_op jit(solution)/shard_map/pallas_call | solution.py:22
  (6 shorter events, 0.1 us)
Async XLA Ops:
  0.0 0.9 %copy-start = (bf16[64,2048]{1,0:T(8,128)(2,1)S(1)}, bf16[64,2048]{1,0:T(8,128)(2,1)}, u32[]{:S(2)}) copy-start(bf16[64,2048]{1,0:T(8,128)(2,1)} %refs_0_.4) | copy-start | bytes 786436
  1.0 7.8 %copy-start.1 = (bf16[64,2048]{1,0:T(8,128)(2,1)S(1)}, bf16[64,2048]{1,0:T(8,128)(2,1)}, u32[]{:S(2)}) copy-start(bf16[64,2048]{1,0:T(8,128)(2,1)} %refs_0_.4) | copy-start | bytes 786436
  1.0 7.7 %collective-permute-start = (bf16[64,512]{1,0:T(8,128)(2,1)S(1)}, bf16[64,512]{1,0:T(8,128)(2,1)S(1)}, u32[]{:S(2)}, u32[]{:S(2)}) collective-permute-start(bf16[64,512]{1,0:T(8,128)(2,1)S(1)} %get-tuple-element.18), channel_id=1, source_target_pairs={{0,12},{4,8},{8,4},{12,0},{1,13},{5,9},{9,5},{13,1},{2,14},{6,10},... | collective-permute-start | bytes 196616 | tf_op jit(solution)/shard_map/ppermute | solution.py:224
  6.1 0.8 %copy-start.2 = (bf16[64,512]{1,0:T(8,128)(2,1)S(1)}, bf16[64,512]{1,0:T(8,128)(2,1)}, u32[]{:S(2)}) copy-start(bf16[64,512]{1,0:T(8,128)(2,1)} %refs_3_.1) | copy-start | bytes 196612
  6.9 6.4 %collective-permute-start.1 = (bf16[128,512]{1,0:T(8,128)(2,1)S(1)}, bf16[128,512]{1,0:T(8,128)(2,1)S(1)}, u32[]{:S(2)}, u32[]{:S(2)}) collective-permute-start(bf16[128,512]{1,0:T(8,128)(2,1)S(1)} %get-tuple-element.21), channel_id=1, source_target_pairs={{0,4},{4,0},{8,12},{12,8},{1,5},{5,1},{9,13},{13,9},{2,6},{6,2},{1... | collective-permute-start | bytes 393224 | tf_op jit(solution)/shard_map/ppermute | solution.py:224
  7.0 1.7 %copy-start.4 = (bf16[64]{0:T(256)(128)(2,1)S(1)}, bf16[64]{0:T(256)(128)(2,1)}, u32[]{:S(2)}) copy-start(bf16[64]{0:T(256)(128)(2,1)} %param.5) | copy-start | bytes 388
  7.0 8.8 %collective-permute-start.2 = (bf16[128,512]{1,0:T(8,128)(2,1)S(1)}, bf16[128,512]{1,0:T(8,128)(2,1)S(1)}, u32[]{:S(2)}, u32[]{:S(2)}) collective-permute-start(bf16[128,512]{1,0:T(8,128)(2,1)S(1)} %get-tuple-element.22), channel_id=1, source_target_pairs={{0,8},{4,12},{8,0},{12,4},{1,9},{5,13},{9,1},{13,5},{2,10},{6,14},... | collective-permute-start | bytes 393224 | tf_op jit(solution)/shard_map/ppermute | solution.py:224
  9.0 11.1 %collective-permute-start.6 = (bf16[144,512]{1,0:T(8,128)(2,1)S(1)}, bf16[144,512]{1,0:T(8,128)(2,1)S(1)}, u32[]{:S(2)}, u32[]{:S(2)}) collective-permute-start(bf16[144,512]{1,0:T(8,128)(2,1)S(1)} %shard_map.38.refs_4_.refs_0_), channel_id=1, source_target_pairs={{0,2},{2,0},{1,3},{3,1},{4,6},{6,4},{5,7},{7,5},{8,10},{10,8},{9,1... | collective-permute-start | bytes 442376 | tf_op jit(solution)/shard_map/ppermute | solution.py:227
  10.9 6.4 %collective-permute-start.5 = (bf16[64,512]{1,0:T(8,128)(2,1)S(1)}, bf16[64,512]{1,0:T(8,128)(2,1)S(1)}, u32[]{:S(2)}, u32[]{:S(2)}) collective-permute-start(bf16[64,512]{1,0:T(8,128)(2,1)S(1)} %collective-permute-done.refs_3_.refs_2_), channel_id=1, source_target_pairs={{0,2},{2,0},{1,3},{3,1},{4,6},{6,4},{5,7},{7,5},{8,10},{10,8},{9,1... | collective-permute-start | bytes 196616 | tf_op jit(solution)/shard_map/ppermute | solution.py:227
  13.3 4.6 %collective-permute-start.7 = (bf16[64,512]{1,0:T(8,128)(2,1)S(1)}, bf16[64,512]{1,0:T(8,128)(2,1)S(1)}, u32[]{:S(2)}, u32[]{:S(2)}) collective-permute-start(bf16[64,512]{1,0:T(8,128)(2,1)S(1)} %shard_map.42.refs_6_), channel_id=1, source_target_pairs={{0,2},{2,0},{1,3},{3,1},{4,6},{6,4},{5,7},{7,5},{8,10},{10,8},{9,1... | collective-permute-start | bytes 196616 | tf_op jit(solution)/shard_map/ppermute | solution.py:227
  15.8 4.3 %collective-permute-start.4 = (bf16[64,512]{1,0:T(8,128)(2,1)S(1)}, bf16[64,512]{1,0:T(8,128)(2,1)S(1)}, u32[]{:S(2)}, u32[]{:S(2)}) collective-permute-start(bf16[64,512]{1,0:T(8,128)(2,1)S(1)} %shard_map.41.refs_0_), channel_id=1, source_target_pairs={{0,2},{2,0},{1,3},{3,1},{4,6},{6,4},{5,7},{7,5},{8,10},{10,8},{9,1... | collective-permute-start | bytes 196616 | tf_op jit(solution)/shard_map/ppermute | solution.py:227
  17.3 4.3 %collective-permute-start.3 = (bf16[64,512]{1,0:T(8,128)(2,1)S(1)}, bf16[64,512]{1,0:T(8,128)(2,1)S(1)}, u32[]{:S(2)}, u32[]{:S(2)}) collective-permute-start(bf16[64,512]{1,0:T(8,128)(2,1)S(1)} %shard_map.40), channel_id=1, source_target_pairs={{0,4},{4,0},{8,12},{12,8},{1,5},{5,1},{9,13},{13,9},{2,6},{6,2},{1... | collective-permute-start | bytes 196616 | tf_op jit(solution)/shard_map/ppermute | solution.py:224
  21.6 5.7 %collective-permute-start.8 = (bf16[192,512]{1,0:T(8,128)(2,1)S(1)}, bf16[192,512]{1,0:T(8,128)(2,1)S(1)}, u32[]{:S(2)}, u32[]{:S(2)}) collective-permute-start(bf16[192,512]{1,0:T(8,128)(2,1)S(1)} %shard_map.44.refs_1_), channel_id=1, source_target_pairs={{0,2},{2,0},{1,3},{3,1},{4,6},{6,4},{5,7},{7,5},{8,10},{10,8},{9,1... | collective-permute-start | bytes 589832 | tf_op jit(solution)/shard_map/ppermute | solution.py:227
  22.2 6.1 %collective-permute-start.9 = (bf16[64,512]{1,0:T(8,128)(2,1)S(1)}, bf16[64,512]{1,0:T(8,128)(2,1)S(1)}, u32[]{:S(2)}, u32[]{:S(2)}) collective-permute-start(bf16[64,512]{1,0:T(8,128)(2,1)S(1)} %get-tuple-element.25), channel_id=1, source_target_pairs={{0,12},{4,8},{8,4},{12,0},{1,13},{5,9},{9,5},{13,1},{2,14},{6,10},... | collective-permute-start | bytes 196616 | tf_op jit(solution)/shard_map/ppermute | solution.py:224
  24.3 5.4 %collective-permute-start.10 = (bf16[64,512]{1,0:T(8,128)(2,1)S(1)}, bf16[64,512]{1,0:T(8,128)(2,1)S(1)}, u32[]{:S(2)}, u32[]{:S(2)}) collective-permute-start(bf16[64,512]{1,0:T(8,128)(2,1)S(1)} %get-tuple-element.26), channel_id=1, source_target_pairs={{0,8},{4,12},{8,0},{12,4},{1,9},{5,13},{9,1},{13,5},{2,10},{6,14},... | collective-permute-start | bytes 196616 | tf_op jit(solution)/shard_map/ppermute | solution.py:224
  24.3 5.4 %collective-permute-start.11 = (bf16[64,512]{1,0:T(8,128)(2,1)S(1)}, bf16[64,512]{1,0:T(8,128)(2,1)S(1)}, u32[]{:S(2)}, u32[]{:S(2)}) collective-permute-start(bf16[64,512]{1,0:T(8,128)(2,1)S(1)} %get-tuple-element.27), channel_id=1, source_target_pairs={{0,4},{4,0},{8,12},{12,8},{1,5},{5,1},{9,13},{13,9},{2,6},{6,2},{1... | collective-permute-start | bytes 196616 | tf_op jit(solution)/shard_map/ppermute | solution.py:224
  29.7 1.8 %copy-start.3 = (bf16[64,512]{1,0:T(8,128)(2,1)S(1)}, bf16[64,512]{1,0:T(8,128)(2,1)}, u32[]{:S(2)}) copy-start(bf16[64,512]{1,0:T(8,128)(2,1)} %refs_3_.1) | copy-start | bytes 196612
  29.8 1.7 %collective-permute-start.12 = (f32[144,512]{1,0:T(8,128)S(1)}, f32[144,512]{1,0:T(8,128)S(1)}, u32[]{:S(2)}, u32[]{:S(2)}) collective-permute-start(f32[144,512]{1,0:T(8,128)S(1)} %get-tuple-element.28.refs_0_), channel_id=1, source_target_pairs={{0,1},{1,0},{2,3},{3,2},{4,5},{5,4},{6,7},{7,6},{8,9},{9,8},{10,11... | collective-permute-start | bytes 884744 | tf_op jit(solution)/shard_map/ppermute | solution.py:230
